TPU v7x, 256 devices: a whole 4x4x8 slice. The times are simulated.
256 devices in a mesh: row: 8 (over x, y_hi), col: 4 (over y_lo, core), depth: 8 (over z).
Axes of the slice: x: 4, y: 4 (y_hi: 2, y_lo: 2; y = y_hi * 2 + y_lo), z: 8, core: 2. Of those that a mesh axis runs over, the one named last changes fastest.
Arguments:
- cotangent: bfloat16 [2048, 24576], P(('depth', 'row'), 'col'), may hold values from -8 to 8
- activations: bfloat16 [2048, 6144], P('depth', ('row', 'col')), may hold values from -8 to 8
- weight: bfloat16 [24576, 6144], P(('col', 'depth'), 'row'), may hold values from -0.0390625 to 0.0390625
- row_prev: float32 [24576], P(('col', 'depth')), as said below
- col_prev: float32 [6144], P('row'), as said below
Outputs:
- input_grad: bfloat16 [2048, 6144], P('depth', ('row', 'col'))
- update: float32 [24576, 6144], P(('col', 'depth'), 'row')
Inputs may be any that keep to these rules, and one draw needn't show every extreme that they name: `row_prev`: positive. `col_prev`: positive.
All inputs are finite; a program needn't handle non-finite values.
Results may differ from a plain program's by a relative error of at most 0.001.
Values may be sent and summed in bfloat16 or wider, within the bound.
No kernel may reach another device: no remote copies, remote signals or barrier semaphores. Data moves between devices by JAX's collectives and lax.ppermute only.
A program may use at most 128 MiB of HBM per device.

v0:
```python
import jax
import jax.numpy as jnp
from jax import lax
from jax.sharding import PartitionSpec as P

D = 6144
FF = 24576


epsilon = 1e-30
decay_rate = 0.9


def body(cotangent, activations, weight, row_prev, col_prev):
    cot_rows = lax.all_gather(cotangent, "row", axis=0, tiled=True)
    act_cols = lax.all_gather(activations, "col", axis=1, tiled=True)
    columns = cot_rows
    summed = jnp.dot(
        columns,
        lax.all_gather(weight, "depth", axis=0, tiled=True),
        preferred_element_type=jnp.float32,
    )
    columns = cot_rows
    gradient = lax.psum_scatter(
        lax.dot_general(
            columns, act_cols, (((0,), (0,)), ((), ())), preferred_element_type=jnp.float32
        ),
        "depth",
        scatter_dimension=0,
        tiled=True,
    )
    input_grad = lax.psum_scatter(summed, "col", scatter_dimension=1, tiled=True).astype(
        jnp.bfloat16
    )
    square = gradient * gradient + epsilon
    row_sums = lax.psum(jnp.sum(square, axis=1), "row")
    row_stats = decay_rate * row_prev + (1.0 - decay_rate) * (row_sums / D)
    col_sums, row_total = lax.psum((jnp.sum(square, axis=0), jnp.sum(row_stats)), ("col", "depth"))
    col_stats = decay_rate * col_prev + (1.0 - decay_rate) * (col_sums / FF)
    row_mean = row_total / FF
    unclipped = gradient * lax.rsqrt(row_stats[:, None] * col_stats[None, :] / row_mean)
    squares_total = lax.psum(jnp.sum(unclipped * unclipped), ("row", "col", "depth"))
    root_mean = jnp.sqrt(squares_total / (FF * D))
    update = unclipped / jnp.maximum(1.0, root_mean)
    return (input_grad, update)


def solution(mesh):
    return jax.shard_map(
        body,
        mesh=mesh,
        in_specs=(
            P(("depth", "row"), "col"),
            P("depth", ("row", "col")),
            P(("col", "depth"), "row"),
            P(("col", "depth")),
            P("row"),
        ),
        out_specs=(P("depth", ("row", "col")), P(("col", "depth"), "row")),
        check_vma=False,
    )
```

profile of v0, /device:TPU:4, one launch (start us, length us, event | category | flops | bytes accessed | tf_op | source)
XLA Modules:
  0.0 547.1 jit_solution(13146661916266332417)
XLA Ops:
  7.2 0.0 all-gather.3.cloned.1.call-start
  7.2 0.7 all-gather.3.cloned.1.call-update
  7.9 0.0 all-gather.5.cloned.1.call-start
  7.9 0.7 all-gather.5.cloned.1.call-update
  8.6 0.0 reduce-scatter.5.cloned.1.call-start
  8.7 6.8 %all_gather.11 = bf16[256,768]{0,1:T(8,128)(2,1)S(1)} all-gather(bf16[256,192]{0,1:T(8,128)(2,1)} %param.6), channel_id=1, replica_groups=mesh['row'=8,'col'=4,'depth'=8] {'col'}, dimensions={1}, use_global_device_ids=true | all-gather | bytes 491520 | tf_op jit(solution)/shard_map/all_gather | solution.py:16
  15.5 64.8 %all-gather.3.cloned.1.call-done = bf16[256,6144]{1,0:T(8,128)(2,1)} async-done(((bf16[32,6144]{1,0:T(8,128)(2,1)}), bf16[256,6144]{1,0:T(8,128)(2,1)}) %all-gather.3.cloned.1.call-update) | async-done | bytes 3145744 | tf_op jit(solution)/shard_map/all_gather | solution.py:15
  80.3 11.0 %fusion.4 = f32[6144,768]{1,0:T(8,128)} fusion(bf16[256,6144]{1,0:T(8,128)(2,1)} %all-gather.3.cloned.1.call-done, bf16[256,768]{0,1:T(8,128)(2,1)S(1)} %all_gather.11), kind=kOutput, calls=%fused_computation.10 | convolution fusion | flops 2415919104 | bytes 22413312 | tf_op jit(solution)/shard_map/dot_general | solution.py:25
  91.3 0.0 reduce-scatter.5.cloned.1.call-update
  91.3 0.0 reduce-scatter.3.cloned.1.call-start
  91.4 94.7 %all-gather.5.cloned.1.call-done = bf16[6144,768]{1,0:T(8,128)(2,1)} async-done(((bf16[768,768]{1,0:T(8,128)(2,1)}), bf16[6144,768]{1,0:T(8,128)(2,1)}) %all-gather.5.cloned.1.call-update) | async-done | bytes 9437200 | tf_op jit(solution)/shard_map/all_gather | solution.py:20
  186.0 0.0 copy-done.1
  186.0 8.4 %fusion.3 = f32[256,768]{0,1:T(8,128)} fusion(bf16[256,6144]{1,0:T(8,128)(2,1)S(1)} %copy-done.1, bf16[6144,768]{1,0:T(8,128)(2,1)} %all-gather.5.cloned.1.call-done), kind=kOutput, calls=%fused_computation.9 | convolution fusion | flops 2415919104 | bytes 13369344 | tf_op jit(solution)/shard_map/dot_general | solution.py:18
  194.4 0.0 reduce-scatter.3.cloned.1.call-update
  194.5 186.1 %reduce-scatter.5.cloned.1.call-done = f32[768,768]{1,0:T(8,128)} async-done(((f32[6144,768]{1,0:T(8,128)}), f32[768,768]{1,0:T(8,128)}) %reduce-scatter.5.cloned.1.call-update) | async-done | bytes 2359312 | tf_op jit(solution)/shard_map/reduce_scatter | solution.py:24
  380.6 2.3 fusion
  382.8 20.0 %psum.28 = f32[768]{0:T(1024)S(1)} all-reduce(f32[768]{0:T(1024)S(1)} %get-tuple-element.3), channel_id=1, replica_groups=mesh['row'=8,'col'=4,'depth'=8] {'row'}, use_global_device_ids=true, to_apply=%region_3.0 | all-reduce | flops 768 | bytes 6144 | tf_op jit(solution)/shard_map/psum | solution.py:36
  402.8 0.6 fusion.2
  403.4 55.4 %all-reduce = (f32[]{:T(128)}, f32[768]{0:T(1024)S(1)}) all-reduce(f32[]{:T(128)} %get-tuple-element.6, f32[768]{0:T(1024)S(1)} %get-tuple-element.2), channel_id=1, replica_groups=mesh['row'=8,'col'=4,'depth'=8] {'col','depth'}, use_global_device_ids=true, to_apply=%region_7.0 | all-reduce | flops 769 | bytes 6152 | tf_op jit(solution)/shard_map/psum | solution.py:38
  459.5 0.0 copy-done
  459.5 1.7 multiply_reduce_fusion
  461.2 1.6 convert_element_type.3
  462.8 75.2 %psum.31 = f32[]{:T(128)} all-reduce(f32[]{:T(128)} %multiply_reduce_fusion), channel_id=1, replica_groups=mesh['row'=8,'col'=4,'depth'=8] {'row','col','depth'}, use_global_device_ids=true, to_apply=%region_9.0 | all-reduce | flops 1 | bytes 8 | tf_op jit(solution)/shard_map/psum | solution.py:42
  538.7 1.9 broadcast_divide_fusion
  (8 shorter events, 0.0 us)
Async XLA Ops:
  7.2 73.1 %all-gather.3.cloned.1.call-start = ((), (), s32[]{:S(2)}) async-start(), calls=%async_computation.2 | async-start | bytes 3538944 | tf_op jit(solution)/shard_map/all_gather | solution.py:15
  7.9 178.1 %all-gather.5.cloned.1.call-start = ((), (), s32[]{:S(2)}) async-start(), calls=%async_computation.3 | async-start | bytes 10616832 | tf_op jit(solution)/shard_map/all_gather | solution.py:20
  8.6 371.9 %reduce-scatter.5.cloned.1.call-start = ((), (), s32[]{:S(2)}) async-start(), calls=%async_computation.5 | async-start | bytes 21233664 | tf_op jit(solution)/shard_map/reduce_scatter | solution.py:24
  91.3 94.7 %copy-start.1 = (bf16[256,6144]{1,0:T(8,128)(2,1)S(1)}, bf16[256,6144]{1,0:T(8,128)(2,1)}, u32[]{:S(2)}) copy-start(bf16[256,6144]{1,0:T(8,128)(2,1)} %all-gather.3.cloned.1.call-done) | copy-start | bytes 9437188
  91.3 369.8 %reduce-scatter.3.cloned.1.call-start = ((), (), s32[]{:S(2)}) async-start(), calls=%async_computation.4 | async-start | bytes 983040 | tf_op jit(solution)/shard_map/reduce_scatter | solution.py:32
  194.4 208.3 %copy-start.2 = (f32[768]{0:T(1024)S(1)}, f32[768]{0:T(1024)}, u32[]{:S(2)}) copy-start(f32[768]{0:T(1024)} %param.8) | copy-start | bytes 9220
  194.4 265.0 %copy-start.3 = (f32[768]{0:T(1024)S(1)}, f32[768]{0:T(1024)}, u32[]{:S(2)}) copy-start(f32[768]{0:T(1024)} %param.9) | copy-start | bytes 9220
  380.6 78.9 %copy-start = (f32[768,768]{1,0:T(8,128)S(1)}, f32[768,768]{1,0:T(8,128)}, u32[]{:S(2)}) copy-start(f32[768,768]{1,0:T(8,128)} %reduce-scatter.5.cloned.1.call-done) | copy-start | bytes 7077892
Sparse Core Ops, SparseCore 0:
  10.6 69.6 all-gather.2
  82.1 103.9 all-gather.4
  188.7 191.8 reduce-scatter.4
  383.5 20.5 reduce-scatter.2
where the time goes:
time: 550 us; the launch traced here: 547 us
  waiting for transfers between devices  347 us (63%)
  blocking collectives  157 us (29%)
  matrix products  19.4 us (4%)
  between operations  15.1 us (3%)
  other arithmetic  7.98 us (1%)
    reduce_scatter x1, waiting for transfers between devices, body(): lax.psum_scatter(lax.dot_general(columns, act_cols, (((0,), (0,)), ((), (...  186 us
    all_gather x1, waiting for transfers between devices, body(): lax.all_gather(weight, 'depth', axis=0, tiled=True)  94.7 us
    psum x1, blocking collectives, body(): lax.psum(jnp.sum(unclipped * unclipped), ('row', 'col', 'depth'))  75.2 us
    all_gather x1, waiting for transfers between devices, body(): cot_rows = lax.all_gather(cotangent, 'row', axis=0, tiled=True)  64.8 us
    psum x1, blocking collectives, body(): lax.psum((jnp.sum(square, axis=0), jnp.sum(row_stats)), ('col', 'depth'))  55.4 us
    psum x1, blocking collectives, body(): row_sums = lax.psum(jnp.sum(square, axis=1), 'row')  20 us
    dot_general x1, matrix products, body(): lax.dot_general(columns, act_cols, (((0,), (0,)), ((), ())), preferred_el...  11 us
  transfers between devices with their start and end apart: 4, of which 3 were waited for; matrix products, arithmetic and copies ran while one was open for 4% of the time, Pallas kernels for 0%

commit v1 on v0

v1 whole, which is shorter than its diff:
```python
import jax
import jax.numpy as jnp
from jax import lax
from jax.experimental import pallas as pl
from jax.experimental.pallas import tpu as pltpu
from jax.sharding import Mesh
from jax.sharding import PartitionSpec as P

D = 6144
FF = 24576
HALF = 384

epsilon = 1e-30
decay_rate = 0.9


def exchange(value, axis, size, bit):
    return lax.ppermute(value, axis, [(i, i ^ bit) for i in range(size)])


def shift(value, axis, size, step):
    return lax.ppermute(value, axis, [(i, (i + step) % size) for i in range(size)])


def total(value, axis, size):
    bit = 1
    while bit < size:
        value = value + exchange(value, axis, size, bit)
        bit *= 2
    return value


def group_kernel(first, rows_ref, cores_ref, *refs):
    cots, owns, recvs = refs[0:4], refs[4:8], refs[8:12]
    keep_ref, send_ref = refs[12:14]
    if first:
        before_refs, outs = None, refs[14:]
    else:
        before_refs, outs = refs[14:16], refs[16:]
    grad_own, grad_recv, part_keep, part_send = outs
    cot = jnp.concatenate([c[...].reshape(256, 768) for c in cots], axis=0)
    for position, (acts, out) in enumerate(((owns, grad_own), (recvs, grad_recv))):
        act = jnp.concatenate([a[...].reshape(256, HALF) for a in acts], axis=0)
        term = lax.dot_general(cot, act, (((0,), (0,)), ((), ())), preferred_element_type=jnp.float32)
        out[...] = term if first else before_refs[position][...] + term
    for weight_ref, out in ((keep_ref, part_keep), (send_ref, part_send)):
        for j in range(4):
            part = jnp.dot(
                cots[j][...].reshape(256, 768), weight_ref[...], preferred_element_type=jnp.float32
            )
            out[:, j] = part.reshape(8, 32, HALF)


def group_call(rows, cores, cots, own, recv, keep, send, before=None):
    first = before is None
    whole = lambda shape: pl.BlockSpec(shape, lambda i, rows, cores: (0,) * len(shape))
    act_spec = lambda j: pl.BlockSpec((8, None, 32, HALF), lambda i, rows, cores: (0, rows[j], 0, 0))
    in_specs = [whole((8, 32, 768))] * 4
    in_specs += [act_spec(j) for j in range(4)] * 2
    in_specs += [whole((768, HALF))] * 2
    operands = list(cots) + [own] * 4 + [recv] * 4 + [keep, send]
    if not first:
        in_specs += [whole((768, HALF))] * 2
        operands += list(before)
    f32 = jnp.float32
    return pl.pallas_call(
        lambda *refs: group_kernel(first, *refs),
        grid_spec=pltpu.PrefetchScalarGridSpec(
            num_scalar_prefetch=2,
            grid=(1,),
            in_specs=in_specs,
            out_specs=[whole((768, HALF))] * 2 + [whole((8, 4, 32, HALF))] * 2,
        ),
        out_shape=[jax.ShapeDtypeStruct((768, HALF), f32)] * 2
        + [jax.ShapeDtypeStruct((8, 4, 32, HALF), f32)] * 2,
        compiler_params=pltpu.CompilerParams(vmem_limit_bytes=48 * 1024 * 1024),
        cost_estimate=pl.CostEstimate(
            flops=4 * 1024 * 768 * 768, bytes_accessed=14 * 1024 * 1024, transcendentals=0
        ),
    )(rows, cores, *operands)


def body(cotangent, activations, weight, row_prev, col_prev):
    x, yh, core = lax.axis_index("x"), lax.axis_index("yh"), lax.axis_index("core")
    yl = lax.axis_index("yl")

    own_cot = lax.all_to_all(cotangent, "z", 1, 0, tiled=True).reshape(8, 32, 768)
    other_cot = exchange(own_cot, "yh", 2, 1)
    right_cot = shift(own_cot, "x", 4, 1)
    left_cot = shift(own_cot, "x", 4, -1)
    far_cot = shift(own_cot, "x", 4, 2)
    other_right = shift(other_cot, "x", 4, 1)
    other_left = shift(other_cot, "x", 4, -1)
    other_far = exchange(far_cot, "yh", 2, 1)
    right, left, far = (x + 3) % 4, (x + 1) % 4, (x + 2) % 4
    rows_first = jnp.stack([x * 2 + yh, right * 2 + yh, left * 2 + yh, x * 2 + 1 - yh]).astype(jnp.int32)
    rows_second = jnp.stack(
        [far * 2 + yh, right * 2 + 1 - yh, left * 2 + 1 - yh, far * 2 + 1 - yh]
    ).astype(jnp.int32)
    cores = jnp.stack([core, 1 - core]).astype(jnp.int32)

    act_cols = lax.all_gather(activations, ("yl", "core"), axis=1, tiled=True)
    act_half = lax.dynamic_slice_in_dim(act_cols, core * HALF, HALF, 1)
    act_own = lax.all_gather(act_half, "z", axis=0, tiled=True).reshape(8, 8, 32, HALF)
    act_recv = exchange(act_own, "core", 2, 1)

    by_core = weight.reshape(768, 2, 2, 192)
    even = by_core[:, :, 0].reshape(768, HALF)
    odd = by_core[:, :, 1].reshape(768, HALF)
    keep = jnp.where(core == 0, even, odd)
    send = jnp.where(core == 0, odd, even)

    g_own, g_recv, keep_1, send_1 = group_call(
        rows_first, cores, [own_cot, right_cot, left_cot, other_cot], act_own, act_recv, keep, send
    )
    g_own, g_recv, keep_2, send_2 = group_call(
        rows_second,
        cores,
        [far_cot, other_right, other_left, other_far],
        act_own,
        act_recv,
        keep,
        send,
        (g_own, g_recv),
    )
    gradient = jnp.where(
        core == 0,
        jnp.concatenate([g_own, g_recv], axis=1),
        jnp.concatenate([g_recv, g_own], axis=1),
    )

    pieces = []
    for kept, sent in ((keep_1, send_1), (keep_2, send_2)):
        summed = kept + exchange(sent, "core", 2, 1)
        pieces.append(lax.psum_scatter(summed, "z", scatter_dimension=0, tiled=True).reshape(4, 32, HALF))
    summed = jnp.concatenate(pieces, axis=0)
    low, high = summed[:, :, :192], summed[:, :, 192:]
    mine = jnp.where(yl == 0, low, high)
    theirs = jnp.where(yl == 0, high, low)
    mine = (mine + exchange(theirs, "yl", 2, 1)).astype(jnp.bfloat16)
    rows = jnp.concatenate([rows_first, rows_second])
    input_grad = jnp.zeros((8, 32, 192), jnp.bfloat16)
    for j in range(8):
        input_grad = lax.dynamic_update_slice(input_grad, mine[j : j + 1], (rows[j], 0, 0))
    input_grad = input_grad.reshape(256, 192)

    square = gradient * gradient + epsilon
    row_sums = total(total(jnp.sum(square, axis=1), "x", 4), "yh", 2)
    row_stats = decay_rate * row_prev + (1.0 - decay_rate) * (row_sums / D)
    scaled = gradient * lax.rsqrt(row_stats)[:, None]
    sums = jnp.concatenate(
        [
            jnp.sum(square, axis=0),
            jnp.sum(scaled * scaled, axis=0),
            jnp.broadcast_to(jnp.sum(row_stats), (128,)),
        ]
    )
    sums = total(total(total(sums, "core", 2), "yl", 2), "z", 8)
    col_sums, scaled_sums, row_total = sums[:768], sums[768:1536], sums[1536]
    col_stats = decay_rate * col_prev + (1.0 - decay_rate) * (col_sums / FF)
    row_mean = row_total / FF
    part = jnp.sum(scaled_sums * row_mean / col_stats)
    squares_total = total(total(jnp.broadcast_to(part, (128,)), "x", 4), "yh", 2)[0]
    root_mean = jnp.sqrt(squares_total / (FF * D))
    unclipped = gradient * lax.rsqrt(row_stats[:, None] * col_stats[None, :] / row_mean)
    update = unclipped / jnp.maximum(1.0, root_mean)
    return (input_grad, update)


def solution(mesh):
    fine = Mesh(mesh.devices.reshape(4, 2, 2, 2, 8), ("x", "yh", "yl", "core", "z"))
    row, col = ("x", "yh"), ("yl", "core")
    return jax.shard_map(
        body,
        mesh=fine,
        in_specs=(
            P(("z",) + row, col),
            P("z", row + col),
            P(col + ("z",), row),
            P(col + ("z",)),
            P(row),
        ),
        out_specs=(P("z", row + col), P(col + ("z",), row)),
        check_vma=False,
    )
```

time: 550 us -> 231 us (0.42)
  waiting for transfers between devices: 347 us -> 138 us
  blocking collectives: 157 us -> 6.89 us
  starting transfers between devices: 0.16 us -> 22.7 us
  matrix products: 19.4 us -> 0 us
  local copies, waits for them, and re-layouts: 0.01 us -> 18.9 us
  Pallas kernels: 0 us -> 15 us
  other arithmetic: 7.98 us -> 13.7 us
    reduce_scatter x2, waiting for transfers between devices: 186 us -> 0.04 us  [body(): lax.psum_scatter(summed, 'z', scatter_dimension=0, tiled=True)]
    psum x3 -> x0, blocking collectives: 151 us -> none  [the longest x1 75.2 us: body(): lax.psum(jnp.sum(unclipped * unclipped), ('row', 'col', 'depth'))]
    all_gather x2 -> x1, waiting for transfers between devices: 159 us -> 46.5 us  [body(): lax.all_gather(act_half, 'z', axis=0, tiled=True).reshape(8, 8, 32, HALF)]
    ppermute x0 -> x22, waiting for transfers between devices: none -> 76.5 us  [the longest x17 58.6 us: exchange(): return lax.ppermute(value, axis, [(i, i ^ bit) for i in range(size)])]
    dot_general x2 -> x0, matrix products: 19.4 us -> none  [the longest x1 11 us: body(): lax.dot_general(columns, act_cols, (((0,), (0,)), ((), ())), preferred_el...]
    ppermute x0 -> x22, starting transfers between devices: none -> 18.1 us  [the longest x17 12.8 us: exchange(): return lax.ppermute(value, axis, [(i, i ^ bit) for i in range(size)])]
    pallas_call x0 -> x2, Pallas kernels: none -> 15 us  [group_call(): pl.pallas_call(lambda *refs: group_kernel(first, *refs), grid_spec=pltpu....]
    all_to_all x0 -> x1, waiting for transfers between devices: none -> 14.6 us  [body(): lax.all_to_all(cotangent, 'z', 1, 0, tiled=True).reshape(8, 32, 768)]
  transfers between devices with their start and end apart: 4 -> 26, of which waited for: 3 -> 22; matrix products, arithmetic and copies ran while one was open for 4% -> 6% of each run, Pallas kernels for 0% -> 3%
where the time goes in v1:
time: 231 us; the launch traced here: 230 us
  waiting for transfers between devices  138 us (60%)
  starting transfers between devices  22.7 us (10%)
  local copies, waits for them, and re-layouts  18.9 us (8%)
  Pallas kernels  15 us (6%)
  between operations  14.8 us (6%)
  other arithmetic  13.7 us (6%)
  blocking collectives  6.89 us (3%)
    ppermute x17, waiting for transfers between devices, exchange(): return lax.ppermute(value, axis, [(i, i ^ bit) for i in range(size)])  58.6 us
    all_gather x1, waiting for transfers between devices, body(): lax.all_gather(act_half, 'z', axis=0, tiled=True).reshape(8, 8, 32, HALF)  46.5 us
    ppermute x5, waiting for transfers between devices, shift(): lax.ppermute(value, axis, [(i, (i + step) % size) for i in range(size)])  17.9 us
    pallas_call x2, Pallas kernels, group_call(): pl.pallas_call(lambda *refs: group_kernel(first, *refs), grid_spec=pltpu....  15 us
    all_to_all x1, waiting for transfers between devices, body(): lax.all_to_all(cotangent, 'z', 1, 0, tiled=True).reshape(8, 32, 768)  14.6 us
    ppermute x17, starting transfers between devices, exchange(): return lax.ppermute(value, axis, [(i, i ^ bit) for i in range(size)])  12.8 us
    unnamed x38, local copies, waits for them, and re-layouts  11.3 us
    all_gather x1, blocking collectives, body(): act_cols = lax.all_gather(activations, ('yl', 'core'), axis=1, tiled=True)  6.89 us
  transfers between devices with their start and end apart: 26, of which 22 were waited for; matrix products, arithmetic and copies ran while one was open for 6% of the time, Pallas kernels for 3%

profile of v1, /device:TPU:4, one launch (start us, length us, event | category | flops | bytes accessed | tf_op | source)
XLA Modules:
  0.0 229.7 jit_solution(2958411524129719335)
XLA Ops:
  7.2 6.9 %all_gather.6 = bf16[256,768]{0,1:T(8,128)(2,1)S(1)} all-gather(bf16[256,192]{0,1:T(8,128)(2,1)} %param.6), channel_id=1, replica_groups=mesh['x'=4,'yh'=2,'yl'=2,'core'=2,'z'=8] {'yl','core'}, dimensions={1}, use_global_device_ids=true | all-gather | bytes 491520 | tf_op jit(solution)/shard_map/all_gather | solution.py:102
  14.8 46.5 %all-gather.2.cloned.1.call-done = bf16[2048,384]{0,1:T(8,128)(2,1)} async-done(((bf16[256,384]{0,1:T(8,128)(2,1)}), bf16[2048,384]{0,1:T(8,128)(2,1)}) %all-gather.2.cloned.1.call-update) | async-done | bytes 1572880 | tf_op jit(solution)/shard_map/all_gather | solution.py:104
  61.4 2.6 %copy.13 = bf16[2048,384]{1,0:T(8,128)(2,1)} copy(bf16[2048,384]{0,1:T(8,128)(2,1)} %all-gather.2.cloned.1.call-done) | data formatting | bytes 3145728 | tf_op jit(solution)/shard_map/all_gather | solution.py:104
  64.7 4.5 %all-to-all-start = ((bf16[32,8,768]{2,0,1:T(8,128)(2,1)}), bf16[32,8,768]{2,0,1:T(8,128)(2,1)S(1)}, u32[]{:S(2)}, u32[]{:S(2)}) async-start(bf16[32,8,768]{2,0,1:T(8,128)(2,1)} %bitcast.23), calls=%async_computation | async-start | bytes 786432 | tf_op jit(solution)/shard_map/all_to_all | solution.py:87
  69.9 14.6 %all-to-all-done = bf16[32,8,768]{2,0,1:T(8,128)(2,1)S(1)} async-done(((bf16[32,8,768]{2,0,1:T(8,128)(2,1)}), bf16[32,8,768]{2,0,1:T(8,128)(2,1)S(1)}, u32[]{:S(2)}, u32[]{:S(2)}) %all-to-all-start) | async-done | bytes 393248 | tf_op jit(solution)/shard_map/all_to_all | solution.py:87
  84.5 3.0 %collective-permute-start.2 = (bf16[8,32,768]{2,1,0:T(8,128)(2,1)S(1)}, bf16[8,32,768]{2,1,0:T(8,128)(2,1)S(1)}, u32[]{:S(2)}, u32[]{:S(2)}) collective-permute-start(bf16[8,32,768]{2,1,0:T(8,128)(2,1)S(1)} %bitcast.25), channel_id=1, source_target_pairs={{0,32},{32,0},{1,33},{33,1},{2,34},{34,2},{3,35},{35,3},{4,36},{36... | collective-permute-start | bytes 1179656 | tf_op jit(solution)/shard_map/ppermute | solution.py:18
  92.3 4.8 %collective-permute-done.2.refs_5_ = bf16[8,32,768]{2,1,0:T(8,128)(2,1)S(1)} collective-permute-done((bf16[8,32,768]{2,1,0:T(8,128)(2,1)S(1)}, bf16[8,32,768]{2,1,0:T(8,128)(2,1)S(1)}, u32[]{:S(2)}, u32[]{:S(2)}) %collective-permute-start.2) | collective-permute-done | bytes 393248 | tf_op jit(solution)/shard_map/ppermute | solution.py:18
  101.0 7.0 %shard_map.68 = (f32[768,384]{1,0:T(8,128)S(1)}, f32[768,384]{1,0:T(8,128)S(1)}, f32[8,4,32,384]{3,2,1,0:T(8,128)}, f32[8,4,32,384]{3,2,1,0:T(8,128)}) custom-call(s32[4]{0:T(128)S(1)} %pad_add_fusion.refs_0_, s32[2]{0:T(128)S(1)} %pad_add_fusion.1.refs_1_, bf16[8,32,768]{2,1,0:T(8,128)(2,1)S(1)} %bitcast.28, ...), custom_call_target="tpu_custom_call" | custom-call | flops 2415919104 | bytes 14680064 | tf_op jit(solution)/shard_map/pallas_call | solution.py:66
  109.1 3.6 %collective-permute-done.4 = f32[8,4,32,384]{3,2,1,0:T(8,128)S(1)} collective-permute-done((f32[8,4,32,384]{3,2,1,0:T(8,128)}, f32[8,4,32,384]{3,2,1,0:T(8,128)S(1)}, u32[]{:S(2)}, u32[]{:S(2)}) %collective-permute-start.4) | collective-permute-done | bytes 1572896 | tf_op jit(solution)/shard_map/ppermute | solution.py:18
  112.7 2.8 %add.137 = f32[8,4,32,384]{3,2,1,0:T(8,128)} add(f32[8,4,32,384]{3,2,1,0:T(8,128)} %get-tuple-element.10, f32[8,4,32,384]{3,2,1,0:T(8,128)S(1)} %collective-permute-done.4) | non-fusion elementwise | flops 393216 | bytes 4718592 | tf_op jit(solution)/shard_map/add | solution.py:134
  119.0 10.3 %collective-permute-done.5.refs_2_ = bf16[8,32,768]{2,1,0:T(8,128)(2,1)S(1)} collective-permute-done((bf16[8,32,768]{2,1,0:T(8,128)(2,1)S(1)}, bf16[8,32,768]{2,1,0:T(8,128)(2,1)S(1)}, u32[]{:S(2)}, u32[]{:S(2)}) %collective-permute-start.5) | collective-permute-done | bytes 393248 | tf_op jit(solution)/shard_map/ppermute | solution.py:22
  131.0 5.5 %collective-permute-done.6.refs_3_ = bf16[8,32,768]{2,1,0:T(8,128)(2,1)S(1)} collective-permute-done((bf16[8,32,768]{2,1,0:T(8,128)(2,1)S(1)}, bf16[8,32,768]{2,1,0:T(8,128)(2,1)S(1)}, u32[]{:S(2)}, u32[]{:S(2)}) %collective-permute-start.6) | collective-permute-done | bytes 393248 | tf_op jit(solution)/shard_map/ppermute | solution.py:22
  145.0 7.9 %shard_map.69 = (f32[768,384]{1,0:T(8,128)S(1)}, f32[768,384]{1,0:T(8,128)S(1)}, f32[8,4,32,384]{3,2,1,0:T(8,128)}, f32[8,4,32,384]{3,2,1,0:T(8,128)}) custom-call(s32[4]{0:T(128)S(1)} %pad_add_fusion.2.refs_0_, s32[2]{0:T(128)S(1)} %pad_add_fusion.1.refs_1_, bf16[8,32,768]{2,1,0:T(8,128)(2,1)S(1)} %copy-done.3, bf16[8,32,768]{2,1,0:T(8,128)(2,1)S(1)} %copy-done.5, ...), custom_call_target="tpu_custom_call" | custom-call | flops 2415919104 | bytes 14680064 | tf_op jit(solution)/shard_map/pallas_call | solution.py:66
  152.9 3.6 %collective-permute-done.9 = f32[8,4,32,384]{3,2,1,0:T(8,128)S(1)} collective-permute-done((f32[8,4,32,384]{3,2,1,0:T(8,128)}, f32[8,4,32,384]{3,2,1,0:T(8,128)S(1)}, u32[]{:S(2)}, u32[]{:S(2)}) %collective-permute-start.9) | collective-permute-done | bytes 1572896 | tf_op jit(solution)/shard_map/ppermute | solution.py:18
  156.6 2.8 %add.144 = f32[8,4,32,384]{3,2,1,0:T(8,128)} add(f32[8,4,32,384]{3,2,1,0:T(8,128)} %get-tuple-element.14, f32[8,4,32,384]{3,2,1,0:T(8,128)S(1)} %collective-permute-done.9) | non-fusion elementwise | flops 393216 | bytes 4718592 | tf_op jit(solution)/shard_map/add | solution.py:134
  164.3 4.3 %collective-permute-done.12 = f32[768]{0:T(1024)S(1)} collective-permute-done((f32[768]{0:T(1024)S(1)}, f32[768]{0:T(1024)S(1)}, u32[]{:S(2)}, u32[]{:S(2)}) %collective-permute-start.12) | collective-permute-done | bytes 3104 | tf_op jit(solution)/shard_map/ppermute | solution.py:18
  169.5 4.2 %collective-permute-done.13 = f32[768]{0:T(1024)S(1)} collective-permute-done((f32[768]{0:T(1024)S(1)}, f32[768]{0:T(1024)S(1)}, u32[]{:S(2)}, u32[]{:S(2)}) %collective-permute-start.13) | collective-permute-done | bytes 3104 | tf_op jit(solution)/shard_map/ppermute | solution.py:18
  177.5 3.0 %collective-permute-done.15 = f32[1664]{0:T(1024)S(1)} collective-permute-done((f32[1664]{0:T(1024)S(1)}, f32[1664]{0:T(1024)S(1)}, u32[]{:S(2)}, u32[]{:S(2)}) %collective-permute-start.15) | collective-permute-done | bytes 6688 | tf_op jit(solution)/shard_map/ppermute | solution.py:18
  180.5 3.7 %collective-permute-done.16 = f32[1664]{0:T(1024)S(1)} collective-permute-done((f32[1664]{0:T(1024)S(1)}, f32[1664]{0:T(1024)S(1)}, u32[]{:S(2)}, u32[]{:S(2)}) %collective-permute-start.16) | collective-permute-done | bytes 6688 | tf_op jit(solution)/shard_map/ppermute | solution.py:18
  184.1 4.7 %collective-permute-done.17 = f32[1664]{0:T(1024)S(1)} collective-permute-done((f32[1664]{0:T(1024)S(1)}, f32[1664]{0:T(1024)S(1)}, u32[]{:S(2)}, u32[]{:S(2)}) %collective-permute-start.17) | collective-permute-done | bytes 6688 | tf_op jit(solution)/shard_map/ppermute | solution.py:18
  188.8 7.6 %collective-permute-done.18 = f32[1664]{0:T(1024)S(1)} collective-permute-done((f32[1664]{0:T(1024)S(1)}, f32[1664]{0:T(1024)S(1)}, u32[]{:S(2)}, u32[]{:S(2)}) %collective-permute-start.18) | collective-permute-done | bytes 6688 | tf_op jit(solution)/shard_map/ppermute | solution.py:18
  204.1 4.3 %collective-permute-done.20 = f32[128]{0:T(128)S(1)} collective-permute-done((f32[128]{0:T(128)S(1)}, f32[128]{0:T(128)S(1)}, u32[]{:S(2)}, u32[]{:S(2)}) %collective-permute-start.20) | collective-permute-done | bytes 544 | tf_op jit(solution)/shard_map/ppermute | solution.py:18
  210.2 4.1 %collective-permute-done.21 = f32[128]{0:T(128)S(1)} collective-permute-done((f32[128]{0:T(128)S(1)}, f32[128]{0:T(128)S(1)}, u32[]{:S(2)}, u32[]{:S(2)}) %collective-permute-start.21) | collective-permute-done | bytes 544 | tf_op jit(solution)/shard_map/ppermute | solution.py:18
  218.3 3.8 %collective-permute-done.10 = f32[8,32,192]{2,1,0:T(8,128)S(1)} collective-permute-done((f32[8,32,192]{2,1,0:T(8,128)S(1)}, f32[8,32,192]{2,1,0:T(8,128)S(1)}, u32[]{:S(2)}, u32[]{:S(2)}) %collective-permute-start.10) | collective-permute-done | bytes 196640 | tf_op jit(solution)/shard_map/ppermute | solution.py:18
  (114 shorter events, 49.0 us)
Async XLA Ops:
  7.2 54.2 %all-gather.2.cloned.1.call-start = ((), (), s32[]{:S(2)}) async-start(), calls=%async_computation.3 | async-start | bytes 1769472 | tf_op jit(solution)/shard_map/all_gather | solution.py:104
  63.9 36.0 %collective-permute-start.3 = (bf16[8,8,32,384]{3,2,1,0:T(8,128)(2,1)}, bf16[8,8,32,384]{3,2,1,0:T(8,128)(2,1)}, u32[]{:S(2)}, u32[]{:S(2)}) collective-permute-start(bf16[8,8,32,384]{3,2,1,0:T(8,128)(2,1)} %bitcast.7.refs_6_.refs_7_.refs_8_.refs_9_), channel_id=1, source_target_pairs={{0,8},{8,0},{1,9},{9,1},{2,10},{10,2},{3,11},{11,3},{4,12},{12,4},... | collective-permute-start | bytes 4718600 | tf_op jit(solution)/shard_map/ppermute | solution.py:18
  64.7 19.8 %all-to-all-start = ((bf16[32,8,768]{2,0,1:T(8,128)(2,1)}), bf16[32,8,768]{2,0,1:T(8,128)(2,1)S(1)}, u32[]{:S(2)}, u32[]{:S(2)}) async-start(bf16[32,8,768]{2,0,1:T(8,128)(2,1)} %bitcast.23), calls=%async_computation | async-start | bytes 786432 | tf_op jit(solution)/shard_map/all_to_all | solution.py:87
  69.2 145.2 %reduce-scatter.3.cloned.1.call-start = ((), (), s32[]{:S(2)}) async-start(), calls=%async_computation.4 | async-start | bytes 1769472 | tf_op jit(solution)/shard_map/reduce_scatter | solution.py:135
  84.5 12.6 %collective-permute-start.2 = (bf16[8,32,768]{2,1,0:T(8,128)(2,1)S(1)}, bf16[8,32,768]{2,1,0:T(8,128)(2,1)S(1)}, u32[]{:S(2)}, u32[]{:S(2)}) collective-permute-start(bf16[8,32,768]{2,1,0:T(8,128)(2,1)S(1)} %bitcast.25), channel_id=1, source_target_pairs={{0,32},{32,0},{1,33},{33,1},{2,34},{34,2},{3,35},{35,3},{4,36},{36... | collective-permute-start | bytes 1179656 | tf_op jit(solution)/shard_map/ppermute | solution.py:18
  87.6 10.8 %collective-permute-start = (bf16[8,32,768]{2,1,0:T(8,128)(2,1)S(1)}, bf16[8,32,768]{2,1,0:T(8,128)(2,1)S(1)}, u32[]{:S(2)}, u32[]{:S(2)}) collective-permute-start(bf16[8,32,768]{2,1,0:T(8,128)(2,1)S(1)} %bitcast.26), channel_id=1, source_target_pairs={{0,64},{64,128},{128,192},{192,0},{1,65},{65,129},{129,193},{193,1... | collective-permute-start | bytes 1179656 | tf_op jit(solution)/shard_map/ppermute | solution.py:22
  88.7 10.5 %collective-permute-start.1 = (bf16[8,32,768]{2,1,0:T(8,128)(2,1)S(1)}, bf16[8,32,768]{2,1,0:T(8,128)(2,1)S(1)}, u32[]{:S(2)}, u32[]{:S(2)}) collective-permute-start(bf16[8,32,768]{2,1,0:T(8,128)(2,1)S(1)} %bitcast.27), channel_id=1, source_target_pairs={{0,192},{64,0},{128,64},{192,128},{1,193},{65,1},{129,65},{193,129... | collective-permute-start | bytes 1179656 | tf_op jit(solution)/shard_map/ppermute | solution.py:22
  109.1 3.6 %collective-permute-start.4 = (f32[8,4,32,384]{3,2,1,0:T(8,128)}, f32[8,4,32,384]{3,2,1,0:T(8,128)S(1)}, u32[]{:S(2)}, u32[]{:S(2)}) collective-permute-start(f32[8,4,32,384]{3,2,1,0:T(8,128)} %get-tuple-element.11), channel_id=1, source_target_pairs={{0,8},{8,0},{1,9},{9,1},{2,10},{10,2},{3,11},{11,3},{4,12},{12,4},... | collective-permute-start | bytes 4718600 | tf_op jit(solution)/shard_map/ppermute | solution.py:18
  115.6 98.8 %reduce-scatter.5.cloned.1.call-start = ((), (), s32[]{:S(2)}) async-start(), calls=%async_computation.5 | async-start | bytes 1769472 | tf_op jit(solution)/shard_map/reduce_scatter | solution.py:135
  115.6 13.6 %collective-permute-start.5 = (bf16[8,32,768]{2,1,0:T(8,128)(2,1)S(1)}, bf16[8,32,768]{2,1,0:T(8,128)(2,1)S(1)}, u32[]{:S(2)}, u32[]{:S(2)}) collective-permute-start(bf16[8,32,768]{2,1,0:T(8,128)(2,1)S(1)} %bitcast.29), channel_id=1, source_target_pairs={{0,128},{64,192},{128,0},{192,64},{1,129},{65,193},{129,1},{193,65... | collective-permute-start | bytes 1179656 | tf_op jit(solution)/shard_map/ppermute | solution.py:22
  116.6 19.9 %collective-permute-start.6 = (bf16[8,32,768]{2,1,0:T(8,128)(2,1)S(1)}, bf16[8,32,768]{2,1,0:T(8,128)(2,1)S(1)}, u32[]{:S(2)}, u32[]{:S(2)}) collective-permute-start(bf16[8,32,768]{2,1,0:T(8,128)(2,1)S(1)} %collective-permute-done.2.refs_5_), channel_id=1, source_target_pairs={{0,64},{64,128},{128,192},{192,0},{1,65},{65,129},{129,193},{193,1... | collective-permute-start | bytes 1179656 | tf_op jit(solution)/shard_map/ppermute | solution.py:22
  118.6 18.6 %collective-permute-start.7 = (bf16[8,32,768]{2,1,0:T(8,128)(2,1)S(1)}, bf16[8,32,768]{2,1,0:T(8,128)(2,1)S(1)}, u32[]{:S(2)}, u32[]{:S(2)}) collective-permute-start(bf16[8,32,768]{2,1,0:T(8,128)(2,1)S(1)} %collective-permute-done.2.refs_5_), channel_id=1, source_target_pairs={{0,192},{64,0},{128,64},{192,128},{1,193},{65,1},{129,65},{193,129... | collective-permute-start | bytes 1179656 | tf_op jit(solution)/shard_map/ppermute | solution.py:22
  129.2 11.0 %collective-permute-start.8 = (bf16[8,32,768]{2,1,0:T(8,128)(2,1)S(1)}, bf16[8,32,768]{2,1,0:T(8,128)(2,1)S(1)}, u32[]{:S(2)}, u32[]{:S(2)}) collective-permute-start(bf16[8,32,768]{2,1,0:T(8,128)(2,1)S(1)} %collective-permute-done.5.refs_2_), channel_id=1, source_target_pairs={{0,32},{32,0},{1,33},{33,1},{2,34},{34,2},{3,35},{35,3},{4,36},{36... | collective-permute-start | bytes 1179656 | tf_op jit(solution)/shard_map/ppermute | solution.py:18
  159.8 3.7 %collective-permute-start.11 = (f32[768]{0:T(1024)S(1)}, f32[768]{0:T(1024)S(1)}, u32[]{:S(2)}, u32[]{:S(2)}) collective-permute-start(f32[768]{0:T(1024)S(1)} %fusion.1), channel_id=1, source_target_pairs={{0,64},{64,0},{128,192},{192,128},{1,65},{65,1},{129,193},{193,129... | collective-permute-start | bytes 9224 | tf_op jit(solution)/shard_map/ppermute | solution.py:18
  163.5 5.1 %collective-permute-start.12 = (f32[768]{0:T(1024)S(1)}, f32[768]{0:T(1024)S(1)}, u32[]{:S(2)}, u32[]{:S(2)}) collective-permute-start(f32[768]{0:T(1024)S(1)} %add.156), channel_id=1, source_target_pairs={{0,128},{64,192},{128,0},{192,64},{1,129},{65,193},{129,1},{193,65... | collective-permute-start | bytes 9224 | tf_op jit(solution)/shard_map/ppermute | solution.py:18
  168.6 5.1 %collective-permute-start.13 = (f32[768]{0:T(1024)S(1)}, f32[768]{0:T(1024)S(1)}, u32[]{:S(2)}, u32[]{:S(2)}) collective-permute-start(f32[768]{0:T(1024)S(1)} %add.157), channel_id=1, source_target_pairs={{0,32},{32,0},{1,33},{33,1},{2,34},{34,2},{3,35},{35,3},{4,36},{36... | collective-permute-start | bytes 9224 | tf_op jit(solution)/shard_map/ppermute | solution.py:18
  176.8 3.7 %collective-permute-start.15 = (f32[1664]{0:T(1024)S(1)}, f32[1664]{0:T(1024)S(1)}, u32[]{:S(2)}, u32[]{:S(2)}) collective-permute-start(f32[1664]{0:T(1024)S(1)} %fusion.7), channel_id=1, source_target_pairs={{0,16},{16,0},{1,17},{17,1},{2,18},{18,2},{3,19},{19,3},{4,20},{20... | collective-permute-start | bytes 19976 | tf_op jit(solution)/shard_map/ppermute | solution.py:18
  180.5 3.7 %collective-permute-start.16 = (f32[1664]{0:T(1024)S(1)}, f32[1664]{0:T(1024)S(1)}, u32[]{:S(2)}, u32[]{:S(2)}) collective-permute-start(f32[1664]{0:T(1024)S(1)} %add.161), channel_id=1, source_target_pairs={{0,1},{1,0},{2,3},{3,2},{4,5},{5,4},{6,7},{7,6},{8,9},{9,8},{10,11... | collective-permute-start | bytes 19976 | tf_op jit(solution)/shard_map/ppermute | solution.py:18
  184.1 4.7 %collective-permute-start.17 = (f32[1664]{0:T(1024)S(1)}, f32[1664]{0:T(1024)S(1)}, u32[]{:S(2)}, u32[]{:S(2)}) collective-permute-start(f32[1664]{0:T(1024)S(1)} %add.162), channel_id=1, source_target_pairs={{0,2},{1,3},{2,0},{3,1},{4,6},{5,7},{6,4},{7,5},{8,10},{9,11},{10,... | collective-permute-start | bytes 19976 | tf_op jit(solution)/shard_map/ppermute | solution.py:18
  188.8 7.6 %collective-permute-start.18 = (f32[1664]{0:T(1024)S(1)}, f32[1664]{0:T(1024)S(1)}, u32[]{:S(2)}, u32[]{:S(2)}) collective-permute-start(f32[1664]{0:T(1024)S(1)} %add.163), channel_id=1, source_target_pairs={{0,4},{1,5},{2,6},{3,7},{4,0},{5,1},{6,2},{7,3},{8,12},{9,13},{10,... | collective-permute-start | bytes 19976 | tf_op jit(solution)/shard_map/ppermute | solution.py:18
  198.9 3.6 %collective-permute-start.19 = (f32[128]{0:T(128)S(1)}, f32[128]{0:T(128)S(1)}, u32[]{:S(2)}, u32[]{:S(2)}) collective-permute-start(f32[128]{0:T(128)S(1)} %broadcast_in_dim.14), channel_id=1, source_target_pairs={{0,64},{64,0},{128,192},{192,128},{1,65},{65,1},{129,193},{193,129... | collective-permute-start | bytes 1544 | tf_op jit(solution)/shard_map/ppermute | solution.py:18
  203.2 5.1 %collective-permute-start.20 = (f32[128]{0:T(128)S(1)}, f32[128]{0:T(128)S(1)}, u32[]{:S(2)}, u32[]{:S(2)}) collective-permute-start(f32[128]{0:T(128)S(1)} %broadcast_add_fusion), channel_id=1, source_target_pairs={{0,128},{64,192},{128,0},{192,64},{1,129},{65,193},{129,1},{193,65... | collective-permute-start | bytes 1544 | tf_op jit(solution)/shard_map/ppermute | solution.py:18
  209.1 5.2 %collective-permute-start.21 = (f32[128]{0:T(128)S(1)}, f32[128]{0:T(128)S(1)}, u32[]{:S(2)}, u32[]{:S(2)}) collective-permute-start(f32[128]{0:T(128)S(1)} %fusion.10), channel_id=1, source_target_pairs={{0,32},{32,0},{1,33},{33,1},{2,34},{34,2},{3,35},{35,3},{4,36},{36... | collective-permute-start | bytes 1544 | tf_op jit(solution)/shard_map/ppermute | solution.py:18
  215.6 6.5 %collective-permute-start.10 = (f32[8,32,192]{2,1,0:T(8,128)S(1)}, f32[8,32,192]{2,1,0:T(8,128)S(1)}, u32[]{:S(2)}, u32[]{:S(2)}) collective-permute-start(f32[8,32,192]{2,1,0:T(8,128)S(1)} %fusion.3), channel_id=1, source_target_pairs={{0,16},{16,0},{1,17},{17,1},{2,18},{18,2},{3,19},{19,3},{4,20},{20... | collective-permute-start | bytes 589832 | tf_op jit(solution)/shard_map/ppermute | solution.py:18
  (20 other events, 196.3 us)
Sparse Core Ops, SparseCore 0:
  14.9 46.3 all-gather.1
  115.7 34.8 reduce-scatter.2
  159.5 35.0 reduce-scatter.4

commit v2 on v1

v2 whole, which is shorter than its diff:
```python
import jax
import jax.numpy as jnp
from jax import lax
from jax.experimental import pallas as pl
from jax.experimental.pallas import tpu as pltpu
from jax.sharding import Mesh
from jax.sharding import PartitionSpec as P

D = 6144
FF = 24576
HALF = 384
STEP = 2
VMEM = 56 * 1024 * 1024

epsilon = 1e-30
decay_rate = 0.9


def exchange(value, axis, size, bit):
    return lax.ppermute(value, axis, [(i, i ^ bit) for i in range(size)])


def shift(value, axis, size, step):
    return lax.ppermute(value, axis, [(i, (i + step) % size) for i in range(size)])


def total(value, axis, size):
    bit = 1
    while bit < size:
        value = value + exchange(value, axis, size, bit)
        bit *= 2
    return value


def partial_kernel(cot_0, cot_1, cot_2, cot_3, keep_ref, send_ref, part_keep, part_send):
    for weight_ref, out in ((keep_ref, part_keep), (send_ref, part_send)):
        for j, cot in enumerate((cot_0, cot_1, cot_2, cot_3)):
            part = jnp.dot(
                cot[...].reshape(256, 768), weight_ref[...], preferred_element_type=jnp.float32
            )
            out[:, j] = part.reshape(8, 32, HALF)


def partial_call(cots, keep, send):
    return pl.pallas_call(
        partial_kernel,
        out_shape=[jax.ShapeDtypeStruct((8, 4, 32, HALF), jnp.float32)] * 2,
        compiler_params=pltpu.CompilerParams(vmem_limit_bytes=VMEM),
        cost_estimate=pl.CostEstimate(
            flops=2 * 1024 * 768 * 768,
            bytes_accessed=6 * 1024 * 1024,
            transcendentals=0,
        ),
    )(*cots, keep, send)


def gradient_kernel(rows_ref, halves_ref, *refs):
    cots, acts, out_ref = refs[:8], refs[8:10], refs[10]
    step = pl.program_id(0)
    cot = jnp.concatenate([c[...].reshape(STEP * 32, 768) for c in cots], axis=0)
    for h in range(2):
        act = jnp.concatenate(
            [acts[h][:, rows_ref[j]].reshape(STEP * 32, HALF) for j in range(8)], axis=0
        )
        term = lax.dot_general(cot, act, (((0,), (0,)), ((), ())), preferred_element_type=jnp.float32)
        columns = pl.ds(pl.multiple_of(halves_ref[h] * HALF, HALF), HALF)

        @pl.when(step == 0)
        def _():
            out_ref[:, columns] = term

        @pl.when(step > 0)
        def _():
            out_ref[:, columns] += term


def gradient_call(rows, halves, cots, acts):
    return pl.pallas_call(
        gradient_kernel,
        grid_spec=pltpu.PrefetchScalarGridSpec(
            num_scalar_prefetch=2,
            grid=(8 // STEP,),
            in_specs=[pl.BlockSpec((STEP, 32, 768), lambda s, rows, halves: (s, 0, 0))] * 8
            + [pl.BlockSpec((STEP, 8, 32, HALF), lambda s, rows, halves: (s, 0, 0, 0))] * 2,
            out_specs=pl.BlockSpec((768, 768), lambda s, rows, halves: (0, 0)),
        ),
        out_shape=jax.ShapeDtypeStruct((768, 768), jnp.float32),
        compiler_params=pltpu.CompilerParams(vmem_limit_bytes=VMEM),
        cost_estimate=pl.CostEstimate(
            flops=2 * 2048 * 768 * 768, bytes_accessed=9 * 1024 * 1024, transcendentals=0
        ),
    )(rows, halves, *cots, *acts)


def body(cotangent, activations, weight, row_prev, col_prev):
    x, yh, core = lax.axis_index("x"), lax.axis_index("yh"), lax.axis_index("core")
    yl = lax.axis_index("yl")

    act_cols = lax.all_gather(activations, ("yl", "core"), axis=1, tiled=True)
    act_half = lax.dynamic_slice_in_dim(act_cols, core * HALF, HALF, 1)
    act_half, cotangent = lax.optimization_barrier((act_half, cotangent))
    act_own = lax.all_gather(act_half, "z", axis=0, tiled=True).reshape(8, 8, 32, HALF)

    own_cot = lax.all_to_all(cotangent, "z", 1, 0, tiled=True).reshape(8, 32, 768)
    own_cot, weight = lax.optimization_barrier((own_cot, weight))
    other_cot = exchange(own_cot, "yh", 2, 1)
    right_cot = shift(own_cot, "x", 4, 1)
    left_cot = shift(own_cot, "x", 4, -1)
    far_cot = shift(own_cot, "x", 4, 2)
    other_right = shift(other_cot, "x", 4, 1)
    other_left = shift(other_cot, "x", 4, -1)
    other_far = exchange(far_cot, "yh", 2, 1)
    right, left, far = (x + 3) % 4, (x + 1) % 4, (x + 2) % 4
    rows = jnp.stack([x * 2 + yh, right * 2 + yh, left * 2 + yh, far * 2 + yh])
    rows = jnp.concatenate([rows, rows + 1 - 2 * yh]).astype(jnp.int32)
    halves = jnp.stack([core, 1 - core]).astype(jnp.int32)
    first = list(lax.optimization_barrier((own_cot, right_cot, left_cot, far_cot, other_right, other_left)))[:4]
    second = [other_cot, other_right, other_left, other_far]

    by_core = weight.reshape(768, 2, 2, 192)
    even = by_core[:, :, 0].reshape(768, HALF)
    odd = by_core[:, :, 1].reshape(768, HALF)
    keep = jnp.where(core == 0, even, odd)
    send = jnp.where(core == 0, odd, even)

    keep_1, send_1 = partial_call(first, keep, send)
    other_far, act_own = lax.optimization_barrier((other_far, act_own))
    second = [other_cot, other_right, other_left, other_far]
    keep_2, send_2 = partial_call(second, keep, send)
    send_2, act_own = lax.optimization_barrier((send_2, act_own))
    sent_2, act_recv = lax.optimization_barrier(
        (exchange(send_2, "core", 2, 1), exchange(act_own, "core", 2, 1))
    )
    gradient = gradient_call(rows, halves, first + second, [act_own, act_recv])

    summed = jnp.concatenate(
        [keep_1 + exchange(send_1, "core", 2, 1), keep_2 + sent_2], axis=1
    )
    summed = lax.psum_scatter(summed, "z", scatter_dimension=0, tiled=True).reshape(8, 32, HALF)
    low, high = summed[:, :, :192], summed[:, :, 192:]
    mine = jnp.where(yl == 0, low, high)
    theirs = jnp.where(yl == 0, high, low)
    mine = (mine + exchange(theirs, "yl", 2, 1)).astype(jnp.bfloat16)
    input_grad = jnp.zeros((8, 32, 192), jnp.bfloat16)
    for j in range(8):
        input_grad = lax.dynamic_update_slice(input_grad, mine[j : j + 1], (rows[j], 0, 0))
    input_grad = input_grad.reshape(256, 192)

    square = gradient * gradient + epsilon
    row_sums = total(total(jnp.sum(square, axis=1), "x", 4), "yh", 2)
    row_stats = decay_rate * row_prev + (1.0 - decay_rate) * (row_sums / D)
    scaled = gradient * lax.rsqrt(row_stats)[:, None]
    sums = jnp.concatenate(
        [
            jnp.sum(square, axis=0),
            jnp.sum(scaled * scaled, axis=0),
            jnp.broadcast_to(jnp.sum(row_stats), (128,)),
        ]
    )
    sums = total(total(total(sums, "core", 2), "yl", 2), "z", 8)
    col_sums, scaled_sums, row_total = sums[:768], sums[768:1536], sums[1536]
    col_stats = decay_rate * col_prev + (1.0 - decay_rate) * (col_sums / FF)
    row_mean = row_total / FF
    part = jnp.sum(scaled_sums * row_mean / col_stats)
    squares_total = total(total(jnp.broadcast_to(part, (128,)), "x", 4), "yh", 2)[0]
    root_mean = jnp.sqrt(squares_total / (FF * D))
    unclipped = gradient * lax.rsqrt(row_stats[:, None] * col_stats[None, :] / row_mean)
    update = unclipped / jnp.maximum(1.0, root_mean)
    return (input_grad, update)


def solution(mesh):
    fine = Mesh(mesh.devices.reshape(4, 2, 2, 2, 8), ("x", "yh", "yl", "core", "z"))
    row, col = ("x", "yh"), ("yl", "core")
    return jax.shard_map(
        body,
        mesh=fine,
        in_specs=(
            P(("z",) + row, col),
            P("z", row + col),
            P(col + ("z",), row),
            P(col + ("z",)),
            P(row),
        ),
        out_specs=(P("z", row + col), P(col + ("z",), row)),
        check_vma=False,
    )
```

time: 231 us -> 178 us (0.77)
  waiting for transfers between devices: 138 us -> 61.7 us
  blocking collectives: 6.89 us -> 32.5 us
  between operations: 14.8 us -> 22.6 us
  local copies, waits for them, and re-layouts: 18.9 us -> 11.6 us
  starting transfers between devices: 22.7 us -> 17.6 us
  Pallas kernels: 15 us -> 19.5 us
    all_gather x1, waiting for transfers between devices: 46.5 us -> 0.01 us  [body(): lax.all_gather(act_half, 'z', axis=0, tiled=True).reshape(8, 8, 32, HALF)]
    all_to_all x0 -> x1, blocking collectives: none -> 25.6 us  [body(): lax.all_to_all(cotangent, 'z', 1, 0, tiled=True).reshape(8, 32, 768)]
    all_to_all x1 -> x0, waiting for transfers between devices: 14.6 us -> none  [body(): lax.all_to_all(cotangent, 'z', 1, 0, tiled=True).reshape(8, 32, 768)]
    ppermute x17, waiting for transfers between devices: 58.6 us -> 48.6 us  [exchange(): return lax.ppermute(value, axis, [(i, i ^ bit) for i in range(size)])]
    unnamed x38 -> x25, local copies, waits for them, and re-layouts: 11.3 us -> 2 us
    add x2, other arithmetic: 5.63 us -> 0.46 us  [the longest x1 0.23 us: body(): keep_2 + sent_2]
    ppermute x5, waiting for transfers between devices: 17.9 us -> 13.1 us  [shift(): lax.ppermute(value, axis, [(i, (i + step) % size) for i in range(size)])]
    pallas_call x2 -> x3, Pallas kernels: 15 us -> 19.5 us  [the longest x2 10 us: partial_call(): pl.pallas_call(partial_kernel, out_shape=[jax.ShapeDtypeStruct((8, 4, 32,...]
  transfers between devices with their start and end apart: 26 -> 24, of which waited for: 22 -> 17; matrix products, arithmetic and copies ran while one was open for 6% -> 10% of each run, Pallas kernels for 3% -> 11%
where the time goes in v2:
time: 178 us; the launch traced here: 177 us
  waiting for transfers between devices  61.7 us (35%)
  blocking collectives  32.5 us (18%)
  between operations  22.6 us (13%)
  Pallas kernels  19.5 us (11%)
  starting transfers between devices  17.6 us (10%)
  local copies, waits for them, and re-layouts  11.6 us (7%)
  other arithmetic  11.6 us (7%)
    ppermute x17, waiting for transfers between devices, exchange(): return lax.ppermute(value, axis, [(i, i ^ bit) for i in range(size)])  48.6 us
    all_to_all x1, blocking collectives, body(): lax.all_to_all(cotangent, 'z', 1, 0, tiled=True).reshape(8, 32, 768)  25.6 us
    ppermute x5, waiting for transfers between devices, shift(): lax.ppermute(value, axis, [(i, (i + step) % size) for i in range(size)])  13.1 us
    ppermute x17, starting transfers between devices, exchange(): return lax.ppermute(value, axis, [(i, i ^ bit) for i in range(size)])  12.8 us
    pallas_call x2, Pallas kernels, partial_call(): pl.pallas_call(partial_kernel, out_shape=[jax.ShapeDtypeStruct((8, 4, 32,...  10 us
    pallas_call x1, Pallas kernels, gradient_call(): pl.pallas_call(gradient_kernel, grid_spec=pltpu.PrefetchScalarGridSpec(nu...  9.5 us
    all_gather x1, blocking collectives, body(): act_cols = lax.all_gather(activations, ('yl', 'core'), axis=1, tiled=True)  6.89 us
    ppermute x5, starting transfers between devices, shift(): lax.ppermute(value, axis, [(i, (i + step) % size) for i in range(size)])  4.69 us
  transfers between devices with their start and end apart: 24, of which 17 were waited for; matrix products, arithmetic and copies ran while one was open for 10% of the time, Pallas kernels for 11%

profile of v2, /device:TPU:4, one launch (start us, length us, event | category | flops | bytes accessed | tf_op | source)
XLA Modules:
  0.0 177.1 jit_solution(13311935940366583715)
XLA Ops:
  7.2 6.9 %all_gather.6 = bf16[256,768]{0,1:T(8,128)(2,1)S(1)} all-gather(bf16[256,192]{0,1:T(8,128)(2,1)} %param.6), channel_id=1, replica_groups=mesh['x'=4,'yh'=2,'yl'=2,'core'=2,'z'=8] {'yl','core'}, dimensions={1}, use_global_device_ids=true | all-gather | bytes 491520 | tf_op jit(solution)/shard_map/all_gather | solution.py:99
  15.9 25.6 %all_to_all.16 = bf16[32,8,768]{2,0,1:T(8,128)(2,1)S(1)} all-to-all(bf16[32,8,768]{2,0,1:T(8,128)(2,1)S(1)} %bitcast.31), channel_id=1, replica_groups=mesh['x'=4,'yh'=2,'yl'=2,'core'=2,'z'=8] {'z'}, dimensions={1} | all-to-all | bytes 786432 | tf_op jit(solution)/shard_map/all_to_all | solution.py:104
  41.5 2.9 %collective-permute-start.3 = (bf16[8,32,768]{2,1,0:T(8,128)(2,1)S(1)}, bf16[8,32,768]{2,1,0:T(8,128)(2,1)S(1)}, u32[]{:S(2)}, u32[]{:S(2)}) collective-permute-start(bf16[8,32,768]{2,1,0:T(8,128)(2,1)S(1)} %bitcast.34), channel_id=1, source_target_pairs={{0,32},{32,0},{1,33},{33,1},{2,34},{34,2},{3,35},{35,3},{4,36},{36... | collective-permute-start | bytes 1179656 | tf_op jit(solution)/shard_map/ppermute | solution.py:20
  44.9 2.1 %collective-permute-start = (bf16[8,32,768]{2,1,0:T(8,128)(2,1)S(1)}, bf16[8,32,768]{2,1,0:T(8,128)(2,1)S(1)}, u32[]{:S(2)}, u32[]{:S(2)}) collective-permute-start(bf16[8,32,768]{2,1,0:T(8,128)(2,1)S(1)} %bitcast.36), channel_id=1, source_target_pairs={{0,64},{64,128},{128,192},{192,0},{1,65},{65,129},{129,193},{193,1... | collective-permute-start | bytes 1179656 | tf_op jit(solution)/shard_map/ppermute | solution.py:24
  47.0 6.5 %collective-permute-done.3.cot_0.refs_4_ = bf16[8,32,768]{2,1,0:T(8,128)(2,1)S(1)} collective-permute-done((bf16[8,32,768]{2,1,0:T(8,128)(2,1)S(1)}, bf16[8,32,768]{2,1,0:T(8,128)(2,1)S(1)}, u32[]{:S(2)}, u32[]{:S(2)}) %collective-permute-start.3) | collective-permute-done | bytes 393248 | tf_op jit(solution)/shard_map/ppermute | solution.py:20
  55.6 2.5 %collective-permute-done.2.cot_3.refs_3_ = bf16[8,32,768]{2,1,0:T(8,128)(2,1)} collective-permute-done((bf16[8,32,768]{2,1,0:T(8,128)(2,1)S(1)}, bf16[8,32,768]{2,1,0:T(8,128)(2,1)}, u32[]{:S(2)}, u32[]{:S(2)}) %collective-permute-start.2) | collective-permute-done | bytes 393248 | tf_op jit(solution)/shard_map/ppermute | solution.py:24
  61.5 3.1 %collective-permute-done.cot_1.refs_1_ = bf16[8,32,768]{2,1,0:T(8,128)(2,1)S(1)} collective-permute-done((bf16[8,32,768]{2,1,0:T(8,128)(2,1)S(1)}, bf16[8,32,768]{2,1,0:T(8,128)(2,1)S(1)}, u32[]{:S(2)}, u32[]{:S(2)}) %collective-permute-start) | collective-permute-done | bytes 393248 | tf_op jit(solution)/shard_map/ppermute | solution.py:24
  65.6 6.6 %collective-permute-done.4.cot_1.refs_5_ = bf16[8,32,768]{2,1,0:T(8,128)(2,1)} collective-permute-done((bf16[8,32,768]{2,1,0:T(8,128)(2,1)S(1)}, bf16[8,32,768]{2,1,0:T(8,128)(2,1)}, u32[]{:S(2)}, u32[]{:S(2)}) %collective-permute-start.4) | collective-permute-done | bytes 393248 | tf_op jit(solution)/shard_map/ppermute | solution.py:24
  72.2 4.7 %shard_map.68 = (f32[8,4,32,384]{3,2,1,0:T(8,128)}, f32[8,4,32,384]{3,2,1,0:T(8,128)}) custom-call(bf16[8,32,768]{2,1,0:T(8,128)(2,1)} %bitcast.38, bf16[8,32,768]{2,1,0:T(8,128)(2,1)} %copy-done.11, bf16[8,32,768]{2,1,0:T(8,128)(2,1)} %collective-permute-done.1.cot_2.refs_2_, bf16[8,32,768]{2,1,0:T(8,128)(2,1)} %collective-permute-done.2.cot_3.refs_3_, ...), custom_call_target="tpu_custom_call" | custom-call | flops 1207959552 | bytes 6291456 | tf_op jit(solution)/shard_map/pallas_call | solution.py:45
  76.9 1.9 %copy.16 = bf16[2048,384]{1,0:T(8,128)(2,1)S(1)} copy(bf16[2048,384]{0,1:T(8,128)(2,1)} %all-gather.2.cloned.1.call-done) | data formatting | bytes 3145728 | tf_op jit(solution)/shard_map/all_gather | solution.py:102
  78.8 5.3 %shard_map.69 = (f32[8,4,32,384]{3,2,1,0:T(8,128)}, f32[8,4,32,384]{3,2,1,0:T(8,128)}) custom-call(bf16[8,32,768]{2,1,0:T(8,128)(2,1)} %copy-done.10, bf16[8,32,768]{2,1,0:T(8,128)(2,1)} %collective-permute-done.4.cot_1.refs_5_, bf16[8,32,768]{2,1,0:T(8,128)(2,1)} %collective-permute-done.5.cot_2.refs_6_, ...), custom_call_target="tpu_custom_call" | custom-call | flops 1207959552 | bytes 6291456 | tf_op jit(solution)/shard_map/pallas_call | solution.py:45
  84.9 5.2 %collective-permute-done.8 = f32[8,4,32,384]{3,2,1,0:T(8,128)S(1)} collective-permute-done((f32[8,4,32,384]{3,2,1,0:T(8,128)}, f32[8,4,32,384]{3,2,1,0:T(8,128)S(1)}, u32[]{:S(2)}, u32[]{:S(2)}) %collective-permute-start.8) | collective-permute-done | bytes 1572896 | tf_op jit(solution)/shard_map/ppermute | solution.py:20
  91.5 2.0 %pad_maximum_fusion = f32[8,8,32,384]{3,2,1,0:T(8,128)} fusion(f32[8,4,32,384]{3,2,1,0:T(8,128)S(1)} %add.119, f32[8,4,32,384]{3,2,1,0:T(8,128)S(1)} %add.118), kind=kLoop, calls=%fused_computation | loop fusion | flops 786432 | bytes 6291456 | tf_op jit(solution)/shard_map/concatenate | solution.py:136
  94.9 9.5 %shard_map.70 = f32[768,768]{1,0:T(8,128)} custom-call(s32[8]{0:T(128)} %concatenate.11.rows_ref, s32[2]{0:T(128)} %pad_add_fusion.halves_ref, bf16[8,32,768]{2,1,0:T(8,128)(2,1)} %bitcast.39, bf16[8,32,768]{2,1,0:T(8,128)(2,1)} %copy-done.11, bf16[8,32,768]{2,1,0:T(8,128)(2,1)} %collective-permute-done.1.cot_2.refs_2_, ...), custom_call_target="tpu_custom_call" | custom-call | flops 2415919104 | bytes 9437184 | tf_op jit(solution)/shard_map/pallas_call | solution.py:78
  104.4 2.1 %fusion.1 = f32[768]{0:T(1024)S(1)} fusion(f32[768,768]{1,0:T(8,128)} %shard_map.70), kind=kLoop, calls=%fused_computation.5 | loop fusion | flops 1768704 | bytes 2362368 | tf_op jit(solution)/shard_map/reduce_sum | solution.py:150
  108.4 1.9 %collective-permute-done.11 = f32[768]{0:T(1024)S(1)} collective-permute-done((f32[768]{0:T(1024)S(1)}, f32[768]{0:T(1024)S(1)}, u32[]{:S(2)}, u32[]{:S(2)}) %collective-permute-start.11) | collective-permute-done | bytes 3104 | tf_op jit(solution)/shard_map/ppermute | solution.py:20
  111.6 3.8 %collective-permute-done.12 = f32[768]{0:T(1024)S(1)} collective-permute-done((f32[768]{0:T(1024)S(1)}, f32[768]{0:T(1024)S(1)}, u32[]{:S(2)}, u32[]{:S(2)}) %collective-permute-start.12) | collective-permute-done | bytes 3104 | tf_op jit(solution)/shard_map/ppermute | solution.py:20
  115.9 4.6 %collective-permute-done.13 = f32[768]{0:T(1024)S(1)} collective-permute-done((f32[768]{0:T(1024)S(1)}, f32[768]{0:T(1024)S(1)}, u32[]{:S(2)}, u32[]{:S(2)}) %collective-permute-start.13) | collective-permute-done | bytes 3104 | tf_op jit(solution)/shard_map/ppermute | solution.py:20
  123.9 3.3 %collective-permute-done.15 = f32[1664]{0:T(1024)S(1)} collective-permute-done((f32[1664]{0:T(1024)S(1)}, f32[1664]{0:T(1024)S(1)}, u32[]{:S(2)}, u32[]{:S(2)}) %collective-permute-start.15) | collective-permute-done | bytes 6688 | tf_op jit(solution)/shard_map/ppermute | solution.py:20
  127.1 3.6 %collective-permute-done.16 = f32[1664]{0:T(1024)S(1)} collective-permute-done((f32[1664]{0:T(1024)S(1)}, f32[1664]{0:T(1024)S(1)}, u32[]{:S(2)}, u32[]{:S(2)}) %collective-permute-start.16) | collective-permute-done | bytes 6688 | tf_op jit(solution)/shard_map/ppermute | solution.py:20
  130.8 4.5 %collective-permute-done.17 = f32[1664]{0:T(1024)S(1)} collective-permute-done((f32[1664]{0:T(1024)S(1)}, f32[1664]{0:T(1024)S(1)}, u32[]{:S(2)}, u32[]{:S(2)}) %collective-permute-start.17) | collective-permute-done | bytes 6688 | tf_op jit(solution)/shard_map/ppermute | solution.py:20
  136.0 6.9 %collective-permute-done.18 = f32[1664]{0:T(1024)S(1)} collective-permute-done((f32[1664]{0:T(1024)S(1)}, f32[1664]{0:T(1024)S(1)}, u32[]{:S(2)}, u32[]{:S(2)}) %collective-permute-start.18) | collective-permute-done | bytes 6688 | tf_op jit(solution)/shard_map/ppermute | solution.py:20
  163.6 1.9 %multiply_divide_fusion = f32[768,768]{1,0:T(8,128)} fusion(f32[768,768]{1,0:T(8,128)S(1)} %copy-done, f32[]{:T(128)} %bitcast.18, f32[]{:T(128)} %bitcast.17, f32[768]{0:T(1024)S(1)} %get-tuple-element.43, f32[768]{0:T(1024)S(1)} %get-tuple-element.45), kind=kLoop, calls=%fused_computation.1 | loop fusion | flops 2359296 | bytes 4724744 | tf_op jit(solution)/shard_map/div | solution.py:168
  165.4 3.7 %collective-permute-done.10 = f32[8,32,192]{2,1,0:T(8,128)S(1)} collective-permute-done((f32[8,32,192]{2,1,0:T(8,128)S(1)}, f32[8,32,192]{2,1,0:T(8,128)S(1)}, u32[]{:S(2)}, u32[]{:S(2)}) %collective-permute-start.10) | collective-permute-done | bytes 196640 | tf_op jit(solution)/shard_map/ppermute | solution.py:20
  (101 shorter events, 33.5 us)
Async XLA Ops:
  7.2 69.7 %all-gather.2.cloned.1.call-start = ((), (), s32[]{:S(2)}) async-start(), calls=%async_computation.2 | async-start | bytes 1769472 | tf_op jit(solution)/shard_map/all_gather | solution.py:102
  14.8 146.7 %reduce-scatter.2.cloned.1.call-start = ((), (), s32[]{:S(2)}) async-start(), calls=%async_computation.3 | async-start | bytes 3538944 | tf_op jit(solution)/shard_map/reduce_scatter | solution.py:139
  41.5 12.1 %collective-permute-start.3 = (bf16[8,32,768]{2,1,0:T(8,128)(2,1)S(1)}, bf16[8,32,768]{2,1,0:T(8,128)(2,1)S(1)}, u32[]{:S(2)}, u32[]{:S(2)}) collective-permute-start(bf16[8,32,768]{2,1,0:T(8,128)(2,1)S(1)} %bitcast.34), channel_id=1, source_target_pairs={{0,32},{32,0},{1,33},{33,1},{2,34},{34,2},{3,35},{35,3},{4,36},{36... | collective-permute-start | bytes 1179656 | tf_op jit(solution)/shard_map/ppermute | solution.py:20
  44.4 13.7 %collective-permute-start.2 = (bf16[8,32,768]{2,1,0:T(8,128)(2,1)S(1)}, bf16[8,32,768]{2,1,0:T(8,128)(2,1)}, u32[]{:S(2)}, u32[]{:S(2)}) collective-permute-start(bf16[8,32,768]{2,1,0:T(8,128)(2,1)S(1)} %bitcast.35), channel_id=1, source_target_pairs={{0,128},{64,192},{128,0},{192,64},{1,129},{65,193},{129,1},{193,65... | collective-permute-start | bytes 1179656 | tf_op jit(solution)/shard_map/ppermute | solution.py:24
  44.9 19.7 %collective-permute-start = (bf16[8,32,768]{2,1,0:T(8,128)(2,1)S(1)}, bf16[8,32,768]{2,1,0:T(8,128)(2,1)S(1)}, u32[]{:S(2)}, u32[]{:S(2)}) collective-permute-start(bf16[8,32,768]{2,1,0:T(8,128)(2,1)S(1)} %bitcast.36), channel_id=1, source_target_pairs={{0,64},{64,128},{128,192},{192,0},{1,65},{65,129},{129,193},{193,1... | collective-permute-start | bytes 1179656 | tf_op jit(solution)/shard_map/ppermute | solution.py:24
  47.0 18.6 %collective-permute-start.1 = (bf16[8,32,768]{2,1,0:T(8,128)(2,1)S(1)}, bf16[8,32,768]{2,1,0:T(8,128)(2,1)}, u32[]{:S(2)}, u32[]{:S(2)}) collective-permute-start(bf16[8,32,768]{2,1,0:T(8,128)(2,1)S(1)} %bitcast.37), channel_id=1, source_target_pairs={{0,192},{64,0},{128,64},{192,128},{1,193},{65,1},{129,65},{193,129... | collective-permute-start | bytes 1179656 | tf_op jit(solution)/shard_map/ppermute | solution.py:24
  53.6 18.6 %collective-permute-start.4 = (bf16[8,32,768]{2,1,0:T(8,128)(2,1)S(1)}, bf16[8,32,768]{2,1,0:T(8,128)(2,1)}, u32[]{:S(2)}, u32[]{:S(2)}) collective-permute-start(bf16[8,32,768]{2,1,0:T(8,128)(2,1)S(1)} %collective-permute-done.3.cot_0.refs_4_), channel_id=1, source_target_pairs={{0,64},{64,128},{128,192},{192,0},{1,65},{65,129},{129,193},{193,1... | collective-permute-start | bytes 1179656 | tf_op jit(solution)/shard_map/ppermute | solution.py:24
  54.8 17.4 %collective-permute-start.5 = (bf16[8,32,768]{2,1,0:T(8,128)(2,1)S(1)}, bf16[8,32,768]{2,1,0:T(8,128)(2,1)}, u32[]{:S(2)}, u32[]{:S(2)}) collective-permute-start(bf16[8,32,768]{2,1,0:T(8,128)(2,1)S(1)} %collective-permute-done.3.cot_0.refs_4_), channel_id=1, source_target_pairs={{0,192},{64,0},{128,64},{192,128},{1,193},{65,1},{129,65},{193,129... | collective-permute-start | bytes 1179656 | tf_op jit(solution)/shard_map/ppermute | solution.py:24
  58.0 20.8 %collective-permute-start.7 = (bf16[8,32,768]{2,1,0:T(8,128)(2,1)}, bf16[8,32,768]{2,1,0:T(8,128)(2,1)}, u32[]{:S(2)}, u32[]{:S(2)}) collective-permute-start(bf16[8,32,768]{2,1,0:T(8,128)(2,1)} %collective-permute-done.2.cot_3.refs_3_), channel_id=1, source_target_pairs={{0,32},{32,0},{1,33},{33,1},{2,34},{34,2},{3,35},{35,3},{4,36},{36... | collective-permute-start | bytes 1179656 | tf_op jit(solution)/shard_map/ppermute | solution.py:20
  76.9 7.7 %collective-permute-start.6 = (f32[8,4,32,384]{3,2,1,0:T(8,128)}, f32[8,4,32,384]{3,2,1,0:T(8,128)S(1)}, u32[]{:S(2)}, u32[]{:S(2)}) collective-permute-start(f32[8,4,32,384]{3,2,1,0:T(8,128)} %get-tuple-element.28), channel_id=1, source_target_pairs={{0,8},{8,0},{1,9},{9,1},{2,10},{10,2},{3,11},{11,3},{4,12},{12,4},... | collective-permute-start | bytes 4718600 | tf_op jit(solution)/shard_map/ppermute | solution.py:20
  84.1 6.0 %collective-permute-start.8 = (f32[8,4,32,384]{3,2,1,0:T(8,128)}, f32[8,4,32,384]{3,2,1,0:T(8,128)S(1)}, u32[]{:S(2)}, u32[]{:S(2)}) collective-permute-start(f32[8,4,32,384]{3,2,1,0:T(8,128)} %get-tuple-element.34), channel_id=1, source_target_pairs={{0,8},{8,0},{1,9},{9,1},{2,10},{10,2},{3,11},{11,3},{4,12},{12,4},... | collective-permute-start | bytes 4718600 | tf_op jit(solution)/shard_map/ppermute | solution.py:20
  84.6 5.5 %collective-permute-start.9 = (bf16[8,8,32,384]{3,2,1,0:T(8,128)(2,1)S(1)}, bf16[8,8,32,384]{3,2,1,0:T(8,128)(2,1)S(1)}, u32[]{:S(2)}, u32[]{:S(2)}) collective-permute-start(bf16[8,8,32,384]{3,2,1,0:T(8,128)(2,1)S(1)} %bitcast.29), channel_id=1, source_target_pairs={{0,8},{8,0},{1,9},{9,1},{2,10},{10,2},{3,11},{11,3},{4,12},{12,4},... | collective-permute-start | bytes 4718600 | tf_op jit(solution)/shard_map/ppermute | solution.py:20
  106.6 3.7 %collective-permute-start.11 = (f32[768]{0:T(1024)S(1)}, f32[768]{0:T(1024)S(1)}, u32[]{:S(2)}, u32[]{:S(2)}) collective-permute-start(f32[768]{0:T(1024)S(1)} %fusion.1), channel_id=1, source_target_pairs={{0,64},{64,0},{128,192},{192,128},{1,65},{65,1},{129,193},{193,129... | collective-permute-start | bytes 9224 | tf_op jit(solution)/shard_map/ppermute | solution.py:20
  110.3 5.1 %collective-permute-start.12 = (f32[768]{0:T(1024)S(1)}, f32[768]{0:T(1024)S(1)}, u32[]{:S(2)}, u32[]{:S(2)}) collective-permute-start(f32[768]{0:T(1024)S(1)} %add.142), channel_id=1, source_target_pairs={{0,128},{64,192},{128,0},{192,64},{1,129},{65,193},{129,1},{193,65... | collective-permute-start | bytes 9224 | tf_op jit(solution)/shard_map/ppermute | solution.py:20
  115.4 5.1 %collective-permute-start.13 = (f32[768]{0:T(1024)S(1)}, f32[768]{0:T(1024)S(1)}, u32[]{:S(2)}, u32[]{:S(2)}) collective-permute-start(f32[768]{0:T(1024)S(1)} %add.143), channel_id=1, source_target_pairs={{0,32},{32,0},{1,33},{33,1},{2,34},{34,2},{3,35},{35,3},{4,36},{36... | collective-permute-start | bytes 9224 | tf_op jit(solution)/shard_map/ppermute | solution.py:20
  122.2 1.3 collective-permute-start.14
  123.5 3.7 %collective-permute-start.15 = (f32[1664]{0:T(1024)S(1)}, f32[1664]{0:T(1024)S(1)}, u32[]{:S(2)}, u32[]{:S(2)}) collective-permute-start(f32[1664]{0:T(1024)S(1)} %fusion.6), channel_id=1, source_target_pairs={{0,16},{16,0},{1,17},{17,1},{2,18},{18,2},{3,19},{19,3},{4,20},{20... | collective-permute-start | bytes 19976 | tf_op jit(solution)/shard_map/ppermute | solution.py:20
  127.1 3.7 %collective-permute-start.16 = (f32[1664]{0:T(1024)S(1)}, f32[1664]{0:T(1024)S(1)}, u32[]{:S(2)}, u32[]{:S(2)}) collective-permute-start(f32[1664]{0:T(1024)S(1)} %add.147), channel_id=1, source_target_pairs={{0,1},{1,0},{2,3},{3,2},{4,5},{5,4},{6,7},{7,6},{8,9},{9,8},{10,11... | collective-permute-start | bytes 19976 | tf_op jit(solution)/shard_map/ppermute | solution.py:20
  130.8 4.5 %collective-permute-start.17 = (f32[1664]{0:T(1024)S(1)}, f32[1664]{0:T(1024)S(1)}, u32[]{:S(2)}, u32[]{:S(2)}) collective-permute-start(f32[1664]{0:T(1024)S(1)} %add.148), channel_id=1, source_target_pairs={{0,2},{1,3},{2,0},{3,1},{4,6},{5,7},{6,4},{7,5},{8,10},{9,11},{10,... | collective-permute-start | bytes 19976 | tf_op jit(solution)/shard_map/ppermute | solution.py:20
  135.3 7.6 %collective-permute-start.18 = (f32[1664]{0:T(1024)S(1)}, f32[1664]{0:T(1024)S(1)}, u32[]{:S(2)}, u32[]{:S(2)}) collective-permute-start(f32[1664]{0:T(1024)S(1)} %add.149), channel_id=1, source_target_pairs={{0,4},{1,5},{2,6},{3,7},{4,0},{5,1},{6,2},{7,3},{8,12},{9,13},{10,... | collective-permute-start | bytes 19976 | tf_op jit(solution)/shard_map/ppermute | solution.py:20
  145.5 4.3 %collective-permute-start.19 = (f32[128]{0:T(128)S(1)}, f32[128]{0:T(128)S(1)}, u32[]{:S(2)}, u32[]{:S(2)}) collective-permute-start(f32[128]{0:T(128)S(1)} %broadcast_in_dim.14), channel_id=1, source_target_pairs={{0,64},{64,0},{128,192},{192,128},{1,65},{65,1},{129,193},{193,129... | collective-permute-start | bytes 1544 | tf_op jit(solution)/shard_map/ppermute | solution.py:20
  150.5 5.1 %collective-permute-start.20 = (f32[128]{0:T(128)S(1)}, f32[128]{0:T(128)S(1)}, u32[]{:S(2)}, u32[]{:S(2)}) collective-permute-start(f32[128]{0:T(128)S(1)} %broadcast_add_fusion), channel_id=1, source_target_pairs={{0,128},{64,192},{128,0},{192,64},{1,129},{65,193},{129,1},{193,65... | collective-permute-start | bytes 1544 | tf_op jit(solution)/shard_map/ppermute | solution.py:20
  156.3 5.1 %collective-permute-start.21 = (f32[128]{0:T(128)S(1)}, f32[128]{0:T(128)S(1)}, u32[]{:S(2)}, u32[]{:S(2)}) collective-permute-start(f32[128]{0:T(128)S(1)} %fusion.10), channel_id=1, source_target_pairs={{0,32},{32,0},{1,33},{33,1},{2,34},{34,2},{3,35},{35,3},{4,36},{36... | collective-permute-start | bytes 1544 | tf_op jit(solution)/shard_map/ppermute | solution.py:20
  162.7 6.5 %collective-permute-start.10 = (f32[8,32,192]{2,1,0:T(8,128)S(1)}, f32[8,32,192]{2,1,0:T(8,128)S(1)}, u32[]{:S(2)}, u32[]{:S(2)}) collective-permute-start(f32[8,32,192]{2,1,0:T(8,128)S(1)} %slice_select_fusion), channel_id=1, source_target_pairs={{0,16},{16,0},{1,17},{17,1},{2,18},{18,2},{3,19},{19,3},{4,20},{20... | collective-permute-start | bytes 589832 | tf_op jit(solution)/shard_map/ppermute | solution.py:20
  (12 other events, 180.9 us)
Sparse Core Ops, SparseCore 0:
  14.9 51.2 all-gather.1
  93.6 40.9 reduce-scatter.1

commit v3 on v2

v3 whole, which is shorter than its diff:
```python
import jax
import jax.numpy as jnp
from jax import lax
from jax.experimental import pallas as pl
from jax.experimental.pallas import tpu as pltpu
from jax.sharding import Mesh
from jax.sharding import PartitionSpec as P

D = 6144
FF = 24576
HALF = 384
VMEM = 56 * 1024 * 1024

epsilon = 1e-30
decay_rate = 0.9


def exchange(value, axis, size, bit):
    return lax.ppermute(value, axis, [(i, i ^ bit) for i in range(size)])


def shift(value, axis, size, step):
    return lax.ppermute(value, axis, [(i, (i + step) % size) for i in range(size)])


def total(value, axis, size):
    bit = 1
    while bit < size:
        value = value + exchange(value, axis, size, bit)
        bit *= 2
    return value


def tokens(refs, count):
    return jnp.concatenate([ref[...].reshape(count * 32, 768) for ref in refs], axis=0)


def product(cot, weight_ref):
    return jnp.dot(cot, weight_ref[...], preferred_element_type=jnp.float32)


def split(part, count):
    return [part[j * count * 32 : (j + 1) * count * 32].reshape(count, 32, HALF) for j in range(4)]


def first_kernel(*refs):
    cots, (keep_ref, send_ref, part_keep, part_send) = refs[:4], refs[4:]
    cot = tokens(cots, 2)
    for weight_ref, out in ((keep_ref, part_keep), (send_ref, part_send)):
        for j, part in enumerate(split(product(cot, weight_ref), 2)):
            out[:, j] = part


def second_kernel(rows_ref, *refs):
    cots, others = refs[:4], refs[4:8]
    keep_ref, other_ref, before_ref, recv_ref, out = refs[8:]
    whole = product(tokens(cots, 2), keep_ref) + product(tokens(others, 2), other_ref)
    for j, part in enumerate(split(whole, 2)):
        out[:, rows_ref[j]] = before_ref[:, j] + recv_ref[:, j]
        out[:, rows_ref[4 + j]] = part


COT = pl.BlockSpec((2, 32, 768), lambda s, *_: (s, 0, 0))
WEIGHT = pl.BlockSpec((768, HALF), lambda s, *_: (0, 0))
PART = pl.BlockSpec((2, 4, 32, HALF), lambda s, *_: (s, 0, 0, 0))


def first_call(cots, keep, send):
    return pl.pallas_call(
        first_kernel,
        grid=(4,),
        in_specs=[COT] * 4 + [WEIGHT] * 2,
        out_specs=[PART] * 2,
        out_shape=[jax.ShapeDtypeStruct((8, 4, 32, HALF), jnp.float32)] * 2,
        compiler_params=pltpu.CompilerParams(vmem_limit_bytes=VMEM),
        cost_estimate=pl.CostEstimate(
            flops=2 * 1024 * 768 * 768, bytes_accessed=6 * 1024 * 1024, transcendentals=0
        ),
    )(*cots, keep, send)


def second_call(rows, cots, others, keep, other, before, received):
    return pl.pallas_call(
        second_kernel,
        grid_spec=pltpu.PrefetchScalarGridSpec(
            num_scalar_prefetch=1,
            grid=(4,),
            in_specs=[COT] * 8 + [WEIGHT] * 2 + [PART] * 2,
            out_specs=pl.BlockSpec((2, 8, 32, HALF), lambda s, rows: (s, 0, 0, 0)),
        ),
        out_shape=jax.ShapeDtypeStruct((8, 8, 32, HALF), jnp.float32),
        compiler_params=pltpu.CompilerParams(vmem_limit_bytes=VMEM),
        cost_estimate=pl.CostEstimate(
            flops=2 * 1024 * 768 * 768, bytes_accessed=10 * 1024 * 1024, transcendentals=0
        ),
    )(rows, *cots, *others, keep, other, before, received)


STEP = 4


def gradient_kernel(rows_ref, halves_ref, *refs):
    cots, acts, (out_ref, row_ref, col_ref) = refs[:8], refs[8:10], refs[10:]
    step = pl.program_id(0)
    act = jnp.concatenate(
        [
            jnp.concatenate([a[:, rows_ref[j]].reshape(STEP * 32, HALF) for j in range(8)], axis=0)
            for a in acts
        ],
        axis=1,
    )
    term = lax.dot_general(
        tokens(cots, STEP), act, (((0,), (0,)), ((), ())), preferred_element_type=jnp.float32
    )
    for h in range(2):
        columns = pl.ds(pl.multiple_of(halves_ref[h] * HALF, HALF), HALF)
        part = term[:, h * HALF : (h + 1) * HALF]

        @pl.when(step == 0)
        def _():
            out_ref[:, columns] = part

        @pl.when(step > 0)
        def _():
            out_ref[:, columns] += part

    @pl.when(step == 8 // STEP - 1)
    def _():
        gradient = out_ref[...]
        square = gradient * gradient + epsilon
        col_ref[...] = jnp.sum(square, axis=0)
        lanes = sum(square[:, k * 128 : (k + 1) * 128] for k in range(6))
        row_ref[...] = jnp.sum(lanes.T, axis=0)


def gradient_call(rows, halves, cots, acts):
    vector = pl.BlockSpec((768,), lambda s, rows, halves: (0,))
    return pl.pallas_call(
        gradient_kernel,
        grid_spec=pltpu.PrefetchScalarGridSpec(
            num_scalar_prefetch=2,
            grid=(8 // STEP,),
            in_specs=[pl.BlockSpec((STEP, 32, 768), lambda s, rows, halves: (s, 0, 0))] * 8
            + [pl.BlockSpec((STEP, 8, 32, HALF), lambda s, rows, halves: (s, 0, 0, 0))] * 2,
            out_specs=[pl.BlockSpec((768, 768), lambda s, rows, halves: (0, 0)), vector, vector],
        ),
        out_shape=[
            jax.ShapeDtypeStruct((768, 768), jnp.float32),
            jax.ShapeDtypeStruct((768,), jnp.float32),
            jax.ShapeDtypeStruct((768,), jnp.float32),
        ],
        compiler_params=pltpu.CompilerParams(vmem_limit_bytes=VMEM),
        cost_estimate=pl.CostEstimate(
            flops=2 * 2048 * 768 * 768, bytes_accessed=9 * 1024 * 1024, transcendentals=0
        ),
    )(rows, halves, *cots, *acts)


def body(cotangent, activations, weight, row_prev, col_prev):
    x, yh, core = lax.axis_index("x"), lax.axis_index("yh"), lax.axis_index("core")
    yl = lax.axis_index("yl")

    act_cols = lax.all_gather(activations, ("yl", "core"), axis=1, tiled=True)
    act_half = lax.dynamic_slice_in_dim(act_cols, core * HALF, HALF, 1)
    act_half, cotangent = lax.optimization_barrier((act_half, cotangent))
    act_own = lax.all_gather(act_half, "z", axis=0, tiled=True).reshape(8, 8, 32, HALF)

    own_cot = lax.all_to_all(cotangent, "z", 1, 0, tiled=True).reshape(8, 32, 768)
    own_cot, weight = lax.optimization_barrier((own_cot, weight))
    other_cot = exchange(own_cot, "yh", 2, 1)
    right_cot = shift(own_cot, "x", 4, 1)
    left_cot = shift(own_cot, "x", 4, -1)
    far_cot = shift(own_cot, "x", 4, 2)
    other_right = shift(other_cot, "x", 4, 1)
    other_left = shift(other_cot, "x", 4, -1)
    other_far = exchange(far_cot, "yh", 2, 1)
    right, left, far = (x + 3) % 4, (x + 1) % 4, (x + 2) % 4
    rows = jnp.stack([x * 2 + yh, right * 2 + yh, left * 2 + yh, far * 2 + yh])
    rows = jnp.concatenate([rows, rows + 1 - 2 * yh]).astype(jnp.int32)
    halves = jnp.stack([core, 1 - core]).astype(jnp.int32)
    first = [own_cot, right_cot, left_cot, far_cot]
    second = [other_cot, other_right, other_left, other_far]

    by_core = weight.reshape(768, 2, 2, 192)
    even = by_core[:, :, 0].reshape(768, HALF)
    odd = by_core[:, :, 1].reshape(768, HALF)
    keep = jnp.where(core == 0, even, odd)
    send = jnp.where(core == 0, odd, even)

    other_keep = exchange(send, "core", 2, 1)

    others = [exchange(cot, "core", 2, 1) for cot in second[:3]]
    *arrived, keep, send, other_keep, act_own = lax.optimization_barrier(
        (*first, *second, *others, keep, send, other_keep, act_own)
    )
    first, second, others = arrived[:4], arrived[4:8], arrived[8:]
    act_recv = exchange(act_own, "core", 2, 1)
    keep_1, send_1 = first_call(first, keep, send)
    recv_1 = exchange(send_1, "core", 2, 1)
    gradient, row_sums, col_sums = gradient_call(rows, halves, first + second, [act_own, act_recv])

    others.append(exchange(second[3], "core", 2, 1))
    row_sums = row_sums + exchange(row_sums, "x", 4, 1)
    others[0], row_sums = lax.optimization_barrier((others[0], row_sums))
    summed = second_call(rows, second, others, keep, other_keep, keep_1, recv_1)
    summed = lax.psum_scatter(summed, "z", scatter_dimension=0, tiled=True).reshape(8, 32, HALF)
    low, high = summed[:, :, :192], summed[:, :, 192:]
    mine = jnp.where(yl == 0, low, high)
    theirs = jnp.where(yl == 0, high, low)
    mine = (mine + exchange(theirs, "yl", 2, 1)).astype(jnp.bfloat16)
    input_grad = mine.reshape(256, 192)

    row_sums = total(row_sums + exchange(row_sums, "x", 4, 2), "yh", 2)
    row_stats = decay_rate * row_prev + (1.0 - decay_rate) * (row_sums / D)
    scaled = gradient * lax.rsqrt(row_stats)[:, None]
    sums = jnp.concatenate(
        [
            col_sums,
            jnp.sum(scaled * scaled, axis=0),
            jnp.broadcast_to(jnp.sum(row_stats), (768,)),
        ]
    )
    sums = total(total(total(sums, "core", 2), "yl", 2), "z", 8)
    col_sums, scaled_sums, row_mean = sums[:768], sums[768:1536], sums[1536:] / FF
    col_stats = decay_rate * col_prev + (1.0 - decay_rate) * (col_sums / FF)
    part = jnp.sum((scaled_sums * row_mean / col_stats).reshape(6, 128), axis=0)
    part = total(total(part, "x", 4), "yh", 2)
    part, input_grad = lax.optimization_barrier((part, input_grad))
    squares_total = jnp.sum(part)
    root_mean = jnp.sqrt(squares_total / (FF * D))
    unclipped = gradient * lax.rsqrt(row_stats[:, None] * col_stats[None, :] / row_mean[None, :])
    update = unclipped / jnp.maximum(1.0, root_mean)
    return (input_grad, update)


def solution(mesh):
    fine = Mesh(mesh.devices.reshape(4, 2, 2, 2, 8), ("x", "yh", "yl", "core", "z"))
    row, col = ("x", "yh"), ("yl", "core")
    return jax.shard_map(
        body,
        mesh=fine,
        in_specs=(
            P(("z",) + row, col),
            P("z", row + col),
            P(col + ("z",), row),
            P(col + ("z",)),
            P(row),
        ),
        out_specs=(P("z", row + col), P(col + ("z",), row)),
        check_vma=False,
    )
```

time: 178 us -> 174 us (0.978)
  waiting for transfers between devices: 61.7 us -> 69.7 us
  between operations: 22.6 us -> 14.9 us
  other arithmetic: 11.6 us -> 7.27 us
    ppermute x17 -> x21, waiting for transfers between devices: 48.6 us -> 53.4 us  [exchange(): return lax.ppermute(value, axis, [(i, i ^ bit) for i in range(size)])]
    ppermute x5, waiting for transfers between devices: 13.1 us -> 16.3 us  [shift(): lax.ppermute(value, axis, [(i, (i + step) % size) for i in range(size)])]
    pallas_call x2, Pallas kernels: 10 us -> 12.5 us  [the longest x1 7.33 us: second_call(): pl.pallas_call(second_kernel, grid_spec=pltpu.PrefetchScalarGridSpec(num_...]
    reduce_sum x3, other arithmetic: 3.3 us -> 0.93 us  [the longest x1 0.6 us: body(): squares_total = jnp.sum(part)]
    optimization_barrier x0 -> x2, local copies, waits for them, and re-layouts: none -> 2.1 us  [body(): lax.optimization_barrier((*first, *second, *others, keep, send, other_kee...]
    concatenate x2 -> x1, other arithmetic: 1.98 us -> 0.01 us  [body(): jnp.concatenate([col_sums, jnp.sum(scaled * scaled, axis=0), jnp.broadcas...]
    ppermute x17 -> x21, starting transfers between devices: 12.8 us -> 12.5 us  [exchange(): return lax.ppermute(value, axis, [(i, i ^ bit) for i in range(size)])]
  transfers between devices with their start and end apart: 24 -> 28, of which waited for: 17 -> 18; matrix products, arithmetic and copies ran while one was open for 10% -> 6% of each run, Pallas kernels for 11% -> 8%
where the time goes in v3:
time: 174 us; the launch traced here: 172 us
  waiting for transfers between devices  69.7 us (40%)
  blocking collectives  32.6 us (19%)
  Pallas kernels  20.4 us (12%)
  starting transfers between devices  17.3 us (10%)
  between operations  14.9 us (9%)
  local copies, waits for them, and re-layouts  10.1 us (6%)
  other arithmetic  7.27 us (4%)
    ppermute x21, waiting for transfers between devices, exchange(): return lax.ppermute(value, axis, [(i, i ^ bit) for i in range(size)])  53.4 us
    all_to_all x1, blocking collectives, body(): lax.all_to_all(cotangent, 'z', 1, 0, tiled=True).reshape(8, 32, 768)  25.7 us
    ppermute x5, waiting for transfers between devices, shift(): lax.ppermute(value, axis, [(i, (i + step) % size) for i in range(size)])  16.3 us
    ppermute x21, starting transfers between devices, exchange(): return lax.ppermute(value, axis, [(i, i ^ bit) for i in range(size)])  12.5 us
    pallas_call x1, Pallas kernels, gradient_call(): pl.pallas_call(gradient_kernel, grid_spec=pltpu.PrefetchScalarGridSpec(nu...  7.87 us
    pallas_call x1, Pallas kernels, second_call(): pl.pallas_call(second_kernel, grid_spec=pltpu.PrefetchScalarGridSpec(num_...  7.33 us
    all_gather x1, blocking collectives, body(): act_cols = lax.all_gather(activations, ('yl', 'core'), axis=1, tiled=True)  6.89 us
    pallas_call x1, Pallas kernels, first_call(): pl.pallas_call(first_kernel, grid=(4,), in_specs=[COT] * 4 + [WEIGHT] * 2...  5.22 us
  transfers between devices with their start and end apart: 28, of which 18 were waited for; matrix products, arithmetic and copies ran while one was open for 6% of the time, Pallas kernels for 8%

profile of v3, /device:TPU:4, one launch (start us, length us, event | category | flops | bytes accessed | tf_op | source)
XLA Modules:
  0.0 172.3 jit_solution(13280871029372479484)
XLA Ops:
  7.2 6.9 %all_gather.6 = bf16[256,768]{0,1:T(8,128)(2,1)S(1)} all-gather(bf16[256,192]{0,1:T(8,128)(2,1)} %param.6), channel_id=1, replica_groups=mesh['x'=4,'yh'=2,'yl'=2,'core'=2,'z'=8] {'yl','core'}, dimensions={1}, use_global_device_ids=true | all-gather | bytes 491520 | tf_op jit(solution)/shard_map/all_gather | solution.py:163
  15.9 25.7 %all_to_all.16 = bf16[32,8,768]{2,0,1:T(8,128)(2,1)} all-to-all(bf16[32,8,768]{2,0,1:T(8,128)(2,1)S(1)} %bitcast.29), channel_id=1, replica_groups=mesh['x'=4,'yh'=2,'yl'=2,'core'=2,'z'=8] {'z'}, dimensions={1} | all-to-all | bytes 786432 | tf_op jit(solution)/shard_map/all_to_all | solution.py:168
  41.6 2.9 %collective-permute-start.3 = (bf16[8,32,768]{2,1,0:T(8,128)(2,1)}, bf16[8,32,768]{2,1,0:T(8,128)(2,1)}, u32[]{:S(2)}, u32[]{:S(2)}) collective-permute-start(bf16[8,32,768]{2,1,0:T(8,128)(2,1)} %bitcast.6.refs_0_), channel_id=1, source_target_pairs={{0,32},{32,0},{1,33},{33,1},{2,34},{34,2},{3,35},{35,3},{4,36},{36... | collective-permute-start | bytes 1179656 | tf_op jit(solution)/shard_map/ppermute | solution.py:19
  45.0 2.2 %collective-permute-start.1 = (bf16[8,32,768]{2,1,0:T(8,128)(2,1)}, bf16[8,32,768]{2,1,0:T(8,128)(2,1)}, u32[]{:S(2)}, u32[]{:S(2)}) collective-permute-start(bf16[8,32,768]{2,1,0:T(8,128)(2,1)} %bitcast.6.refs_0_), channel_id=1, source_target_pairs={{0,192},{64,0},{128,64},{192,128},{1,193},{65,1},{129,65},{193,129... | collective-permute-start | bytes 1179656 | tf_op jit(solution)/shard_map/ppermute | solution.py:23
  47.8 6.2 %collective-permute-done.3.refs_4_.refs_0_ = bf16[8,32,768]{2,1,0:T(8,128)(2,1)} collective-permute-done((bf16[8,32,768]{2,1,0:T(8,128)(2,1)}, bf16[8,32,768]{2,1,0:T(8,128)(2,1)}, u32[]{:S(2)}, u32[]{:S(2)}) %collective-permute-start.3) | collective-permute-done | bytes 393248 | tf_op jit(solution)/shard_map/ppermute | solution.py:19
  56.4 2.0 %collective-permute-done.2.refs_3_ = bf16[8,32,768]{2,1,0:T(8,128)(2,1)} collective-permute-done((bf16[8,32,768]{2,1,0:T(8,128)(2,1)}, bf16[8,32,768]{2,1,0:T(8,128)(2,1)}, u32[]{:S(2)}, u32[]{:S(2)}) %collective-permute-start.2) | collective-permute-done | bytes 393248 | tf_op jit(solution)/shard_map/ppermute | solution.py:23
  58.4 7.5 %collective-permute-done.1.refs_2_ = bf16[8,32,768]{2,1,0:T(8,128)(2,1)} collective-permute-done((bf16[8,32,768]{2,1,0:T(8,128)(2,1)}, bf16[8,32,768]{2,1,0:T(8,128)(2,1)}, u32[]{:S(2)}, u32[]{:S(2)}) %collective-permute-start.1) | collective-permute-done | bytes 393248 | tf_op jit(solution)/shard_map/ppermute | solution.py:23
  66.5 5.8 %collective-permute-done.5.refs_6_.refs_2_ = bf16[8,32,768]{2,1,0:T(8,128)(2,1)} collective-permute-done((bf16[8,32,768]{2,1,0:T(8,128)(2,1)}, bf16[8,32,768]{2,1,0:T(8,128)(2,1)}, u32[]{:S(2)}, u32[]{:S(2)}) %collective-permute-start.5) | collective-permute-done | bytes 393248 | tf_op jit(solution)/shard_map/ppermute | solution.py:23
  73.3 1.9 %copy.22 = bf16[2048,384]{1,0:T(8,128)(2,1)S(1)} copy(bf16[2048,384]{0,1:T(8,128)(2,1)} %all-gather.2.cloned.1.call-done) | data formatting | bytes 3145728 | tf_op jit(solution)/shard_map/all_gather | solution.py:166
  75.2 4.0 %collective-permute-done.6.refs_7_.refs_3_ = bf16[8,32,768]{2,1,0:T(8,128)(2,1)} collective-permute-done((bf16[8,32,768]{2,1,0:T(8,128)(2,1)}, bf16[8,32,768]{2,1,0:T(8,128)(2,1)}, u32[]{:S(2)}, u32[]{:S(2)}) %collective-permute-start.6) | collective-permute-done | bytes 393248 | tf_op jit(solution)/shard_map/ppermute | solution.py:19
  81.4 5.2 %shard_map.69 = (f32[8,4,32,384]{3,2,1,0:T(8,128)}, f32[8,4,32,384]{3,2,1,0:T(8,128)}) custom-call(bf16[8,32,768]{2,1,0:T(8,128)(2,1)} %bitcast.6.refs_0_, bf16[8,32,768]{2,1,0:T(8,128)(2,1)} %collective-permute-done.refs_1_, bf16[8,32,768]{2,1,0:T(8,128)(2,1)} %collective-permute-done.1.refs_2_, bf16[8,32,768]{2,1,0:T(8,128)(2,1)} %collective-permute-done.2.refs_3_, ...), custom_call_target="tpu_custom_call" | custom-call | flops 1207959552 | bytes 6291456 | tf_op jit(solution)/shard_map/pallas_call | solution.py:69
  88.9 7.9 %shard_map.68 = (f32[768,768]{1,0:T(8,128)}, f32[768]{0:T(1024)}, f32[768]{0:T(1024)}) custom-call(s32[8]{0:T(128)} %concatenate.7.rows_ref, s32[2]{0:T(128)} %pad_add_fusion.halves_ref, bf16[8,32,768]{2,1,0:T(8,128)(2,1)} %bitcast.6.refs_0_, bf16[8,32,768]{2,1,0:T(8,128)(2,1)} %collective-permute-done.refs_1_, ...), custom_call_target="tpu_custom_call" | custom-call | flops 2415919104 | bytes 9437184 | tf_op jit(solution)/shard_map/pallas_call | solution.py:138
  97.2 3.5 %collective-permute-done.12 = f32[768]{0:T(1024)S(1)} collective-permute-done((f32[768]{0:T(1024)}, f32[768]{0:T(1024)S(1)}, u32[]{:S(2)}, u32[]{:S(2)}) %collective-permute-start.12) | collective-permute-done | bytes 3104 | tf_op jit(solution)/shard_map/ppermute | solution.py:19
  102.7 7.3 %shard_map.70 = f32[8,8,32,384]{3,2,1,0:T(8,128)} custom-call(s32[8]{0:T(128)} %concatenate.7.rows_ref, bf16[8,32,768]{2,1,0:T(8,128)(2,1)} %collective-permute-done.3.refs_4_.refs_0_, bf16[8,32,768]{2,1,0:T(8,128)(2,1)} %collective-permute-done.4.refs_5_.refs_1_, bf16[8,32,768]{2,1,0:T(8,128)(2,1)} %collective-permute-done.5.refs_6_.refs_2_, ...), custom_call_target="tpu_custom_call" | custom-call | flops 1207959552 | bytes 10485760 | tf_op jit(solution)/shard_map/pallas_call | solution.py:83
  111.8 3.6 %collective-permute-done.13 = f32[768]{0:T(1024)S(1)} collective-permute-done((f32[768]{0:T(1024)S(1)}, f32[768]{0:T(1024)S(1)}, u32[]{:S(2)}, u32[]{:S(2)}) %collective-permute-start.13) | collective-permute-done | bytes 3104 | tf_op jit(solution)/shard_map/ppermute | solution.py:19
  116.0 4.5 %collective-permute-done.14 = f32[768]{0:T(1024)S(1)} collective-permute-done((f32[768]{0:T(1024)S(1)}, f32[768]{0:T(1024)S(1)}, u32[]{:S(2)}, u32[]{:S(2)}) %collective-permute-start.14) | collective-permute-done | bytes 3104 | tf_op jit(solution)/shard_map/ppermute | solution.py:19
  123.9 3.1 %collective-permute-done.16 = f32[2304]{0:T(1024)S(1)} collective-permute-done((f32[2304]{0:T(1024)S(1)}, f32[2304]{0:T(1024)S(1)}, u32[]{:S(2)}, u32[]{:S(2)}) %collective-permute-start.16) | collective-permute-done | bytes 9248 | tf_op jit(solution)/shard_map/ppermute | solution.py:19
  127.3 3.5 %collective-permute-done.17 = f32[2304]{0:T(1024)S(1)} collective-permute-done((f32[2304]{0:T(1024)S(1)}, f32[2304]{0:T(1024)S(1)}, u32[]{:S(2)}, u32[]{:S(2)}) %collective-permute-start.17) | collective-permute-done | bytes 9248 | tf_op jit(solution)/shard_map/ppermute | solution.py:19
  131.4 4.2 %collective-permute-done.18 = f32[2304]{0:T(1024)S(1)} collective-permute-done((f32[2304]{0:T(1024)S(1)}, f32[2304]{0:T(1024)S(1)}, u32[]{:S(2)}, u32[]{:S(2)}) %collective-permute-start.18) | collective-permute-done | bytes 9248 | tf_op jit(solution)/shard_map/ppermute | solution.py:19
  136.5 7.3 %collective-permute-done.19 = f32[2304]{0:T(1024)S(1)} collective-permute-done((f32[2304]{0:T(1024)S(1)}, f32[2304]{0:T(1024)S(1)}, u32[]{:S(2)}, u32[]{:S(2)}) %collective-permute-start.19) | collective-permute-done | bytes 9248 | tf_op jit(solution)/shard_map/ppermute | solution.py:19
  144.0 3.5 %collective-permute-done.20 = f32[128]{0:T(128)S(1)} collective-permute-done((f32[128]{0:T(128)S(1)}, f32[128]{0:T(128)S(1)}, u32[]{:S(2)}, u32[]{:S(2)}) %collective-permute-start.20) | collective-permute-done | bytes 544 | tf_op jit(solution)/shard_map/ppermute | solution.py:19
  149.1 3.4 %collective-permute-done.21 = f32[128]{0:T(128)S(1)} collective-permute-done((f32[128]{0:T(128)S(1)}, f32[128]{0:T(128)S(1)}, u32[]{:S(2)}, u32[]{:S(2)}) %collective-permute-start.21) | collective-permute-done | bytes 544 | tf_op jit(solution)/shard_map/ppermute | solution.py:19
  155.0 2.7 %collective-permute-done.22 = f32[128]{0:T(128)S(1)} collective-permute-done((f32[128]{0:T(128)S(1)}, f32[128]{0:T(128)S(1)}, u32[]{:S(2)}, u32[]{:S(2)}) %collective-permute-start.22) | collective-permute-done | bytes 544 | tf_op jit(solution)/shard_map/ppermute | solution.py:19
  157.7 2.7 %collective-permute-done.25 = f32[8,32,192]{2,1,0:T(8,128)S(1)} collective-permute-done((f32[8,32,192]{2,1,0:T(8,128)S(1)}, f32[8,32,192]{2,1,0:T(8,128)S(1)}, u32[]{:S(2)}, u32[]{:S(2)}) %collective-permute-start.25) | collective-permute-done | bytes 196640 | tf_op jit(solution)/shard_map/ppermute | solution.py:19
  (88 shorter events, 29.9 us)
Async XLA Ops:
  7.2 66.1 %all-gather.2.cloned.1.call-start = ((), (), s32[]{:S(2)}) async-start(), calls=%async_computation.2 | async-start | bytes 1769472 | tf_op jit(solution)/shard_map/all_gather | solution.py:166
  14.8 137.9 %reduce-scatter.2.cloned.1.call-start = ((), (), s32[]{:S(2)}) async-start(), calls=%async_computation.3 | async-start | bytes 3538944 | tf_op jit(solution)/shard_map/reduce_scatter | solution.py:206
  41.6 12.4 %collective-permute-start.3 = (bf16[8,32,768]{2,1,0:T(8,128)(2,1)}, bf16[8,32,768]{2,1,0:T(8,128)(2,1)}, u32[]{:S(2)}, u32[]{:S(2)}) collective-permute-start(bf16[8,32,768]{2,1,0:T(8,128)(2,1)} %bitcast.6.refs_0_), channel_id=1, source_target_pairs={{0,32},{32,0},{1,33},{33,1},{2,34},{34,2},{3,35},{35,3},{4,36},{36... | collective-permute-start | bytes 1179656 | tf_op jit(solution)/shard_map/ppermute | solution.py:19
  44.5 13.9 %collective-permute-start.2 = (bf16[8,32,768]{2,1,0:T(8,128)(2,1)}, bf16[8,32,768]{2,1,0:T(8,128)(2,1)}, u32[]{:S(2)}, u32[]{:S(2)}) collective-permute-start(bf16[8,32,768]{2,1,0:T(8,128)(2,1)} %bitcast.6.refs_0_), channel_id=1, source_target_pairs={{0,128},{64,192},{128,0},{192,64},{1,129},{65,193},{129,1},{193,65... | collective-permute-start | bytes 1179656 | tf_op jit(solution)/shard_map/ppermute | solution.py:23
  45.0 20.9 %collective-permute-start.1 = (bf16[8,32,768]{2,1,0:T(8,128)(2,1)}, bf16[8,32,768]{2,1,0:T(8,128)(2,1)}, u32[]{:S(2)}, u32[]{:S(2)}) collective-permute-start(bf16[8,32,768]{2,1,0:T(8,128)(2,1)} %bitcast.6.refs_0_), channel_id=1, source_target_pairs={{0,192},{64,0},{128,64},{192,128},{1,193},{65,1},{129,65},{193,129... | collective-permute-start | bytes 1179656 | tf_op jit(solution)/shard_map/ppermute | solution.py:23
  47.1 18.8 %collective-permute-start = (bf16[8,32,768]{2,1,0:T(8,128)(2,1)}, bf16[8,32,768]{2,1,0:T(8,128)(2,1)}, u32[]{:S(2)}, u32[]{:S(2)}) collective-permute-start(bf16[8,32,768]{2,1,0:T(8,128)(2,1)} %bitcast.6.refs_0_), channel_id=1, source_target_pairs={{0,64},{64,128},{128,192},{192,0},{1,65},{65,129},{129,193},{193,1... | collective-permute-start | bytes 1179656 | tf_op jit(solution)/shard_map/ppermute | solution.py:23
  54.0 18.4 %collective-permute-start.5 = (bf16[8,32,768]{2,1,0:T(8,128)(2,1)}, bf16[8,32,768]{2,1,0:T(8,128)(2,1)}, u32[]{:S(2)}, u32[]{:S(2)}) collective-permute-start(bf16[8,32,768]{2,1,0:T(8,128)(2,1)} %collective-permute-done.3.refs_4_.refs_0_), channel_id=1, source_target_pairs={{0,192},{64,0},{128,64},{192,128},{1,193},{65,1},{129,65},{193,129... | collective-permute-start | bytes 1179656 | tf_op jit(solution)/shard_map/ppermute | solution.py:23
  54.5 18.8 %collective-permute-start.4 = (bf16[8,32,768]{2,1,0:T(8,128)(2,1)}, bf16[8,32,768]{2,1,0:T(8,128)(2,1)}, u32[]{:S(2)}, u32[]{:S(2)}) collective-permute-start(bf16[8,32,768]{2,1,0:T(8,128)(2,1)} %collective-permute-done.3.refs_4_.refs_0_), channel_id=1, source_target_pairs={{0,64},{64,128},{128,192},{192,0},{1,65},{65,129},{129,193},{193,1... | collective-permute-start | bytes 1179656 | tf_op jit(solution)/shard_map/ppermute | solution.py:23
  58.4 16.8 %collective-permute-start.10 = (bf16[768,384]{1,0:T(8,128)(2,1)S(1)}, bf16[768,384]{1,0:T(8,128)(2,1)}, u32[]{:S(2)}, u32[]{:S(2)}) collective-permute-start(bf16[768,384]{1,0:T(8,128)(2,1)S(1)} %copy.21), channel_id=1, source_target_pairs={{0,8},{8,0},{1,9},{9,1},{2,10},{10,2},{3,11},{11,3},{4,12},{12,4},... | collective-permute-start | bytes 1769480 | tf_op jit(solution)/shard_map/ppermute | solution.py:19
  65.9 9.3 %collective-permute-start.7 = (bf16[8,32,768]{2,1,0:T(8,128)(2,1)}, bf16[8,32,768]{2,1,0:T(8,128)(2,1)}, u32[]{:S(2)}, u32[]{:S(2)}) collective-permute-start(bf16[8,32,768]{2,1,0:T(8,128)(2,1)} %collective-permute-done.3.refs_4_.refs_0_), channel_id=1, source_target_pairs={{0,8},{8,0},{1,9},{9,1},{2,10},{10,2},{3,11},{11,3},{4,12},{12,4},... | collective-permute-start | bytes 1179656 | tf_op jit(solution)/shard_map/ppermute | solution.py:19
  65.9 13.3 %collective-permute-start.6 = (bf16[8,32,768]{2,1,0:T(8,128)(2,1)}, bf16[8,32,768]{2,1,0:T(8,128)(2,1)}, u32[]{:S(2)}, u32[]{:S(2)}) collective-permute-start(bf16[8,32,768]{2,1,0:T(8,128)(2,1)} %collective-permute-done.2.refs_3_), channel_id=1, source_target_pairs={{0,32},{32,0},{1,33},{33,1},{2,34},{34,2},{3,35},{35,3},{4,36},{36... | collective-permute-start | bytes 1179656 | tf_op jit(solution)/shard_map/ppermute | solution.py:19
  72.4 6.9 %collective-permute-start.9 = (bf16[8,32,768]{2,1,0:T(8,128)(2,1)}, bf16[8,32,768]{2,1,0:T(8,128)(2,1)}, u32[]{:S(2)}, u32[]{:S(2)}) collective-permute-start(bf16[8,32,768]{2,1,0:T(8,128)(2,1)} %collective-permute-done.5.refs_6_.refs_2_), channel_id=1, source_target_pairs={{0,8},{8,0},{1,9},{9,1},{2,10},{10,2},{3,11},{11,3},{4,12},{12,4},... | collective-permute-start | bytes 1179656 | tf_op jit(solution)/shard_map/ppermute | solution.py:19
  73.3 6.0 %collective-permute-start.8 = (bf16[8,32,768]{2,1,0:T(8,128)(2,1)}, bf16[8,32,768]{2,1,0:T(8,128)(2,1)}, u32[]{:S(2)}, u32[]{:S(2)}) collective-permute-start(bf16[8,32,768]{2,1,0:T(8,128)(2,1)} %collective-permute-done.4.refs_5_.refs_1_), channel_id=1, source_target_pairs={{0,8},{8,0},{1,9},{9,1},{2,10},{10,2},{3,11},{11,3},{4,12},{12,4},... | collective-permute-start | bytes 1179656 | tf_op jit(solution)/shard_map/ppermute | solution.py:19
  79.3 9.6 %collective-permute-start.11 = (bf16[8,8,32,384]{3,2,1,0:T(8,128)(2,1)S(1)}, bf16[8,8,32,384]{3,2,1,0:T(8,128)(2,1)}, u32[]{:S(2)}, u32[]{:S(2)}) collective-permute-start(bf16[8,8,32,384]{3,2,1,0:T(8,128)(2,1)S(1)} %bitcast.27), channel_id=1, source_target_pairs={{0,8},{8,0},{1,9},{9,1},{2,10},{10,2},{3,11},{11,3},{4,12},{12,4},... | collective-permute-start | bytes 4718600 | tf_op jit(solution)/shard_map/ppermute | solution.py:19
  86.6 14.8 %collective-permute-start.24 = (f32[8,4,32,384]{3,2,1,0:T(8,128)}, f32[8,4,32,384]{3,2,1,0:T(8,128)S(1)}, u32[]{:S(2)}, u32[]{:S(2)}) collective-permute-start(f32[8,4,32,384]{3,2,1,0:T(8,128)} %get-tuple-element.55), channel_id=1, source_target_pairs={{0,8},{8,0},{1,9},{9,1},{2,10},{10,2},{3,11},{11,3},{4,12},{12,4},... | collective-permute-start | bytes 4718600 | tf_op jit(solution)/shard_map/ppermute | solution.py:19
  87.2 14.2 %collective-permute-start.23 = (bf16[8,32,768]{2,1,0:T(8,128)(2,1)}, bf16[8,32,768]{2,1,0:T(8,128)(2,1)S(1)}, u32[]{:S(2)}, u32[]{:S(2)}) collective-permute-start(bf16[8,32,768]{2,1,0:T(8,128)(2,1)} %collective-permute-done.6.refs_7_.refs_3_), channel_id=1, source_target_pairs={{0,8},{8,0},{1,9},{9,1},{2,10},{10,2},{3,11},{11,3},{4,12},{12,4},... | collective-permute-start | bytes 1179656 | tf_op jit(solution)/shard_map/ppermute | solution.py:19
  96.8 3.9 %collective-permute-start.12 = (f32[768]{0:T(1024)}, f32[768]{0:T(1024)S(1)}, u32[]{:S(2)}, u32[]{:S(2)}) collective-permute-start(f32[768]{0:T(1024)} %get-tuple-element.46), channel_id=1, source_target_pairs={{0,64},{64,0},{128,192},{192,128},{1,65},{65,1},{129,193},{193,129... | collective-permute-start | bytes 9224 | tf_op jit(solution)/shard_map/ppermute | solution.py:19
  110.1 5.2 %collective-permute-start.13 = (f32[768]{0:T(1024)S(1)}, f32[768]{0:T(1024)S(1)}, u32[]{:S(2)}, u32[]{:S(2)}) collective-permute-start(f32[768]{0:T(1024)S(1)} %add.93), channel_id=1, source_target_pairs={{0,128},{64,192},{128,0},{192,64},{1,129},{65,193},{129,1},{193,65... | collective-permute-start | bytes 9224 | tf_op jit(solution)/shard_map/ppermute | solution.py:19
  115.3 5.1 %collective-permute-start.14 = (f32[768]{0:T(1024)S(1)}, f32[768]{0:T(1024)S(1)}, u32[]{:S(2)}, u32[]{:S(2)}) collective-permute-start(f32[768]{0:T(1024)S(1)} %add.94), channel_id=1, source_target_pairs={{0,32},{32,0},{1,33},{33,1},{2,34},{34,2},{3,35},{35,3},{4,36},{36... | collective-permute-start | bytes 9224 | tf_op jit(solution)/shard_map/ppermute | solution.py:19
  130.8 4.9 %collective-permute-start.18 = (f32[2304]{0:T(1024)S(1)}, f32[2304]{0:T(1024)S(1)}, u32[]{:S(2)}, u32[]{:S(2)}) collective-permute-start(f32[2304]{0:T(1024)S(1)} %add.99), channel_id=1, source_target_pairs={{0,2},{1,3},{2,0},{3,1},{4,6},{5,7},{6,4},{7,5},{8,10},{9,11},{10,... | collective-permute-start | bytes 27656 | tf_op jit(solution)/shard_map/ppermute | solution.py:19
  135.7 8.2 %collective-permute-start.19 = (f32[2304]{0:T(1024)S(1)}, f32[2304]{0:T(1024)S(1)}, u32[]{:S(2)}, u32[]{:S(2)}) collective-permute-start(f32[2304]{0:T(1024)S(1)} %add.100), channel_id=1, source_target_pairs={{0,4},{1,5},{2,6},{3,7},{4,0},{5,1},{6,2},{7,3},{8,12},{9,13},{10,... | collective-permute-start | bytes 27656 | tf_op jit(solution)/shard_map/ppermute | solution.py:19
  147.5 5.0 %collective-permute-start.21 = (f32[128]{0:T(128)S(1)}, f32[128]{0:T(128)S(1)}, u32[]{:S(2)}, u32[]{:S(2)}) collective-permute-start(f32[128]{0:T(128)S(1)} %add.103), channel_id=1, source_target_pairs={{0,128},{64,192},{128,0},{192,64},{1,129},{65,193},{129,1},{193,65... | collective-permute-start | bytes 1544 | tf_op jit(solution)/shard_map/ppermute | solution.py:19
  152.6 5.1 %collective-permute-start.22 = (f32[128]{0:T(128)S(1)}, f32[128]{0:T(128)S(1)}, u32[]{:S(2)}, u32[]{:S(2)}) collective-permute-start(f32[128]{0:T(128)S(1)} %add.104), channel_id=1, source_target_pairs={{0,32},{32,0},{1,33},{33,1},{2,34},{34,2},{3,35},{35,3},{4,36},{36... | collective-permute-start | bytes 1544 | tf_op jit(solution)/shard_map/ppermute | solution.py:19
  153.9 6.5 %collective-permute-start.25 = (f32[8,32,192]{2,1,0:T(8,128)S(1)}, f32[8,32,192]{2,1,0:T(8,128)S(1)}, u32[]{:S(2)}, u32[]{:S(2)}) collective-permute-start(f32[8,32,192]{2,1,0:T(8,128)S(1)} %slice_select_fusion), channel_id=1, source_target_pairs={{0,16},{16,0},{1,17},{17,1},{2,18},{18,2},{3,19},{19,3},{4,20},{20... | collective-permute-start | bytes 589832 | tf_op jit(solution)/shard_map/ppermute | solution.py:19
  (12 other events, 132.9 us)
Sparse Core Ops, SparseCore 0:
  14.9 51.2 all-gather.1
  110.3 40.5 reduce-scatter.1

commit v4 on v3

--- a/solution.py
+++ b/solution.py
@@ -9,6 +9,7 @@
 D = 6144
 FF = 24576
 HALF = 384
+FIRST, SECOND = 3, 5
 VMEM = 56 * 1024 * 1024
 
 epsilon = 1e-30
@@ -40,11 +41,12 @@
 
 
 def split(part, count):
-    return [part[j * count * 32 : (j + 1) * count * 32].reshape(count, 32, HALF) for j in range(4)]
+    rows = count * 32
+    return [part[k : k + rows].reshape(count, 32, HALF) for k in range(0, part.shape[0], rows)]
 
 
 def first_kernel(*refs):
-    cots, (keep_ref, send_ref, part_keep, part_send) = refs[:4], refs[4:]
+    cots, (keep_ref, send_ref, part_keep, part_send) = refs[:FIRST], refs[FIRST:]
     cot = tokens(cots, 2)
     for weight_ref, out in ((keep_ref, part_keep), (send_ref, part_send)):
         for j, part in enumerate(split(product(cot, weight_ref), 2)):
@@ -52,26 +54,27 @@
 
 
 def second_kernel(rows_ref, *refs):
-    cots, others = refs[:4], refs[4:8]
-    keep_ref, other_ref, before_ref, recv_ref, out = refs[8:]
+    cots, others = refs[:SECOND], refs[SECOND : 2 * SECOND]
+    keep_ref, other_ref, before_ref, recv_ref, out = refs[2 * SECOND :]
     whole = product(tokens(cots, 2), keep_ref) + product(tokens(others, 2), other_ref)
+    for j in range(FIRST):
+        out[:, rows_ref[j]] = before_ref[:, j] + recv_ref[:, j]
     for j, part in enumerate(split(whole, 2)):
-        out[:, rows_ref[j]] = before_ref[:, j] + recv_ref[:, j]
-        out[:, rows_ref[4 + j]] = part
+        out[:, rows_ref[FIRST + j]] = part
 
 
 COT = pl.BlockSpec((2, 32, 768), lambda s, *_: (s, 0, 0))
 WEIGHT = pl.BlockSpec((768, HALF), lambda s, *_: (0, 0))
-PART = pl.BlockSpec((2, 4, 32, HALF), lambda s, *_: (s, 0, 0, 0))
+PART = pl.BlockSpec((2, FIRST, 32, HALF), lambda s, *_: (s, 0, 0, 0))
 
 
 def first_call(cots, keep, send):
     return pl.pallas_call(
         first_kernel,
         grid=(4,),
-        in_specs=[COT] * 4 + [WEIGHT] * 2,
+        in_specs=[COT] * FIRST + [WEIGHT] * 2,
         out_specs=[PART] * 2,
-        out_shape=[jax.ShapeDtypeStruct((8, 4, 32, HALF), jnp.float32)] * 2,
+        out_shape=[jax.ShapeDtypeStruct((8, FIRST, 32, HALF), jnp.float32)] * 2,
         compiler_params=pltpu.CompilerParams(vmem_limit_bytes=VMEM),
         cost_estimate=pl.CostEstimate(
             flops=2 * 1024 * 768 * 768, bytes_accessed=6 * 1024 * 1024, transcendentals=0
@@ -85,7 +88,7 @@
         grid_spec=pltpu.PrefetchScalarGridSpec(
             num_scalar_prefetch=1,
             grid=(4,),
-            in_specs=[COT] * 8 + [WEIGHT] * 2 + [PART] * 2,
+            in_specs=[COT] * 2 * SECOND + [WEIGHT] * 2 + [PART] * 2,
             out_specs=pl.BlockSpec((2, 8, 32, HALF), lambda s, rows: (s, 0, 0, 0)),
         ),
         out_shape=jax.ShapeDtypeStruct((8, 8, 32, HALF), jnp.float32),
@@ -175,11 +178,12 @@
     other_left = shift(other_cot, "x", 4, -1)
     other_far = exchange(far_cot, "yh", 2, 1)
     right, left, far = (x + 3) % 4, (x + 1) % 4, (x + 2) % 4
-    rows = jnp.stack([x * 2 + yh, right * 2 + yh, left * 2 + yh, far * 2 + yh])
-    rows = jnp.concatenate([rows, rows + 1 - 2 * yh]).astype(jnp.int32)
+    columns = [x, x, far, right, left, right, left, far]
+    sides = [yh, 1 - yh, yh, yh, yh, 1 - yh, 1 - yh, 1 - yh]
+    rows = jnp.stack([c * 2 + side for c, side in zip(columns, sides)]).astype(jnp.int32)
     halves = jnp.stack([core, 1 - core]).astype(jnp.int32)
-    first = [own_cot, right_cot, left_cot, far_cot]
-    second = [other_cot, other_right, other_left, other_far]
+    first = [own_cot, other_cot, far_cot]
+    second = [right_cot, left_cot, other_right, other_left, other_far]
 
     by_core = weight.reshape(768, 2, 2, 192)
     even = by_core[:, :, 0].reshape(768, HALF)
@@ -187,28 +191,22 @@
     keep = jnp.where(core == 0, even, odd)
     send = jnp.where(core == 0, odd, even)
 
+    keep_1, send_1 = first_call(first, keep, send)
+    others = [exchange(cot, "core", 2, 1) for cot in second[:2]]
+    *arrived, keep, send, keep_1, send_1, rows, halves, act_own = lax.optimization_barrier(
+        (*first, *second, *others, keep, send, keep_1, send_1, rows, halves, act_own)
+    )
+    first, second, others = arrived[:FIRST], arrived[FIRST:8], arrived[8:]
+    act_recv = exchange(act_own, "core", 2, 1)
+    recv_1 = exchange(send_1, "core", 2, 1)
     other_keep = exchange(send, "core", 2, 1)
-
-    others = [exchange(cot, "core", 2, 1) for cot in second[:3]]
-    *arrived, keep, send, other_keep, act_own = lax.optimization_barrier(
-        (*first, *second, *others, keep, send, other_keep, act_own)
-    )
-    first, second, others = arrived[:4], arrived[4:8], arrived[8:]
-    act_recv = exchange(act_own, "core", 2, 1)
-    keep_1, send_1 = first_call(first, keep, send)
-    recv_1 = exchange(send_1, "core", 2, 1)
     gradient, row_sums, col_sums = gradient_call(rows, halves, first + second, [act_own, act_recv])
 
-    others.append(exchange(second[3], "core", 2, 1))
+    others += [exchange(cot, "core", 2, 1) for cot in second[2:]]
     row_sums = row_sums + exchange(row_sums, "x", 4, 1)
     others[0], row_sums = lax.optimization_barrier((others[0], row_sums))
     summed = second_call(rows, second, others, keep, other_keep, keep_1, recv_1)
-    summed = lax.psum_scatter(summed, "z", scatter_dimension=0, tiled=True).reshape(8, 32, HALF)
-    low, high = summed[:, :, :192], summed[:, :, 192:]
-    mine = jnp.where(yl == 0, low, high)
-    theirs = jnp.where(yl == 0, high, low)
-    mine = (mine + exchange(theirs, "yl", 2, 1)).astype(jnp.bfloat16)
-    input_grad = mine.reshape(256, 192)
+    summed = lax.psum_scatter(summed, "z", scatter_dimension=0, tiled=True)
 
     row_sums = total(row_sums + exchange(row_sums, "x", 4, 2), "yh", 2)
     row_stats = decay_rate * row_prev + (1.0 - decay_rate) * (row_sums / D)
@@ -224,8 +222,18 @@
     col_sums, scaled_sums, row_mean = sums[:768], sums[768:1536], sums[1536:] / FF
     col_stats = decay_rate * col_prev + (1.0 - decay_rate) * (col_sums / FF)
     part = jnp.sum((scaled_sums * row_mean / col_stats).reshape(6, 128), axis=0)
-    part = total(total(part, "x", 4), "yh", 2)
+    part = part + exchange(part, "x", 4, 1)
+    part, summed = lax.optimization_barrier((part, summed))
+    part = total(part + exchange(part, "x", 4, 2), "yh", 2)
+
+    summed = summed.reshape(8, 32, HALF)
+    low, high = summed[:, :, :192], summed[:, :, 192:]
+    mine = jnp.where(yl == 0, low, high)
+    theirs = jnp.where(yl == 0, high, low)
+    mine = (mine + exchange(theirs, "yl", 2, 1)).astype(jnp.bfloat16)
+    input_grad = mine.reshape(256, 192)
     part, input_grad = lax.optimization_barrier((part, input_grad))
+
     squares_total = jnp.sum(part)
     root_mean = jnp.sqrt(squares_total / (FF * D))
     unclipped = gradient * lax.rsqrt(row_stats[:, None] * col_stats[None, :] / row_mean[None, :])

time: 174 us -> 170 us (0.977)
  waiting for transfers between devices: 69.7 us -> 61.5 us
  starting transfers between devices: 17.3 us -> 19.9 us
    ppermute x5, waiting for transfers between devices: 16.3 us -> 9.16 us  [shift(): lax.ppermute(value, axis, [(i, (i + step) % size) for i in range(size)])]
    ppermute x21 -> x22, waiting for transfers between devices: 53.4 us -> 48.7 us  [exchange(): return lax.ppermute(value, axis, [(i, i ^ bit) for i in range(size)])]
    reduce_scatter x1, waiting for transfers between devices: 0.01 us -> 3.59 us  [body(): summed = lax.psum_scatter(summed, 'z', scatter_dimension=0, tiled=True)]
    ppermute x21 -> x22, starting transfers between devices: 12.5 us -> 15.1 us  [exchange(): return lax.ppermute(value, axis, [(i, i ^ bit) for i in range(size)])]
  transfers between devices with their start and end apart: 28 -> 29, of which waited for: 18 -> 18; matrix products, arithmetic and copies ran while one was open for 6% -> 7% of each run, Pallas kernels for 8% -> 8%
where the time goes in v4:
time: 170 us; the launch traced here: 167 us
  waiting for transfers between devices  61.5 us (36%)
  blocking collectives  32.5 us (19%)
  Pallas kernels  20.4 us (12%)
  starting transfers between devices  19.9 us (12%)
  between operations  15 us (9%)
  local copies, waits for them, and re-layouts  10.9 us (6%)
  other arithmetic  7.3 us (4%)
    ppermute x22, waiting for transfers between devices, exchange(): return lax.ppermute(value, axis, [(i, i ^ bit) for i in range(size)])  48.7 us
    all_to_all x1, blocking collectives, body(): lax.all_to_all(cotangent, 'z', 1, 0, tiled=True).reshape(8, 32, 768)  25.6 us
    ppermute x22, starting transfers between devices, exchange(): return lax.ppermute(value, axis, [(i, i ^ bit) for i in range(size)])  15.1 us
    ppermute x5, waiting for transfers between devices, shift(): lax.ppermute(value, axis, [(i, (i + step) % size) for i in range(size)])  9.16 us
    pallas_call x1, Pallas kernels, gradient_call(): pl.pallas_call(gradient_kernel, grid_spec=pltpu.PrefetchScalarGridSpec(nu...  7.87 us
    pallas_call x1, Pallas kernels, second_call(): pl.pallas_call(second_kernel, grid_spec=pltpu.PrefetchScalarGridSpec(num_...  7.65 us
    all_gather x1, blocking collectives, body(): act_cols = lax.all_gather(activations, ('yl', 'core'), axis=1, tiled=True)  6.89 us
    pallas_call x1, Pallas kernels, first_call(): pl.pallas_call(first_kernel, grid=(4,), in_specs=[COT] * FIRST + [WEIGHT]...  4.83 us
  transfers between devices with their start and end apart: 29, of which 18 were waited for; matrix products, arithmetic and copies ran while one was open for 7% of the time, Pallas kernels for 8%

profile of v4, /device:TPU:4, one launch (start us, length us, event | category | flops | bytes accessed | tf_op | source)
XLA Modules:
  0.0 167.3 jit_solution(4896360404011727096)
XLA Ops:
  7.2 6.9 %all_gather.6 = bf16[256,768]{0,1:T(8,128)(2,1)S(1)} all-gather(bf16[256,192]{0,1:T(8,128)(2,1)} %param.6), channel_id=1, replica_groups=mesh['x'=4,'yh'=2,'yl'=2,'core'=2,'z'=8] {'yl','core'}, dimensions={1}, use_global_device_ids=true | all-gather | bytes 491520 | tf_op jit(solution)/shard_map/all_gather | solution.py:166
  15.9 25.6 %all_to_all.16 = bf16[32,8,768]{2,0,1:T(8,128)(2,1)S(1)} all-to-all(bf16[32,8,768]{2,0,1:T(8,128)(2,1)S(1)} %bitcast.34), channel_id=1, replica_groups=mesh['x'=4,'yh'=2,'yl'=2,'core'=2,'z'=8] {'z'}, dimensions={1} | all-to-all | bytes 786432 | tf_op jit(solution)/shard_map/all_to_all | solution.py:171
  41.5 2.9 %collective-permute-start = (bf16[8,32,768]{2,1,0:T(8,128)(2,1)S(1)}, bf16[8,32,768]{2,1,0:T(8,128)(2,1)}, u32[]{:S(2)}, u32[]{:S(2)}) collective-permute-start(bf16[8,32,768]{2,1,0:T(8,128)(2,1)S(1)} %bitcast.37), channel_id=1, source_target_pairs={{0,32},{32,0},{1,33},{33,1},{2,34},{34,2},{3,35},{35,3},{4,36},{36... | collective-permute-start | bytes 1179656 | tf_op jit(solution)/shard_map/ppermute | solution.py:20
  44.9 2.1 %collective-permute-start.2 = (bf16[8,32,768]{2,1,0:T(8,128)(2,1)S(1)}, bf16[8,32,768]{2,1,0:T(8,128)(2,1)S(1)}, u32[]{:S(2)}, u32[]{:S(2)}) collective-permute-start(bf16[8,32,768]{2,1,0:T(8,128)(2,1)S(1)} %bitcast.39), channel_id=1, source_target_pairs={{0,64},{64,128},{128,192},{192,0},{1,65},{65,129},{129,193},{193,1... | collective-permute-start | bytes 1179656 | tf_op jit(solution)/shard_map/ppermute | solution.py:24
  47.0 6.6 %collective-permute-done.refs_1_ = bf16[8,32,768]{2,1,0:T(8,128)(2,1)} collective-permute-done((bf16[8,32,768]{2,1,0:T(8,128)(2,1)S(1)}, bf16[8,32,768]{2,1,0:T(8,128)(2,1)}, u32[]{:S(2)}, u32[]{:S(2)}) %collective-permute-start) | collective-permute-done | bytes 393248 | tf_op jit(solution)/shard_map/ppermute | solution.py:20
  55.7 2.4 %collective-permute-done.1.refs_2_ = bf16[8,32,768]{2,1,0:T(8,128)(2,1)} collective-permute-done((bf16[8,32,768]{2,1,0:T(8,128)(2,1)S(1)}, bf16[8,32,768]{2,1,0:T(8,128)(2,1)}, u32[]{:S(2)}, u32[]{:S(2)}) %collective-permute-start.1) | collective-permute-done | bytes 393248 | tf_op jit(solution)/shard_map/ppermute | solution.py:24
  58.7 5.9 %collective-permute-done.2.refs_3_.refs_0_ = bf16[8,32,768]{2,1,0:T(8,128)(2,1)S(1)} collective-permute-done((bf16[8,32,768]{2,1,0:T(8,128)(2,1)S(1)}, bf16[8,32,768]{2,1,0:T(8,128)(2,1)S(1)}, u32[]{:S(2)}, u32[]{:S(2)}) %collective-permute-start.2) | collective-permute-done | bytes 393248 | tf_op jit(solution)/shard_map/ppermute | solution.py:24
  69.8 4.8 %shard_map.68 = (f32[8,3,32,384]{3,2,1,0:T(8,128)}, f32[8,3,32,384]{3,2,1,0:T(8,128)}) custom-call(bf16[8,32,768]{2,1,0:T(8,128)(2,1)} %bitcast.41, bf16[8,32,768]{2,1,0:T(8,128)(2,1)} %collective-permute-done.refs_1_, bf16[8,32,768]{2,1,0:T(8,128)(2,1)} %collective-permute-done.1.refs_2_, bf16[768,384]{1,0:T(8,128)(2,1)} %copy.21.refs_3_, ...), custom_call_target="tpu_custom_call" | custom-call | flops 1207959552 | bytes 6291456 | tf_op jit(solution)/shard_map/pallas_call | solution.py:72
  74.6 1.9 %copy.23 = bf16[2048,384]{1,0:T(8,128)(2,1)S(1)} copy(bf16[2048,384]{0,1:T(8,128)(2,1)} %all-gather.2.cloned.1.call-done) | data formatting | bytes 3145728 | tf_op jit(solution)/shard_map/all_gather | solution.py:169
  78.2 3.2 %collective-permute-done.9.refs_9_ = bf16[8,8,32,384]{3,2,1,0:T(8,128)(2,1)} collective-permute-done((bf16[8,8,32,384]{3,2,1,0:T(8,128)(2,1)S(1)}, bf16[8,8,32,384]{3,2,1,0:T(8,128)(2,1)}, u32[]{:S(2)}, u32[]{:S(2)}) %collective-permute-start.9) | collective-permute-done | bytes 1572896 | tf_op jit(solution)/shard_map/ppermute | solution.py:20
  81.4 7.9 %shard_map.69 = (f32[768,768]{1,0:T(8,128)}, f32[768]{0:T(1024)}, f32[768]{0:T(1024)}) custom-call(s32[8]{0:T(128)} %stack.44.rows_ref, s32[2]{0:T(128)} %pad_add_fusion.halves_ref, bf16[8,32,768]{2,1,0:T(8,128)(2,1)} %bitcast.42, bf16[8,32,768]{2,1,0:T(8,128)(2,1)} %collective-permute-done.refs_1_, bf16[8,32,768]{2,1,0:T(8,128)(2,1)} %collective-permute-done.1.refs_2_, ...), custom_call_target="tpu_custom_call" | custom-call | flops 2415919104 | bytes 9437184 | tf_op jit(solution)/shard_map/pallas_call | solution.py:141
  90.0 3.2 %collective-permute-done.10 = f32[768]{0:T(1024)S(1)} collective-permute-done((f32[768]{0:T(1024)}, f32[768]{0:T(1024)S(1)}, u32[]{:S(2)}, u32[]{:S(2)}) %collective-permute-start.10) | collective-permute-done | bytes 3104 | tf_op jit(solution)/shard_map/ppermute | solution.py:20
  96.2 7.7 %shard_map.70 = f32[8,8,32,384]{3,2,1,0:T(8,128)} custom-call(s32[8]{0:T(128)} %stack.44.rows_ref, bf16[8,32,768]{2,1,0:T(8,128)(2,1)} %copy-done.5, bf16[8,32,768]{2,1,0:T(8,128)(2,1)} %copy-done.6, bf16[8,32,768]{2,1,0:T(8,128)(2,1)} %collective-permute-done.4.refs_5_.refs_2_, bf16[8,32,768]{2,1,0:T(8,128)(2,1)} %collective-permute-done.5.refs_6_.refs_3_, ...), custom_call_target="tpu_custom_call" | custom-call | flops 1207959552 | bytes 10485760 | tf_op jit(solution)/shard_map/pallas_call | solution.py:86
  105.5 3.6 %collective-permute-done.11 = f32[768]{0:T(1024)S(1)} collective-permute-done((f32[768]{0:T(1024)S(1)}, f32[768]{0:T(1024)S(1)}, u32[]{:S(2)}, u32[]{:S(2)}) %collective-permute-start.11) | collective-permute-done | bytes 3104 | tf_op jit(solution)/shard_map/ppermute | solution.py:20
  109.8 4.5 %collective-permute-done.12 = f32[768]{0:T(1024)S(1)} collective-permute-done((f32[768]{0:T(1024)S(1)}, f32[768]{0:T(1024)S(1)}, u32[]{:S(2)}, u32[]{:S(2)}) %collective-permute-start.12) | collective-permute-done | bytes 3104 | tf_op jit(solution)/shard_map/ppermute | solution.py:20
  117.7 3.1 %collective-permute-done.14 = f32[2304]{0:T(1024)S(1)} collective-permute-done((f32[2304]{0:T(1024)S(1)}, f32[2304]{0:T(1024)S(1)}, u32[]{:S(2)}, u32[]{:S(2)}) %collective-permute-start.14) | collective-permute-done | bytes 9248 | tf_op jit(solution)/shard_map/ppermute | solution.py:20
  121.0 3.6 %collective-permute-done.15 = f32[2304]{0:T(1024)S(1)} collective-permute-done((f32[2304]{0:T(1024)S(1)}, f32[2304]{0:T(1024)S(1)}, u32[]{:S(2)}, u32[]{:S(2)}) %collective-permute-start.15) | collective-permute-done | bytes 9248 | tf_op jit(solution)/shard_map/ppermute | solution.py:20
  125.2 4.3 %collective-permute-done.16 = f32[2304]{0:T(1024)S(1)} collective-permute-done((f32[2304]{0:T(1024)S(1)}, f32[2304]{0:T(1024)S(1)}, u32[]{:S(2)}, u32[]{:S(2)}) %collective-permute-start.16) | collective-permute-done | bytes 9248 | tf_op jit(solution)/shard_map/ppermute | solution.py:20
  130.3 7.4 %collective-permute-done.17 = f32[2304]{0:T(1024)S(1)} collective-permute-done((f32[2304]{0:T(1024)S(1)}, f32[2304]{0:T(1024)S(1)}, u32[]{:S(2)}, u32[]{:S(2)}) %collective-permute-start.17) | collective-permute-done | bytes 9248 | tf_op jit(solution)/shard_map/ppermute | solution.py:20
  137.9 3.4 %collective-permute-done.18 = f32[128]{0:T(128)S(1)} collective-permute-done((f32[128]{0:T(128)S(1)}, f32[128]{0:T(128)S(1)}, u32[]{:S(2)}, u32[]{:S(2)}) %collective-permute-start.18) | collective-permute-done | bytes 544 | tf_op jit(solution)/shard_map/ppermute | solution.py:20
  141.3 3.6 %reduce-scatter.2.cloned.1.call-done = f32[1,8,32,384]{3,2,1,0:T(8,128)} async-done(((f32[8,8,32,384]{3,2,1,0:T(8,128)}), f32[1,8,32,384]{3,2,1,0:T(8,128)}) %reduce-scatter.2.cloned.1.call-update) | async-done | bytes 393232 | tf_op jit(solution)/shard_map/reduce_scatter | solution.py:209
  149.9 2.9 %collective-permute-start.25 = (f32[128]{0:T(128)S(1)}, f32[128]{0:T(128)S(1)}, u32[]{:S(2)}, u32[]{:S(2)}) collective-permute-start(f32[128]{0:T(128)S(1)} %add.116), channel_id=1, source_target_pairs={{0,32},{32,0},{1,33},{33,1},{2,34},{34,2},{3,35},{35,3},{4,36},{36... | collective-permute-start | bytes 1544 | tf_op jit(solution)/shard_map/ppermute | solution.py:20
  152.8 2.6 %collective-permute-done.25 = f32[128]{0:T(128)S(1)} collective-permute-done((f32[128]{0:T(128)S(1)}, f32[128]{0:T(128)S(1)}, u32[]{:S(2)}, u32[]{:S(2)}) %collective-permute-start.25) | collective-permute-done | bytes 544 | tf_op jit(solution)/shard_map/ppermute | solution.py:20
  158.6 1.9 %multiply_divide_fusion = f32[768,768]{1,0:T(8,128)} fusion(f32[768,768]{1,0:T(8,128)S(1)} %copy-done, f32[]{:T(128)S(6)} %max_shard_map.3, f32[768]{0:T(1024)S(1)} %slice_multiply_fusion.1, f32[768]{0:T(1024)S(1)} %get-tuple-element.73, f32[768]{0:T(1024)S(1)} %get-tuple-element.75), kind=kLoop, calls=%fused_computation | loop fusion | flops 2359296 | bytes 4727812 | tf_op jit(solution)/shard_map/div | solution.py:240
  (100 shorter events, 30.5 us)
Async XLA Ops:
  7.2 67.5 %all-gather.2.cloned.1.call-start = ((), (), s32[]{:S(2)}) async-start(), calls=%async_computation.2 | async-start | bytes 1769472 | tf_op jit(solution)/shard_map/all_gather | solution.py:169
  14.8 130.1 %reduce-scatter.2.cloned.1.call-start = ((), (), s32[]{:S(2)}) async-start(), calls=%async_computation.3 | async-start | bytes 3538944 | tf_op jit(solution)/shard_map/reduce_scatter | solution.py:209
  41.5 12.2 %collective-permute-start = (bf16[8,32,768]{2,1,0:T(8,128)(2,1)S(1)}, bf16[8,32,768]{2,1,0:T(8,128)(2,1)}, u32[]{:S(2)}, u32[]{:S(2)}) collective-permute-start(bf16[8,32,768]{2,1,0:T(8,128)(2,1)S(1)} %bitcast.37), channel_id=1, source_target_pairs={{0,32},{32,0},{1,33},{33,1},{2,34},{34,2},{3,35},{35,3},{4,36},{36... | collective-permute-start | bytes 1179656 | tf_op jit(solution)/shard_map/ppermute | solution.py:20
  44.4 13.7 %collective-permute-start.1 = (bf16[8,32,768]{2,1,0:T(8,128)(2,1)S(1)}, bf16[8,32,768]{2,1,0:T(8,128)(2,1)}, u32[]{:S(2)}, u32[]{:S(2)}) collective-permute-start(bf16[8,32,768]{2,1,0:T(8,128)(2,1)S(1)} %bitcast.38), channel_id=1, source_target_pairs={{0,128},{64,192},{128,0},{192,64},{1,129},{65,193},{129,1},{193,65... | collective-permute-start | bytes 1179656 | tf_op jit(solution)/shard_map/ppermute | solution.py:24
  44.9 19.7 %collective-permute-start.2 = (bf16[8,32,768]{2,1,0:T(8,128)(2,1)S(1)}, bf16[8,32,768]{2,1,0:T(8,128)(2,1)S(1)}, u32[]{:S(2)}, u32[]{:S(2)}) collective-permute-start(bf16[8,32,768]{2,1,0:T(8,128)(2,1)S(1)} %bitcast.39), channel_id=1, source_target_pairs={{0,64},{64,128},{128,192},{192,0},{1,65},{65,129},{129,193},{193,1... | collective-permute-start | bytes 1179656 | tf_op jit(solution)/shard_map/ppermute | solution.py:24
  47.0 18.5 %collective-permute-start.3 = (bf16[8,32,768]{2,1,0:T(8,128)(2,1)S(1)}, bf16[8,32,768]{2,1,0:T(8,128)(2,1)S(1)}, u32[]{:S(2)}, u32[]{:S(2)}) collective-permute-start(bf16[8,32,768]{2,1,0:T(8,128)(2,1)S(1)} %bitcast.40), channel_id=1, source_target_pairs={{0,192},{64,0},{128,64},{192,128},{1,193},{65,1},{129,65},{193,129... | collective-permute-start | bytes 1179656 | tf_op jit(solution)/shard_map/ppermute | solution.py:24
  53.7 22.9 %collective-permute-start.4 = (bf16[8,32,768]{2,1,0:T(8,128)(2,1)}, bf16[8,32,768]{2,1,0:T(8,128)(2,1)}, u32[]{:S(2)}, u32[]{:S(2)}) collective-permute-start(bf16[8,32,768]{2,1,0:T(8,128)(2,1)} %collective-permute-done.refs_1_), channel_id=1, source_target_pairs={{0,64},{64,128},{128,192},{192,0},{1,65},{65,129},{129,193},{193,1... | collective-permute-start | bytes 1179656 | tf_op jit(solution)/shard_map/ppermute | solution.py:24
  54.9 21.7 %collective-permute-start.5 = (bf16[8,32,768]{2,1,0:T(8,128)(2,1)}, bf16[8,32,768]{2,1,0:T(8,128)(2,1)}, u32[]{:S(2)}, u32[]{:S(2)}) collective-permute-start(bf16[8,32,768]{2,1,0:T(8,128)(2,1)} %collective-permute-done.refs_1_), channel_id=1, source_target_pairs={{0,192},{64,0},{128,64},{192,128},{1,193},{65,1},{129,65},{193,129... | collective-permute-start | bytes 1179656 | tf_op jit(solution)/shard_map/ppermute | solution.py:24
  58.0 18.5 %collective-permute-start.6 = (bf16[8,32,768]{2,1,0:T(8,128)(2,1)}, bf16[8,32,768]{2,1,0:T(8,128)(2,1)}, u32[]{:S(2)}, u32[]{:S(2)}) collective-permute-start(bf16[8,32,768]{2,1,0:T(8,128)(2,1)} %collective-permute-done.1.refs_2_), channel_id=1, source_target_pairs={{0,32},{32,0},{1,33},{33,1},{2,34},{34,2},{3,35},{35,3},{4,36},{36... | collective-permute-start | bytes 1179656 | tf_op jit(solution)/shard_map/ppermute | solution.py:20
  64.6 11.9 %collective-permute-start.7 = (bf16[8,32,768]{2,1,0:T(8,128)(2,1)S(1)}, bf16[8,32,768]{2,1,0:T(8,128)(2,1)}, u32[]{:S(2)}, u32[]{:S(2)}) collective-permute-start(bf16[8,32,768]{2,1,0:T(8,128)(2,1)S(1)} %collective-permute-done.2.refs_3_.refs_0_), channel_id=1, source_target_pairs={{0,8},{8,0},{1,9},{9,1},{2,10},{10,2},{3,11},{11,3},{4,12},{12,4},... | collective-permute-start | bytes 1179656 | tf_op jit(solution)/shard_map/ppermute | solution.py:20
  65.5 11.1 %collective-permute-start.8 = (bf16[8,32,768]{2,1,0:T(8,128)(2,1)S(1)}, bf16[8,32,768]{2,1,0:T(8,128)(2,1)}, u32[]{:S(2)}, u32[]{:S(2)}) collective-permute-start(bf16[8,32,768]{2,1,0:T(8,128)(2,1)S(1)} %collective-permute-done.3.refs_4_.refs_1_), channel_id=1, source_target_pairs={{0,8},{8,0},{1,9},{9,1},{2,10},{10,2},{3,11},{11,3},{4,12},{12,4},... | collective-permute-start | bytes 1179656 | tf_op jit(solution)/shard_map/ppermute | solution.py:20
  76.6 4.8 %collective-permute-start.9 = (bf16[8,8,32,384]{3,2,1,0:T(8,128)(2,1)S(1)}, bf16[8,8,32,384]{3,2,1,0:T(8,128)(2,1)}, u32[]{:S(2)}, u32[]{:S(2)}) collective-permute-start(bf16[8,8,32,384]{3,2,1,0:T(8,128)(2,1)S(1)} %bitcast.32), channel_id=1, source_target_pairs={{0,8},{8,0},{1,9},{9,1},{2,10},{10,2},{3,11},{11,3},{4,12},{12,4},... | collective-permute-start | bytes 4718600 | tf_op jit(solution)/shard_map/ppermute | solution.py:20
  77.1 18.1 %collective-permute-start.23 = (f32[8,3,32,384]{3,2,1,0:T(8,128)}, f32[8,3,32,384]{3,2,1,0:T(8,128)}, u32[]{:S(2)}, u32[]{:S(2)}) collective-permute-start(f32[8,3,32,384]{3,2,1,0:T(8,128)} %get-tuple-element.61), channel_id=1, source_target_pairs={{0,8},{8,0},{1,9},{9,1},{2,10},{10,2},{3,11},{11,3},{4,12},{12,4},... | collective-permute-start | bytes 3538952 | tf_op jit(solution)/shard_map/ppermute | solution.py:20
  77.5 17.6 %collective-permute-start.22 = (bf16[768,384]{1,0:T(8,128)(2,1)S(1)}, bf16[768,384]{1,0:T(8,128)(2,1)S(1)}, u32[]{:S(2)}, u32[]{:S(2)}) collective-permute-start(bf16[768,384]{1,0:T(8,128)(2,1)S(1)} %copy.24), channel_id=1, source_target_pairs={{0,8},{8,0},{1,9},{9,1},{2,10},{10,2},{3,11},{11,3},{4,12},{12,4},... | collective-permute-start | bytes 1769480 | tf_op jit(solution)/shard_map/ppermute | solution.py:20
  89.3 3.9 %collective-permute-start.10 = (f32[768]{0:T(1024)}, f32[768]{0:T(1024)S(1)}, u32[]{:S(2)}, u32[]{:S(2)}) collective-permute-start(f32[768]{0:T(1024)} %get-tuple-element.54), channel_id=1, source_target_pairs={{0,64},{64,0},{128,192},{192,128},{1,65},{65,1},{129,193},{193,129... | collective-permute-start | bytes 9224 | tf_op jit(solution)/shard_map/ppermute | solution.py:20
  89.4 5.5 %collective-permute-start.19 = (bf16[8,32,768]{2,1,0:T(8,128)(2,1)}, bf16[8,32,768]{2,1,0:T(8,128)(2,1)S(1)}, u32[]{:S(2)}, u32[]{:S(2)}) collective-permute-start(bf16[8,32,768]{2,1,0:T(8,128)(2,1)} %collective-permute-done.4.refs_5_.refs_2_), channel_id=1, source_target_pairs={{0,8},{8,0},{1,9},{9,1},{2,10},{10,2},{3,11},{11,3},{4,12},{12,4},... | collective-permute-start | bytes 1179656 | tf_op jit(solution)/shard_map/ppermute | solution.py:20
  89.8 5.1 %collective-permute-start.20 = (bf16[8,32,768]{2,1,0:T(8,128)(2,1)}, bf16[8,32,768]{2,1,0:T(8,128)(2,1)S(1)}, u32[]{:S(2)}, u32[]{:S(2)}) collective-permute-start(bf16[8,32,768]{2,1,0:T(8,128)(2,1)} %collective-permute-done.5.refs_6_.refs_3_), channel_id=1, source_target_pairs={{0,8},{8,0},{1,9},{9,1},{2,10},{10,2},{3,11},{11,3},{4,12},{12,4},... | collective-permute-start | bytes 1179656 | tf_op jit(solution)/shard_map/ppermute | solution.py:20
  103.9 5.2 %collective-permute-start.11 = (f32[768]{0:T(1024)S(1)}, f32[768]{0:T(1024)S(1)}, u32[]{:S(2)}, u32[]{:S(2)}) collective-permute-start(f32[768]{0:T(1024)S(1)} %add.105), channel_id=1, source_target_pairs={{0,128},{64,192},{128,0},{192,64},{1,129},{65,193},{129,1},{193,65... | collective-permute-start | bytes 9224 | tf_op jit(solution)/shard_map/ppermute | solution.py:20
  109.1 5.1 %collective-permute-start.12 = (f32[768]{0:T(1024)S(1)}, f32[768]{0:T(1024)S(1)}, u32[]{:S(2)}, u32[]{:S(2)}) collective-permute-start(f32[768]{0:T(1024)S(1)} %add.106), channel_id=1, source_target_pairs={{0,32},{32,0},{1,33},{33,1},{2,34},{34,2},{3,35},{35,3},{4,36},{36... | collective-permute-start | bytes 9224 | tf_op jit(solution)/shard_map/ppermute | solution.py:20
  124.7 4.9 %collective-permute-start.16 = (f32[2304]{0:T(1024)S(1)}, f32[2304]{0:T(1024)S(1)}, u32[]{:S(2)}, u32[]{:S(2)}) collective-permute-start(f32[2304]{0:T(1024)S(1)} %add.111), channel_id=1, source_target_pairs={{0,2},{1,3},{2,0},{3,1},{4,6},{5,7},{6,4},{7,5},{8,10},{9,11},{10,... | collective-permute-start | bytes 27656 | tf_op jit(solution)/shard_map/ppermute | solution.py:20
  129.5 8.1 %collective-permute-start.17 = (f32[2304]{0:T(1024)S(1)}, f32[2304]{0:T(1024)S(1)}, u32[]{:S(2)}, u32[]{:S(2)}) collective-permute-start(f32[2304]{0:T(1024)S(1)} %add.112), channel_id=1, source_target_pairs={{0,4},{1,5},{2,6},{3,7},{4,0},{5,1},{6,2},{7,3},{8,12},{9,13},{10,... | collective-permute-start | bytes 27656 | tf_op jit(solution)/shard_map/ppermute | solution.py:20
  144.9 5.0 %collective-permute-start.24 = (f32[128]{0:T(128)S(1)}, f32[128]{0:T(128)S(1)}, u32[]{:S(2)}, u32[]{:S(2)}) collective-permute-start(f32[128]{0:T(128)S(1)} %add.115), channel_id=1, source_target_pairs={{0,128},{64,192},{128,0},{192,64},{1,129},{65,193},{129,1},{193,65... | collective-permute-start | bytes 1544 | tf_op jit(solution)/shard_map/ppermute | solution.py:20
  146.8 8.6 %collective-permute-start.26 = (f32[8,32,192]{2,1,0:T(8,128)S(1)}, f32[8,32,192]{2,1,0:T(8,128)S(1)}, u32[]{:S(2)}, u32[]{:S(2)}) collective-permute-start(f32[8,32,192]{2,1,0:T(8,128)S(1)} %slice_select_fusion), channel_id=1, source_target_pairs={{0,16},{16,0},{1,17},{17,1},{2,18},{18,2},{3,19},{19,3},{4,20},{20... | collective-permute-start | bytes 589832 | tf_op jit(solution)/shard_map/ppermute | solution.py:20
  149.9 5.5 %collective-permute-start.25 = (f32[128]{0:T(128)S(1)}, f32[128]{0:T(128)S(1)}, u32[]{:S(2)}, u32[]{:S(2)}) collective-permute-start(f32[128]{0:T(128)S(1)} %add.116), channel_id=1, source_target_pairs={{0,32},{32,0},{1,33},{33,1},{2,34},{34,2},{3,35},{35,3},{4,36},{36... | collective-permute-start | bytes 1544 | tf_op jit(solution)/shard_map/ppermute | solution.py:20
  (18 other events, 180.9 us)
Sparse Core Ops, SparseCore 0:
  14.9 51.2 all-gather.1
  104.0 40.8 reduce-scatter.1

commit v5 on v4

--- a/solution.py
+++ b/solution.py
@@ -30,6 +30,37 @@
         value = value + exchange(value, axis, size, bit)
         bit *= 2
     return value
+
+
+def reduce_four(value, axis, size, bits):
+    others = [exchange(value, axis, size, bit) for bit in bits]
+    for other in others:
+        value = value + other
+    return value
+
+
+def weight_kernel(core_ref, weight_ref, keep_ref, send_ref):
+    weight = weight_ref[...]
+    even = jnp.concatenate([weight[:, :192], weight[:, HALF : HALF + 192]], axis=1)
+    odd = jnp.concatenate([weight[:, 192:HALF], weight[:, HALF + 192 :]], axis=1)
+    first = core_ref[0] == 0
+    keep_ref[...] = jnp.where(first, even, odd)
+    send_ref[...] = jnp.where(first, odd, even)
+
+
+def weight_call(halves, weight):
+    spec = pl.BlockSpec((256, HALF), lambda s, halves: (s, 0))
+    return pl.pallas_call(
+        weight_kernel,
+        grid_spec=pltpu.PrefetchScalarGridSpec(
+            num_scalar_prefetch=1,
+            grid=(3,),
+            in_specs=[pl.BlockSpec((256, 768), lambda s, halves: (s, 0))],
+            out_specs=[spec, spec],
+        ),
+        out_shape=[jax.ShapeDtypeStruct((768, HALF), jnp.bfloat16)] * 2,
+        compiler_params=pltpu.CompilerParams(vmem_limit_bytes=VMEM),
+    )(halves, weight)
 
 
 def tokens(refs, count):
@@ -170,61 +201,52 @@
 
     own_cot = lax.all_to_all(cotangent, "z", 1, 0, tiled=True).reshape(8, 32, 768)
     own_cot, weight = lax.optimization_barrier((own_cot, weight))
+    right, left, far = (x + 3) % 4, (x + 1) % 4, (x + 2) % 4
+    columns = [x, x, far, right, left, far, right, left]
+    sides = [yh, 1 - yh, yh, yh, yh, 1 - yh, 1 - yh, 1 - yh]
+    rows = jnp.stack([c * 2 + side for c, side in zip(columns, sides)]).astype(jnp.int32)
+    halves = jnp.stack([core, 1 - core]).astype(jnp.int32)
+    keep, send = weight_call(halves, weight)
+
     other_cot = exchange(own_cot, "yh", 2, 1)
+    other_cot, keep, send, rows, halves = lax.optimization_barrier((other_cot, keep, send, rows, halves))
     right_cot = shift(own_cot, "x", 4, 1)
     left_cot = shift(own_cot, "x", 4, -1)
     far_cot = shift(own_cot, "x", 4, 2)
     other_right = shift(other_cot, "x", 4, 1)
     other_left = shift(other_cot, "x", 4, -1)
     other_far = exchange(far_cot, "yh", 2, 1)
-    right, left, far = (x + 3) % 4, (x + 1) % 4, (x + 2) % 4
-    columns = [x, x, far, right, left, right, left, far]
-    sides = [yh, 1 - yh, yh, yh, yh, 1 - yh, 1 - yh, 1 - yh]
-    rows = jnp.stack([c * 2 + side for c, side in zip(columns, sides)]).astype(jnp.int32)
-    halves = jnp.stack([core, 1 - core]).astype(jnp.int32)
     first = [own_cot, other_cot, far_cot]
-    second = [right_cot, left_cot, other_right, other_left, other_far]
-
-    by_core = weight.reshape(768, 2, 2, 192)
-    even = by_core[:, :, 0].reshape(768, HALF)
-    odd = by_core[:, :, 1].reshape(768, HALF)
-    keep = jnp.where(core == 0, even, odd)
-    send = jnp.where(core == 0, odd, even)
+    second = [right_cot, left_cot, other_far, other_right, other_left]
 
     keep_1, send_1 = first_call(first, keep, send)
-    others = [exchange(cot, "core", 2, 1) for cot in second[:2]]
-    *arrived, keep, send, keep_1, send_1, rows, halves, act_own = lax.optimization_barrier(
-        (*first, *second, *others, keep, send, keep_1, send_1, rows, halves, act_own)
+    keep_1, send_1, *second[:2] = lax.optimization_barrier((keep_1, send_1, *second[:2]))
+    others = [exchange(cot, "core", 2, 1) for cot in second[:5]]
+    other_keep = exchange(send, "core", 2, 1)
+    *arrived, other_keep, keep_1, send_1, act_own = lax.optimization_barrier(
+        (*first, *second, *others, other_keep, keep_1, send_1, act_own)
     )
     first, second, others = arrived[:FIRST], arrived[FIRST:8], arrived[8:]
+    recv_1 = exchange(send_1, "core", 2, 1)
+    others += [exchange(cot, "core", 2, 1) for cot in second[5:]]
     act_recv = exchange(act_own, "core", 2, 1)
-    recv_1 = exchange(send_1, "core", 2, 1)
-    other_keep = exchange(send, "core", 2, 1)
+    summed = second_call(rows, second, others, keep, other_keep, keep_1, recv_1)
+    summed, act_recv = lax.optimization_barrier((summed, act_recv))
+    summed = lax.psum_scatter(summed, "z", scatter_dimension=0, tiled=True)
     gradient, row_sums, col_sums = gradient_call(rows, halves, first + second, [act_own, act_recv])
 
-    others += [exchange(cot, "core", 2, 1) for cot in second[2:]]
-    row_sums = row_sums + exchange(row_sums, "x", 4, 1)
-    others[0], row_sums = lax.optimization_barrier((others[0], row_sums))
-    summed = second_call(rows, second, others, keep, other_keep, keep_1, recv_1)
-    summed = lax.psum_scatter(summed, "z", scatter_dimension=0, tiled=True)
-
-    row_sums = total(row_sums + exchange(row_sums, "x", 4, 2), "yh", 2)
+    row_sums = total(reduce_four(row_sums, "x", 4, (1, 2, 3)), "yh", 2)
     row_stats = decay_rate * row_prev + (1.0 - decay_rate) * (row_sums / D)
     scaled = gradient * lax.rsqrt(row_stats)[:, None]
-    sums = jnp.concatenate(
-        [
-            col_sums,
-            jnp.sum(scaled * scaled, axis=0),
-            jnp.broadcast_to(jnp.sum(row_stats), (768,)),
-        ]
-    )
-    sums = total(total(total(sums, "core", 2), "yl", 2), "z", 8)
-    col_sums, scaled_sums, row_mean = sums[:768], sums[768:1536], sums[1536:] / FF
-    col_stats = decay_rate * col_prev + (1.0 - decay_rate) * (col_sums / FF)
-    part = jnp.sum((scaled_sums * row_mean / col_stats).reshape(6, 128), axis=0)
-    part = part + exchange(part, "x", 4, 1)
-    part, summed = lax.optimization_barrier((part, summed))
-    part = total(part + exchange(part, "x", 4, 2), "yh", 2)
+    sums = jnp.concatenate([col_sums, jnp.sum(scaled * scaled, axis=0), row_stats])
+    sums = total(total(sums, "core", 2), "yl", 2)
+    sums = sums + exchange(sums, "z", 8, 1)
+    sums = reduce_four(sums, "z", 8, (2, 4, 6))
+    sums, summed = lax.optimization_barrier((sums, summed))
+    row_mean = jnp.sum(sums[1536:]) / FF
+    col_stats = decay_rate * col_prev + (1.0 - decay_rate) * (sums[:768] / FF)
+    part = jnp.sum((sums[768:1536] / col_stats).reshape(6, 128), axis=0)
+    part = total(reduce_four(part, "x", 4, (1, 2, 3)), "yh", 2)
 
     summed = summed.reshape(8, 32, HALF)
     low, high = summed[:, :, :192], summed[:, :, 192:]
@@ -234,9 +256,9 @@
     input_grad = mine.reshape(256, 192)
     part, input_grad = lax.optimization_barrier((part, input_grad))
 
-    squares_total = jnp.sum(part)
+    squares_total = jnp.sum(part) * row_mean
     root_mean = jnp.sqrt(squares_total / (FF * D))
-    unclipped = gradient * lax.rsqrt(row_stats[:, None] * col_stats[None, :] / row_mean[None, :])
+    unclipped = gradient * lax.rsqrt(row_stats[:, None] * col_stats[None, :] / row_mean)
     update = unclipped / jnp.maximum(1.0, root_mean)
     return (input_grad, update)
 

time: 170 us -> 158 us (0.929)
  waiting for transfers between devices: 61.5 us -> 38.6 us
  starting transfers between devices: 19.9 us -> 31.1 us
  local copies, waits for them, and re-layouts: 10.9 us -> 6.16 us
  Pallas kernels: 20.4 us -> 24.4 us
    ppermute x22 -> x25, waiting for transfers between devices: 48.7 us -> 28.2 us  [exchange(): return lax.ppermute(value, axis, [(i, i ^ bit) for i in range(size)])]
    ppermute x22 -> x25, starting transfers between devices: 15.1 us -> 26.2 us  [exchange(): return lax.ppermute(value, axis, [(i, i ^ bit) for i in range(size)])]
    pallas_call x0 -> x1, Pallas kernels: none -> 3.97 us  [weight_call(): pl.pallas_call(weight_kernel, grid_spec=pltpu.PrefetchScalarGridSpec(num_...]
    reduce_scatter x1, waiting for transfers between devices: 3.59 us -> 0.54 us  [body(): summed = lax.psum_scatter(summed, 'z', scatter_dimension=0, tiled=True)]
    select_n x2 -> x0, local copies, waits for them, and re-layouts: 2.18 us -> none  [the longest x1 1.12 us: body(): send = jnp.where(core == 0, odd, even)]
    optimization_barrier x3 -> x0, local copies, waits for them, and re-layouts: 1.99 us -> none  [the longest x2 1.36 us: body(): lax.optimization_barrier((*first, *second, *others, keep, send, keep_1, s...]
    reduce_sum x1, other arithmetic: 0.3 us -> 2.01 us  [body(): jnp.sum(scaled * scaled, axis=0)]
  transfers between devices with their start and end apart: 29 -> 32, of which waited for: 18 -> 18; matrix products, arithmetic and copies ran while one was open for 7% -> 6% of each run, Pallas kernels for 8% -> 16%
where the time goes in v5:
time: 158 us; the launch traced here: 157 us
  waiting for transfers between devices  38.6 us (24%)
  blocking collectives  32.3 us (20%)
  starting transfers between devices  31.1 us (20%)
  Pallas kernels  24.4 us (15%)
  between operations  15.6 us (10%)
  other arithmetic  8.82 us (6%)
  local copies, waits for them, and re-layouts  6.16 us (4%)
    ppermute x25, waiting for transfers between devices, exchange(): return lax.ppermute(value, axis, [(i, i ^ bit) for i in range(size)])  28.2 us
    ppermute x25, starting transfers between devices, exchange(): return lax.ppermute(value, axis, [(i, i ^ bit) for i in range(size)])  26.2 us
    all_to_all x1, blocking collectives, body(): lax.all_to_all(cotangent, 'z', 1, 0, tiled=True).reshape(8, 32, 768)  25.6 us
    ppermute x5, waiting for transfers between devices, shift(): lax.ppermute(value, axis, [(i, (i + step) % size) for i in range(size)])  9.79 us
    pallas_call x1, Pallas kernels, gradient_call(): pl.pallas_call(gradient_kernel, grid_spec=pltpu.PrefetchScalarGridSpec(nu...  7.88 us
    pallas_call x1, Pallas kernels, second_call(): pl.pallas_call(second_kernel, grid_spec=pltpu.PrefetchScalarGridSpec(num_...  7.66 us
    all_gather x1, blocking collectives, body(): act_cols = lax.all_gather(activations, ('yl', 'core'), axis=1, tiled=True)  6.76 us
    pallas_call x1, Pallas kernels, first_call(): pl.pallas_call(first_kernel, grid=(4,), in_specs=[COT] * FIRST + [WEIGHT]...  4.85 us
  transfers between devices with their start and end apart: 32, of which 18 were waited for; matrix products, arithmetic and copies ran while one was open for 6% of the time, Pallas kernels for 16%

profile of v5, /device:TPU:4, one launch (start us, length us, event | category | flops | bytes accessed | tf_op | source)
XLA Modules:
  0.0 156.9 jit_solution(12343188469845222029)
XLA Ops:
  7.2 6.8 %all_gather.6 = bf16[256,768]{0,1:T(8,128)(2,1)S(1)} all-gather(bf16[256,192]{0,1:T(8,128)(2,1)} %param.6), channel_id=1, replica_groups=mesh['x'=4,'yh'=2,'yl'=2,'core'=2,'z'=8] {'yl','core'}, dimensions={1}, use_global_device_ids=true | all-gather | bytes 491520 | tf_op jit(solution)/shard_map/all_gather | solution.py:197
  15.8 25.6 %all_to_all.16 = bf16[32,8,768]{2,0,1:T(8,128)(2,1)S(1)} all-to-all(bf16[32,8,768]{2,0,1:T(8,128)(2,1)S(1)} %bitcast.24), channel_id=1, replica_groups=mesh['x'=4,'yh'=2,'yl'=2,'core'=2,'z'=8] {'z'}, dimensions={1} | all-to-all | bytes 786432 | tf_op jit(solution)/shard_map/all_to_all | solution.py:202
  41.3 2.9 %collective-permute-start = (bf16[8,32,768]{2,1,0:T(8,128)(2,1)S(1)}, bf16[8,32,768]{2,1,0:T(8,128)(2,1)S(1)}, u32[]{:S(2)}, u32[]{:S(2)}) collective-permute-start(bf16[8,32,768]{2,1,0:T(8,128)(2,1)S(1)} %bitcast.27), channel_id=1, source_target_pairs={{0,32},{32,0},{1,33},{33,1},{2,34},{34,2},{3,35},{35,3},{4,36},{36... | collective-permute-start | bytes 1179656 | tf_op jit(solution)/shard_map/ppermute | solution.py:20
  44.7 2.2 %collective-permute-start.3 = (bf16[8,32,768]{2,1,0:T(8,128)(2,1)S(1)}, bf16[8,32,768]{2,1,0:T(8,128)(2,1)S(1)}, u32[]{:S(2)}, u32[]{:S(2)}) collective-permute-start(bf16[8,32,768]{2,1,0:T(8,128)(2,1)S(1)} %bitcast.29), channel_id=1, source_target_pairs={{0,192},{64,0},{128,64},{192,128},{1,193},{65,1},{129,65},{193,129... | collective-permute-start | bytes 1179656 | tf_op jit(solution)/shard_map/ppermute | solution.py:24
  48.2 4.0 %shard_map.68 = (bf16[768,384]{1,0:T(8,128)(2,1)}, bf16[768,384]{1,0:T(8,128)(2,1)}) custom-call(s32[2]{0:T(128)} %pad_add_fusion.core_ref.halves_ref, bf16[768,768]{1,0:T(8,128)(2,1)} %weight_ref), custom_call_target="tpu_custom_call" | custom-call | tf_op jit(solution)/shard_map/pallas_call | solution.py:53
  55.6 2.3 %collective-permute-done.1.refs_2_ = bf16[8,32,768]{2,1,0:T(8,128)(2,1)S(1)} collective-permute-done((bf16[8,32,768]{2,1,0:T(8,128)(2,1)S(1)}, bf16[8,32,768]{2,1,0:T(8,128)(2,1)S(1)}, u32[]{:S(2)}, u32[]{:S(2)}) %collective-permute-start.1) | collective-permute-done | bytes 393248 | tf_op jit(solution)/shard_map/ppermute | solution.py:24
  58.6 4.8 %shard_map.69 = (f32[8,3,32,384]{3,2,1,0:T(8,128)}, f32[8,3,32,384]{3,2,1,0:T(8,128)}) custom-call(bf16[8,32,768]{2,1,0:T(8,128)(2,1)} %bitcast.31, bf16[8,32,768]{2,1,0:T(8,128)(2,1)} %copy-done.11, bf16[8,32,768]{2,1,0:T(8,128)(2,1)} %copy-done.12, bf16[768,384]{1,0:T(8,128)(2,1)} %get-tuple-element.53.refs_3_.refs_10_, ...), custom_call_target="tpu_custom_call" | custom-call | flops 1207959552 | bytes 6291456 | tf_op jit(solution)/shard_map/pallas_call | solution.py:103
  63.4 1.9 %collective-permute-done.3.refs_1_.refs_4_ = bf16[8,32,768]{2,1,0:T(8,128)(2,1)S(1)} collective-permute-done((bf16[8,32,768]{2,1,0:T(8,128)(2,1)S(1)}, bf16[8,32,768]{2,1,0:T(8,128)(2,1)S(1)}, u32[]{:S(2)}, u32[]{:S(2)}) %collective-permute-start.3) | collective-permute-done | bytes 393248 | tf_op jit(solution)/shard_map/ppermute | solution.py:24
  67.2 4.7 %collective-permute-done.6.refs_4_.refs_7_ = bf16[8,32,768]{2,1,0:T(8,128)(2,1)} collective-permute-done((bf16[8,32,768]{2,1,0:T(8,128)(2,1)S(1)}, bf16[8,32,768]{2,1,0:T(8,128)(2,1)}, u32[]{:S(2)}, u32[]{:S(2)}) %collective-permute-start.6) | collective-permute-done | bytes 393248 | tf_op jit(solution)/shard_map/ppermute | solution.py:24
  73.4 1.9 %copy.13 = bf16[2048,384]{1,0:T(8,128)(2,1)S(1)} copy(bf16[2048,384]{0,1:T(8,128)(2,1)} %all-gather.2.cloned.1.call-done) | data formatting | bytes 3145728 | tf_op jit(solution)/shard_map/all_gather | solution.py:200
  76.0 4.8 %collective-permute-done.13.refs_13_ = f32[8,3,32,384]{3,2,1,0:T(8,128)S(1)} collective-permute-done((f32[8,3,32,384]{3,2,1,0:T(8,128)}, f32[8,3,32,384]{3,2,1,0:T(8,128)S(1)}, u32[]{:S(2)}, u32[]{:S(2)}) %collective-permute-start.13) | collective-permute-done | bytes 1179680 | tf_op jit(solution)/shard_map/ppermute | solution.py:20
  81.8 7.7 %shard_map.70 = f32[8,8,32,384]{3,2,1,0:T(8,128)} custom-call(s32[8]{0:T(128)} %stack.47.rows_ref, bf16[8,32,768]{2,1,0:T(8,128)(2,1)} %copy-done.6, bf16[8,32,768]{2,1,0:T(8,128)(2,1)} %copy-done.5, bf16[8,32,768]{2,1,0:T(8,128)(2,1)} %collective-permute-done.4.refs_2_.refs_5_, bf16[8,32,768]{2,1,0:T(8,128)(2,1)} %collective-permute-done.5.refs_3_.refs_6_, ...), custom_call_target="tpu_custom_call" | custom-call | flops 1207959552 | bytes 10485760 | tf_op jit(solution)/shard_map/pallas_call | solution.py:117
  89.5 7.9 %shard_map.71 = (f32[768,768]{1,0:T(8,128)}, f32[768]{0:T(1024)}, f32[768]{0:T(1024)}) custom-call(s32[8]{0:T(128)} %stack.47.rows_ref, s32[2]{0:T(128)} %pad_add_fusion.core_ref.halves_ref, bf16[8,32,768]{2,1,0:T(8,128)(2,1)} %bitcast.32, bf16[8,32,768]{2,1,0:T(8,128)(2,1)} %copy-done.11, bf16[8,32,768]{2,1,0:T(8,128)(2,1)} %copy-done.12, ...), custom_call_target="tpu_custom_call" | custom-call | flops 2415919104 | bytes 9437184 | tf_op jit(solution)/shard_map/pallas_call | solution.py:172
  98.6 2.8 %collective-permute-start.16 = (f32[768]{0:T(1024)}, f32[768]{0:T(1024)S(1)}, u32[]{:S(2)}, u32[]{:S(2)}) collective-permute-start(f32[768]{0:T(1024)} %get-tuple-element.82), channel_id=1, source_target_pairs={{0,128},{64,192},{128,0},{192,64},{1,129},{65,193},{129,1},{193,65... | collective-permute-start | bytes 9224 | tf_op jit(solution)/shard_map/ppermute | solution.py:20
  101.6 2.3 %collective-permute-done.16 = f32[768]{0:T(1024)S(1)} collective-permute-done((f32[768]{0:T(1024)}, f32[768]{0:T(1024)S(1)}, u32[]{:S(2)}, u32[]{:S(2)}) %collective-permute-start.16) | collective-permute-done | bytes 3104 | tf_op jit(solution)/shard_map/ppermute | solution.py:20
  106.7 4.4 %collective-permute-done.18 = f32[768]{0:T(1024)S(1)} collective-permute-done((f32[768]{0:T(1024)S(1)}, f32[768]{0:T(1024)S(1)}, u32[]{:S(2)}, u32[]{:S(2)}) %collective-permute-start.18) | collective-permute-done | bytes 3104 | tf_op jit(solution)/shard_map/ppermute | solution.py:20
  111.0 2.0 %multiply_reduce_fusion = f32[768]{0:T(1024)S(1)} fusion(f32[768,768]{1,0:T(8,128)} %get-tuple-element.81, f32[768]{0:T(1024)S(1)} %get-tuple-element.96), kind=kLoop, calls=%fused_computation.1 | loop fusion | flops 1768704 | bytes 2365440 | tf_op jit(solution)/shard_map/reduce_sum | solution.py:241
  114.9 3.2 %collective-permute-done.20 = f32[2304]{0:T(1024)S(1)} collective-permute-done((f32[2304]{0:T(1024)S(1)}, f32[2304]{0:T(1024)S(1)}, u32[]{:S(2)}, u32[]{:S(2)}) %collective-permute-start.20) | collective-permute-done | bytes 9248 | tf_op jit(solution)/shard_map/ppermute | solution.py:20
  118.1 3.8 %collective-permute-done.21 = f32[2304]{0:T(1024)S(1)} collective-permute-done((f32[2304]{0:T(1024)S(1)}, f32[2304]{0:T(1024)S(1)}, u32[]{:S(2)}, u32[]{:S(2)}) %collective-permute-start.21) | collective-permute-done | bytes 9248 | tf_op jit(solution)/shard_map/ppermute | solution.py:20
  124.2 4.1 %collective-permute-start.22 = (f32[2304]{0:T(1024)S(1)}, f32[2304]{0:T(1024)S(1)}, u32[]{:S(2)}, u32[]{:S(2)}) collective-permute-start(f32[2304]{0:T(1024)S(1)} %add.121), channel_id=1, source_target_pairs={{0,2},{1,3},{2,0},{3,1},{4,6},{5,7},{6,4},{7,5},{8,10},{9,11},{10,... | collective-permute-start | bytes 27656 | tf_op jit(solution)/shard_map/ppermute | solution.py:20
  131.9 2.4 %collective-permute-start.26 = (f32[128]{0:T(128)S(1)}, f32[128]{0:T(128)S(1)}, u32[]{:S(2)}, u32[]{:S(2)}) collective-permute-start(f32[128]{0:T(128)S(1)} %get-tuple-element.94), channel_id=1, source_target_pairs={{0,128},{64,192},{128,0},{192,64},{1,129},{65,193},{129,1},{193,65... | collective-permute-start | bytes 1544 | tf_op jit(solution)/shard_map/ppermute | solution.py:20
  136.2 1.9 %collective-permute-start.29 = (f32[8,32,192]{2,1,0:T(8,128)S(1)}, f32[8,32,192]{2,1,0:T(8,128)S(1)}, u32[]{:S(2)}, u32[]{:S(2)}) collective-permute-start(f32[8,32,192]{2,1,0:T(8,128)S(1)} %slice_select_fusion), channel_id=1, source_target_pairs={{0,16},{16,0},{1,17},{17,1},{2,18},{18,2},{3,19},{19,3},{4,20},{20... | collective-permute-start | bytes 589832 | tf_op jit(solution)/shard_map/ppermute | solution.py:20
  138.1 2.9 %collective-permute-start.28 = (f32[128]{0:T(128)S(1)}, f32[128]{0:T(128)S(1)}, u32[]{:S(2)}, u32[]{:S(2)}) collective-permute-start(f32[128]{0:T(128)S(1)} %add_add_fusion.2), channel_id=1, source_target_pairs={{0,32},{32,0},{1,33},{33,1},{2,34},{34,2},{3,35},{35,3},{4,36},{36... | collective-permute-start | bytes 1544 | tf_op jit(solution)/shard_map/ppermute | solution.py:20
  142.3 2.7 %collective-permute-done.28 = f32[128]{0:T(128)S(1)} collective-permute-done((f32[128]{0:T(128)S(1)}, f32[128]{0:T(128)S(1)}, u32[]{:S(2)}, u32[]{:S(2)}) %collective-permute-start.28) | collective-permute-done | bytes 544 | tf_op jit(solution)/shard_map/ppermute | solution.py:20
  (96 shorter events, 31.7 us)
Async XLA Ops:
  7.2 66.2 %all-gather.2.cloned.1.call-start = ((), (), s32[]{:S(2)}) async-start(), calls=%async_computation.2 | async-start | bytes 1769472 | tf_op jit(solution)/shard_map/all_gather | solution.py:200
  14.7 116.2 %reduce-scatter.2.cloned.1.call-start = ((), (), s32[]{:S(2)}) async-start(), calls=%async_computation.3 | async-start | bytes 3538944 | tf_op jit(solution)/shard_map/reduce_scatter | solution.py:235
  41.3 12.1 %collective-permute-start = (bf16[8,32,768]{2,1,0:T(8,128)(2,1)S(1)}, bf16[8,32,768]{2,1,0:T(8,128)(2,1)S(1)}, u32[]{:S(2)}, u32[]{:S(2)}) collective-permute-start(bf16[8,32,768]{2,1,0:T(8,128)(2,1)S(1)} %bitcast.27), channel_id=1, source_target_pairs={{0,32},{32,0},{1,33},{33,1},{2,34},{34,2},{3,35},{35,3},{4,36},{36... | collective-permute-start | bytes 1179656 | tf_op jit(solution)/shard_map/ppermute | solution.py:20
  44.2 13.6 %collective-permute-start.1 = (bf16[8,32,768]{2,1,0:T(8,128)(2,1)S(1)}, bf16[8,32,768]{2,1,0:T(8,128)(2,1)S(1)}, u32[]{:S(2)}, u32[]{:S(2)}) collective-permute-start(bf16[8,32,768]{2,1,0:T(8,128)(2,1)S(1)} %bitcast.28), channel_id=1, source_target_pairs={{0,128},{64,192},{128,0},{192,64},{1,129},{65,193},{129,1},{193,65... | collective-permute-start | bytes 1179656 | tf_op jit(solution)/shard_map/ppermute | solution.py:24
  44.7 20.6 %collective-permute-start.3 = (bf16[8,32,768]{2,1,0:T(8,128)(2,1)S(1)}, bf16[8,32,768]{2,1,0:T(8,128)(2,1)S(1)}, u32[]{:S(2)}, u32[]{:S(2)}) collective-permute-start(bf16[8,32,768]{2,1,0:T(8,128)(2,1)S(1)} %bitcast.29), channel_id=1, source_target_pairs={{0,192},{64,0},{128,64},{192,128},{1,193},{65,1},{129,65},{193,129... | collective-permute-start | bytes 1179656 | tf_op jit(solution)/shard_map/ppermute | solution.py:24
  46.9 18.4 %collective-permute-start.2 = (bf16[8,32,768]{2,1,0:T(8,128)(2,1)S(1)}, bf16[8,32,768]{2,1,0:T(8,128)(2,1)S(1)}, u32[]{:S(2)}, u32[]{:S(2)}) collective-permute-start(bf16[8,32,768]{2,1,0:T(8,128)(2,1)S(1)} %bitcast.30), channel_id=1, source_target_pairs={{0,64},{64,128},{128,192},{192,0},{1,65},{65,129},{129,193},{193,1... | collective-permute-start | bytes 1179656 | tf_op jit(solution)/shard_map/ppermute | solution.py:24
  53.4 18.5 %collective-permute-start.6 = (bf16[8,32,768]{2,1,0:T(8,128)(2,1)S(1)}, bf16[8,32,768]{2,1,0:T(8,128)(2,1)}, u32[]{:S(2)}, u32[]{:S(2)}) collective-permute-start(bf16[8,32,768]{2,1,0:T(8,128)(2,1)S(1)} %collective-permute-done.refs_1_), channel_id=1, source_target_pairs={{0,192},{64,0},{128,64},{192,128},{1,193},{65,1},{129,65},{193,129... | collective-permute-start | bytes 1179656 | tf_op jit(solution)/shard_map/ppermute | solution.py:24
  54.3 18.5 %collective-permute-start.5 = (bf16[8,32,768]{2,1,0:T(8,128)(2,1)S(1)}, bf16[8,32,768]{2,1,0:T(8,128)(2,1)}, u32[]{:S(2)}, u32[]{:S(2)}) collective-permute-start(bf16[8,32,768]{2,1,0:T(8,128)(2,1)S(1)} %collective-permute-done.refs_1_), channel_id=1, source_target_pairs={{0,64},{64,128},{128,192},{192,0},{1,65},{65,129},{129,193},{193,1... | collective-permute-start | bytes 1179656 | tf_op jit(solution)/shard_map/ppermute | solution.py:24
  57.8 9.4 %collective-permute-start.4 = (bf16[8,32,768]{2,1,0:T(8,128)(2,1)S(1)}, bf16[8,32,768]{2,1,0:T(8,128)(2,1)}, u32[]{:S(2)}, u32[]{:S(2)}) collective-permute-start(bf16[8,32,768]{2,1,0:T(8,128)(2,1)S(1)} %collective-permute-done.1.refs_2_), channel_id=1, source_target_pairs={{0,32},{32,0},{1,33},{33,1},{2,34},{34,2},{3,35},{35,3},{4,36},{36... | collective-permute-start | bytes 1179656 | tf_op jit(solution)/shard_map/ppermute | solution.py:20
  65.3 7.5 %collective-permute-start.7 = (bf16[8,32,768]{2,1,0:T(8,128)(2,1)S(1)}, bf16[8,32,768]{2,1,0:T(8,128)(2,1)S(1)}, u32[]{:S(2)}, u32[]{:S(2)}) collective-permute-start(bf16[8,32,768]{2,1,0:T(8,128)(2,1)S(1)} %collective-permute-done.2.refs_0_.refs_3_), channel_id=1, source_target_pairs={{0,8},{8,0},{1,9},{9,1},{2,10},{10,2},{3,11},{11,3},{4,12},{12,4},... | collective-permute-start | bytes 1179656 | tf_op jit(solution)/shard_map/ppermute | solution.py:20
  65.4 9.8 %collective-permute-start.12 = (bf16[768,384]{1,0:T(8,128)(2,1)}, bf16[768,384]{1,0:T(8,128)(2,1)S(1)}, u32[]{:S(2)}, u32[]{:S(2)}) collective-permute-start(bf16[768,384]{1,0:T(8,128)(2,1)} %get-tuple-element.54.refs_4_), channel_id=1, source_target_pairs={{0,8},{8,0},{1,9},{9,1},{2,10},{10,2},{3,11},{11,3},{4,12},{12,4},... | collective-permute-start | bytes 1769480 | tf_op jit(solution)/shard_map/ppermute | solution.py:20
  67.2 8.0 %collective-permute-start.8 = (bf16[8,32,768]{2,1,0:T(8,128)(2,1)S(1)}, bf16[8,32,768]{2,1,0:T(8,128)(2,1)}, u32[]{:S(2)}, u32[]{:S(2)}) collective-permute-start(bf16[8,32,768]{2,1,0:T(8,128)(2,1)S(1)} %collective-permute-done.3.refs_1_.refs_4_), channel_id=1, source_target_pairs={{0,8},{8,0},{1,9},{9,1},{2,10},{10,2},{3,11},{11,3},{4,12},{12,4},... | collective-permute-start | bytes 1179656 | tf_op jit(solution)/shard_map/ppermute | solution.py:20
  75.5 14.0 %collective-permute-start.14 = (bf16[8,8,32,384]{3,2,1,0:T(8,128)(2,1)S(1)}, bf16[8,8,32,384]{3,2,1,0:T(8,128)(2,1)}, u32[]{:S(2)}, u32[]{:S(2)}) collective-permute-start(bf16[8,8,32,384]{3,2,1,0:T(8,128)(2,1)S(1)} %bitcast.22), channel_id=1, source_target_pairs={{0,8},{8,0},{1,9},{9,1},{2,10},{10,2},{3,11},{11,3},{4,12},{12,4},... | collective-permute-start | bytes 4718600 | tf_op jit(solution)/shard_map/ppermute | solution.py:20
  75.6 5.2 %collective-permute-start.13 = (f32[8,3,32,384]{3,2,1,0:T(8,128)}, f32[8,3,32,384]{3,2,1,0:T(8,128)S(1)}, u32[]{:S(2)}, u32[]{:S(2)}) collective-permute-start(f32[8,3,32,384]{3,2,1,0:T(8,128)} %get-tuple-element.78), channel_id=1, source_target_pairs={{0,8},{8,0},{1,9},{9,1},{2,10},{10,2},{3,11},{11,3},{4,12},{12,4},... | collective-permute-start | bytes 3538952 | tf_op jit(solution)/shard_map/ppermute | solution.py:20
  97.5 4.2 %collective-permute-start.17 = (f32[768]{0:T(1024)}, f32[768]{0:T(1024)S(1)}, u32[]{:S(2)}, u32[]{:S(2)}) collective-permute-start(f32[768]{0:T(1024)} %get-tuple-element.82), channel_id=1, source_target_pairs={{0,192},{64,128},{128,64},{192,0},{1,193},{65,129},{129,65},{193,1... | collective-permute-start | bytes 9224 | tf_op jit(solution)/shard_map/ppermute | solution.py:20
  98.6 5.3 %collective-permute-start.16 = (f32[768]{0:T(1024)}, f32[768]{0:T(1024)S(1)}, u32[]{:S(2)}, u32[]{:S(2)}) collective-permute-start(f32[768]{0:T(1024)} %get-tuple-element.82), channel_id=1, source_target_pairs={{0,128},{64,192},{128,0},{192,64},{1,129},{65,193},{129,1},{193,65... | collective-permute-start | bytes 9224 | tf_op jit(solution)/shard_map/ppermute | solution.py:20
  105.9 5.1 %collective-permute-start.18 = (f32[768]{0:T(1024)S(1)}, f32[768]{0:T(1024)S(1)}, u32[]{:S(2)}, u32[]{:S(2)}) collective-permute-start(f32[768]{0:T(1024)S(1)} %add_add_fusion.1), channel_id=1, source_target_pairs={{0,32},{32,0},{1,33},{33,1},{2,34},{34,2},{3,35},{35,3},{4,36},{36... | collective-permute-start | bytes 9224 | tf_op jit(solution)/shard_map/ppermute | solution.py:20
  121.8 6.5 %collective-permute-start.24 = (f32[2304]{0:T(1024)S(1)}, f32[2304]{0:T(1024)S(1)}, u32[]{:S(2)}, u32[]{:S(2)}) collective-permute-start(f32[2304]{0:T(1024)S(1)} %add.121), channel_id=1, source_target_pairs={{0,6},{1,7},{2,4},{3,5},{4,2},{5,3},{6,0},{7,1},{8,14},{9,15},{10,... | collective-permute-start | bytes 27656 | tf_op jit(solution)/shard_map/ppermute | solution.py:20
  122.5 7.7 %collective-permute-start.23 = (f32[2304]{0:T(1024)S(1)}, f32[2304]{0:T(1024)S(1)}, u32[]{:S(2)}, u32[]{:S(2)}) collective-permute-start(f32[2304]{0:T(1024)S(1)} %add.121), channel_id=1, source_target_pairs={{0,4},{1,5},{2,6},{3,7},{4,0},{5,1},{6,2},{7,3},{8,12},{9,13},{10,... | collective-permute-start | bytes 27656 | tf_op jit(solution)/shard_map/ppermute | solution.py:20
  124.2 6.1 %collective-permute-start.22 = (f32[2304]{0:T(1024)S(1)}, f32[2304]{0:T(1024)S(1)}, u32[]{:S(2)}, u32[]{:S(2)}) collective-permute-start(f32[2304]{0:T(1024)S(1)} %add.121), channel_id=1, source_target_pairs={{0,2},{1,3},{2,0},{3,1},{4,6},{5,7},{6,4},{7,5},{8,10},{9,11},{10,... | collective-permute-start | bytes 27656 | tf_op jit(solution)/shard_map/ppermute | solution.py:20
  130.9 7.2 %collective-permute-start.27 = (f32[128]{0:T(128)S(1)}, f32[128]{0:T(128)S(1)}, u32[]{:S(2)}, u32[]{:S(2)}) collective-permute-start(f32[128]{0:T(128)S(1)} %get-tuple-element.94), channel_id=1, source_target_pairs={{0,192},{64,128},{128,64},{192,0},{1,193},{65,129},{129,65},{193,1... | collective-permute-start | bytes 1544 | tf_op jit(solution)/shard_map/ppermute | solution.py:20
  131.9 6.2 %collective-permute-start.26 = (f32[128]{0:T(128)S(1)}, f32[128]{0:T(128)S(1)}, u32[]{:S(2)}, u32[]{:S(2)}) collective-permute-start(f32[128]{0:T(128)S(1)} %get-tuple-element.94), channel_id=1, source_target_pairs={{0,128},{64,192},{128,0},{192,64},{1,129},{65,193},{129,1},{193,65... | collective-permute-start | bytes 1544 | tf_op jit(solution)/shard_map/ppermute | solution.py:20
  136.2 8.8 %collective-permute-start.29 = (f32[8,32,192]{2,1,0:T(8,128)S(1)}, f32[8,32,192]{2,1,0:T(8,128)S(1)}, u32[]{:S(2)}, u32[]{:S(2)}) collective-permute-start(f32[8,32,192]{2,1,0:T(8,128)S(1)} %slice_select_fusion), channel_id=1, source_target_pairs={{0,16},{16,0},{1,17},{17,1},{2,18},{18,2},{3,19},{19,3},{4,20},{20... | collective-permute-start | bytes 589832 | tf_op jit(solution)/shard_map/ppermute | solution.py:20
  138.1 6.9 %collective-permute-start.28 = (f32[128]{0:T(128)S(1)}, f32[128]{0:T(128)S(1)}, u32[]{:S(2)}, u32[]{:S(2)}) collective-permute-start(f32[128]{0:T(128)S(1)} %add_add_fusion.2), channel_id=1, source_target_pairs={{0,32},{32,0},{1,33},{33,1},{2,34},{34,2},{3,35},{35,3},{4,36},{36... | collective-permute-start | bytes 1544 | tf_op jit(solution)/shard_map/ppermute | solution.py:20
  (21 other events, 228.7 us)
Sparse Core Ops, SparseCore 0:
  14.8 51.1 all-gather.1
  89.6 41.1 reduce-scatter.1

commit v6 on v5

--- a/solution.py
+++ b/solution.py
@@ -10,7 +10,7 @@
 FF = 24576
 HALF = 384
 FIRST, SECOND = 3, 5
-VMEM = 56 * 1024 * 1024
+VMEM = 28 * 1024 * 1024
 
 epsilon = 1e-30
 decay_rate = 0.9
@@ -63,127 +63,97 @@
     )(halves, weight)
 
 
-def tokens(refs, count):
-    return jnp.concatenate([ref[...].reshape(count * 32, 768) for ref in refs], axis=0)
-
-
-def product(cot, weight_ref):
-    return jnp.dot(cot, weight_ref[...], preferred_element_type=jnp.float32)
-
-
-def split(part, count):
-    rows = count * 32
-    return [part[k : k + rows].reshape(count, 32, HALF) for k in range(0, part.shape[0], rows)]
+VECTORS = pl.BlockSpec(memory_space=pltpu.VMEM)
+SCALARS = pl.BlockSpec(memory_space=pltpu.SMEM)
+PARAMS = pltpu.CompilerParams(vmem_limit_bytes=VMEM)
+
+
+def tokens(refs):
+    return jnp.concatenate([ref[...].reshape(256, 768) for ref in refs], axis=0)
 
 
 def first_kernel(*refs):
-    cots, (keep_ref, send_ref, part_keep, part_send) = refs[:FIRST], refs[FIRST:]
-    cot = tokens(cots, 2)
-    for weight_ref, out in ((keep_ref, part_keep), (send_ref, part_send)):
-        for j, part in enumerate(split(product(cot, weight_ref), 2)):
-            out[:, j] = part
+    cot = tokens(refs[:FIRST])
+    keep_ref, send_ref, out, *sent = refs[FIRST:]
+    kept = jnp.dot(cot, keep_ref[...], preferred_element_type=jnp.float32)
+    other = jnp.dot(cot, send_ref[...], preferred_element_type=jnp.float32)
+    for j in range(FIRST):
+        out[:, j] = kept[j * 256 : (j + 1) * 256].reshape(8, 32, HALF)
+        sent[j][...] = other[j * 256 : (j + 1) * 256].reshape(8, 32, HALF)
 
 
 def second_kernel(rows_ref, *refs):
-    cots, others = refs[:SECOND], refs[SECOND : 2 * SECOND]
-    keep_ref, other_ref, before_ref, recv_ref, out = refs[2 * SECOND :]
-    whole = product(tokens(cots, 2), keep_ref) + product(tokens(others, 2), other_ref)
+    cots, others = tokens(refs[:SECOND]), tokens(refs[SECOND : 2 * SECOND])
+    keep_ref, other_ref, before_ref, *received, out = refs[2 * SECOND :]
+    part = jnp.dot(cots, keep_ref[...], preferred_element_type=jnp.float32) + jnp.dot(
+        others, other_ref[...], preferred_element_type=jnp.float32
+    )
     for j in range(FIRST):
-        out[:, rows_ref[j]] = before_ref[:, j] + recv_ref[:, j]
-    for j, part in enumerate(split(whole, 2)):
-        out[:, rows_ref[FIRST + j]] = part
-
-
-COT = pl.BlockSpec((2, 32, 768), lambda s, *_: (s, 0, 0))
-WEIGHT = pl.BlockSpec((768, HALF), lambda s, *_: (0, 0))
-PART = pl.BlockSpec((2, FIRST, 32, HALF), lambda s, *_: (s, 0, 0, 0))
+        out[:, rows_ref[j]] = before_ref[:, j] + received[j][...]
+    for j in range(SECOND):
+        out[:, rows_ref[FIRST + j]] = part[j * 256 : (j + 1) * 256].reshape(8, 32, HALF)
 
 
 def first_call(cots, keep, send):
     return pl.pallas_call(
         first_kernel,
-        grid=(4,),
-        in_specs=[COT] * FIRST + [WEIGHT] * 2,
-        out_specs=[PART] * 2,
-        out_shape=[jax.ShapeDtypeStruct((8, FIRST, 32, HALF), jnp.float32)] * 2,
-        compiler_params=pltpu.CompilerParams(vmem_limit_bytes=VMEM),
+        in_specs=[VECTORS] * (FIRST + 2),
+        out_specs=[VECTORS] * (1 + FIRST),
+        out_shape=[jax.ShapeDtypeStruct((8, FIRST, 32, HALF), jnp.float32)]
+        + [jax.ShapeDtypeStruct((8, 32, HALF), jnp.float32)] * FIRST,
+        compiler_params=PARAMS,
         cost_estimate=pl.CostEstimate(
-            flops=2 * 1024 * 768 * 768, bytes_accessed=6 * 1024 * 1024, transcendentals=0
+            flops=FIRST * 4 * 256 * 768 * HALF, bytes_accessed=4 * 1024 * 1024, transcendentals=0
         ),
     )(*cots, keep, send)
 
 
-def second_call(rows, cots, others, keep, other, before, received):
+def second_call(rows, cots, others, keep, other_keep, before, received):
     return pl.pallas_call(
         second_kernel,
-        grid_spec=pltpu.PrefetchScalarGridSpec(
-            num_scalar_prefetch=1,
-            grid=(4,),
-            in_specs=[COT] * 2 * SECOND + [WEIGHT] * 2 + [PART] * 2,
-            out_specs=pl.BlockSpec((2, 8, 32, HALF), lambda s, rows: (s, 0, 0, 0)),
-        ),
+        in_specs=[SCALARS] + [VECTORS] * (2 * SECOND + 3 + FIRST),
+        out_specs=VECTORS,
         out_shape=jax.ShapeDtypeStruct((8, 8, 32, HALF), jnp.float32),
-        compiler_params=pltpu.CompilerParams(vmem_limit_bytes=VMEM),
+        compiler_params=PARAMS,
         cost_estimate=pl.CostEstimate(
-            flops=2 * 1024 * 768 * 768, bytes_accessed=10 * 1024 * 1024, transcendentals=0
-        ),
-    )(rows, *cots, *others, keep, other, before, received)
-
-
-STEP = 4
+            flops=SECOND * 4 * 256 * 768 * HALF, bytes_accessed=8 * 1024 * 1024, transcendentals=0
+        ),
+    )(rows, *cots, *others, keep, other_keep, before, *received)
 
 
 def gradient_kernel(rows_ref, halves_ref, *refs):
     cots, acts, (out_ref, row_ref, col_ref) = refs[:8], refs[8:10], refs[10:]
-    step = pl.program_id(0)
     act = jnp.concatenate(
         [
-            jnp.concatenate([a[:, rows_ref[j]].reshape(STEP * 32, HALF) for j in range(8)], axis=0)
+            jnp.concatenate([a[:, rows_ref[j]].reshape(256, HALF) for j in range(8)], axis=0)
             for a in acts
         ],
         axis=1,
     )
-    term = lax.dot_general(
-        tokens(cots, STEP), act, (((0,), (0,)), ((), ())), preferred_element_type=jnp.float32
+    whole = lax.dot_general(
+        tokens(cots), act, (((0,), (0,)), ((), ())), preferred_element_type=jnp.float32
     )
     for h in range(2):
         columns = pl.ds(pl.multiple_of(halves_ref[h] * HALF, HALF), HALF)
-        part = term[:, h * HALF : (h + 1) * HALF]
-
-        @pl.when(step == 0)
-        def _():
-            out_ref[:, columns] = part
-
-        @pl.when(step > 0)
-        def _():
-            out_ref[:, columns] += part
-
-    @pl.when(step == 8 // STEP - 1)
-    def _():
-        gradient = out_ref[...]
-        square = gradient * gradient + epsilon
-        col_ref[...] = jnp.sum(square, axis=0)
-        lanes = sum(square[:, k * 128 : (k + 1) * 128] for k in range(6))
-        row_ref[...] = jnp.sum(lanes.T, axis=0)
+        out_ref[:, columns] = whole[:, h * HALF : (h + 1) * HALF]
+    gradient = out_ref[...]
+    square = gradient * gradient + epsilon
+    col_ref[...] = jnp.sum(square, axis=0)
+    lanes = sum(square[:, k * 128 : (k + 1) * 128] for k in range(6))
+    row_ref[...] = jnp.sum(lanes.T, axis=0)
 
 
 def gradient_call(rows, halves, cots, acts):
-    vector = pl.BlockSpec((768,), lambda s, rows, halves: (0,))
     return pl.pallas_call(
         gradient_kernel,
-        grid_spec=pltpu.PrefetchScalarGridSpec(
-            num_scalar_prefetch=2,
-            grid=(8 // STEP,),
-            in_specs=[pl.BlockSpec((STEP, 32, 768), lambda s, rows, halves: (s, 0, 0))] * 8
-            + [pl.BlockSpec((STEP, 8, 32, HALF), lambda s, rows, halves: (s, 0, 0, 0))] * 2,
-            out_specs=[pl.BlockSpec((768, 768), lambda s, rows, halves: (0, 0)), vector, vector],
-        ),
+        in_specs=[SCALARS] * 2 + [VECTORS] * 10,
+        out_specs=[VECTORS] * 3,
         out_shape=[
             jax.ShapeDtypeStruct((768, 768), jnp.float32),
             jax.ShapeDtypeStruct((768,), jnp.float32),
             jax.ShapeDtypeStruct((768,), jnp.float32),
         ],
-        compiler_params=pltpu.CompilerParams(vmem_limit_bytes=VMEM),
+        compiler_params=PARAMS,
         cost_estimate=pl.CostEstimate(
             flops=2 * 2048 * 768 * 768, bytes_accessed=9 * 1024 * 1024, transcendentals=0
         ),
@@ -219,18 +189,17 @@
     first = [own_cot, other_cot, far_cot]
     second = [right_cot, left_cot, other_far, other_right, other_left]
 
-    keep_1, send_1 = first_call(first, keep, send)
-    keep_1, send_1, *second[:2] = lax.optimization_barrier((keep_1, send_1, *second[:2]))
-    others = [exchange(cot, "core", 2, 1) for cot in second[:5]]
+    kept, *sent = first_call(first, keep, send)
+    second[0], second[1], *sent = lax.optimization_barrier((second[0], second[1], *sent))
+    received = [exchange(part, "core", 2, 1) for part in sent]
+    others = [exchange(cot, "core", 2, 1) for cot in second]
     other_keep = exchange(send, "core", 2, 1)
-    *arrived, other_keep, keep_1, send_1, act_own = lax.optimization_barrier(
-        (*first, *second, *others, other_keep, keep_1, send_1, act_own)
-    )
-    first, second, others = arrived[:FIRST], arrived[FIRST:8], arrived[8:]
-    recv_1 = exchange(send_1, "core", 2, 1)
-    others += [exchange(cot, "core", 2, 1) for cot in second[5:]]
+    *arrived, other_keep, kept, act_own = lax.optimization_barrier(
+        (*first, *second, *others, *received, other_keep, kept, act_own)
+    )
+    first, second, others, received = arrived[:FIRST], arrived[FIRST:8], arrived[8:13], arrived[13:]
     act_recv = exchange(act_own, "core", 2, 1)
-    summed = second_call(rows, second, others, keep, other_keep, keep_1, recv_1)
+    summed = second_call(rows, second, others, keep, other_keep, kept, received)
     summed, act_recv = lax.optimization_barrier((summed, act_recv))
     summed = lax.psum_scatter(summed, "z", scatter_dimension=0, tiled=True)
     gradient, row_sums, col_sums = gradient_call(rows, halves, first + second, [act_own, act_recv])
@@ -241,8 +210,8 @@
     sums = jnp.concatenate([col_sums, jnp.sum(scaled * scaled, axis=0), row_stats])
     sums = total(total(sums, "core", 2), "yl", 2)
     sums = sums + exchange(sums, "z", 8, 1)
+    sums, summed = lax.optimization_barrier((sums, summed))
     sums = reduce_four(sums, "z", 8, (2, 4, 6))
-    sums, summed = lax.optimization_barrier((sums, summed))
     row_mean = jnp.sum(sums[1536:]) / FF
     col_stats = decay_rate * col_prev + (1.0 - decay_rate) * (sums[:768] / FF)
     part = jnp.sum((sums[768:1536] / col_stats).reshape(6, 128), axis=0)

time: 158 us -> 167 us (1.057)
  local copies, waits for them, and re-layouts: 6.16 us -> 14.1 us
  Pallas kernels: 24.4 us -> 17.2 us
  waiting for transfers between devices: 38.6 us -> 44.7 us
  starting transfers between devices: 31.1 us -> 36.2 us
  other arithmetic: 8.82 us -> 5.85 us
    reduce_scatter x1, waiting for transfers between devices: 0.54 us -> 13.1 us  [body(): summed = lax.psum_scatter(summed, 'z', scatter_dimension=0, tiled=True)]
    unnamed x27 -> x31, local copies, waits for them, and re-layouts: 1.91 us -> 10.4 us
    ppermute x25 -> x27, waiting for transfers between devices: 28.2 us -> 20.6 us  [exchange(): return lax.ppermute(value, axis, [(i, i ^ bit) for i in range(size)])]
    pallas_call x3, Pallas kernels: 20.4 us -> 15 us  [the longest x1 6.15 us: second_call(): pl.pallas_call(second_kernel, in_specs=[SCALARS] + [VECTORS] * (2 * SECON...]
    ppermute x25 -> x27, starting transfers between devices: 26.2 us -> 31.3 us  [exchange(): return lax.ppermute(value, axis, [(i, i ^ bit) for i in range(size)])]
    pallas_call x1, Pallas kernels: 3.97 us -> 2.19 us  [weight_call(): pl.pallas_call(weight_kernel, grid_spec=pltpu.PrefetchScalarGridSpec(num_...]
    reduce_sum x1, other arithmetic: 2.01 us -> 0.31 us  [body(): jnp.sum(scaled * scaled, axis=0)]
  transfers between devices with their start and end apart: 32 -> 34, of which waited for: 18 -> 13; matrix products, arithmetic and copies ran while one was open for 6% -> 3% of each run, Pallas kernels for 16% -> 10%
where the time goes in v6:
time: 167 us; the launch traced here: 166 us
  waiting for transfers between devices  44.7 us (27%)
  starting transfers between devices  36.2 us (22%)
  blocking collectives  32.5 us (19%)
  Pallas kernels  17.2 us (10%)
  between operations  15.6 us (9%)
  local copies, waits for them, and re-layouts  14.1 us (8%)
  other arithmetic  5.85 us (4%)
    ppermute x27, starting transfers between devices, exchange(): return lax.ppermute(value, axis, [(i, i ^ bit) for i in range(size)])  31.3 us
    all_to_all x1, blocking collectives, body(): lax.all_to_all(cotangent, 'z', 1, 0, tiled=True).reshape(8, 32, 768)  25.6 us
    ppermute x27, waiting for transfers between devices, exchange(): return lax.ppermute(value, axis, [(i, i ^ bit) for i in range(size)])  20.6 us
    reduce_scatter x1, waiting for transfers between devices, body(): summed = lax.psum_scatter(summed, 'z', scatter_dimension=0, tiled=True)  13.1 us
    ppermute x5, waiting for transfers between devices, shift(): lax.ppermute(value, axis, [(i, (i + step) % size) for i in range(size)])  11 us
    unnamed x31, local copies, waits for them, and re-layouts  10.4 us
    all_gather x1, blocking collectives, body(): act_cols = lax.all_gather(activations, ('yl', 'core'), axis=1, tiled=True)  6.89 us
    pallas_call x1, Pallas kernels, second_call(): pl.pallas_call(second_kernel, in_specs=[SCALARS] + [VECTORS] * (2 * SECON...  6.15 us
  transfers between devices with their start and end apart: 34, of which 13 were waited for; matrix products, arithmetic and copies ran while one was open for 3% of the time, Pallas kernels for 10%

profile of v6, /device:TPU:4, one launch (start us, length us, event | category | flops | bytes accessed | tf_op | source)
XLA Modules:
  0.0 166.0 jit_solution(17552677548067996388)
XLA Ops:
  7.2 6.9 %all_gather.6 = bf16[256,768]{0,1:T(8,128)(2,1)S(1)} all-gather(bf16[256,192]{0,1:T(8,128)(2,1)} %param.6), channel_id=1, replica_groups=mesh['x'=4,'yh'=2,'yl'=2,'core'=2,'z'=8] {'yl','core'}, dimensions={1}, use_global_device_ids=true | all-gather | bytes 491520 | tf_op jit(solution)/shard_map/all_gather | solution.py:167
  15.9 25.6 %all_to_all.16 = bf16[32,8,768]{2,0,1:T(8,128)(2,1)S(1)} all-to-all(bf16[32,8,768]{2,0,1:T(8,128)(2,1)S(1)} %bitcast.32), channel_id=1, replica_groups=mesh['x'=4,'yh'=2,'yl'=2,'core'=2,'z'=8] {'z'}, dimensions={1} | all-to-all | bytes 786432 | tf_op jit(solution)/shard_map/all_to_all | solution.py:172
  42.0 2.9 %collective-permute-start = (bf16[8,32,768]{2,1,0:T(8,128)(2,1)S(1)}, bf16[8,32,768]{2,1,0:T(8,128)(2,1)}, u32[]{:S(2)}, u32[]{:S(2)}) collective-permute-start(bf16[8,32,768]{2,1,0:T(8,128)(2,1)S(1)} %bitcast.25), channel_id=1, source_target_pairs={{0,32},{32,0},{1,33},{33,1},{2,34},{34,2},{3,35},{35,3},{4,36},{36... | collective-permute-start | bytes 1179656 | tf_op jit(solution)/shard_map/ppermute | solution.py:20
  45.0 2.1 %collective-permute-start.2 = (bf16[8,32,768]{2,1,0:T(8,128)(2,1)S(1)}, bf16[8,32,768]{2,1,0:T(8,128)(2,1)}, u32[]{:S(2)}, u32[]{:S(2)}) collective-permute-start(bf16[8,32,768]{2,1,0:T(8,128)(2,1)S(1)} %bitcast.26), channel_id=1, source_target_pairs={{0,64},{64,128},{128,192},{192,0},{1,65},{65,129},{129,193},{193,1... | collective-permute-start | bytes 1179656 | tf_op jit(solution)/shard_map/ppermute | solution.py:24
  47.3 2.2 %shard_map.68 = (bf16[768,384]{1,0:T(8,128)(2,1)S(1)}, bf16[768,384]{1,0:T(8,128)(2,1)}) custom-call(s32[2]{0:T(128)S(1)} %pad_add_fusion.core_ref.halves_ref, bf16[768,768]{1,0:T(8,128)(2,1)S(1)} %copy-done.2), custom_call_target="tpu_custom_call" | custom-call | tf_op jit(solution)/shard_map/pallas_call | solution.py:53
  49.5 5.7 %collective-permute-done.1.refs_2_ = bf16[8,32,768]{2,1,0:T(8,128)(2,1)} collective-permute-done((bf16[8,32,768]{2,1,0:T(8,128)(2,1)S(1)}, bf16[8,32,768]{2,1,0:T(8,128)(2,1)}, u32[]{:S(2)}, u32[]{:S(2)}) %collective-permute-start.1) | collective-permute-done | bytes 393248 | tf_op jit(solution)/shard_map/ppermute | solution.py:24
  55.2 2.9 %collective-permute-start.4 = (bf16[8,32,768]{2,1,0:T(8,128)(2,1)}, bf16[8,32,768]{2,1,0:T(8,128)(2,1)}, u32[]{:S(2)}, u32[]{:S(2)}) collective-permute-start(bf16[8,32,768]{2,1,0:T(8,128)(2,1)} %collective-permute-done.1.refs_2_), channel_id=1, source_target_pairs={{0,32},{32,0},{1,33},{33,1},{2,34},{34,2},{3,35},{35,3},{4,36},{36... | collective-permute-start | bytes 1179656 | tf_op jit(solution)/shard_map/ppermute | solution.py:20
  60.1 3.4 %shard_map.69 = (f32[8,3,32,384]{3,2,1,0:T(8,128)S(1)}, f32[8,32,384]{2,1,0:T(8,128)S(1)}, f32[8,32,384]{2,1,0:T(8,128)S(1)}, f32[8,32,384]{2,1,0:T(8,128)}) custom-call(bf16[8,32,768]{2,1,0:T(8,128)(2,1)S(1)} %bitcast.28, bf16[8,32,768]{2,1,0:T(8,128)(2,1)} %collective-permute-done.refs_1_, bf16[8,32,768]{2,1,0:T(8,128)(2,1)} %collective-permute-done.1.refs_2_, ...), custom_call_target="tpu_custom_call" | custom-call | flops 905969664 | bytes 4194304 | tf_op jit(solution)/shard_map/pallas_call | solution.py:98
  65.2 5.3 %collective-permute-done.5.refs_3_.refs_6_ = bf16[8,32,768]{2,1,0:T(8,128)(2,1)} collective-permute-done((bf16[8,32,768]{2,1,0:T(8,128)(2,1)}, bf16[8,32,768]{2,1,0:T(8,128)(2,1)}, u32[]{:S(2)}, u32[]{:S(2)}) %collective-permute-start.5) | collective-permute-done | bytes 393248 | tf_op jit(solution)/shard_map/ppermute | solution.py:24
  75.1 1.9 %copy.13 = bf16[2048,384]{1,0:T(8,128)(2,1)S(1)} copy(bf16[2048,384]{0,1:T(8,128)(2,1)} %all-gather.2.cloned.1.call-done) | data formatting | bytes 3145728 | tf_op jit(solution)/shard_map/all_gather | solution.py:170
  81.6 6.1 %shard_map.70 = f32[8,8,32,384]{3,2,1,0:T(8,128)} custom-call(s32[8]{0:T(128)S(1)} %stack.47.rows_ref, bf16[8,32,768]{2,1,0:T(8,128)(2,1)} %collective-permute-done.2.refs_0_.refs_3_, bf16[8,32,768]{2,1,0:T(8,128)(2,1)} %collective-permute-done.3.refs_1_.refs_4_, bf16[8,32,768]{2,1,0:T(8,128)(2,1)} %collective-permute-done.4.refs_2_.refs_5_, ...), custom_call_target="tpu_custom_call" | custom-call | flops 1509949440 | bytes 8388608 | tf_op jit(solution)/shard_map/pallas_call | solution.py:112
  90.1 5.4 %shard_map.71 = (f32[768,768]{1,0:T(8,128)S(1)}, f32[768]{0:T(1024)S(1)}, f32[768]{0:T(1024)S(1)}) custom-call(s32[8]{0:T(128)S(1)} %stack.47.rows_ref, s32[2]{0:T(128)S(1)} %pad_add_fusion.core_ref.halves_ref, bf16[8,32,768]{2,1,0:T(8,128)(2,1)S(1)} %bitcast.29, bf16[8,32,768]{2,1,0:T(8,128)(2,1)} %collective-permute-done.refs_1_, ...), custom_call_target="tpu_custom_call" | custom-call | flops 2415919104 | bytes 9437184 | tf_op jit(solution)/shard_map/pallas_call | solution.py:147
  96.2 2.4 %collective-permute-start.18 = (f32[768]{0:T(1024)S(1)}, f32[768]{0:T(1024)S(1)}, u32[]{:S(2)}, u32[]{:S(2)}) collective-permute-start(f32[768]{0:T(1024)S(1)} %get-tuple-element.92), channel_id=1, source_target_pairs={{0,128},{64,192},{128,0},{192,64},{1,129},{65,193},{129,1},{193,65... | collective-permute-start | bytes 9224 | tf_op jit(solution)/shard_map/ppermute | solution.py:20
  102.3 2.8 %collective-permute-start.20 = (f32[768]{0:T(1024)S(1)}, f32[768]{0:T(1024)S(1)}, u32[]{:S(2)}, u32[]{:S(2)}) collective-permute-start(f32[768]{0:T(1024)S(1)} %add_add_fusion.1), channel_id=1, source_target_pairs={{0,32},{32,0},{1,33},{33,1},{2,34},{34,2},{3,35},{35,3},{4,36},{36... | collective-permute-start | bytes 9224 | tf_op jit(solution)/shard_map/ppermute | solution.py:20
  105.1 2.3 %collective-permute-done.20 = f32[768]{0:T(1024)S(1)} collective-permute-done((f32[768]{0:T(1024)S(1)}, f32[768]{0:T(1024)S(1)}, u32[]{:S(2)}, u32[]{:S(2)}) %collective-permute-start.20) | collective-permute-done | bytes 3104 | tf_op jit(solution)/shard_map/ppermute | solution.py:20
  109.8 2.9 %collective-permute-done.22 = f32[2304]{0:T(1024)S(1)} collective-permute-done((f32[2304]{0:T(1024)S(1)}, f32[2304]{0:T(1024)S(1)}, u32[]{:S(2)}, u32[]{:S(2)}) %collective-permute-start.22) | collective-permute-done | bytes 9248 | tf_op jit(solution)/shard_map/ppermute | solution.py:20
  112.7 4.1 %collective-permute-done.23 = f32[2304]{0:T(1024)S(1)} collective-permute-done((f32[2304]{0:T(1024)S(1)}, f32[2304]{0:T(1024)S(1)}, u32[]{:S(2)}, u32[]{:S(2)}) %collective-permute-start.23) | collective-permute-done | bytes 9248 | tf_op jit(solution)/shard_map/ppermute | solution.py:20
  116.9 13.1 %reduce-scatter.2.cloned.1.call-done = f32[1,8,32,384]{3,2,1,0:T(8,128)} async-done(((f32[8,8,32,384]{3,2,1,0:T(8,128)}), f32[1,8,32,384]{3,2,1,0:T(8,128)}) %reduce-scatter.2.cloned.1.call-update) | async-done | bytes 393232 | tf_op jit(solution)/shard_map/reduce_scatter | solution.py:204
  129.9 2.2 %collective-permute-start.26 = (f32[2304]{0:T(1024)S(1)}, f32[2304]{0:T(1024)S(1)}, u32[]{:S(2)}, u32[]{:S(2)}) collective-permute-start(f32[2304]{0:T(1024)S(1)} %add.121), channel_id=1, source_target_pairs={{0,6},{1,7},{2,4},{3,5},{4,2},{5,3},{6,0},{7,1},{8,14},{9,15},{10,... | collective-permute-start | bytes 27656 | tf_op jit(solution)/shard_map/ppermute | solution.py:20
  132.1 3.3 %collective-permute-start.25 = (f32[2304]{0:T(1024)S(1)}, f32[2304]{0:T(1024)S(1)}, u32[]{:S(2)}, u32[]{:S(2)}) collective-permute-start(f32[2304]{0:T(1024)S(1)} %add.121), channel_id=1, source_target_pairs={{0,4},{1,5},{2,6},{3,7},{4,0},{5,1},{6,2},{7,3},{8,12},{9,13},{10,... | collective-permute-start | bytes 27656 | tf_op jit(solution)/shard_map/ppermute | solution.py:20
  136.4 3.3 %collective-permute-done.25 = f32[2304]{0:T(1024)S(1)} collective-permute-done((f32[2304]{0:T(1024)S(1)}, f32[2304]{0:T(1024)S(1)}, u32[]{:S(2)}, u32[]{:S(2)}) %collective-permute-start.25) | collective-permute-done | bytes 9248 | tf_op jit(solution)/shard_map/ppermute | solution.py:20
  140.9 2.5 %collective-permute-start.28 = (f32[128]{0:T(128)S(1)}, f32[128]{0:T(128)S(1)}, u32[]{:S(2)}, u32[]{:S(2)}) collective-permute-start(f32[128]{0:T(128)S(1)} %get-tuple-element.104), channel_id=1, source_target_pairs={{0,128},{64,192},{128,0},{192,64},{1,129},{65,193},{129,1},{193,65... | collective-permute-start | bytes 1544 | tf_op jit(solution)/shard_map/ppermute | solution.py:20
  147.1 3.1 %collective-permute-start.30 = (f32[128]{0:T(128)S(1)}, f32[128]{0:T(128)S(1)}, u32[]{:S(2)}, u32[]{:S(2)}) collective-permute-start(f32[128]{0:T(128)S(1)} %add_add_fusion.2), channel_id=1, source_target_pairs={{0,32},{32,0},{1,33},{33,1},{2,34},{34,2},{3,35},{35,3},{4,36},{36... | collective-permute-start | bytes 1544 | tf_op jit(solution)/shard_map/ppermute | solution.py:20
  151.5 2.6 %collective-permute-done.30 = f32[128]{0:T(128)S(1)} collective-permute-done((f32[128]{0:T(128)S(1)}, f32[128]{0:T(128)S(1)}, u32[]{:S(2)}, u32[]{:S(2)}) %collective-permute-start.30) | collective-permute-done | bytes 544 | tf_op jit(solution)/shard_map/ppermute | solution.py:20
  (104 shorter events, 35.4 us)
Async XLA Ops:
  7.2 68.0 %all-gather.2.cloned.1.call-start = ((), (), s32[]{:S(2)}) async-start(), calls=%async_computation.2 | async-start | bytes 1769472 | tf_op jit(solution)/shard_map/all_gather | solution.py:170
  14.8 115.1 %reduce-scatter.2.cloned.1.call-start = ((), (), s32[]{:S(2)}) async-start(), calls=%async_computation.3 | async-start | bytes 3538944 | tf_op jit(solution)/shard_map/reduce_scatter | solution.py:204
  41.5 13.7 %collective-permute-start.1 = (bf16[8,32,768]{2,1,0:T(8,128)(2,1)S(1)}, bf16[8,32,768]{2,1,0:T(8,128)(2,1)}, u32[]{:S(2)}, u32[]{:S(2)}) collective-permute-start(bf16[8,32,768]{2,1,0:T(8,128)(2,1)S(1)} %bitcast.24), channel_id=1, source_target_pairs={{0,128},{64,192},{128,0},{192,64},{1,129},{65,193},{129,1},{193,65... | collective-permute-start | bytes 1179656 | tf_op jit(solution)/shard_map/ppermute | solution.py:24
  42.0 16.1 %collective-permute-start = (bf16[8,32,768]{2,1,0:T(8,128)(2,1)S(1)}, bf16[8,32,768]{2,1,0:T(8,128)(2,1)}, u32[]{:S(2)}, u32[]{:S(2)}) collective-permute-start(bf16[8,32,768]{2,1,0:T(8,128)(2,1)S(1)} %bitcast.25), channel_id=1, source_target_pairs={{0,32},{32,0},{1,33},{33,1},{2,34},{34,2},{3,35},{35,3},{4,36},{36... | collective-permute-start | bytes 1179656 | tf_op jit(solution)/shard_map/ppermute | solution.py:20
  45.0 18.6 %collective-permute-start.2 = (bf16[8,32,768]{2,1,0:T(8,128)(2,1)S(1)}, bf16[8,32,768]{2,1,0:T(8,128)(2,1)}, u32[]{:S(2)}, u32[]{:S(2)}) collective-permute-start(bf16[8,32,768]{2,1,0:T(8,128)(2,1)S(1)} %bitcast.26), channel_id=1, source_target_pairs={{0,64},{64,128},{128,192},{192,0},{1,65},{65,129},{129,193},{193,1... | collective-permute-start | bytes 1179656 | tf_op jit(solution)/shard_map/ppermute | solution.py:24
  47.1 16.5 %collective-permute-start.3 = (bf16[8,32,768]{2,1,0:T(8,128)(2,1)S(1)}, bf16[8,32,768]{2,1,0:T(8,128)(2,1)}, u32[]{:S(2)}, u32[]{:S(2)}) collective-permute-start(bf16[8,32,768]{2,1,0:T(8,128)(2,1)S(1)} %bitcast.27), channel_id=1, source_target_pairs={{0,192},{64,0},{128,64},{192,128},{1,193},{65,1},{129,65},{193,129... | collective-permute-start | bytes 1179656 | tf_op jit(solution)/shard_map/ppermute | solution.py:24
  55.2 10.0 %collective-permute-start.4 = (bf16[8,32,768]{2,1,0:T(8,128)(2,1)}, bf16[8,32,768]{2,1,0:T(8,128)(2,1)}, u32[]{:S(2)}, u32[]{:S(2)}) collective-permute-start(bf16[8,32,768]{2,1,0:T(8,128)(2,1)} %collective-permute-done.1.refs_2_), channel_id=1, source_target_pairs={{0,32},{32,0},{1,33},{33,1},{2,34},{34,2},{3,35},{35,3},{4,36},{36... | collective-permute-start | bytes 1179656 | tf_op jit(solution)/shard_map/ppermute | solution.py:20
  58.0 12.5 %collective-permute-start.5 = (bf16[8,32,768]{2,1,0:T(8,128)(2,1)}, bf16[8,32,768]{2,1,0:T(8,128)(2,1)}, u32[]{:S(2)}, u32[]{:S(2)}) collective-permute-start(bf16[8,32,768]{2,1,0:T(8,128)(2,1)} %collective-permute-done.refs_1_), channel_id=1, source_target_pairs={{0,64},{64,128},{128,192},{192,0},{1,65},{65,129},{129,193},{193,1... | collective-permute-start | bytes 1179656 | tf_op jit(solution)/shard_map/ppermute | solution.py:24
  59.3 11.2 %collective-permute-start.6 = (bf16[8,32,768]{2,1,0:T(8,128)(2,1)}, bf16[8,32,768]{2,1,0:T(8,128)(2,1)}, u32[]{:S(2)}, u32[]{:S(2)}) collective-permute-start(bf16[8,32,768]{2,1,0:T(8,128)(2,1)} %collective-permute-done.refs_1_), channel_id=1, source_target_pairs={{0,192},{64,0},{128,64},{192,128},{1,193},{65,1},{129,65},{193,129... | collective-permute-start | bytes 1179656 | tf_op jit(solution)/shard_map/ppermute | solution.py:24
  63.5 7.5 %collective-permute-start.7 = (bf16[8,32,768]{2,1,0:T(8,128)(2,1)}, bf16[8,32,768]{2,1,0:T(8,128)(2,1)S(1)}, u32[]{:S(2)}, u32[]{:S(2)}) collective-permute-start(bf16[8,32,768]{2,1,0:T(8,128)(2,1)} %collective-permute-done.2.refs_0_.refs_3_), channel_id=1, source_target_pairs={{0,8},{8,0},{1,9},{9,1},{2,10},{10,2},{3,11},{11,3},{4,12},{12,4},... | collective-permute-start | bytes 1179656 | tf_op jit(solution)/shard_map/ppermute | solution.py:20
  63.5 8.3 %collective-permute-start.8 = (bf16[8,32,768]{2,1,0:T(8,128)(2,1)}, bf16[8,32,768]{2,1,0:T(8,128)(2,1)S(1)}, u32[]{:S(2)}, u32[]{:S(2)}) collective-permute-start(bf16[8,32,768]{2,1,0:T(8,128)(2,1)} %collective-permute-done.3.refs_1_.refs_4_), channel_id=1, source_target_pairs={{0,8},{8,0},{1,9},{9,1},{2,10},{10,2},{3,11},{11,3},{4,12},{12,4},... | collective-permute-start | bytes 1179656 | tf_op jit(solution)/shard_map/ppermute | solution.py:20
  65.2 7.9 %collective-permute-start.12 = (f32[8,32,384]{2,1,0:T(8,128)S(1)}, f32[8,32,384]{2,1,0:T(8,128)S(1)}, u32[]{:S(2)}, u32[]{:S(2)}) collective-permute-start(f32[8,32,384]{2,1,0:T(8,128)S(1)} %get-tuple-element.65), channel_id=1, source_target_pairs={{0,8},{8,0},{1,9},{9,1},{2,10},{10,2},{3,11},{11,3},{4,12},{12,4},... | collective-permute-start | bytes 1179656 | tf_op jit(solution)/shard_map/ppermute | solution.py:20
  70.5 6.5 %collective-permute-start.15 = (bf16[768,384]{1,0:T(8,128)(2,1)}, bf16[768,384]{1,0:T(8,128)(2,1)}, u32[]{:S(2)}, u32[]{:S(2)}) collective-permute-start(bf16[768,384]{1,0:T(8,128)(2,1)} %get-tuple-element.59.refs_4_), channel_id=1, source_target_pairs={{0,8},{8,0},{1,9},{9,1},{2,10},{10,2},{3,11},{11,3},{4,12},{12,4},... | collective-permute-start | bytes 1769480 | tf_op jit(solution)/shard_map/ppermute | solution.py:20
  71.8 5.2 %collective-permute-start.14 = (f32[8,32,384]{2,1,0:T(8,128)}, f32[8,32,384]{2,1,0:T(8,128)}, u32[]{:S(2)}, u32[]{:S(2)}) collective-permute-start(f32[8,32,384]{2,1,0:T(8,128)} %get-tuple-element.67), channel_id=1, source_target_pairs={{0,8},{8,0},{1,9},{9,1},{2,10},{10,2},{3,11},{11,3},{4,12},{12,4},... | collective-permute-start | bytes 1179656 | tf_op jit(solution)/shard_map/ppermute | solution.py:20
  77.1 10.6 %collective-permute-start.16 = (bf16[8,8,32,384]{3,2,1,0:T(8,128)(2,1)S(1)}, bf16[8,8,32,384]{3,2,1,0:T(8,128)(2,1)}, u32[]{:S(2)}, u32[]{:S(2)}) collective-permute-start(bf16[8,8,32,384]{3,2,1,0:T(8,128)(2,1)S(1)} %bitcast.22), channel_id=1, source_target_pairs={{0,8},{8,0},{1,9},{9,1},{2,10},{10,2},{3,11},{11,3},{4,12},{12,4},... | collective-permute-start | bytes 4718600 | tf_op jit(solution)/shard_map/ppermute | solution.py:20
  96.2 5.1 %collective-permute-start.18 = (f32[768]{0:T(1024)S(1)}, f32[768]{0:T(1024)S(1)}, u32[]{:S(2)}, u32[]{:S(2)}) collective-permute-start(f32[768]{0:T(1024)S(1)} %get-tuple-element.92), channel_id=1, source_target_pairs={{0,128},{64,192},{128,0},{192,64},{1,129},{65,193},{129,1},{193,65... | collective-permute-start | bytes 9224 | tf_op jit(solution)/shard_map/ppermute | solution.py:20
  102.3 5.1 %collective-permute-start.20 = (f32[768]{0:T(1024)S(1)}, f32[768]{0:T(1024)S(1)}, u32[]{:S(2)}, u32[]{:S(2)}) collective-permute-start(f32[768]{0:T(1024)S(1)} %add_add_fusion.1), channel_id=1, source_target_pairs={{0,32},{32,0},{1,33},{33,1},{2,34},{34,2},{3,35},{35,3},{4,36},{36... | collective-permute-start | bytes 9224 | tf_op jit(solution)/shard_map/ppermute | solution.py:20
  129.9 6.5 %collective-permute-start.26 = (f32[2304]{0:T(1024)S(1)}, f32[2304]{0:T(1024)S(1)}, u32[]{:S(2)}, u32[]{:S(2)}) collective-permute-start(f32[2304]{0:T(1024)S(1)} %add.121), channel_id=1, source_target_pairs={{0,6},{1,7},{2,4},{3,5},{4,2},{5,3},{6,0},{7,1},{8,14},{9,15},{10,... | collective-permute-start | bytes 27656 | tf_op jit(solution)/shard_map/ppermute | solution.py:20
  132.1 7.6 %collective-permute-start.25 = (f32[2304]{0:T(1024)S(1)}, f32[2304]{0:T(1024)S(1)}, u32[]{:S(2)}, u32[]{:S(2)}) collective-permute-start(f32[2304]{0:T(1024)S(1)} %add.121), channel_id=1, source_target_pairs={{0,4},{1,5},{2,6},{3,7},{4,0},{5,1},{6,2},{7,3},{8,12},{9,13},{10,... | collective-permute-start | bytes 27656 | tf_op jit(solution)/shard_map/ppermute | solution.py:20
  135.4 4.7 %collective-permute-start.24 = (f32[2304]{0:T(1024)S(1)}, f32[2304]{0:T(1024)S(1)}, u32[]{:S(2)}, u32[]{:S(2)}) collective-permute-start(f32[2304]{0:T(1024)S(1)} %add.121), channel_id=1, source_target_pairs={{0,2},{1,3},{2,0},{3,1},{4,6},{5,7},{6,4},{7,5},{8,10},{9,11},{10,... | collective-permute-start | bytes 27656 | tf_op jit(solution)/shard_map/ppermute | solution.py:20
  140.2 6.9 %collective-permute-start.29 = (f32[128]{0:T(128)S(1)}, f32[128]{0:T(128)S(1)}, u32[]{:S(2)}, u32[]{:S(2)}) collective-permute-start(f32[128]{0:T(128)S(1)} %get-tuple-element.104), channel_id=1, source_target_pairs={{0,192},{64,128},{128,64},{192,0},{1,193},{65,129},{129,65},{193,1... | collective-permute-start | bytes 1544 | tf_op jit(solution)/shard_map/ppermute | solution.py:20
  140.9 6.2 %collective-permute-start.28 = (f32[128]{0:T(128)S(1)}, f32[128]{0:T(128)S(1)}, u32[]{:S(2)}, u32[]{:S(2)}) collective-permute-start(f32[128]{0:T(128)S(1)} %get-tuple-element.104), channel_id=1, source_target_pairs={{0,128},{64,192},{128,0},{192,64},{1,129},{65,193},{129,1},{193,65... | collective-permute-start | bytes 1544 | tf_op jit(solution)/shard_map/ppermute | solution.py:20
  145.5 8.6 %collective-permute-start.31 = (f32[8,32,192]{2,1,0:T(8,128)S(1)}, f32[8,32,192]{2,1,0:T(8,128)S(1)}, u32[]{:S(2)}, u32[]{:S(2)}) collective-permute-start(f32[8,32,192]{2,1,0:T(8,128)S(1)} %slice_select_fusion), channel_id=1, source_target_pairs={{0,16},{16,0},{1,17},{17,1},{2,18},{18,2},{3,19},{19,3},{4,20},{20... | collective-permute-start | bytes 589832 | tf_op jit(solution)/shard_map/ppermute | solution.py:20
  147.1 7.0 %collective-permute-start.30 = (f32[128]{0:T(128)S(1)}, f32[128]{0:T(128)S(1)}, u32[]{:S(2)}, u32[]{:S(2)}) collective-permute-start(f32[128]{0:T(128)S(1)} %add_add_fusion.2), channel_id=1, source_target_pairs={{0,32},{32,0},{1,33},{33,1},{2,34},{34,2},{3,35},{35,3},{4,36},{36... | collective-permute-start | bytes 1544 | tf_op jit(solution)/shard_map/ppermute | solution.py:20
  (25 other events, 190.2 us)
Sparse Core Ops, SparseCore 0:
  14.9 51.2 all-gather.1
  87.9 42.0 reduce-scatter.1

commit v7 on v6

--- a/solution.py
+++ b/solution.py
@@ -11,6 +11,7 @@
 HALF = 384
 FIRST, SECOND = 3, 5
 VMEM = 28 * 1024 * 1024
+STEP = 4
 
 epsilon = 1e-30
 decay_rate = 0.9
@@ -59,17 +60,17 @@
             out_specs=[spec, spec],
         ),
         out_shape=[jax.ShapeDtypeStruct((768, HALF), jnp.bfloat16)] * 2,
-        compiler_params=pltpu.CompilerParams(vmem_limit_bytes=VMEM),
+        compiler_params=pltpu.CompilerParams(vmem_limit_bytes=60 * 1024 * 1024),
     )(halves, weight)
 
 
 VECTORS = pl.BlockSpec(memory_space=pltpu.VMEM)
 SCALARS = pl.BlockSpec(memory_space=pltpu.SMEM)
-PARAMS = pltpu.CompilerParams(vmem_limit_bytes=VMEM)
+PARAMS = pltpu.CompilerParams(vmem_limit_bytes=60 * 1024 * 1024)
 
 
 def tokens(refs):
-    return jnp.concatenate([ref[...].reshape(256, 768) for ref in refs], axis=0)
+    return jnp.concatenate([ref[...].reshape(-1, 768) for ref in refs], axis=0)
 
 
 def first_kernel(*refs):
@@ -91,7 +92,8 @@
     for j in range(FIRST):
         out[:, rows_ref[j]] = before_ref[:, j] + received[j][...]
     for j in range(SECOND):
-        out[:, rows_ref[FIRST + j]] = part[j * 256 : (j + 1) * 256].reshape(8, 32, HALF)
+        rows = part[j * STEP * 32 : (j + 1) * STEP * 32]
+        out[:, rows_ref[FIRST + j]] = rows.reshape(STEP, 32, HALF)
 
 
 def first_call(cots, keep, send):
@@ -109,12 +111,23 @@
 
 
 def second_call(rows, cots, others, keep, other_keep, before, received):
+    def step_spec(*shape):
+        return pl.BlockSpec((STEP, *shape), lambda s, rows: (s,) + (0,) * len(shape))
+
+    weight = pl.BlockSpec((768, HALF), lambda s, rows: (0, 0))
     return pl.pallas_call(
         second_kernel,
-        in_specs=[SCALARS] + [VECTORS] * (2 * SECOND + 3 + FIRST),
-        out_specs=VECTORS,
+        grid_spec=pltpu.PrefetchScalarGridSpec(
+            num_scalar_prefetch=1,
+            grid=(8 // STEP,),
+            in_specs=[step_spec(32, 768)] * (2 * SECOND)
+            + [weight] * 2
+            + [step_spec(FIRST, 32, HALF)]
+            + [step_spec(32, HALF)] * FIRST,
+            out_specs=step_spec(8, 32, HALF),
+        ),
         out_shape=jax.ShapeDtypeStruct((8, 8, 32, HALF), jnp.float32),
-        compiler_params=PARAMS,
+        compiler_params=pltpu.CompilerParams(vmem_limit_bytes=60 * 1024 * 1024),
         cost_estimate=pl.CostEstimate(
             flops=SECOND * 4 * 256 * 768 * HALF, bytes_accessed=8 * 1024 * 1024, transcendentals=0
         ),
@@ -210,12 +223,13 @@
     sums = jnp.concatenate([col_sums, jnp.sum(scaled * scaled, axis=0), row_stats])
     sums = total(total(sums, "core", 2), "yl", 2)
     sums = sums + exchange(sums, "z", 8, 1)
-    sums, summed = lax.optimization_barrier((sums, summed))
     sums = reduce_four(sums, "z", 8, (2, 4, 6))
     row_mean = jnp.sum(sums[1536:]) / FF
     col_stats = decay_rate * col_prev + (1.0 - decay_rate) * (sums[:768] / FF)
     part = jnp.sum((sums[768:1536] / col_stats).reshape(6, 128), axis=0)
-    part = total(reduce_four(part, "x", 4, (1, 2, 3)), "yh", 2)
+    part = reduce_four(part, "x", 4, (1, 2, 3))
+    part, summed = lax.optimization_barrier((part, summed))
+    part = total(part, "yh", 2)
 
     summed = summed.reshape(8, 32, HALF)
     low, high = summed[:, :, :192], summed[:, :, 192:]

time: 167 us -> 151 us (0.904)
  waiting for transfers between devices: 44.7 us -> 31.1 us
  local copies, waits for them, and re-layouts: 14.1 us -> 5.84 us
  Pallas kernels: 17.2 us -> 21.4 us
  other arithmetic: 5.85 us -> 8.81 us
    reduce_scatter x1, waiting for transfers between devices: 13.1 us -> 0.01 us  [body(): summed = lax.psum_scatter(summed, 'z', scatter_dimension=0, tiled=True)]
    unnamed x31 -> x27, local copies, waits for them, and re-layouts: 10.4 us -> 1.58 us
    ppermute x5, waiting for transfers between devices: 11 us -> 8.3 us  [shift(): lax.ppermute(value, axis, [(i, (i + step) % size) for i in range(size)])]
    ppermute x27, waiting for transfers between devices: 20.6 us -> 22.8 us  [exchange(): return lax.ppermute(value, axis, [(i, i ^ bit) for i in range(size)])]
    pallas_call x1, Pallas kernels: 2.19 us -> 3.98 us  [weight_call(): pl.pallas_call(weight_kernel, grid_spec=pltpu.PrefetchScalarGridSpec(num_...]
    reduce_sum x1, other arithmetic: 0.31 us -> 2 us  [body(): jnp.sum(scaled * scaled, axis=0)]
  transfers between devices with their start and end apart: 34 -> 34, of which waited for: 13 -> 17; matrix products, arithmetic and copies ran while one was open for 3% -> 5% of each run, Pallas kernels for 10% -> 14%
where the time goes in v7:
time: 151 us; the launch traced here: 150 us
  starting transfers between devices  34.9 us (23%)
  blocking collectives  32.3 us (21%)
  waiting for transfers between devices  31.1 us (21%)
  Pallas kernels  21.4 us (14%)
  between operations  15.6 us (10%)
  other arithmetic  8.81 us (6%)
  local copies, waits for them, and re-layouts  5.84 us (4%)
    ppermute x27, starting transfers between devices, exchange(): return lax.ppermute(value, axis, [(i, i ^ bit) for i in range(size)])  30.2 us
    all_to_all x1, blocking collectives, body(): lax.all_to_all(cotangent, 'z', 1, 0, tiled=True).reshape(8, 32, 768)  25.6 us
    ppermute x27, waiting for transfers between devices, exchange(): return lax.ppermute(value, axis, [(i, i ^ bit) for i in range(size)])  22.8 us
    ppermute x5, waiting for transfers between devices, shift(): lax.ppermute(value, axis, [(i, (i + step) % size) for i in range(size)])  8.3 us
    pallas_call x1, Pallas kernels, gradient_call(): pl.pallas_call(gradient_kernel, in_specs=[SCALARS] * 2 + [VECTORS] * 10,...  7.01 us
    all_gather x1, blocking collectives, body(): act_cols = lax.all_gather(activations, ('yl', 'core'), axis=1, tiled=True)  6.76 us
    pallas_call x1, Pallas kernels, second_call(): pl.pallas_call(second_kernel, grid_spec=pltpu.PrefetchScalarGridSpec(num_...  6.57 us
    ppermute x5, starting transfers between devices, shift(): lax.ppermute(value, axis, [(i, (i + step) % size) for i in range(size)])  4.69 us
  transfers between devices with their start and end apart: 34, of which 17 were waited for; matrix products, arithmetic and copies ran while one was open for 5% of the time, Pallas kernels for 14%

profile of v7, /device:TPU:4, one launch (start us, length us, event | category | flops | bytes accessed | tf_op | source)
XLA Modules:
  0.0 150.0 jit_solution(923987878318032633)
XLA Ops:
  7.2 6.8 %all_gather.6 = bf16[256,768]{0,1:T(8,128)(2,1)S(1)} all-gather(bf16[256,192]{0,1:T(8,128)(2,1)} %param.6), channel_id=1, replica_groups=mesh['x'=4,'yh'=2,'yl'=2,'core'=2,'z'=8] {'yl','core'}, dimensions={1}, use_global_device_ids=true | all-gather | bytes 491520 | tf_op jit(solution)/shard_map/all_gather | solution.py:180
  15.8 25.6 %all_to_all.16 = bf16[32,8,768]{2,0,1:T(8,128)(2,1)S(1)} all-to-all(bf16[32,8,768]{2,0,1:T(8,128)(2,1)S(1)} %bitcast.26), channel_id=1, replica_groups=mesh['x'=4,'yh'=2,'yl'=2,'core'=2,'z'=8] {'z'}, dimensions={1} | all-to-all | bytes 786432 | tf_op jit(solution)/shard_map/all_to_all | solution.py:185
  41.9 2.9 %collective-permute-start = (bf16[8,32,768]{2,1,0:T(8,128)(2,1)S(1)}, bf16[8,32,768]{2,1,0:T(8,128)(2,1)S(1)}, u32[]{:S(2)}, u32[]{:S(2)}) collective-permute-start(bf16[8,32,768]{2,1,0:T(8,128)(2,1)S(1)} %bitcast.30), channel_id=1, source_target_pairs={{0,32},{32,0},{1,33},{33,1},{2,34},{34,2},{3,35},{35,3},{4,36},{36... | collective-permute-start | bytes 1179656 | tf_op jit(solution)/shard_map/ppermute | solution.py:21
  45.4 2.1 %collective-permute-start.2 = (bf16[8,32,768]{2,1,0:T(8,128)(2,1)S(1)}, bf16[8,32,768]{2,1,0:T(8,128)(2,1)S(1)}, u32[]{:S(2)}, u32[]{:S(2)}) collective-permute-start(bf16[8,32,768]{2,1,0:T(8,128)(2,1)S(1)} %bitcast.31), channel_id=1, source_target_pairs={{0,64},{64,128},{128,192},{192,0},{1,65},{65,129},{129,193},{193,1... | collective-permute-start | bytes 1179656 | tf_op jit(solution)/shard_map/ppermute | solution.py:25
  48.2 4.0 %shard_map.68 = (bf16[768,384]{1,0:T(8,128)(2,1)}, bf16[768,384]{1,0:T(8,128)(2,1)}) custom-call(s32[2]{0:T(128)} %pad_add_fusion.core_ref.halves_ref, bf16[768,768]{1,0:T(8,128)(2,1)} %weight_ref), custom_call_target="tpu_custom_call" | custom-call | tf_op jit(solution)/shard_map/pallas_call | solution.py:54
  52.2 2.7 %collective-permute-done.1.refs_2_ = bf16[8,32,768]{2,1,0:T(8,128)(2,1)S(1)} collective-permute-done((bf16[8,32,768]{2,1,0:T(8,128)(2,1)S(1)}, bf16[8,32,768]{2,1,0:T(8,128)(2,1)S(1)}, u32[]{:S(2)}, u32[]{:S(2)}) %collective-permute-start.1) | collective-permute-done | bytes 393248 | tf_op jit(solution)/shard_map/ppermute | solution.py:25
  54.9 2.9 %collective-permute-start.4 = (bf16[8,32,768]{2,1,0:T(8,128)(2,1)S(1)}, bf16[8,32,768]{2,1,0:T(8,128)(2,1)}, u32[]{:S(2)}, u32[]{:S(2)}) collective-permute-start(bf16[8,32,768]{2,1,0:T(8,128)(2,1)S(1)} %collective-permute-done.1.refs_2_), channel_id=1, source_target_pairs={{0,32},{32,0},{1,33},{33,1},{2,34},{34,2},{3,35},{35,3},{4,36},{36... | collective-permute-start | bytes 1179656 | tf_op jit(solution)/shard_map/ppermute | solution.py:21
  59.9 3.9 %shard_map.69 = (f32[8,3,32,384]{3,2,1,0:T(8,128)}, f32[8,32,384]{2,1,0:T(8,128)}, f32[8,32,384]{2,1,0:T(8,128)}, f32[8,32,384]{2,1,0:T(8,128)}) custom-call(bf16[8,32,768]{2,1,0:T(8,128)(2,1)} %bitcast.33, bf16[8,32,768]{2,1,0:T(8,128)(2,1)} %copy-done.12, bf16[8,32,768]{2,1,0:T(8,128)(2,1)} %copy-done.11, ...), custom_call_target="tpu_custom_call" | custom-call | flops 905969664 | bytes 4194304 | tf_op jit(solution)/shard_map/pallas_call | solution.py:100
  64.8 5.5 %collective-permute-done.5.refs_3_.refs_6_ = bf16[8,32,768]{2,1,0:T(8,128)(2,1)} collective-permute-done((bf16[8,32,768]{2,1,0:T(8,128)(2,1)S(1)}, bf16[8,32,768]{2,1,0:T(8,128)(2,1)}, u32[]{:S(2)}, u32[]{:S(2)}) %collective-permute-start.5) | collective-permute-done | bytes 393248 | tf_op jit(solution)/shard_map/ppermute | solution.py:25
  72.9 1.9 %copy.13 = bf16[2048,384]{1,0:T(8,128)(2,1)S(1)} copy(bf16[2048,384]{0,1:T(8,128)(2,1)} %all-gather.2.cloned.1.call-done) | data formatting | bytes 3145728 | tf_op jit(solution)/shard_map/all_gather | solution.py:183
  75.7 6.6 %shard_map.70 = f32[8,8,32,384]{3,2,1,0:T(8,128)} custom-call(s32[8]{0:T(128)} %stack.47.rows_ref, bf16[8,32,768]{2,1,0:T(8,128)(2,1)} %copy-done.4, bf16[8,32,768]{2,1,0:T(8,128)(2,1)} %copy-done.5, bf16[8,32,768]{2,1,0:T(8,128)(2,1)} %collective-permute-done.4.refs_2_.refs_5_, bf16[8,32,768]{2,1,0:T(8,128)(2,1)} %collective-permute-done.5.refs_3_.refs_6_, ...), custom_call_target="tpu_custom_call" | custom-call | flops 1509949440 | bytes 8388608 | tf_op jit(solution)/shard_map/pallas_call | solution.py:118
  82.3 7.0 %shard_map.71 = (f32[768,768]{1,0:T(8,128)}, f32[768]{0:T(1024)}, f32[768]{0:T(1024)}) custom-call(s32[8]{0:T(128)} %stack.47.rows_ref, s32[2]{0:T(128)} %pad_add_fusion.core_ref.halves_ref, bf16[8,32,768]{2,1,0:T(8,128)(2,1)} %bitcast.34, bf16[8,32,768]{2,1,0:T(8,128)(2,1)} %copy-done.12, bf16[8,32,768]{2,1,0:T(8,128)(2,1)} %copy-done.11, ...), custom_call_target="tpu_custom_call" | custom-call | flops 2415919104 | bytes 9437184 | tf_op jit(solution)/shard_map/pallas_call | solution.py:160
  90.2 2.0 %collective-permute-start.18 = (f32[768]{0:T(1024)}, f32[768]{0:T(1024)S(1)}, u32[]{:S(2)}, u32[]{:S(2)}) collective-permute-start(f32[768]{0:T(1024)} %get-tuple-element.92), channel_id=1, source_target_pairs={{0,128},{64,192},{128,0},{192,64},{1,129},{65,193},{129,1},{193,65... | collective-permute-start | bytes 9224 | tf_op jit(solution)/shard_map/ppermute | solution.py:21
  93.6 2.0 %collective-permute-done.18 = f32[768]{0:T(1024)S(1)} collective-permute-done((f32[768]{0:T(1024)}, f32[768]{0:T(1024)S(1)}, u32[]{:S(2)}, u32[]{:S(2)}) %collective-permute-start.18) | collective-permute-done | bytes 3104 | tf_op jit(solution)/shard_map/ppermute | solution.py:21
  96.7 2.8 %collective-permute-start.20 = (f32[768]{0:T(1024)S(1)}, f32[768]{0:T(1024)S(1)}, u32[]{:S(2)}, u32[]{:S(2)}) collective-permute-start(f32[768]{0:T(1024)S(1)} %add_add_fusion.1), channel_id=1, source_target_pairs={{0,32},{32,0},{1,33},{33,1},{2,34},{34,2},{3,35},{35,3},{4,36},{36... | collective-permute-start | bytes 9224 | tf_op jit(solution)/shard_map/ppermute | solution.py:21
  99.5 2.3 %collective-permute-done.20 = f32[768]{0:T(1024)S(1)} collective-permute-done((f32[768]{0:T(1024)S(1)}, f32[768]{0:T(1024)S(1)}, u32[]{:S(2)}, u32[]{:S(2)}) %collective-permute-start.20) | collective-permute-done | bytes 3104 | tf_op jit(solution)/shard_map/ppermute | solution.py:21
  101.8 2.0 %multiply_reduce_fusion = f32[768]{0:T(1024)S(1)} fusion(f32[768,768]{1,0:T(8,128)} %get-tuple-element.91, f32[768]{0:T(1024)S(1)} %get-tuple-element.106), kind=kLoop, calls=%fused_computation.1 | loop fusion | flops 1768704 | bytes 2365440 | tf_op jit(solution)/shard_map/reduce_sum | solution.py:223
  105.9 2.9 %collective-permute-done.22 = f32[2304]{0:T(1024)S(1)} collective-permute-done((f32[2304]{0:T(1024)S(1)}, f32[2304]{0:T(1024)S(1)}, u32[]{:S(2)}, u32[]{:S(2)}) %collective-permute-start.22) | collective-permute-done | bytes 9248 | tf_op jit(solution)/shard_map/ppermute | solution.py:21
  108.8 4.2 %collective-permute-done.23 = f32[2304]{0:T(1024)S(1)} collective-permute-done((f32[2304]{0:T(1024)S(1)}, f32[2304]{0:T(1024)S(1)}, u32[]{:S(2)}, u32[]{:S(2)}) %collective-permute-start.23) | collective-permute-done | bytes 9248 | tf_op jit(solution)/shard_map/ppermute | solution.py:21
  115.0 4.5 %collective-permute-start.24 = (f32[2304]{0:T(1024)S(1)}, f32[2304]{0:T(1024)S(1)}, u32[]{:S(2)}, u32[]{:S(2)}) collective-permute-start(f32[2304]{0:T(1024)S(1)} %add.121), channel_id=1, source_target_pairs={{0,2},{1,3},{2,0},{3,1},{4,6},{5,7},{6,4},{7,5},{8,10},{9,11},{10,... | collective-permute-start | bytes 27656 | tf_op jit(solution)/shard_map/ppermute | solution.py:21
  122.5 2.7 %collective-permute-start.28 = (f32[128]{0:T(128)S(1)}, f32[128]{0:T(128)S(1)}, u32[]{:S(2)}, u32[]{:S(2)}) collective-permute-start(f32[128]{0:T(128)S(1)} %get-tuple-element.104), channel_id=1, source_target_pairs={{0,128},{64,192},{128,0},{192,64},{1,129},{65,193},{129,1},{193,65... | collective-permute-start | bytes 1544 | tf_op jit(solution)/shard_map/ppermute | solution.py:21
  130.8 3.0 %collective-permute-start.30 = (f32[128]{0:T(128)S(1)}, f32[128]{0:T(128)S(1)}, u32[]{:S(2)}, u32[]{:S(2)}) collective-permute-start(f32[128]{0:T(128)S(1)} %add_add_fusion.2), channel_id=1, source_target_pairs={{0,32},{32,0},{1,33},{33,1},{2,34},{34,2},{3,35},{35,3},{4,36},{36... | collective-permute-start | bytes 1544 | tf_op jit(solution)/shard_map/ppermute | solution.py:21
  135.0 3.1 %collective-permute-done.30 = f32[128]{0:T(128)S(1)} collective-permute-done((f32[128]{0:T(128)S(1)}, f32[128]{0:T(128)S(1)}, u32[]{:S(2)}, u32[]{:S(2)}) %collective-permute-start.30) | collective-permute-done | bytes 544 | tf_op jit(solution)/shard_map/ppermute | solution.py:21
  141.3 1.9 %multiply_divide_fusion = f32[768,768]{1,0:T(8,128)} fusion(f32[768,768]{1,0:T(8,128)S(1)} %copy-done, f32[]{:T(128)S(6)} %max_shard_map.3, f32[]{:T(128)S(6)} %div.26, f32[768]{0:T(1024)S(1)} %get-tuple-element.105, f32[768]{0:T(1024)S(1)} %get-tuple-element.107), kind=kLoop, calls=%fused_computation | loop fusion | flops 2359296 | bytes 4724744 | tf_op jit(solution)/shard_map/div | solution.py:245
  (100 shorter events, 29.3 us)
Async XLA Ops:
  7.2 65.8 %all-gather.2.cloned.1.call-start = ((), (), s32[]{:S(2)}) async-start(), calls=%async_computation.2 | async-start | bytes 1769472 | tf_op jit(solution)/shard_map/all_gather | solution.py:183
  14.7 114.1 %reduce-scatter.2.cloned.1.call-start = ((), (), s32[]{:S(2)}) async-start(), calls=%async_computation.3 | async-start | bytes 3538944 | tf_op jit(solution)/shard_map/reduce_scatter | solution.py:217
  41.3 13.6 %collective-permute-start.1 = (bf16[8,32,768]{2,1,0:T(8,128)(2,1)S(1)}, bf16[8,32,768]{2,1,0:T(8,128)(2,1)S(1)}, u32[]{:S(2)}, u32[]{:S(2)}) collective-permute-start(bf16[8,32,768]{2,1,0:T(8,128)(2,1)S(1)} %bitcast.29), channel_id=1, source_target_pairs={{0,128},{64,192},{128,0},{192,64},{1,129},{65,193},{129,1},{193,65... | collective-permute-start | bytes 1179656 | tf_op jit(solution)/shard_map/ppermute | solution.py:25
  41.9 16.0 %collective-permute-start = (bf16[8,32,768]{2,1,0:T(8,128)(2,1)S(1)}, bf16[8,32,768]{2,1,0:T(8,128)(2,1)S(1)}, u32[]{:S(2)}, u32[]{:S(2)}) collective-permute-start(bf16[8,32,768]{2,1,0:T(8,128)(2,1)S(1)} %bitcast.30), channel_id=1, source_target_pairs={{0,32},{32,0},{1,33},{33,1},{2,34},{34,2},{3,35},{35,3},{4,36},{36... | collective-permute-start | bytes 1179656 | tf_op jit(solution)/shard_map/ppermute | solution.py:21
  45.4 18.4 %collective-permute-start.2 = (bf16[8,32,768]{2,1,0:T(8,128)(2,1)S(1)}, bf16[8,32,768]{2,1,0:T(8,128)(2,1)S(1)}, u32[]{:S(2)}, u32[]{:S(2)}) collective-permute-start(bf16[8,32,768]{2,1,0:T(8,128)(2,1)S(1)} %bitcast.31), channel_id=1, source_target_pairs={{0,64},{64,128},{128,192},{192,0},{1,65},{65,129},{129,193},{193,1... | collective-permute-start | bytes 1179656 | tf_op jit(solution)/shard_map/ppermute | solution.py:25
  47.5 16.3 %collective-permute-start.3 = (bf16[8,32,768]{2,1,0:T(8,128)(2,1)S(1)}, bf16[8,32,768]{2,1,0:T(8,128)(2,1)S(1)}, u32[]{:S(2)}, u32[]{:S(2)}) collective-permute-start(bf16[8,32,768]{2,1,0:T(8,128)(2,1)S(1)} %bitcast.32), channel_id=1, source_target_pairs={{0,192},{64,0},{128,64},{192,128},{1,193},{65,1},{129,65},{193,129... | collective-permute-start | bytes 1179656 | tf_op jit(solution)/shard_map/ppermute | solution.py:25
  54.9 9.9 %collective-permute-start.4 = (bf16[8,32,768]{2,1,0:T(8,128)(2,1)S(1)}, bf16[8,32,768]{2,1,0:T(8,128)(2,1)}, u32[]{:S(2)}, u32[]{:S(2)}) collective-permute-start(bf16[8,32,768]{2,1,0:T(8,128)(2,1)S(1)} %collective-permute-done.1.refs_2_), channel_id=1, source_target_pairs={{0,32},{32,0},{1,33},{33,1},{2,34},{34,2},{3,35},{35,3},{4,36},{36... | collective-permute-start | bytes 1179656 | tf_op jit(solution)/shard_map/ppermute | solution.py:21
  57.9 12.5 %collective-permute-start.5 = (bf16[8,32,768]{2,1,0:T(8,128)(2,1)S(1)}, bf16[8,32,768]{2,1,0:T(8,128)(2,1)}, u32[]{:S(2)}, u32[]{:S(2)}) collective-permute-start(bf16[8,32,768]{2,1,0:T(8,128)(2,1)S(1)} %collective-permute-done.refs_1_), channel_id=1, source_target_pairs={{0,64},{64,128},{128,192},{192,0},{1,65},{65,129},{129,193},{193,1... | collective-permute-start | bytes 1179656 | tf_op jit(solution)/shard_map/ppermute | solution.py:25
  59.0 11.3 %collective-permute-start.6 = (bf16[8,32,768]{2,1,0:T(8,128)(2,1)S(1)}, bf16[8,32,768]{2,1,0:T(8,128)(2,1)}, u32[]{:S(2)}, u32[]{:S(2)}) collective-permute-start(bf16[8,32,768]{2,1,0:T(8,128)(2,1)S(1)} %collective-permute-done.refs_1_), channel_id=1, source_target_pairs={{0,192},{64,0},{128,64},{192,128},{1,193},{65,1},{129,65},{193,129... | collective-permute-start | bytes 1179656 | tf_op jit(solution)/shard_map/ppermute | solution.py:25
  63.8 7.1 %collective-permute-start.7 = (bf16[8,32,768]{2,1,0:T(8,128)(2,1)S(1)}, bf16[8,32,768]{2,1,0:T(8,128)(2,1)S(1)}, u32[]{:S(2)}, u32[]{:S(2)}) collective-permute-start(bf16[8,32,768]{2,1,0:T(8,128)(2,1)S(1)} %collective-permute-done.2.refs_0_.refs_3_), channel_id=1, source_target_pairs={{0,8},{8,0},{1,9},{9,1},{2,10},{10,2},{3,11},{11,3},{4,12},{12,4},... | collective-permute-start | bytes 1179656 | tf_op jit(solution)/shard_map/ppermute | solution.py:21
  63.9 7.1 %collective-permute-start.8 = (bf16[8,32,768]{2,1,0:T(8,128)(2,1)S(1)}, bf16[8,32,768]{2,1,0:T(8,128)(2,1)S(1)}, u32[]{:S(2)}, u32[]{:S(2)}) collective-permute-start(bf16[8,32,768]{2,1,0:T(8,128)(2,1)S(1)} %collective-permute-done.3.refs_1_.refs_4_), channel_id=1, source_target_pairs={{0,8},{8,0},{1,9},{9,1},{2,10},{10,2},{3,11},{11,3},{4,12},{12,4},... | collective-permute-start | bytes 1179656 | tf_op jit(solution)/shard_map/ppermute | solution.py:21
  64.8 7.3 %collective-permute-start.12 = (f32[8,32,384]{2,1,0:T(8,128)}, f32[8,32,384]{2,1,0:T(8,128)}, u32[]{:S(2)}, u32[]{:S(2)}) collective-permute-start(f32[8,32,384]{2,1,0:T(8,128)} %get-tuple-element.65), channel_id=1, source_target_pairs={{0,8},{8,0},{1,9},{9,1},{2,10},{10,2},{3,11},{11,3},{4,12},{12,4},... | collective-permute-start | bytes 1179656 | tf_op jit(solution)/shard_map/ppermute | solution.py:21
  70.4 4.4 %collective-permute-start.15 = (bf16[768,384]{1,0:T(8,128)(2,1)}, bf16[768,384]{1,0:T(8,128)(2,1)S(1)}, u32[]{:S(2)}, u32[]{:S(2)}) collective-permute-start(bf16[768,384]{1,0:T(8,128)(2,1)} %get-tuple-element.59.refs_4_), channel_id=1, source_target_pairs={{0,8},{8,0},{1,9},{9,1},{2,10},{10,2},{3,11},{11,3},{4,12},{12,4},... | collective-permute-start | bytes 1769480 | tf_op jit(solution)/shard_map/ppermute | solution.py:21
  75.5 6.8 %collective-permute-start.16 = (bf16[8,8,32,384]{3,2,1,0:T(8,128)(2,1)S(1)}, bf16[8,8,32,384]{3,2,1,0:T(8,128)(2,1)}, u32[]{:S(2)}, u32[]{:S(2)}) collective-permute-start(bf16[8,8,32,384]{3,2,1,0:T(8,128)(2,1)S(1)} %bitcast.24), channel_id=1, source_target_pairs={{0,8},{8,0},{1,9},{9,1},{2,10},{10,2},{3,11},{11,3},{4,12},{12,4},... | collective-permute-start | bytes 4718600 | tf_op jit(solution)/shard_map/ppermute | solution.py:21
  89.4 4.2 %collective-permute-start.19 = (f32[768]{0:T(1024)}, f32[768]{0:T(1024)S(1)}, u32[]{:S(2)}, u32[]{:S(2)}) collective-permute-start(f32[768]{0:T(1024)} %get-tuple-element.92), channel_id=1, source_target_pairs={{0,192},{64,128},{128,64},{192,0},{1,193},{65,129},{129,65},{193,1... | collective-permute-start | bytes 9224 | tf_op jit(solution)/shard_map/ppermute | solution.py:21
  90.2 5.3 %collective-permute-start.18 = (f32[768]{0:T(1024)}, f32[768]{0:T(1024)S(1)}, u32[]{:S(2)}, u32[]{:S(2)}) collective-permute-start(f32[768]{0:T(1024)} %get-tuple-element.92), channel_id=1, source_target_pairs={{0,128},{64,192},{128,0},{192,64},{1,129},{65,193},{129,1},{193,65... | collective-permute-start | bytes 9224 | tf_op jit(solution)/shard_map/ppermute | solution.py:21
  96.7 5.1 %collective-permute-start.20 = (f32[768]{0:T(1024)S(1)}, f32[768]{0:T(1024)S(1)}, u32[]{:S(2)}, u32[]{:S(2)}) collective-permute-start(f32[768]{0:T(1024)S(1)} %add_add_fusion.1), channel_id=1, source_target_pairs={{0,32},{32,0},{1,33},{33,1},{2,34},{34,2},{3,35},{35,3},{4,36},{36... | collective-permute-start | bytes 9224 | tf_op jit(solution)/shard_map/ppermute | solution.py:21
  108.8 4.2 %collective-permute-start.23 = (f32[2304]{0:T(1024)S(1)}, f32[2304]{0:T(1024)S(1)}, u32[]{:S(2)}, u32[]{:S(2)}) collective-permute-start(f32[2304]{0:T(1024)S(1)} %add.120), channel_id=1, source_target_pairs={{0,1},{1,0},{2,3},{3,2},{4,5},{5,4},{6,7},{7,6},{8,9},{9,8},{10,11... | collective-permute-start | bytes 27656 | tf_op jit(solution)/shard_map/ppermute | solution.py:21
  113.0 6.5 %collective-permute-start.26 = (f32[2304]{0:T(1024)S(1)}, f32[2304]{0:T(1024)S(1)}, u32[]{:S(2)}, u32[]{:S(2)}) collective-permute-start(f32[2304]{0:T(1024)S(1)} %add.121), channel_id=1, source_target_pairs={{0,6},{1,7},{2,4},{3,5},{4,2},{5,3},{6,0},{7,1},{8,14},{9,15},{10,... | collective-permute-start | bytes 27656 | tf_op jit(solution)/shard_map/ppermute | solution.py:21
  113.1 8.0 %collective-permute-start.25 = (f32[2304]{0:T(1024)S(1)}, f32[2304]{0:T(1024)S(1)}, u32[]{:S(2)}, u32[]{:S(2)}) collective-permute-start(f32[2304]{0:T(1024)S(1)} %add.121), channel_id=1, source_target_pairs={{0,4},{1,5},{2,6},{3,7},{4,0},{5,1},{6,2},{7,3},{8,12},{9,13},{10,... | collective-permute-start | bytes 27656 | tf_op jit(solution)/shard_map/ppermute | solution.py:21
  115.0 6.8 %collective-permute-start.24 = (f32[2304]{0:T(1024)S(1)}, f32[2304]{0:T(1024)S(1)}, u32[]{:S(2)}, u32[]{:S(2)}) collective-permute-start(f32[2304]{0:T(1024)S(1)} %add.121), channel_id=1, source_target_pairs={{0,2},{1,3},{2,0},{3,1},{4,6},{5,7},{6,4},{7,5},{8,10},{9,11},{10,... | collective-permute-start | bytes 27656 | tf_op jit(solution)/shard_map/ppermute | solution.py:21
  122.5 5.0 %collective-permute-start.28 = (f32[128]{0:T(128)S(1)}, f32[128]{0:T(128)S(1)}, u32[]{:S(2)}, u32[]{:S(2)}) collective-permute-start(f32[128]{0:T(128)S(1)} %get-tuple-element.104), channel_id=1, source_target_pairs={{0,128},{64,192},{128,0},{192,64},{1,129},{65,193},{129,1},{193,65... | collective-permute-start | bytes 1544 | tf_op jit(solution)/shard_map/ppermute | solution.py:21
  129.9 8.2 %collective-permute-start.31 = (f32[8,32,192]{2,1,0:T(8,128)S(1)}, f32[8,32,192]{2,1,0:T(8,128)S(1)}, u32[]{:S(2)}, u32[]{:S(2)}) collective-permute-start(f32[8,32,192]{2,1,0:T(8,128)S(1)} %slice_select_fusion), channel_id=1, source_target_pairs={{0,16},{16,0},{1,17},{17,1},{2,18},{18,2},{3,19},{19,3},{4,20},{20... | collective-permute-start | bytes 589832 | tf_op jit(solution)/shard_map/ppermute | solution.py:21
  130.8 7.3 %collective-permute-start.30 = (f32[128]{0:T(128)S(1)}, f32[128]{0:T(128)S(1)}, u32[]{:S(2)}, u32[]{:S(2)}) collective-permute-start(f32[128]{0:T(128)S(1)} %add_add_fusion.2), channel_id=1, source_target_pairs={{0,32},{32,0},{1,33},{33,1},{2,34},{34,2},{3,35},{35,3},{4,36},{36... | collective-permute-start | bytes 1544 | tf_op jit(solution)/shard_map/ppermute | solution.py:21
  (23 other events, 213.1 us)
Sparse Core Ops, SparseCore 0:
  14.8 51.0 all-gather.1
  82.4 43.1 reduce-scatter.1

commit v8 on v7

--- a/solution.py
+++ b/solution.py
@@ -1,6 +1,7 @@
 import jax
 import jax.numpy as jnp
 from jax import lax
+from jax.experimental.layout import Layout, with_layout_constraint
 from jax.experimental import pallas as pl
 from jax.experimental.pallas import tpu as pltpu
 from jax.sharding import Mesh
@@ -177,10 +178,19 @@
     x, yh, core = lax.axis_index("x"), lax.axis_index("yh"), lax.axis_index("core")
     yl = lax.axis_index("yl")
 
-    act_cols = lax.all_gather(activations, ("yl", "core"), axis=1, tiled=True)
-    act_half = lax.dynamic_slice_in_dim(act_cols, core * HALF, HALF, 1)
+    near = lax.ppermute(activations, ("yl", "core"), [(0, 2), (3, 1), (1, 0), (2, 3)])
+    cross = lax.ppermute(activations, ("yl", "core"), [(1, 2), (2, 1)])
+    same = jnp.where(yl == core, activations, near)
+    opposite = jnp.where(yl == core, near, cross)
+    act_half = jnp.where(
+        core == 0,
+        jnp.concatenate([same, opposite], axis=1),
+        jnp.concatenate([opposite, same], axis=1),
+    )
+    act_half = with_layout_constraint(act_half, Layout((0, 1)))
     act_half, cotangent = lax.optimization_barrier((act_half, cotangent))
-    act_own = lax.all_gather(act_half, "z", axis=0, tiled=True).reshape(8, 8, 32, HALF)
+    act_own = lax.all_gather(act_half, "z", axis=0, tiled=True)
+    act_own = with_layout_constraint(act_own, Layout((0, 1))).reshape(8, 8, 32, HALF)
 
     own_cot = lax.all_to_all(cotangent, "z", 1, 0, tiled=True).reshape(8, 32, 768)
     own_cot, weight = lax.optimization_barrier((own_cot, weight))
@@ -227,9 +237,10 @@
     row_mean = jnp.sum(sums[1536:]) / FF
     col_stats = decay_rate * col_prev + (1.0 - decay_rate) * (sums[:768] / FF)
     part = jnp.sum((sums[768:1536] / col_stats).reshape(6, 128), axis=0)
-    part = reduce_four(part, "x", 4, (1, 2, 3))
+    others = [exchange(part, "x", 4, bit) for bit in (1, 2, 3)]
+    part = part + others[0]
     part, summed = lax.optimization_barrier((part, summed))
-    part = total(part, "yh", 2)
+    part = total(part + others[1] + others[2], "yh", 2)
 
     summed = summed.reshape(8, 32, HALF)
     low, high = summed[:, :, :192], summed[:, :, 192:]

time: 151 us -> 148 us (0.980)
  blocking collectives: 32.3 us -> 22.9 us
  waiting for transfers between devices: 31.1 us -> 35.8 us
  starting transfers between devices: 34.9 us -> 37.7 us
  local copies, waits for them, and re-layouts: 5.84 us -> 4.25 us
    all_gather x1 -> x0, blocking collectives: 6.76 us -> none  [body(): act_cols = lax.all_gather(activations, ('yl', 'core'), axis=1, tiled=True)]
    all_to_all x1, blocking collectives: 25.6 us -> 22.9 us  [body(): lax.all_to_all(cotangent, 'z', 1, 0, tiled=True).reshape(8, 32, 768)]
    ppermute x0 -> x2, starting transfers between devices: none -> 2.32 us  [the longest x1 1.66 us: body(): lax.ppermute(activations, ('yl', 'core'), [(0, 2), (3, 1), (1, 0), (2, 3)])]
    ppermute x27, waiting for transfers between devices: 22.8 us -> 24.8 us  [exchange(): return lax.ppermute(value, axis, [(i, i ^ bit) for i in range(size)])]
    all_gather x1 -> x0, local copies, waits for them, and re-layouts: 1.87 us -> none  [body(): lax.all_gather(act_half, 'z', axis=0, tiled=True).reshape(8, 8, 32, HALF)]
    ppermute x0 -> x2, waiting for transfers between devices: none -> 1.85 us  [the longest x1 1.85 us: body(): lax.ppermute(activations, ('yl', 'core'), [(0, 2), (3, 1), (1, 0), (2, 3)])]
  transfers between devices with their start and end apart: 34 -> 36, of which waited for: 17 -> 17; matrix products, arithmetic and copies ran while one was open for 5% -> 5% of each run, Pallas kernels for 14% -> 15%
where the time goes in v8:
time: 148 us; the launch traced here: 147 us
  starting transfers between devices  37.7 us (25%)
  waiting for transfers between devices  35.8 us (24%)
  blocking collectives  22.9 us (15%)
  Pallas kernels  21.5 us (15%)
  between operations  15.6 us (11%)
  other arithmetic  9.65 us (7%)
  local copies, waits for them, and re-layouts  4.25 us (3%)
    ppermute x27, starting transfers between devices, exchange(): return lax.ppermute(value, axis, [(i, i ^ bit) for i in range(size)])  30.6 us
    ppermute x27, waiting for transfers between devices, exchange(): return lax.ppermute(value, axis, [(i, i ^ bit) for i in range(size)])  24.8 us
    all_to_all x1, blocking collectives, body(): lax.all_to_all(cotangent, 'z', 1, 0, tiled=True).reshape(8, 32, 768)  22.9 us
    ppermute x5, waiting for transfers between devices, shift(): lax.ppermute(value, axis, [(i, (i + step) % size) for i in range(size)])  9.02 us
    pallas_call x1, Pallas kernels, gradient_call(): pl.pallas_call(gradient_kernel, in_specs=[SCALARS] * 2 + [VECTORS] * 10,...  7.06 us
    pallas_call x1, Pallas kernels, second_call(): pl.pallas_call(second_kernel, grid_spec=pltpu.PrefetchScalarGridSpec(num_...  6.57 us
    ppermute x5, starting transfers between devices, shift(): lax.ppermute(value, axis, [(i, (i + step) % size) for i in range(size)])  4.71 us
    pallas_call x1, Pallas kernels, weight_call(): pl.pallas_call(weight_kernel, grid_spec=pltpu.PrefetchScalarGridSpec(num_...  4 us
  transfers between devices with their start and end apart: 36, of which 17 were waited for; matrix products, arithmetic and copies ran while one was open for 5% of the time, Pallas kernels for 15%

profile of v8, /device:TPU:4, one launch (start us, length us, event | category | flops | bytes accessed | tf_op | source)
XLA Modules:
  0.0 147.4 jit_solution(11356127270041651066)
XLA Ops:
  14.4 22.9 %all_to_all.16 = bf16[32,8,768]{2,0,1:T(8,128)(2,1)S(1)} all-to-all(bf16[32,8,768]{2,0,1:T(8,128)(2,1)S(1)} %bitcast.24), channel_id=1, replica_groups=mesh['x'=4,'yh'=2,'yl'=2,'core'=2,'z'=8] {'z'}, dimensions={1} | all-to-all | bytes 786432 | tf_op jit(solution)/shard_map/all_to_all | solution.py:195
  37.8 2.5 %collective-permute-start.2 = (bf16[8,32,768]{2,1,0:T(8,128)(2,1)S(1)}, bf16[8,32,768]{2,1,0:T(8,128)(2,1)S(1)}, u32[]{:S(2)}, u32[]{:S(2)}) collective-permute-start(bf16[8,32,768]{2,1,0:T(8,128)(2,1)S(1)} %bitcast.28), channel_id=1, source_target_pairs={{0,32},{32,0},{1,33},{33,1},{2,34},{34,2},{3,35},{35,3},{4,36},{36... | collective-permute-start | bytes 1179656 | tf_op jit(solution)/shard_map/ppermute | solution.py:22
  40.9 2.1 %collective-permute-start.4 = (bf16[8,32,768]{2,1,0:T(8,128)(2,1)S(1)}, bf16[8,32,768]{2,1,0:T(8,128)(2,1)S(1)}, u32[]{:S(2)}, u32[]{:S(2)}) collective-permute-start(bf16[8,32,768]{2,1,0:T(8,128)(2,1)S(1)} %bitcast.29), channel_id=1, source_target_pairs={{0,64},{64,128},{128,192},{192,0},{1,65},{65,129},{129,193},{193,1... | collective-permute-start | bytes 1179656 | tf_op jit(solution)/shard_map/ppermute | solution.py:26
  43.8 4.0 %shard_map.68 = (bf16[768,384]{1,0:T(8,128)(2,1)}, bf16[768,384]{1,0:T(8,128)(2,1)}) custom-call(s32[2]{0:T(128)} %pad_add_fusion.core_ref.halves_ref, bf16[768,768]{1,0:T(8,128)(2,1)} %weight_ref), custom_call_target="tpu_custom_call" | custom-call | tf_op jit(solution)/shard_map/pallas_call | solution.py:55
  48.6 2.0 %collective-permute-start.6 = (bf16[8,32,768]{2,1,0:T(8,128)(2,1)S(1)}, bf16[8,32,768]{2,1,0:T(8,128)(2,1)S(1)}, u32[]{:S(2)}, u32[]{:S(2)}) collective-permute-start(bf16[8,32,768]{2,1,0:T(8,128)(2,1)S(1)} %collective-permute-done.3.refs_2_), channel_id=1, source_target_pairs={{0,32},{32,0},{1,33},{33,1},{2,34},{34,2},{3,35},{35,3},{4,36},{36... | collective-permute-start | bytes 1179656 | tf_op jit(solution)/shard_map/ppermute | solution.py:22
  52.6 3.9 %shard_map.69 = (f32[8,3,32,384]{3,2,1,0:T(8,128)}, f32[8,32,384]{2,1,0:T(8,128)}, f32[8,32,384]{2,1,0:T(8,128)}, f32[8,32,384]{2,1,0:T(8,128)}) custom-call(bf16[8,32,768]{2,1,0:T(8,128)(2,1)} %bitcast.31, bf16[8,32,768]{2,1,0:T(8,128)(2,1)} %copy-done.19, bf16[8,32,768]{2,1,0:T(8,128)(2,1)} %copy-done.18, ...), custom_call_target="tpu_custom_call" | custom-call | flops 905969664 | bytes 4194304 | tf_op jit(solution)/shard_map/pallas_call | solution.py:101
  56.5 2.6 %collective-permute-done.4.refs_0_.refs_3_ = bf16[8,32,768]{2,1,0:T(8,128)(2,1)S(1)} collective-permute-done((bf16[8,32,768]{2,1,0:T(8,128)(2,1)S(1)}, bf16[8,32,768]{2,1,0:T(8,128)(2,1)S(1)}, u32[]{:S(2)}, u32[]{:S(2)}) %collective-permute-start.4) | collective-permute-done | bytes 393248 | tf_op jit(solution)/shard_map/ppermute | solution.py:26
  59.1 2.3 %collective-permute-start.9 = (bf16[8,32,768]{2,1,0:T(8,128)(2,1)S(1)}, bf16[8,32,768]{2,1,0:T(8,128)(2,1)S(1)}, u32[]{:S(2)}, u32[]{:S(2)}) collective-permute-start(bf16[8,32,768]{2,1,0:T(8,128)(2,1)S(1)} %collective-permute-done.4.refs_0_.refs_3_), channel_id=1, source_target_pairs={{0,8},{8,0},{1,9},{9,1},{2,10},{10,2},{3,11},{11,3},{4,12},{12,4},... | collective-permute-start | bytes 1179656 | tf_op jit(solution)/shard_map/ppermute | solution.py:22
  61.9 5.6 %collective-permute-done.7.refs_3_.refs_6_ = bf16[8,32,768]{2,1,0:T(8,128)(2,1)S(1)} collective-permute-done((bf16[8,32,768]{2,1,0:T(8,128)(2,1)S(1)}, bf16[8,32,768]{2,1,0:T(8,128)(2,1)S(1)}, u32[]{:S(2)}, u32[]{:S(2)}) %collective-permute-start.7) | collective-permute-done | bytes 393248 | tf_op jit(solution)/shard_map/ppermute | solution.py:26
  73.3 6.6 %shard_map.70 = f32[8,8,32,384]{3,2,1,0:T(8,128)} custom-call(s32[8]{0:T(128)} %stack.47.rows_ref, bf16[8,32,768]{2,1,0:T(8,128)(2,1)} %copy-done.3, bf16[8,32,768]{2,1,0:T(8,128)(2,1)} %copy-done.4, bf16[8,32,768]{2,1,0:T(8,128)(2,1)} %copy-done.5, bf16[8,32,768]{2,1,0:T(8,128)(2,1)} %copy-done.6, bf16[8,32,768]{2,1,0:T(8,128)(2,1)} %copy-done.7, ...), custom_call_target="tpu_custom_call" | custom-call | flops 1509949440 | bytes 8388608 | tf_op jit(solution)/shard_map/pallas_call | solution.py:119
  79.9 7.1 %shard_map.71 = (f32[768,768]{1,0:T(8,128)}, f32[768]{0:T(1024)}, f32[768]{0:T(1024)}) custom-call(s32[8]{0:T(128)} %stack.47.rows_ref, s32[2]{0:T(128)} %pad_add_fusion.core_ref.halves_ref, bf16[8,32,768]{2,1,0:T(8,128)(2,1)} %bitcast.32, bf16[8,32,768]{2,1,0:T(8,128)(2,1)} %copy-done.19, bf16[8,32,768]{2,1,0:T(8,128)(2,1)} %copy-done.18, ...), custom_call_target="tpu_custom_call" | custom-call | flops 2415919104 | bytes 9437184 | tf_op jit(solution)/shard_map/pallas_call | solution.py:161
  87.5 2.2 %collective-permute-start.20 = (f32[768]{0:T(1024)}, f32[768]{0:T(1024)S(1)}, u32[]{:S(2)}, u32[]{:S(2)}) collective-permute-start(f32[768]{0:T(1024)} %get-tuple-element.92), channel_id=1, source_target_pairs={{0,128},{64,192},{128,0},{192,64},{1,129},{65,193},{129,1},{193,65... | collective-permute-start | bytes 9224 | tf_op jit(solution)/shard_map/ppermute | solution.py:22
  94.2 2.5 %collective-permute-start.22 = (f32[768]{0:T(1024)S(1)}, f32[768]{0:T(1024)S(1)}, u32[]{:S(2)}, u32[]{:S(2)}) collective-permute-start(f32[768]{0:T(1024)S(1)} %add_add_fusion.1), channel_id=1, source_target_pairs={{0,32},{32,0},{1,33},{33,1},{2,34},{34,2},{3,35},{35,3},{4,36},{36... | collective-permute-start | bytes 9224 | tf_op jit(solution)/shard_map/ppermute | solution.py:22
  96.6 2.6 %collective-permute-done.22 = f32[768]{0:T(1024)S(1)} collective-permute-done((f32[768]{0:T(1024)S(1)}, f32[768]{0:T(1024)S(1)}, u32[]{:S(2)}, u32[]{:S(2)}) %collective-permute-start.22) | collective-permute-done | bytes 3104 | tf_op jit(solution)/shard_map/ppermute | solution.py:22
  99.3 2.0 %multiply_reduce_fusion = f32[768]{0:T(1024)S(1)} fusion(f32[768,768]{1,0:T(8,128)} %get-tuple-element.91, f32[768]{0:T(1024)S(1)} %get-tuple-element.106), kind=kLoop, calls=%fused_computation.1 | loop fusion | flops 1768704 | bytes 2365440 | tf_op jit(solution)/shard_map/reduce_sum | solution.py:233
  102.6 3.7 %collective-permute-done.24 = f32[2304]{0:T(1024)S(1)} collective-permute-done((f32[2304]{0:T(1024)S(1)}, f32[2304]{0:T(1024)S(1)}, u32[]{:S(2)}, u32[]{:S(2)}) %collective-permute-start.24) | collective-permute-done | bytes 9248 | tf_op jit(solution)/shard_map/ppermute | solution.py:22
  106.3 4.1 %collective-permute-done.25 = f32[2304]{0:T(1024)S(1)} collective-permute-done((f32[2304]{0:T(1024)S(1)}, f32[2304]{0:T(1024)S(1)}, u32[]{:S(2)}, u32[]{:S(2)}) %collective-permute-start.25) | collective-permute-done | bytes 9248 | tf_op jit(solution)/shard_map/ppermute | solution.py:22
  110.4 2.7 %collective-permute-start.28 = (f32[2304]{0:T(1024)S(1)}, f32[2304]{0:T(1024)S(1)}, u32[]{:S(2)}, u32[]{:S(2)}) collective-permute-start(f32[2304]{0:T(1024)S(1)} %add.117), channel_id=1, source_target_pairs={{0,6},{1,7},{2,4},{3,5},{4,2},{5,3},{6,0},{7,1},{8,14},{9,15},{10,... | collective-permute-start | bytes 27656 | tf_op jit(solution)/shard_map/ppermute | solution.py:22
  114.2 2.7 %collective-permute-start.26 = (f32[2304]{0:T(1024)S(1)}, f32[2304]{0:T(1024)S(1)}, u32[]{:S(2)}, u32[]{:S(2)}) collective-permute-start(f32[2304]{0:T(1024)S(1)} %add.117), channel_id=1, source_target_pairs={{0,2},{1,3},{2,0},{3,1},{4,6},{5,7},{6,4},{7,5},{8,10},{9,11},{10,... | collective-permute-start | bytes 27656 | tf_op jit(solution)/shard_map/ppermute | solution.py:22
  116.9 4.3 %collective-permute-done.27 = f32[2304]{0:T(1024)S(1)} collective-permute-done((f32[2304]{0:T(1024)S(1)}, f32[2304]{0:T(1024)S(1)}, u32[]{:S(2)}, u32[]{:S(2)}) %collective-permute-start.27) | collective-permute-done | bytes 9248 | tf_op jit(solution)/shard_map/ppermute | solution.py:22
  123.4 2.0 %collective-permute-start.30 = (f32[128]{0:T(128)S(1)}, f32[128]{0:T(128)S(1)}, u32[]{:S(2)}, u32[]{:S(2)}) collective-permute-start(f32[128]{0:T(128)S(1)} %get-tuple-element.104), channel_id=1, source_target_pairs={{0,128},{64,192},{128,0},{192,64},{1,129},{65,193},{129,1},{193,65... | collective-permute-start | bytes 1544 | tf_op jit(solution)/shard_map/ppermute | solution.py:22
  128.4 2.9 %collective-permute-start.32 = (f32[128]{0:T(128)S(1)}, f32[128]{0:T(128)S(1)}, u32[]{:S(2)}, u32[]{:S(2)}) collective-permute-start(f32[128]{0:T(128)S(1)} %add_add_fusion.2), channel_id=1, source_target_pairs={{0,32},{32,0},{1,33},{33,1},{2,34},{34,2},{3,35},{35,3},{4,36},{36... | collective-permute-start | bytes 1544 | tf_op jit(solution)/shard_map/ppermute | solution.py:22
  132.5 3.0 %collective-permute-done.32 = f32[128]{0:T(128)S(1)} collective-permute-done((f32[128]{0:T(128)S(1)}, f32[128]{0:T(128)S(1)}, u32[]{:S(2)}, u32[]{:S(2)}) %collective-permute-start.32) | collective-permute-done | bytes 544 | tf_op jit(solution)/shard_map/ppermute | solution.py:22
  138.7 1.9 %multiply_divide_fusion = f32[768,768]{1,0:T(8,128)} fusion(f32[768,768]{1,0:T(8,128)S(1)} %copy-done, f32[]{:T(128)S(6)} %max_shard_map.3, f32[]{:T(128)S(6)} %div.26, f32[768]{0:T(1024)S(1)} %get-tuple-element.105, f32[768]{0:T(1024)S(1)} %get-tuple-element.107), kind=kLoop, calls=%fused_computation | loop fusion | flops 2359296 | bytes 4724744 | tf_op jit(solution)/shard_map/div | solution.py:256
  (119 shorter events, 33.8 us)
Async XLA Ops:
  7.2 65.9 %all-gather.2.cloned.1.call-start = ((), (), s32[]{:S(2)}) async-start(), calls=%async_computation.2 | async-start | bytes 1769472 | tf_op jit(solution)/shard_map/all_gather | solution.py:192
  8.2 4.2 %collective-permute-start = (bf16[256,192]{1,0:T(8,128)(2,1)S(1)}, bf16[256,192]{1,0:T(8,128)(2,1)S(1)}, u32[]{:S(2)}, u32[]{:S(2)}) collective-permute-start(bf16[256,192]{1,0:T(8,128)(2,1)S(1)} %copy.17), channel_id=1, source_target_pairs={{0,16},{24,8},{8,0},{16,24},{1,17},{25,9},{9,1},{17,25},{2,18},{26... | collective-permute-start | bytes 294920 | tf_op jit(solution)/shard_map/ppermute | solution.py:181
  13.3 112.2 %reduce-scatter.2.cloned.1.call-start = ((), (), s32[]{:S(2)}) async-start(), calls=%async_computation.3 | async-start | bytes 3538944 | tf_op jit(solution)/shard_map/reduce_scatter | solution.py:227
  37.3 11.3 %collective-permute-start.3 = (bf16[8,32,768]{2,1,0:T(8,128)(2,1)S(1)}, bf16[8,32,768]{2,1,0:T(8,128)(2,1)S(1)}, u32[]{:S(2)}, u32[]{:S(2)}) collective-permute-start(bf16[8,32,768]{2,1,0:T(8,128)(2,1)S(1)} %bitcast.27), channel_id=1, source_target_pairs={{0,128},{64,192},{128,0},{192,64},{1,129},{65,193},{129,1},{193,65... | collective-permute-start | bytes 1179656 | tf_op jit(solution)/shard_map/ppermute | solution.py:26
  37.8 12.8 %collective-permute-start.2 = (bf16[8,32,768]{2,1,0:T(8,128)(2,1)S(1)}, bf16[8,32,768]{2,1,0:T(8,128)(2,1)S(1)}, u32[]{:S(2)}, u32[]{:S(2)}) collective-permute-start(bf16[8,32,768]{2,1,0:T(8,128)(2,1)S(1)} %bitcast.28), channel_id=1, source_target_pairs={{0,32},{32,0},{1,33},{33,1},{2,34},{34,2},{3,35},{35,3},{4,36},{36... | collective-permute-start | bytes 1179656 | tf_op jit(solution)/shard_map/ppermute | solution.py:22
  40.9 18.2 %collective-permute-start.4 = (bf16[8,32,768]{2,1,0:T(8,128)(2,1)S(1)}, bf16[8,32,768]{2,1,0:T(8,128)(2,1)S(1)}, u32[]{:S(2)}, u32[]{:S(2)}) collective-permute-start(bf16[8,32,768]{2,1,0:T(8,128)(2,1)S(1)} %bitcast.29), channel_id=1, source_target_pairs={{0,64},{64,128},{128,192},{192,0},{1,65},{65,129},{129,193},{193,1... | collective-permute-start | bytes 1179656 | tf_op jit(solution)/shard_map/ppermute | solution.py:26
  43.0 16.1 %collective-permute-start.5 = (bf16[8,32,768]{2,1,0:T(8,128)(2,1)S(1)}, bf16[8,32,768]{2,1,0:T(8,128)(2,1)S(1)}, u32[]{:S(2)}, u32[]{:S(2)}) collective-permute-start(bf16[8,32,768]{2,1,0:T(8,128)(2,1)S(1)} %bitcast.30), channel_id=1, source_target_pairs={{0,192},{64,0},{128,64},{192,128},{1,193},{65,1},{129,65},{193,129... | collective-permute-start | bytes 1179656 | tf_op jit(solution)/shard_map/ppermute | solution.py:26
  48.6 12.9 %collective-permute-start.6 = (bf16[8,32,768]{2,1,0:T(8,128)(2,1)S(1)}, bf16[8,32,768]{2,1,0:T(8,128)(2,1)S(1)}, u32[]{:S(2)}, u32[]{:S(2)}) collective-permute-start(bf16[8,32,768]{2,1,0:T(8,128)(2,1)S(1)} %collective-permute-done.3.refs_2_), channel_id=1, source_target_pairs={{0,32},{32,0},{1,33},{33,1},{2,34},{34,2},{3,35},{35,3},{4,36},{36... | collective-permute-start | bytes 1179656 | tf_op jit(solution)/shard_map/ppermute | solution.py:22
  50.6 16.9 %collective-permute-start.7 = (bf16[8,32,768]{2,1,0:T(8,128)(2,1)S(1)}, bf16[8,32,768]{2,1,0:T(8,128)(2,1)S(1)}, u32[]{:S(2)}, u32[]{:S(2)}) collective-permute-start(bf16[8,32,768]{2,1,0:T(8,128)(2,1)S(1)} %collective-permute-done.2.refs_1_), channel_id=1, source_target_pairs={{0,64},{64,128},{128,192},{192,0},{1,65},{65,129},{129,193},{193,1... | collective-permute-start | bytes 1179656 | tf_op jit(solution)/shard_map/ppermute | solution.py:26
  51.8 15.9 %collective-permute-start.8 = (bf16[8,32,768]{2,1,0:T(8,128)(2,1)S(1)}, bf16[8,32,768]{2,1,0:T(8,128)(2,1)S(1)}, u32[]{:S(2)}, u32[]{:S(2)}) collective-permute-start(bf16[8,32,768]{2,1,0:T(8,128)(2,1)S(1)} %collective-permute-done.2.refs_1_), channel_id=1, source_target_pairs={{0,192},{64,0},{128,64},{192,128},{1,193},{65,1},{129,65},{193,129... | collective-permute-start | bytes 1179656 | tf_op jit(solution)/shard_map/ppermute | solution.py:26
  59.1 8.9 %collective-permute-start.9 = (bf16[8,32,768]{2,1,0:T(8,128)(2,1)S(1)}, bf16[8,32,768]{2,1,0:T(8,128)(2,1)S(1)}, u32[]{:S(2)}, u32[]{:S(2)}) collective-permute-start(bf16[8,32,768]{2,1,0:T(8,128)(2,1)S(1)} %collective-permute-done.4.refs_0_.refs_3_), channel_id=1, source_target_pairs={{0,8},{8,0},{1,9},{9,1},{2,10},{10,2},{3,11},{11,3},{4,12},{12,4},... | collective-permute-start | bytes 1179656 | tf_op jit(solution)/shard_map/ppermute | solution.py:22
  61.4 6.8 %collective-permute-start.10 = (bf16[8,32,768]{2,1,0:T(8,128)(2,1)S(1)}, bf16[8,32,768]{2,1,0:T(8,128)(2,1)S(1)}, u32[]{:S(2)}, u32[]{:S(2)}) collective-permute-start(bf16[8,32,768]{2,1,0:T(8,128)(2,1)S(1)} %collective-permute-done.5.refs_1_.refs_4_), channel_id=1, source_target_pairs={{0,8},{8,0},{1,9},{9,1},{2,10},{10,2},{3,11},{11,3},{4,12},{12,4},... | collective-permute-start | bytes 1179656 | tf_op jit(solution)/shard_map/ppermute | solution.py:22
  61.5 7.1 %collective-permute-start.14 = (f32[8,32,384]{2,1,0:T(8,128)}, f32[8,32,384]{2,1,0:T(8,128)S(1)}, u32[]{:S(2)}, u32[]{:S(2)}) collective-permute-start(f32[8,32,384]{2,1,0:T(8,128)} %get-tuple-element.65), channel_id=1, source_target_pairs={{0,8},{8,0},{1,9},{9,1},{2,10},{10,2},{3,11},{11,3},{4,12},{12,4},... | collective-permute-start | bytes 1179656 | tf_op jit(solution)/shard_map/ppermute | solution.py:22
  73.1 6.8 %collective-permute-start.18 = (bf16[8,8,32,384]{3,2,1,0:T(8,128)(2,1)}, bf16[8,8,32,384]{3,2,1,0:T(8,128)(2,1)}, u32[]{:S(2)}, u32[]{:S(2)}) collective-permute-start(bf16[8,8,32,384]{3,2,1,0:T(8,128)(2,1)} %bitcast.33), channel_id=1, source_target_pairs={{0,8},{8,0},{1,9},{9,1},{2,10},{10,2},{3,11},{11,3},{4,12},{12,4},... | collective-permute-start | bytes 4718600 | tf_op jit(solution)/shard_map/ppermute | solution.py:22
  87.0 4.2 %collective-permute-start.21 = (f32[768]{0:T(1024)}, f32[768]{0:T(1024)S(1)}, u32[]{:S(2)}, u32[]{:S(2)}) collective-permute-start(f32[768]{0:T(1024)} %get-tuple-element.92), channel_id=1, source_target_pairs={{0,192},{64,128},{128,64},{192,0},{1,193},{65,129},{129,65},{193,1... | collective-permute-start | bytes 9224 | tf_op jit(solution)/shard_map/ppermute | solution.py:22
  87.5 5.3 %collective-permute-start.20 = (f32[768]{0:T(1024)}, f32[768]{0:T(1024)S(1)}, u32[]{:S(2)}, u32[]{:S(2)}) collective-permute-start(f32[768]{0:T(1024)} %get-tuple-element.92), channel_id=1, source_target_pairs={{0,128},{64,192},{128,0},{192,64},{1,129},{65,193},{129,1},{193,65... | collective-permute-start | bytes 9224 | tf_op jit(solution)/shard_map/ppermute | solution.py:22
  94.2 5.1 %collective-permute-start.22 = (f32[768]{0:T(1024)S(1)}, f32[768]{0:T(1024)S(1)}, u32[]{:S(2)}, u32[]{:S(2)}) collective-permute-start(f32[768]{0:T(1024)S(1)} %add_add_fusion.1), channel_id=1, source_target_pairs={{0,32},{32,0},{1,33},{33,1},{2,34},{34,2},{3,35},{35,3},{4,36},{36... | collective-permute-start | bytes 9224 | tf_op jit(solution)/shard_map/ppermute | solution.py:22
  110.4 6.5 %collective-permute-start.28 = (f32[2304]{0:T(1024)S(1)}, f32[2304]{0:T(1024)S(1)}, u32[]{:S(2)}, u32[]{:S(2)}) collective-permute-start(f32[2304]{0:T(1024)S(1)} %add.117), channel_id=1, source_target_pairs={{0,6},{1,7},{2,4},{3,5},{4,2},{5,3},{6,0},{7,1},{8,14},{9,15},{10,... | collective-permute-start | bytes 27656 | tf_op jit(solution)/shard_map/ppermute | solution.py:22
  113.1 8.0 %collective-permute-start.27 = (f32[2304]{0:T(1024)S(1)}, f32[2304]{0:T(1024)S(1)}, u32[]{:S(2)}, u32[]{:S(2)}) collective-permute-start(f32[2304]{0:T(1024)S(1)} %add.117), channel_id=1, source_target_pairs={{0,4},{1,5},{2,6},{3,7},{4,0},{5,1},{6,2},{7,3},{8,12},{9,13},{10,... | collective-permute-start | bytes 27656 | tf_op jit(solution)/shard_map/ppermute | solution.py:22
  114.2 7.0 %collective-permute-start.26 = (f32[2304]{0:T(1024)S(1)}, f32[2304]{0:T(1024)S(1)}, u32[]{:S(2)}, u32[]{:S(2)}) collective-permute-start(f32[2304]{0:T(1024)S(1)} %add.117), channel_id=1, source_target_pairs={{0,2},{1,3},{2,0},{3,1},{4,6},{5,7},{6,4},{7,5},{8,10},{9,11},{10,... | collective-permute-start | bytes 27656 | tf_op jit(solution)/shard_map/ppermute | solution.py:22
  122.5 5.7 %collective-permute-start.31 = (f32[128]{0:T(128)S(1)}, f32[128]{0:T(128)S(1)}, u32[]{:S(2)}, u32[]{:S(2)}) collective-permute-start(f32[128]{0:T(128)S(1)} %get-tuple-element.104), channel_id=1, source_target_pairs={{0,192},{64,128},{128,64},{192,0},{1,193},{65,129},{129,65},{193,1... | collective-permute-start | bytes 1544 | tf_op jit(solution)/shard_map/ppermute | solution.py:22
  123.4 5.0 %collective-permute-start.30 = (f32[128]{0:T(128)S(1)}, f32[128]{0:T(128)S(1)}, u32[]{:S(2)}, u32[]{:S(2)}) collective-permute-start(f32[128]{0:T(128)S(1)} %get-tuple-element.104), channel_id=1, source_target_pairs={{0,128},{64,192},{128,0},{192,64},{1,129},{65,193},{129,1},{193,65... | collective-permute-start | bytes 1544 | tf_op jit(solution)/shard_map/ppermute | solution.py:22
  126.7 8.8 %collective-permute-start.33 = (f32[8,32,192]{2,1,0:T(8,128)S(1)}, f32[8,32,192]{2,1,0:T(8,128)S(1)}, u32[]{:S(2)}, u32[]{:S(2)}) collective-permute-start(f32[8,32,192]{2,1,0:T(8,128)S(1)} %slice_select_fusion), channel_id=1, source_target_pairs={{0,16},{16,0},{1,17},{17,1},{2,18},{18,2},{3,19},{19,3},{4,20},{20... | collective-permute-start | bytes 589832 | tf_op jit(solution)/shard_map/ppermute | solution.py:22
  128.4 7.1 %collective-permute-start.32 = (f32[128]{0:T(128)S(1)}, f32[128]{0:T(128)S(1)}, u32[]{:S(2)}, u32[]{:S(2)}) collective-permute-start(f32[128]{0:T(128)S(1)} %add_add_fusion.2), channel_id=1, source_target_pairs={{0,32},{32,0},{1,33},{33,1},{2,34},{34,2},{3,35},{35,3},{4,36},{36... | collective-permute-start | bytes 1544 | tf_op jit(solution)/shard_map/ppermute | solution.py:22
  (32 other events, 253.3 us)
Sparse Core Ops, SparseCore 0:
  13.4 46.8 all-gather.1
  80.0 45.4 reduce-scatter.1

commit v9 on v8

--- a/solution.py
+++ b/solution.py
@@ -41,28 +41,33 @@
     return value
 
 
-def weight_kernel(core_ref, weight_ref, keep_ref, send_ref):
-    weight = weight_ref[...]
-    even = jnp.concatenate([weight[:, :192], weight[:, HALF : HALF + 192]], axis=1)
-    odd = jnp.concatenate([weight[:, 192:HALF], weight[:, HALF + 192 :]], axis=1)
+def weight_kernel(core_ref, weight_ref, other_ref, keep_ref, send_ref, other_keep_ref):
+    def columns(weight, odd):
+        start = 192 if odd else 0
+        return jnp.concatenate([weight[:, start : start + 192], weight[:, HALF + start : HALF + start + 192]], axis=1)
+
+    weight, other = weight_ref[...], other_ref[...]
     first = core_ref[0] == 0
+    even, odd = columns(weight, False), columns(weight, True)
     keep_ref[...] = jnp.where(first, even, odd)
     send_ref[...] = jnp.where(first, odd, even)
-
-
-def weight_call(halves, weight):
-    spec = pl.BlockSpec((256, HALF), lambda s, halves: (s, 0))
+    other_keep_ref[...] = jnp.where(first, columns(other, False), columns(other, True))
+
+
+def weight_call(halves, weight, other):
+    whole = pl.BlockSpec((256, 768), lambda s, halves: (s, 0))
+    half = pl.BlockSpec((256, HALF), lambda s, halves: (s, 0))
     return pl.pallas_call(
         weight_kernel,
         grid_spec=pltpu.PrefetchScalarGridSpec(
             num_scalar_prefetch=1,
             grid=(3,),
-            in_specs=[pl.BlockSpec((256, 768), lambda s, halves: (s, 0))],
-            out_specs=[spec, spec],
-        ),
-        out_shape=[jax.ShapeDtypeStruct((768, HALF), jnp.bfloat16)] * 2,
+            in_specs=[whole, whole],
+            out_specs=[half] * 3,
+        ),
+        out_shape=[jax.ShapeDtypeStruct((768, HALF), jnp.bfloat16)] * 3,
         compiler_params=pltpu.CompilerParams(vmem_limit_bytes=60 * 1024 * 1024),
-    )(halves, weight)
+    )(halves, weight, other)
 
 
 VECTORS = pl.BlockSpec(memory_space=pltpu.VMEM)
@@ -189,20 +194,23 @@
     )
     act_half = with_layout_constraint(act_half, Layout((0, 1)))
     act_half, cotangent = lax.optimization_barrier((act_half, cotangent))
+    other_weight = exchange(weight, "core", 2, 1)
     act_own = lax.all_gather(act_half, "z", axis=0, tiled=True)
     act_own = with_layout_constraint(act_own, Layout((0, 1))).reshape(8, 8, 32, HALF)
 
     own_cot = lax.all_to_all(cotangent, "z", 1, 0, tiled=True).reshape(8, 32, 768)
-    own_cot, weight = lax.optimization_barrier((own_cot, weight))
+    own_cot, weight, other_weight = lax.optimization_barrier((own_cot, weight, other_weight))
     right, left, far = (x + 3) % 4, (x + 1) % 4, (x + 2) % 4
     columns = [x, x, far, right, left, far, right, left]
     sides = [yh, 1 - yh, yh, yh, yh, 1 - yh, 1 - yh, 1 - yh]
     rows = jnp.stack([c * 2 + side for c, side in zip(columns, sides)]).astype(jnp.int32)
     halves = jnp.stack([core, 1 - core]).astype(jnp.int32)
-    keep, send = weight_call(halves, weight)
+    keep, send, other_keep = weight_call(halves, weight, other_weight)
 
     other_cot = exchange(own_cot, "yh", 2, 1)
-    other_cot, keep, send, rows, halves = lax.optimization_barrier((other_cot, keep, send, rows, halves))
+    other_cot, keep, send, other_keep, rows, halves = lax.optimization_barrier(
+        (other_cot, keep, send, other_keep, rows, halves)
+    )
     right_cot = shift(own_cot, "x", 4, 1)
     left_cot = shift(own_cot, "x", 4, -1)
     far_cot = shift(own_cot, "x", 4, 2)
@@ -216,9 +224,8 @@
     second[0], second[1], *sent = lax.optimization_barrier((second[0], second[1], *sent))
     received = [exchange(part, "core", 2, 1) for part in sent]
     others = [exchange(cot, "core", 2, 1) for cot in second]
-    other_keep = exchange(send, "core", 2, 1)
-    *arrived, other_keep, kept, act_own = lax.optimization_barrier(
-        (*first, *second, *others, *received, other_keep, kept, act_own)
+    *arrived, kept, act_own = lax.optimization_barrier(
+        (*first, *second, *others, *received, kept, act_own)
     )
     first, second, others, received = arrived[:FIRST], arrived[FIRST:8], arrived[8:13], arrived[13:]
     act_recv = exchange(act_own, "core", 2, 1)
@@ -240,7 +247,8 @@
     others = [exchange(part, "x", 4, bit) for bit in (1, 2, 3)]
     part = part + others[0]
     part, summed = lax.optimization_barrier((part, summed))
-    part = total(part + others[1] + others[2], "yh", 2)
+    part = part + others[1] + others[2]
+    last = exchange(part, "yh", 2, 1)
 
     summed = summed.reshape(8, 32, HALF)
     low, high = summed[:, :, :192], summed[:, :, 192:]
@@ -248,9 +256,9 @@
     theirs = jnp.where(yl == 0, high, low)
     mine = (mine + exchange(theirs, "yl", 2, 1)).astype(jnp.bfloat16)
     input_grad = mine.reshape(256, 192)
-    part, input_grad = lax.optimization_barrier((part, input_grad))
-
-    squares_total = jnp.sum(part) * row_mean
+    last, input_grad = lax.optimization_barrier((last, input_grad))
+
+    squares_total = jnp.sum(part + last) * row_mean
     root_mean = jnp.sqrt(squares_total / (FF * D))
     unclipped = gradient * lax.rsqrt(row_stats[:, None] * col_stats[None, :] / row_mean)
     update = unclipped / jnp.maximum(1.0, root_mean)

time: 148 us -> 150 us (1.014)
  starting transfers between devices: 37.7 us -> 39.2 us
    ppermute x27, waiting for transfers between devices: 24.8 us -> 28.8 us  [exchange(): return lax.ppermute(value, axis, [(i, i ^ bit) for i in range(size)])]
    ppermute x5, waiting for transfers between devices: 9.02 us -> 6.14 us  [shift(): lax.ppermute(value, axis, [(i, (i + step) % size) for i in range(size)])]
  transfers between devices with their start and end apart: 36 -> 36, of which waited for: 17 -> 14; matrix products, arithmetic and copies ran while one was open for 5% -> 6% of each run, Pallas kernels for 15% -> 15%
where the time goes in v9:
time: 150 us; the launch traced here: 149 us
  starting transfers between devices  39.2 us (26%)
  waiting for transfers between devices  35.4 us (24%)
  blocking collectives  22.9 us (15%)
  Pallas kernels  21.9 us (15%)
  between operations  15.6 us (10%)
  other arithmetic  9.69 us (6%)
  local copies, waits for them, and re-layouts  4.18 us (3%)
    ppermute x27, starting transfers between devices, exchange(): return lax.ppermute(value, axis, [(i, i ^ bit) for i in range(size)])  32 us
    ppermute x27, waiting for transfers between devices, exchange(): return lax.ppermute(value, axis, [(i, i ^ bit) for i in range(size)])  28.8 us
    all_to_all x1, blocking collectives, body(): lax.all_to_all(cotangent, 'z', 1, 0, tiled=True).reshape(8, 32, 768)  22.9 us
    pallas_call x1, Pallas kernels, gradient_call(): pl.pallas_call(gradient_kernel, in_specs=[SCALARS] * 2 + [VECTORS] * 10,...  7.04 us
    pallas_call x1, Pallas kernels, second_call(): pl.pallas_call(second_kernel, grid_spec=pltpu.PrefetchScalarGridSpec(num_...  6.57 us
    ppermute x5, waiting for transfers between devices, shift(): lax.ppermute(value, axis, [(i, (i + step) % size) for i in range(size)])  6.14 us
    ppermute x5, starting transfers between devices, shift(): lax.ppermute(value, axis, [(i, (i + step) % size) for i in range(size)])  4.83 us
    pallas_call x1, Pallas kernels, weight_call(): pl.pallas_call(weight_kernel, grid_spec=pltpu.PrefetchScalarGridSpec(num_...  4.46 us
  transfers between devices with their start and end apart: 36, of which 14 were waited for; matrix products, arithmetic and copies ran while one was open for 6% of the time, Pallas kernels for 15%

profile of v9, /device:TPU:4, one launch (start us, length us, event | category | flops | bytes accessed | tf_op | source)
XLA Modules:
  0.0 148.9 jit_solution(9945054684976400952)
XLA Ops:
  8.2 1.7 %collective-permute-start = (bf16[256,192]{1,0:T(8,128)(2,1)S(1)}, bf16[256,192]{1,0:T(8,128)(2,1)S(1)}, u32[]{:S(2)}, u32[]{:S(2)}) collective-permute-start(bf16[256,192]{1,0:T(8,128)(2,1)S(1)} %copy.17), channel_id=1, source_target_pairs={{0,16},{24,8},{8,0},{16,24},{1,17},{25,9},{9,1},{17,25},{2,18},{26... | collective-permute-start | bytes 294920 | tf_op jit(solution)/shard_map/ppermute | solution.py:186
  14.4 22.9 %all_to_all.16 = bf16[32,8,768]{2,0,1:T(8,128)(2,1)S(1)} all-to-all(bf16[32,8,768]{2,0,1:T(8,128)(2,1)S(1)} %bitcast.24), channel_id=1, replica_groups=mesh['x'=4,'yh'=2,'yl'=2,'core'=2,'z'=8] {'z'}, dimensions={1} | all-to-all | bytes 786432 | tf_op jit(solution)/shard_map/all_to_all | solution.py:201
  37.9 2.5 %collective-permute-start.3 = (bf16[8,32,768]{2,1,0:T(8,128)(2,1)S(1)}, bf16[8,32,768]{2,1,0:T(8,128)(2,1)}, u32[]{:S(2)}, u32[]{:S(2)}) collective-permute-start(bf16[8,32,768]{2,1,0:T(8,128)(2,1)S(1)} %bitcast.28), channel_id=1, source_target_pairs={{0,32},{32,0},{1,33},{33,1},{2,34},{34,2},{3,35},{35,3},{4,36},{36... | collective-permute-start | bytes 1179656 | tf_op jit(solution)/shard_map/ppermute | solution.py:22
  40.4 2.1 %collective-permute-start.5 = (bf16[8,32,768]{2,1,0:T(8,128)(2,1)S(1)}, bf16[8,32,768]{2,1,0:T(8,128)(2,1)S(1)}, u32[]{:S(2)}, u32[]{:S(2)}) collective-permute-start(bf16[8,32,768]{2,1,0:T(8,128)(2,1)S(1)} %bitcast.29), channel_id=1, source_target_pairs={{0,64},{64,128},{128,192},{192,0},{1,65},{65,129},{129,193},{193,1... | collective-permute-start | bytes 1179656 | tf_op jit(solution)/shard_map/ppermute | solution.py:26
  42.5 6.1 %collective-permute-done.4.refs_2_ = bf16[8,32,768]{2,1,0:T(8,128)(2,1)S(1)} collective-permute-done((bf16[8,32,768]{2,1,0:T(8,128)(2,1)S(1)}, bf16[8,32,768]{2,1,0:T(8,128)(2,1)S(1)}, u32[]{:S(2)}, u32[]{:S(2)}) %collective-permute-start.4) | collective-permute-done | bytes 393248 | tf_op jit(solution)/shard_map/ppermute | solution.py:26
  48.7 2.0 %collective-permute-start.7 = (bf16[8,32,768]{2,1,0:T(8,128)(2,1)S(1)}, bf16[8,32,768]{2,1,0:T(8,128)(2,1)S(1)}, u32[]{:S(2)}, u32[]{:S(2)}) collective-permute-start(bf16[8,32,768]{2,1,0:T(8,128)(2,1)S(1)} %collective-permute-done.4.refs_2_), channel_id=1, source_target_pairs={{0,32},{32,0},{1,33},{33,1},{2,34},{34,2},{3,35},{35,3},{4,36},{36... | collective-permute-start | bytes 1179656 | tf_op jit(solution)/shard_map/ppermute | solution.py:22
  51.9 4.5 %shard_map.68 = (bf16[768,384]{1,0:T(8,128)(2,1)}, bf16[768,384]{1,0:T(8,128)(2,1)}, bf16[768,384]{1,0:T(8,128)(2,1)}) custom-call(s32[2]{0:T(128)} %pad_add_fusion.core_ref.halves_ref, bf16[768,768]{1,0:T(8,128)(2,1)} %weight_ref, bf16[768,768]{1,0:T(8,128)(2,1)} %copy-done.1), custom_call_target="tpu_custom_call" | custom-call | tf_op jit(solution)/shard_map/pallas_call | solution.py:60
  58.5 3.9 %shard_map.69 = (f32[8,3,32,384]{3,2,1,0:T(8,128)}, f32[8,32,384]{2,1,0:T(8,128)}, f32[8,32,384]{2,1,0:T(8,128)}, f32[8,32,384]{2,1,0:T(8,128)}) custom-call(bf16[8,32,768]{2,1,0:T(8,128)(2,1)} %bitcast.31, bf16[8,32,768]{2,1,0:T(8,128)(2,1)} %collective-permute-done.3.refs_1_, bf16[8,32,768]{2,1,0:T(8,128)(2,1)} %copy-done.18, ...), custom_call_target="tpu_custom_call" | custom-call | flops 905969664 | bytes 4194304 | tf_op jit(solution)/shard_map/pallas_call | solution.py:106
  62.3 4.9 %collective-permute-start.10 = (bf16[8,32,768]{2,1,0:T(8,128)(2,1)S(1)}, bf16[8,32,768]{2,1,0:T(8,128)(2,1)S(1)}, u32[]{:S(2)}, u32[]{:S(2)}) collective-permute-start(bf16[8,32,768]{2,1,0:T(8,128)(2,1)S(1)} %collective-permute-done.5.refs_0_.refs_3_), channel_id=1, source_target_pairs={{0,8},{8,0},{1,9},{9,1},{2,10},{10,2},{3,11},{11,3},{4,12},{12,4},... | collective-permute-start | bytes 1179656 | tf_op jit(solution)/shard_map/ppermute | solution.py:22
  73.8 6.6 %shard_map.70 = f32[8,8,32,384]{3,2,1,0:T(8,128)} custom-call(s32[8]{0:T(128)} %stack.47.rows_ref, bf16[8,32,768]{2,1,0:T(8,128)(2,1)} %copy-done.3, bf16[8,32,768]{2,1,0:T(8,128)(2,1)} %copy-done.4, bf16[8,32,768]{2,1,0:T(8,128)(2,1)} %copy-done.5, bf16[8,32,768]{2,1,0:T(8,128)(2,1)} %copy-done.6, bf16[8,32,768]{2,1,0:T(8,128)(2,1)} %copy-done.7, ...), custom_call_target="tpu_custom_call" | custom-call | flops 1509949440 | bytes 8388608 | tf_op jit(solution)/shard_map/pallas_call | solution.py:124
  80.5 7.0 %shard_map.71 = (f32[768,768]{1,0:T(8,128)}, f32[768]{0:T(1024)}, f32[768]{0:T(1024)}) custom-call(s32[8]{0:T(128)} %stack.47.rows_ref, s32[2]{0:T(128)} %pad_add_fusion.core_ref.halves_ref, bf16[8,32,768]{2,1,0:T(8,128)(2,1)} %bitcast.32, bf16[8,32,768]{2,1,0:T(8,128)(2,1)} %collective-permute-done.3.refs_1_, bf16[8,32,768]{2,1,0:T(8,128)(2,1)} %copy-done.18, ...), custom_call_target="tpu_custom_call" | custom-call | flops 2415919104 | bytes 9437184 | tf_op jit(solution)/shard_map/pallas_call | solution.py:166
  88.5 2.9 %collective-permute-start.20 = (f32[768]{0:T(1024)}, f32[768]{0:T(1024)S(1)}, u32[]{:S(2)}, u32[]{:S(2)}) collective-permute-start(f32[768]{0:T(1024)} %get-tuple-element.96), channel_id=1, source_target_pairs={{0,128},{64,192},{128,0},{192,64},{1,129},{65,193},{129,1},{193,65... | collective-permute-start | bytes 9224 | tf_op jit(solution)/shard_map/ppermute | solution.py:22
  91.7 2.1 %collective-permute-done.20 = f32[768]{0:T(1024)S(1)} collective-permute-done((f32[768]{0:T(1024)}, f32[768]{0:T(1024)S(1)}, u32[]{:S(2)}, u32[]{:S(2)}) %collective-permute-start.20) | collective-permute-done | bytes 3104 | tf_op jit(solution)/shard_map/ppermute | solution.py:22
  95.9 1.6 %collective-permute-start.22 = (f32[768]{0:T(1024)S(1)}, f32[768]{0:T(1024)S(1)}, u32[]{:S(2)}, u32[]{:S(2)}) collective-permute-start(f32[768]{0:T(1024)S(1)} %add_add_fusion.1), channel_id=1, source_target_pairs={{0,32},{32,0},{1,33},{33,1},{2,34},{34,2},{3,35},{35,3},{4,36},{36... | collective-permute-start | bytes 9224 | tf_op jit(solution)/shard_map/ppermute | solution.py:22
  97.5 3.5 %collective-permute-done.22 = f32[768]{0:T(1024)S(1)} collective-permute-done((f32[768]{0:T(1024)S(1)}, f32[768]{0:T(1024)S(1)}, u32[]{:S(2)}, u32[]{:S(2)}) %collective-permute-start.22) | collective-permute-done | bytes 3104 | tf_op jit(solution)/shard_map/ppermute | solution.py:22
  101.0 2.0 %multiply_reduce_fusion = f32[768]{0:T(1024)S(1)} fusion(f32[768,768]{1,0:T(8,128)} %get-tuple-element.95, f32[768]{0:T(1024)S(1)} %get-tuple-element.110), kind=kLoop, calls=%fused_computation.1 | loop fusion | flops 1768704 | bytes 2365440 | tf_op jit(solution)/shard_map/reduce_sum | solution.py:240
  104.3 3.7 %collective-permute-done.24 = f32[2304]{0:T(1024)S(1)} collective-permute-done((f32[2304]{0:T(1024)S(1)}, f32[2304]{0:T(1024)S(1)}, u32[]{:S(2)}, u32[]{:S(2)}) %collective-permute-start.24) | collective-permute-done | bytes 9248 | tf_op jit(solution)/shard_map/ppermute | solution.py:22
  108.0 4.0 %collective-permute-done.25 = f32[2304]{0:T(1024)S(1)} collective-permute-done((f32[2304]{0:T(1024)S(1)}, f32[2304]{0:T(1024)S(1)}, u32[]{:S(2)}, u32[]{:S(2)}) %collective-permute-start.25) | collective-permute-done | bytes 9248 | tf_op jit(solution)/shard_map/ppermute | solution.py:22
  112.0 4.6 %collective-permute-start.28 = (f32[2304]{0:T(1024)S(1)}, f32[2304]{0:T(1024)S(1)}, u32[]{:S(2)}, u32[]{:S(2)}) collective-permute-start(f32[2304]{0:T(1024)S(1)} %add.117), channel_id=1, source_target_pairs={{0,6},{1,7},{2,4},{3,5},{4,2},{5,3},{6,0},{7,1},{8,14},{9,15},{10,... | collective-permute-start | bytes 27656 | tf_op jit(solution)/shard_map/ppermute | solution.py:22
  116.6 2.4 %collective-permute-start.26 = (f32[2304]{0:T(1024)S(1)}, f32[2304]{0:T(1024)S(1)}, u32[]{:S(2)}, u32[]{:S(2)}) collective-permute-start(f32[2304]{0:T(1024)S(1)} %add.117), channel_id=1, source_target_pairs={{0,2},{1,3},{2,0},{3,1},{4,6},{5,7},{6,4},{7,5},{8,10},{9,11},{10,... | collective-permute-start | bytes 27656 | tf_op jit(solution)/shard_map/ppermute | solution.py:22
  118.9 5.4 %collective-permute-done.27 = f32[2304]{0:T(1024)S(1)} collective-permute-done((f32[2304]{0:T(1024)S(1)}, f32[2304]{0:T(1024)S(1)}, u32[]{:S(2)}, u32[]{:S(2)}) %collective-permute-start.27) | collective-permute-done | bytes 9248 | tf_op jit(solution)/shard_map/ppermute | solution.py:22
  124.8 2.3 %collective-permute-start.29 = (f32[128]{0:T(128)S(1)}, f32[128]{0:T(128)S(1)}, u32[]{:S(2)}, u32[]{:S(2)}) collective-permute-start(f32[128]{0:T(128)S(1)} %get-tuple-element.108), channel_id=1, source_target_pairs={{0,64},{64,0},{128,192},{192,128},{1,65},{65,1},{129,193},{193,129... | collective-permute-start | bytes 1544 | tf_op jit(solution)/shard_map/ppermute | solution.py:22
  133.0 3.9 %collective-permute-done.33 = f32[8,32,192]{2,1,0:T(8,128)S(1)} collective-permute-done((f32[8,32,192]{2,1,0:T(8,128)S(1)}, f32[8,32,192]{2,1,0:T(8,128)S(1)}, u32[]{:S(2)}, u32[]{:S(2)}) %collective-permute-start.33) | collective-permute-done | bytes 196640 | tf_op jit(solution)/shard_map/ppermute | solution.py:22
  140.2 1.9 %multiply_divide_fusion = f32[768,768]{1,0:T(8,128)} fusion(f32[768,768]{1,0:T(8,128)S(1)} %copy-done, f32[]{:T(128)S(6)} %max_shard_map.3, f32[]{:T(128)S(6)} %div.26, f32[768]{0:T(1024)S(1)} %get-tuple-element.109, f32[768]{0:T(1024)S(1)} %get-tuple-element.111), kind=kLoop, calls=%fused_computation | loop fusion | flops 2359296 | bytes 4724744 | tf_op jit(solution)/shard_map/div | solution.py:264
  (116 shorter events, 29.0 us)
Async XLA Ops:
  7.2 66.2 %all-gather.2.cloned.1.call-start = ((), (), s32[]{:S(2)}) async-start(), calls=%async_computation.2 | async-start | bytes 1769472 | tf_op jit(solution)/shard_map/all_gather | solution.py:198
  8.2 4.2 %collective-permute-start = (bf16[256,192]{1,0:T(8,128)(2,1)S(1)}, bf16[256,192]{1,0:T(8,128)(2,1)S(1)}, u32[]{:S(2)}, u32[]{:S(2)}) collective-permute-start(bf16[256,192]{1,0:T(8,128)(2,1)S(1)} %copy.17), channel_id=1, source_target_pairs={{0,16},{24,8},{8,0},{16,24},{1,17},{25,9},{9,1},{17,25},{2,18},{26... | collective-permute-start | bytes 294920 | tf_op jit(solution)/shard_map/ppermute | solution.py:186
  10.5 26.7 %collective-permute-start.2 = (bf16[768,768]{1,0:T(8,128)(2,1)}, bf16[768,768]{1,0:T(8,128)(2,1)S(1)}, u32[]{:S(2)}, u32[]{:S(2)}) collective-permute-start(bf16[768,768]{1,0:T(8,128)(2,1)} %weight_ref), channel_id=1, source_target_pairs={{0,8},{8,0},{1,9},{9,1},{2,10},{10,2},{3,11},{11,3},{4,12},{12,4},... | collective-permute-start | bytes 3538952 | tf_op jit(solution)/shard_map/ppermute | solution.py:22
  13.3 116.0 %reduce-scatter.2.cloned.1.call-start = ((), (), s32[]{:S(2)}) async-start(), calls=%async_computation.3 | async-start | bytes 3538944 | tf_op jit(solution)/shard_map/reduce_scatter | solution.py:234
  37.3 11.4 %collective-permute-start.4 = (bf16[8,32,768]{2,1,0:T(8,128)(2,1)S(1)}, bf16[8,32,768]{2,1,0:T(8,128)(2,1)S(1)}, u32[]{:S(2)}, u32[]{:S(2)}) collective-permute-start(bf16[8,32,768]{2,1,0:T(8,128)(2,1)S(1)} %bitcast.27), channel_id=1, source_target_pairs={{0,128},{64,192},{128,0},{192,64},{1,129},{65,193},{129,1},{193,65... | collective-permute-start | bytes 1179656 | tf_op jit(solution)/shard_map/ppermute | solution.py:26
  37.9 18.5 %collective-permute-start.3 = (bf16[8,32,768]{2,1,0:T(8,128)(2,1)S(1)}, bf16[8,32,768]{2,1,0:T(8,128)(2,1)}, u32[]{:S(2)}, u32[]{:S(2)}) collective-permute-start(bf16[8,32,768]{2,1,0:T(8,128)(2,1)S(1)} %bitcast.28), channel_id=1, source_target_pairs={{0,32},{32,0},{1,33},{33,1},{2,34},{34,2},{3,35},{35,3},{4,36},{36... | collective-permute-start | bytes 1179656 | tf_op jit(solution)/shard_map/ppermute | solution.py:22
  40.4 21.9 %collective-permute-start.5 = (bf16[8,32,768]{2,1,0:T(8,128)(2,1)S(1)}, bf16[8,32,768]{2,1,0:T(8,128)(2,1)S(1)}, u32[]{:S(2)}, u32[]{:S(2)}) collective-permute-start(bf16[8,32,768]{2,1,0:T(8,128)(2,1)S(1)} %bitcast.29), channel_id=1, source_target_pairs={{0,64},{64,128},{128,192},{192,0},{1,65},{65,129},{129,193},{193,1... | collective-permute-start | bytes 1179656 | tf_op jit(solution)/shard_map/ppermute | solution.py:26
  42.5 19.8 %collective-permute-start.6 = (bf16[8,32,768]{2,1,0:T(8,128)(2,1)S(1)}, bf16[8,32,768]{2,1,0:T(8,128)(2,1)S(1)}, u32[]{:S(2)}, u32[]{:S(2)}) collective-permute-start(bf16[8,32,768]{2,1,0:T(8,128)(2,1)S(1)} %bitcast.30), channel_id=1, source_target_pairs={{0,192},{64,0},{128,64},{192,128},{1,193},{65,1},{129,65},{193,129... | collective-permute-start | bytes 1179656 | tf_op jit(solution)/shard_map/ppermute | solution.py:26
  48.7 18.6 %collective-permute-start.7 = (bf16[8,32,768]{2,1,0:T(8,128)(2,1)S(1)}, bf16[8,32,768]{2,1,0:T(8,128)(2,1)S(1)}, u32[]{:S(2)}, u32[]{:S(2)}) collective-permute-start(bf16[8,32,768]{2,1,0:T(8,128)(2,1)S(1)} %collective-permute-done.4.refs_2_), channel_id=1, source_target_pairs={{0,32},{32,0},{1,33},{33,1},{2,34},{34,2},{3,35},{35,3},{4,36},{36... | collective-permute-start | bytes 1179656 | tf_op jit(solution)/shard_map/ppermute | solution.py:22
  56.4 11.3 %collective-permute-start.8 = (bf16[8,32,768]{2,1,0:T(8,128)(2,1)}, bf16[8,32,768]{2,1,0:T(8,128)(2,1)S(1)}, u32[]{:S(2)}, u32[]{:S(2)}) collective-permute-start(bf16[8,32,768]{2,1,0:T(8,128)(2,1)} %collective-permute-done.3.refs_1_), channel_id=1, source_target_pairs={{0,64},{64,128},{128,192},{192,0},{1,65},{65,129},{129,193},{193,1... | collective-permute-start | bytes 1179656 | tf_op jit(solution)/shard_map/ppermute | solution.py:26
  57.6 11.0 %collective-permute-start.9 = (bf16[8,32,768]{2,1,0:T(8,128)(2,1)}, bf16[8,32,768]{2,1,0:T(8,128)(2,1)S(1)}, u32[]{:S(2)}, u32[]{:S(2)}) collective-permute-start(bf16[8,32,768]{2,1,0:T(8,128)(2,1)} %collective-permute-done.3.refs_1_), channel_id=1, source_target_pairs={{0,192},{64,0},{128,64},{192,128},{1,193},{65,1},{129,65},{193,129... | collective-permute-start | bytes 1179656 | tf_op jit(solution)/shard_map/ppermute | solution.py:26
  62.3 7.3 %collective-permute-start.10 = (bf16[8,32,768]{2,1,0:T(8,128)(2,1)S(1)}, bf16[8,32,768]{2,1,0:T(8,128)(2,1)S(1)}, u32[]{:S(2)}, u32[]{:S(2)}) collective-permute-start(bf16[8,32,768]{2,1,0:T(8,128)(2,1)S(1)} %collective-permute-done.5.refs_0_.refs_3_), channel_id=1, source_target_pairs={{0,8},{8,0},{1,9},{9,1},{2,10},{10,2},{3,11},{11,3},{4,12},{12,4},... | collective-permute-start | bytes 1179656 | tf_op jit(solution)/shard_map/ppermute | solution.py:22
  73.4 7.0 %collective-permute-start.18 = (bf16[8,8,32,384]{3,2,1,0:T(8,128)(2,1)}, bf16[8,8,32,384]{3,2,1,0:T(8,128)(2,1)}, u32[]{:S(2)}, u32[]{:S(2)}) collective-permute-start(bf16[8,8,32,384]{3,2,1,0:T(8,128)(2,1)} %bitcast.33), channel_id=1, source_target_pairs={{0,8},{8,0},{1,9},{9,1},{2,10},{10,2},{3,11},{11,3},{4,12},{12,4},... | collective-permute-start | bytes 4718600 | tf_op jit(solution)/shard_map/ppermute | solution.py:22
  87.5 4.2 %collective-permute-start.21 = (f32[768]{0:T(1024)}, f32[768]{0:T(1024)S(1)}, u32[]{:S(2)}, u32[]{:S(2)}) collective-permute-start(f32[768]{0:T(1024)} %get-tuple-element.96), channel_id=1, source_target_pairs={{0,192},{64,128},{128,64},{192,0},{1,193},{65,129},{129,65},{193,1... | collective-permute-start | bytes 9224 | tf_op jit(solution)/shard_map/ppermute | solution.py:22
  88.5 5.3 %collective-permute-start.20 = (f32[768]{0:T(1024)}, f32[768]{0:T(1024)S(1)}, u32[]{:S(2)}, u32[]{:S(2)}) collective-permute-start(f32[768]{0:T(1024)} %get-tuple-element.96), channel_id=1, source_target_pairs={{0,128},{64,192},{128,0},{192,64},{1,129},{65,193},{129,1},{193,65... | collective-permute-start | bytes 9224 | tf_op jit(solution)/shard_map/ppermute | solution.py:22
  95.9 5.1 %collective-permute-start.22 = (f32[768]{0:T(1024)S(1)}, f32[768]{0:T(1024)S(1)}, u32[]{:S(2)}, u32[]{:S(2)}) collective-permute-start(f32[768]{0:T(1024)S(1)} %add_add_fusion.1), channel_id=1, source_target_pairs={{0,32},{32,0},{1,33},{33,1},{2,34},{34,2},{3,35},{35,3},{4,36},{36... | collective-permute-start | bytes 9224 | tf_op jit(solution)/shard_map/ppermute | solution.py:22
  112.0 6.9 %collective-permute-start.28 = (f32[2304]{0:T(1024)S(1)}, f32[2304]{0:T(1024)S(1)}, u32[]{:S(2)}, u32[]{:S(2)}) collective-permute-start(f32[2304]{0:T(1024)S(1)} %add.117), channel_id=1, source_target_pairs={{0,6},{1,7},{2,4},{3,5},{4,2},{5,3},{6,0},{7,1},{8,14},{9,15},{10,... | collective-permute-start | bytes 27656 | tf_op jit(solution)/shard_map/ppermute | solution.py:22
  116.6 7.8 %collective-permute-start.27 = (f32[2304]{0:T(1024)S(1)}, f32[2304]{0:T(1024)S(1)}, u32[]{:S(2)}, u32[]{:S(2)}) collective-permute-start(f32[2304]{0:T(1024)S(1)} %add.117), channel_id=1, source_target_pairs={{0,4},{1,5},{2,6},{3,7},{4,0},{5,1},{6,2},{7,3},{8,12},{9,13},{10,... | collective-permute-start | bytes 27656 | tf_op jit(solution)/shard_map/ppermute | solution.py:22
  116.6 7.8 %collective-permute-start.26 = (f32[2304]{0:T(1024)S(1)}, f32[2304]{0:T(1024)S(1)}, u32[]{:S(2)}, u32[]{:S(2)}) collective-permute-start(f32[2304]{0:T(1024)S(1)} %add.117), channel_id=1, source_target_pairs={{0,2},{1,3},{2,0},{3,1},{4,6},{5,7},{6,4},{7,5},{8,10},{9,11},{10,... | collective-permute-start | bytes 27656 | tf_op jit(solution)/shard_map/ppermute | solution.py:22
  124.4 6.4 %collective-permute-start.31 = (f32[128]{0:T(128)S(1)}, f32[128]{0:T(128)S(1)}, u32[]{:S(2)}, u32[]{:S(2)}) collective-permute-start(f32[128]{0:T(128)S(1)} %get-tuple-element.108), channel_id=1, source_target_pairs={{0,192},{64,128},{128,64},{192,0},{1,193},{65,129},{129,65},{193,1... | collective-permute-start | bytes 1544 | tf_op jit(solution)/shard_map/ppermute | solution.py:22
  124.8 4.4 %collective-permute-start.29 = (f32[128]{0:T(128)S(1)}, f32[128]{0:T(128)S(1)}, u32[]{:S(2)}, u32[]{:S(2)}) collective-permute-start(f32[128]{0:T(128)S(1)} %get-tuple-element.108), channel_id=1, source_target_pairs={{0,64},{64,0},{128,192},{192,128},{1,65},{65,1},{129,193},{193,129... | collective-permute-start | bytes 1544 | tf_op jit(solution)/shard_map/ppermute | solution.py:22
  127.1 5.0 %collective-permute-start.30 = (f32[128]{0:T(128)S(1)}, f32[128]{0:T(128)S(1)}, u32[]{:S(2)}, u32[]{:S(2)}) collective-permute-start(f32[128]{0:T(128)S(1)} %get-tuple-element.108), channel_id=1, source_target_pairs={{0,128},{64,192},{128,0},{192,64},{1,129},{65,193},{129,1},{193,65... | collective-permute-start | bytes 1544 | tf_op jit(solution)/shard_map/ppermute | solution.py:22
  130.5 6.5 %collective-permute-start.33 = (f32[8,32,192]{2,1,0:T(8,128)S(1)}, f32[8,32,192]{2,1,0:T(8,128)S(1)}, u32[]{:S(2)}, u32[]{:S(2)}) collective-permute-start(f32[8,32,192]{2,1,0:T(8,128)S(1)} %slice_select_fusion), channel_id=1, source_target_pairs={{0,16},{16,0},{1,17},{17,1},{2,18},{18,2},{3,19},{19,3},{4,20},{20... | collective-permute-start | bytes 589832 | tf_op jit(solution)/shard_map/ppermute | solution.py:22
  132.2 5.9 %collective-permute-start.32 = (f32[128]{0:T(128)S(1)}, f32[128]{0:T(128)S(1)}, u32[]{:S(2)}, u32[]{:S(2)}) collective-permute-start(f32[128]{0:T(128)S(1)} %add_add_fusion.2), channel_id=1, source_target_pairs={{0,32},{32,0},{1,33},{33,1},{2,34},{34,2},{3,35},{35,3},{4,36},{36... | collective-permute-start | bytes 1544 | tf_op jit(solution)/shard_map/ppermute | solution.py:22
  (31 other events, 264.6 us)
Sparse Core Ops, SparseCore 0:
  13.4 46.9 all-gather.1
  80.6 45.3 reduce-scatter.1

commit v10 on v8

--- a/solution.py
+++ b/solution.py
@@ -188,12 +188,12 @@
         jnp.concatenate([opposite, same], axis=1),
     )
     act_half = with_layout_constraint(act_half, Layout((0, 1)))
-    act_half, cotangent = lax.optimization_barrier((act_half, cotangent))
+    blocks = cotangent.reshape(32, 8, 768).transpose(1, 0, 2)
+    act_half, blocks, weight = lax.optimization_barrier((act_half, blocks, weight))
     act_own = lax.all_gather(act_half, "z", axis=0, tiled=True)
     act_own = with_layout_constraint(act_own, Layout((0, 1))).reshape(8, 8, 32, HALF)
 
-    own_cot = lax.all_to_all(cotangent, "z", 1, 0, tiled=True).reshape(8, 32, 768)
-    own_cot, weight = lax.optimization_barrier((own_cot, weight))
+    own_cot = lax.all_to_all(blocks, "z", 0, 0, tiled=True)
     right, left, far = (x + 3) % 4, (x + 1) % 4, (x + 2) % 4
     columns = [x, x, far, right, left, far, right, left]
     sides = [yh, 1 - yh, yh, yh, yh, 1 - yh, 1 - yh, 1 - yh]
@@ -201,8 +201,11 @@
     halves = jnp.stack([core, 1 - core]).astype(jnp.int32)
     keep, send = weight_call(halves, weight)
 
+    other_keep = exchange(send, "core", 2, 1)
+    own_cot, keep, send, other_keep, rows, halves = lax.optimization_barrier(
+        (own_cot, keep, send, other_keep, rows, halves)
+    )
     other_cot = exchange(own_cot, "yh", 2, 1)
-    other_cot, keep, send, rows, halves = lax.optimization_barrier((other_cot, keep, send, rows, halves))
     right_cot = shift(own_cot, "x", 4, 1)
     left_cot = shift(own_cot, "x", 4, -1)
     far_cot = shift(own_cot, "x", 4, 2)
@@ -213,10 +216,11 @@
     second = [right_cot, left_cot, other_far, other_right, other_left]
 
     kept, *sent = first_call(first, keep, send)
-    second[0], second[1], *sent = lax.optimization_barrier((second[0], second[1], *sent))
+    second[0], second[1], second[2], *sent = lax.optimization_barrier(
+        (second[0], second[1], second[2], *sent)
+    )
     received = [exchange(part, "core", 2, 1) for part in sent]
     others = [exchange(cot, "core", 2, 1) for cot in second]
-    other_keep = exchange(send, "core", 2, 1)
     *arrived, other_keep, kept, act_own = lax.optimization_barrier(
         (*first, *second, *others, *received, other_keep, kept, act_own)
     )

time: 148 us -> 146 us (0.986)
  blocking collectives: 22.9 us -> 0 us
  starting transfers between devices: 37.7 us -> 48.2 us
  waiting for transfers between devices: 35.8 us -> 44.6 us
  local copies, waits for them, and re-layouts: 4.25 us -> 5.79 us
    all_to_all x1 -> x0, blocking collectives: 22.9 us -> none  [body(): lax.all_to_all(cotangent, 'z', 1, 0, tiled=True).reshape(8, 32, 768)]
    all_to_all x0 -> x1, starting transfers between devices: none -> 8.48 us  [body(): own_cot = lax.all_to_all(blocks, 'z', 0, 0, tiled=True)]
    ppermute x5, waiting for transfers between devices: 9.02 us -> 14.6 us  [shift(): lax.ppermute(value, axis, [(i, (i + step) % size) for i in range(size)])]
    all_to_all x0 -> x1, waiting for transfers between devices: none -> 5.52 us  [body(): own_cot = lax.all_to_all(blocks, 'z', 0, 0, tiled=True)]
    ppermute x27, starting transfers between devices: 30.6 us -> 32.6 us  [exchange(): return lax.ppermute(value, axis, [(i, i ^ bit) for i in range(size)])]
    ppermute x1, waiting for transfers between devices: 1.85 us -> 0.07 us  [body(): lax.ppermute(activations, ('yl', 'core'), [(0, 2), (3, 1), (1, 0), (2, 3)])]
    reshape x0 -> x1, local copies, waits for them, and re-layouts: none -> 1.77 us  [body(): blocks = cotangent.reshape(32, 8, 768).transpose(1, 0, 2)]
    unnamed x42 -> x40, local copies, waits for them, and re-layouts: 2.54 us -> 3.42 us
  transfers between devices with their start and end apart: 36 -> 37, of which waited for: 17 -> 17; matrix products, arithmetic and copies ran while one was open for 5% -> 5% of each run, Pallas kernels for 15% -> 15%
where the time goes in v10:
time: 146 us; the launch traced here: 145 us
  starting transfers between devices  48.2 us (33%)
  waiting for transfers between devices  44.6 us (31%)
  Pallas kernels  21.5 us (15%)
  between operations  15.6 us (11%)
  other arithmetic  9.75 us (7%)
  local copies, waits for them, and re-layouts  5.79 us (4%)
    ppermute x27, starting transfers between devices, exchange(): return lax.ppermute(value, axis, [(i, i ^ bit) for i in range(size)])  32.6 us
    ppermute x27, waiting for transfers between devices, exchange(): return lax.ppermute(value, axis, [(i, i ^ bit) for i in range(size)])  24.3 us
    ppermute x5, waiting for transfers between devices, shift(): lax.ppermute(value, axis, [(i, (i + step) % size) for i in range(size)])  14.6 us
    all_to_all x1, starting transfers between devices, body(): own_cot = lax.all_to_all(blocks, 'z', 0, 0, tiled=True)  8.48 us
    pallas_call x1, Pallas kernels, gradient_call(): pl.pallas_call(gradient_kernel, in_specs=[SCALARS] * 2 + [VECTORS] * 10,...  7.06 us
    pallas_call x1, Pallas kernels, second_call(): pl.pallas_call(second_kernel, grid_spec=pltpu.PrefetchScalarGridSpec(num_...  6.56 us
    all_to_all x1, waiting for transfers between devices, body(): own_cot = lax.all_to_all(blocks, 'z', 0, 0, tiled=True)  5.52 us
    ppermute x5, starting transfers between devices, shift(): lax.ppermute(value, axis, [(i, (i + step) % size) for i in range(size)])  4.7 us
  transfers between devices with their start and end apart: 37, of which 17 were waited for; matrix products, arithmetic and copies ran while one was open for 5% of the time, Pallas kernels for 15%

profile of v10, /device:TPU:4, one launch (start us, length us, event | category | flops | bytes accessed | tf_op | source)
XLA Modules:
  0.0 145.4 jit_solution(1089461547332013859)
XLA Ops:
  13.3 8.5 %all-to-all-start = ((bf16[8,32,768]{2,1,0:T(8,128)(2,1)}), bf16[8,32,768]{2,1,0:T(8,128)(2,1)S(1)}, u32[]{:S(2)}, u32[]{:S(2)}) async-start(bf16[8,32,768]{2,1,0:T(8,128)(2,1)} %bitcast.23), calls=%async_computation | async-start | bytes 786432 | tf_op jit(solution)/shard_map/all_to_all | solution.py:196
  22.5 4.0 %shard_map.68 = (bf16[768,384]{1,0:T(8,128)(2,1)}, bf16[768,384]{1,0:T(8,128)(2,1)}) custom-call(s32[2]{0:T(128)} %pad_add_fusion.core_ref.halves_ref, bf16[768,768]{1,0:T(8,128)(2,1)} %weight_ref), custom_call_target="tpu_custom_call" | custom-call | tf_op jit(solution)/shard_map/pallas_call | solution.py:55
  26.5 2.4 %collective-permute-start.2 = (bf16[768,384]{1,0:T(8,128)(2,1)}, bf16[768,384]{1,0:T(8,128)(2,1)S(1)}, u32[]{:S(2)}, u32[]{:S(2)}) collective-permute-start(bf16[768,384]{1,0:T(8,128)(2,1)} %get-tuple-element.59.refs_4_), channel_id=1, source_target_pairs={{0,8},{8,0},{1,9},{9,1},{2,10},{10,2},{3,11},{11,3},{4,12},{12,4},... | collective-permute-start | bytes 1769480 | tf_op jit(solution)/shard_map/ppermute | solution.py:22
  30.7 5.5 %all-to-all-done.refs_0_ = bf16[8,32,768]{2,1,0:T(8,128)(2,1)S(1)} async-done(((bf16[8,32,768]{2,1,0:T(8,128)(2,1)}), bf16[8,32,768]{2,1,0:T(8,128)(2,1)S(1)}, u32[]{:S(2)}, u32[]{:S(2)}) %all-to-all-start) | async-done | bytes 393248 | tf_op jit(solution)/shard_map/all_to_all | solution.py:196
  36.7 2.2 %collective-permute-start.3 = (bf16[8,32,768]{2,1,0:T(8,128)(2,1)S(1)}, bf16[8,32,768]{2,1,0:T(8,128)(2,1)}, u32[]{:S(2)}, u32[]{:S(2)}) collective-permute-start(bf16[8,32,768]{2,1,0:T(8,128)(2,1)S(1)} %all-to-all-done.refs_0_), channel_id=1, source_target_pairs={{0,32},{32,0},{1,33},{33,1},{2,34},{34,2},{3,35},{35,3},{4,36},{36... | collective-permute-start | bytes 1179656 | tf_op jit(solution)/shard_map/ppermute | solution.py:22
  39.0 2.1 %collective-permute-start.5 = (bf16[8,32,768]{2,1,0:T(8,128)(2,1)S(1)}, bf16[8,32,768]{2,1,0:T(8,128)(2,1)S(1)}, u32[]{:S(2)}, u32[]{:S(2)}) collective-permute-start(bf16[8,32,768]{2,1,0:T(8,128)(2,1)S(1)} %all-to-all-done.refs_0_), channel_id=1, source_target_pairs={{0,64},{64,128},{128,192},{192,0},{1,65},{65,129},{129,193},{193,1... | collective-permute-start | bytes 1179656 | tf_op jit(solution)/shard_map/ppermute | solution.py:26
  41.1 6.4 %collective-permute-done.4.refs_2_ = bf16[8,32,768]{2,1,0:T(8,128)(2,1)S(1)} collective-permute-done((bf16[8,32,768]{2,1,0:T(8,128)(2,1)S(1)}, bf16[8,32,768]{2,1,0:T(8,128)(2,1)S(1)}, u32[]{:S(2)}, u32[]{:S(2)}) %collective-permute-start.4) | collective-permute-done | bytes 393248 | tf_op jit(solution)/shard_map/ppermute | solution.py:26
  51.1 3.9 %shard_map.69 = (f32[8,3,32,384]{3,2,1,0:T(8,128)}, f32[8,32,384]{2,1,0:T(8,128)}, f32[8,32,384]{2,1,0:T(8,128)}, f32[8,32,384]{2,1,0:T(8,128)}) custom-call(bf16[8,32,768]{2,1,0:T(8,128)(2,1)} %copy-done.2, bf16[8,32,768]{2,1,0:T(8,128)(2,1)} %collective-permute-done.3.refs_1_, bf16[8,32,768]{2,1,0:T(8,128)(2,1)} %copy-done.18, ...), custom_call_target="tpu_custom_call" | custom-call | flops 905969664 | bytes 4194304 | tf_op jit(solution)/shard_map/pallas_call | solution.py:101
  55.0 3.0 %collective-permute-done.5.refs_0_.refs_3_ = bf16[8,32,768]{2,1,0:T(8,128)(2,1)S(1)} collective-permute-done((bf16[8,32,768]{2,1,0:T(8,128)(2,1)S(1)}, bf16[8,32,768]{2,1,0:T(8,128)(2,1)S(1)}, u32[]{:S(2)}, u32[]{:S(2)}) %collective-permute-start.5) | collective-permute-done | bytes 393248 | tf_op jit(solution)/shard_map/ppermute | solution.py:26
  58.1 2.8 %collective-permute-start.10 = (bf16[8,32,768]{2,1,0:T(8,128)(2,1)S(1)}, bf16[8,32,768]{2,1,0:T(8,128)(2,1)S(1)}, u32[]{:S(2)}, u32[]{:S(2)}) collective-permute-start(bf16[8,32,768]{2,1,0:T(8,128)(2,1)S(1)} %collective-permute-done.5.refs_0_.refs_3_), channel_id=1, source_target_pairs={{0,8},{8,0},{1,9},{9,1},{2,10},{10,2},{3,11},{11,3},{4,12},{12,4},... | collective-permute-start | bytes 1179656 | tf_op jit(solution)/shard_map/ppermute | solution.py:22
  61.3 5.1 %collective-permute-done.8.refs_3_.refs_6_ = bf16[8,32,768]{2,1,0:T(8,128)(2,1)S(1)} collective-permute-done((bf16[8,32,768]{2,1,0:T(8,128)(2,1)}, bf16[8,32,768]{2,1,0:T(8,128)(2,1)S(1)}, u32[]{:S(2)}, u32[]{:S(2)}) %collective-permute-start.8) | collective-permute-done | bytes 393248 | tf_op jit(solution)/shard_map/ppermute | solution.py:26
  72.3 6.6 %shard_map.70 = f32[8,8,32,384]{3,2,1,0:T(8,128)} custom-call(s32[8]{0:T(128)} %stack.47.rows_ref, bf16[8,32,768]{2,1,0:T(8,128)(2,1)} %copy-done.3, bf16[8,32,768]{2,1,0:T(8,128)(2,1)} %copy-done.4, bf16[8,32,768]{2,1,0:T(8,128)(2,1)} %copy-done.5, bf16[8,32,768]{2,1,0:T(8,128)(2,1)} %copy-done.6, bf16[8,32,768]{2,1,0:T(8,128)(2,1)} %copy-done.7, ...), custom_call_target="tpu_custom_call" | custom-call | flops 1509949440 | bytes 8388608 | tf_op jit(solution)/shard_map/pallas_call | solution.py:119
  78.9 7.1 %shard_map.71 = (f32[768,768]{1,0:T(8,128)}, f32[768]{0:T(1024)}, f32[768]{0:T(1024)}) custom-call(s32[8]{0:T(128)} %stack.47.rows_ref, s32[2]{0:T(128)} %pad_add_fusion.core_ref.halves_ref, bf16[8,32,768]{2,1,0:T(8,128)(2,1)} %copy-done.2, bf16[8,32,768]{2,1,0:T(8,128)(2,1)} %collective-permute-done.3.refs_1_, bf16[8,32,768]{2,1,0:T(8,128)(2,1)} %copy-done.18, ...), custom_call_target="tpu_custom_call" | custom-call | flops 2415919104 | bytes 9437184 | tf_op jit(solution)/shard_map/pallas_call | solution.py:161
  86.5 2.1 %collective-permute-start.20 = (f32[768]{0:T(1024)}, f32[768]{0:T(1024)S(1)}, u32[]{:S(2)}, u32[]{:S(2)}) collective-permute-start(f32[768]{0:T(1024)} %get-tuple-element.94), channel_id=1, source_target_pairs={{0,128},{64,192},{128,0},{192,64},{1,129},{65,193},{129,1},{193,65... | collective-permute-start | bytes 9224 | tf_op jit(solution)/shard_map/ppermute | solution.py:22
  93.0 2.3 %collective-permute-start.22 = (f32[768]{0:T(1024)S(1)}, f32[768]{0:T(1024)S(1)}, u32[]{:S(2)}, u32[]{:S(2)}) collective-permute-start(f32[768]{0:T(1024)S(1)} %add_add_fusion.1), channel_id=1, source_target_pairs={{0,32},{32,0},{1,33},{33,1},{2,34},{34,2},{3,35},{35,3},{4,36},{36... | collective-permute-start | bytes 9224 | tf_op jit(solution)/shard_map/ppermute | solution.py:22
  95.4 2.8 %collective-permute-done.22 = f32[768]{0:T(1024)S(1)} collective-permute-done((f32[768]{0:T(1024)S(1)}, f32[768]{0:T(1024)S(1)}, u32[]{:S(2)}, u32[]{:S(2)}) %collective-permute-start.22) | collective-permute-done | bytes 3104 | tf_op jit(solution)/shard_map/ppermute | solution.py:22
  101.5 3.7 %collective-permute-done.24 = f32[2304]{0:T(1024)S(1)} collective-permute-done((f32[2304]{0:T(1024)S(1)}, f32[2304]{0:T(1024)S(1)}, u32[]{:S(2)}, u32[]{:S(2)}) %collective-permute-start.24) | collective-permute-done | bytes 9248 | tf_op jit(solution)/shard_map/ppermute | solution.py:22
  105.2 3.8 %collective-permute-done.25 = f32[2304]{0:T(1024)S(1)} collective-permute-done((f32[2304]{0:T(1024)S(1)}, f32[2304]{0:T(1024)S(1)}, u32[]{:S(2)}, u32[]{:S(2)}) %collective-permute-start.25) | collective-permute-done | bytes 9248 | tf_op jit(solution)/shard_map/ppermute | solution.py:22
  109.0 2.2 %collective-permute-start.28 = (f32[2304]{0:T(1024)S(1)}, f32[2304]{0:T(1024)S(1)}, u32[]{:S(2)}, u32[]{:S(2)}) collective-permute-start(f32[2304]{0:T(1024)S(1)} %add.117), channel_id=1, source_target_pairs={{0,6},{1,7},{2,4},{3,5},{4,2},{5,3},{6,0},{7,1},{8,14},{9,15},{10,... | collective-permute-start | bytes 27656 | tf_op jit(solution)/shard_map/ppermute | solution.py:22
  112.9 2.6 %collective-permute-start.26 = (f32[2304]{0:T(1024)S(1)}, f32[2304]{0:T(1024)S(1)}, u32[]{:S(2)}, u32[]{:S(2)}) collective-permute-start(f32[2304]{0:T(1024)S(1)} %add.117), channel_id=1, source_target_pairs={{0,2},{1,3},{2,0},{3,1},{4,6},{5,7},{6,4},{7,5},{8,10},{9,11},{10,... | collective-permute-start | bytes 27656 | tf_op jit(solution)/shard_map/ppermute | solution.py:22
  115.5 3.8 %collective-permute-done.27 = f32[2304]{0:T(1024)S(1)} collective-permute-done((f32[2304]{0:T(1024)S(1)}, f32[2304]{0:T(1024)S(1)}, u32[]{:S(2)}, u32[]{:S(2)}) %collective-permute-start.27) | collective-permute-done | bytes 9248 | tf_op jit(solution)/shard_map/ppermute | solution.py:22
  121.4 2.2 %collective-permute-start.30 = (f32[128]{0:T(128)S(1)}, f32[128]{0:T(128)S(1)}, u32[]{:S(2)}, u32[]{:S(2)}) collective-permute-start(f32[128]{0:T(128)S(1)} %get-tuple-element.106), channel_id=1, source_target_pairs={{0,128},{64,192},{128,0},{192,64},{1,129},{65,193},{129,1},{193,65... | collective-permute-start | bytes 1544 | tf_op jit(solution)/shard_map/ppermute | solution.py:22
  126.6 2.7 %collective-permute-start.32 = (f32[128]{0:T(128)S(1)}, f32[128]{0:T(128)S(1)}, u32[]{:S(2)}, u32[]{:S(2)}) collective-permute-start(f32[128]{0:T(128)S(1)} %add_add_fusion.2), channel_id=1, source_target_pairs={{0,32},{32,0},{1,33},{33,1},{2,34},{34,2},{3,35},{35,3},{4,36},{36... | collective-permute-start | bytes 1544 | tf_op jit(solution)/shard_map/ppermute | solution.py:22
  130.5 3.0 %collective-permute-done.32 = f32[128]{0:T(128)S(1)} collective-permute-done((f32[128]{0:T(128)S(1)}, f32[128]{0:T(128)S(1)}, u32[]{:S(2)}, u32[]{:S(2)}) %collective-permute-start.32) | collective-permute-done | bytes 544 | tf_op jit(solution)/shard_map/ppermute | solution.py:22
  (118 shorter events, 39.2 us)
Async XLA Ops:
  7.2 64.9 %all-gather.2.cloned.1.call-start = ((), (), s32[]{:S(2)}) async-start(), calls=%async_computation.2 | async-start | bytes 1769472 | tf_op jit(solution)/shard_map/all_gather | solution.py:193
  13.3 22.9 %all-to-all-start = ((bf16[8,32,768]{2,1,0:T(8,128)(2,1)}), bf16[8,32,768]{2,1,0:T(8,128)(2,1)S(1)}, u32[]{:S(2)}, u32[]{:S(2)}) async-start(bf16[8,32,768]{2,1,0:T(8,128)(2,1)} %bitcast.23), calls=%async_computation | async-start | bytes 786432 | tf_op jit(solution)/shard_map/all_to_all | solution.py:196
  21.8 101.9 %reduce-scatter.2.cloned.1.call-start = ((), (), s32[]{:S(2)}) async-start(), calls=%async_computation.3 | async-start | bytes 3538944 | tf_op jit(solution)/shard_map/reduce_scatter | solution.py:231
  36.2 11.3 %collective-permute-start.4 = (bf16[8,32,768]{2,1,0:T(8,128)(2,1)S(1)}, bf16[8,32,768]{2,1,0:T(8,128)(2,1)S(1)}, u32[]{:S(2)}, u32[]{:S(2)}) collective-permute-start(bf16[8,32,768]{2,1,0:T(8,128)(2,1)S(1)} %all-to-all-done.refs_0_), channel_id=1, source_target_pairs={{0,128},{64,192},{128,0},{192,64},{1,129},{65,193},{129,1},{193,65... | collective-permute-start | bytes 1179656 | tf_op jit(solution)/shard_map/ppermute | solution.py:26
  36.7 12.3 %collective-permute-start.3 = (bf16[8,32,768]{2,1,0:T(8,128)(2,1)S(1)}, bf16[8,32,768]{2,1,0:T(8,128)(2,1)}, u32[]{:S(2)}, u32[]{:S(2)}) collective-permute-start(bf16[8,32,768]{2,1,0:T(8,128)(2,1)S(1)} %all-to-all-done.refs_0_), channel_id=1, source_target_pairs={{0,32},{32,0},{1,33},{33,1},{2,34},{34,2},{3,35},{35,3},{4,36},{36... | collective-permute-start | bytes 1179656 | tf_op jit(solution)/shard_map/ppermute | solution.py:22
  39.0 19.1 %collective-permute-start.5 = (bf16[8,32,768]{2,1,0:T(8,128)(2,1)S(1)}, bf16[8,32,768]{2,1,0:T(8,128)(2,1)S(1)}, u32[]{:S(2)}, u32[]{:S(2)}) collective-permute-start(bf16[8,32,768]{2,1,0:T(8,128)(2,1)S(1)} %all-to-all-done.refs_0_), channel_id=1, source_target_pairs={{0,64},{64,128},{128,192},{192,0},{1,65},{65,129},{129,193},{193,1... | collective-permute-start | bytes 1179656 | tf_op jit(solution)/shard_map/ppermute | solution.py:26
  41.1 17.0 %collective-permute-start.6 = (bf16[8,32,768]{2,1,0:T(8,128)(2,1)S(1)}, bf16[8,32,768]{2,1,0:T(8,128)(2,1)S(1)}, u32[]{:S(2)}, u32[]{:S(2)}) collective-permute-start(bf16[8,32,768]{2,1,0:T(8,128)(2,1)S(1)} %all-to-all-done.refs_0_), channel_id=1, source_target_pairs={{0,192},{64,0},{128,64},{192,128},{1,193},{65,1},{129,65},{193,129... | collective-permute-start | bytes 1179656 | tf_op jit(solution)/shard_map/ppermute | solution.py:26
  47.5 10.5 %collective-permute-start.7 = (bf16[8,32,768]{2,1,0:T(8,128)(2,1)S(1)}, bf16[8,32,768]{2,1,0:T(8,128)(2,1)S(1)}, u32[]{:S(2)}, u32[]{:S(2)}) collective-permute-start(bf16[8,32,768]{2,1,0:T(8,128)(2,1)S(1)} %collective-permute-done.4.refs_2_), channel_id=1, source_target_pairs={{0,32},{32,0},{1,33},{33,1},{2,34},{34,2},{3,35},{35,3},{4,36},{36... | collective-permute-start | bytes 1179656 | tf_op jit(solution)/shard_map/ppermute | solution.py:22
  49.1 17.4 %collective-permute-start.8 = (bf16[8,32,768]{2,1,0:T(8,128)(2,1)}, bf16[8,32,768]{2,1,0:T(8,128)(2,1)S(1)}, u32[]{:S(2)}, u32[]{:S(2)}) collective-permute-start(bf16[8,32,768]{2,1,0:T(8,128)(2,1)} %collective-permute-done.3.refs_1_), channel_id=1, source_target_pairs={{0,64},{64,128},{128,192},{192,0},{1,65},{65,129},{129,193},{193,1... | collective-permute-start | bytes 1179656 | tf_op jit(solution)/shard_map/ppermute | solution.py:26
  50.4 16.2 %collective-permute-start.9 = (bf16[8,32,768]{2,1,0:T(8,128)(2,1)}, bf16[8,32,768]{2,1,0:T(8,128)(2,1)S(1)}, u32[]{:S(2)}, u32[]{:S(2)}) collective-permute-start(bf16[8,32,768]{2,1,0:T(8,128)(2,1)} %collective-permute-done.3.refs_1_), channel_id=1, source_target_pairs={{0,192},{64,0},{128,64},{192,128},{1,193},{65,1},{129,65},{193,129... | collective-permute-start | bytes 1179656 | tf_op jit(solution)/shard_map/ppermute | solution.py:26
  58.1 8.9 %collective-permute-start.10 = (bf16[8,32,768]{2,1,0:T(8,128)(2,1)S(1)}, bf16[8,32,768]{2,1,0:T(8,128)(2,1)S(1)}, u32[]{:S(2)}, u32[]{:S(2)}) collective-permute-start(bf16[8,32,768]{2,1,0:T(8,128)(2,1)S(1)} %collective-permute-done.5.refs_0_.refs_3_), channel_id=1, source_target_pairs={{0,8},{8,0},{1,9},{9,1},{2,10},{10,2},{3,11},{11,3},{4,12},{12,4},... | collective-permute-start | bytes 1179656 | tf_op jit(solution)/shard_map/ppermute | solution.py:22
  60.8 6.3 %collective-permute-start.11 = (bf16[8,32,768]{2,1,0:T(8,128)(2,1)S(1)}, bf16[8,32,768]{2,1,0:T(8,128)(2,1)S(1)}, u32[]{:S(2)}, u32[]{:S(2)}) collective-permute-start(bf16[8,32,768]{2,1,0:T(8,128)(2,1)S(1)} %collective-permute-done.6.refs_1_.refs_4_), channel_id=1, source_target_pairs={{0,8},{8,0},{1,9},{9,1},{2,10},{10,2},{3,11},{11,3},{4,12},{12,4},... | collective-permute-start | bytes 1179656 | tf_op jit(solution)/shard_map/ppermute | solution.py:22
  60.8 6.7 %collective-permute-start.12 = (bf16[8,32,768]{2,1,0:T(8,128)(2,1)S(1)}, bf16[8,32,768]{2,1,0:T(8,128)(2,1)S(1)}, u32[]{:S(2)}, u32[]{:S(2)}) collective-permute-start(bf16[8,32,768]{2,1,0:T(8,128)(2,1)S(1)} %collective-permute-done.7.refs_2_.refs_5_), channel_id=1, source_target_pairs={{0,8},{8,0},{1,9},{9,1},{2,10},{10,2},{3,11},{11,3},{4,12},{12,4},... | collective-permute-start | bytes 1179656 | tf_op jit(solution)/shard_map/ppermute | solution.py:22
  66.6 4.6 %collective-permute-start.16 = (f32[8,32,384]{2,1,0:T(8,128)}, f32[8,32,384]{2,1,0:T(8,128)S(1)}, u32[]{:S(2)}, u32[]{:S(2)}) collective-permute-start(f32[8,32,384]{2,1,0:T(8,128)} %get-tuple-element.67), channel_id=1, source_target_pairs={{0,8},{8,0},{1,9},{9,1},{2,10},{10,2},{3,11},{11,3},{4,12},{12,4},... | collective-permute-start | bytes 1179656 | tf_op jit(solution)/shard_map/ppermute | solution.py:22
  72.1 6.8 %collective-permute-start.18 = (bf16[8,8,32,384]{3,2,1,0:T(8,128)(2,1)}, bf16[8,8,32,384]{3,2,1,0:T(8,128)(2,1)}, u32[]{:S(2)}, u32[]{:S(2)}) collective-permute-start(bf16[8,8,32,384]{3,2,1,0:T(8,128)(2,1)} %bitcast.28), channel_id=1, source_target_pairs={{0,8},{8,0},{1,9},{9,1},{2,10},{10,2},{3,11},{11,3},{4,12},{12,4},... | collective-permute-start | bytes 4718600 | tf_op jit(solution)/shard_map/ppermute | solution.py:22
  86.5 5.3 %collective-permute-start.20 = (f32[768]{0:T(1024)}, f32[768]{0:T(1024)S(1)}, u32[]{:S(2)}, u32[]{:S(2)}) collective-permute-start(f32[768]{0:T(1024)} %get-tuple-element.94), channel_id=1, source_target_pairs={{0,128},{64,192},{128,0},{192,64},{1,129},{65,193},{129,1},{193,65... | collective-permute-start | bytes 9224 | tf_op jit(solution)/shard_map/ppermute | solution.py:22
  93.0 5.1 %collective-permute-start.22 = (f32[768]{0:T(1024)S(1)}, f32[768]{0:T(1024)S(1)}, u32[]{:S(2)}, u32[]{:S(2)}) collective-permute-start(f32[768]{0:T(1024)S(1)} %add_add_fusion.1), channel_id=1, source_target_pairs={{0,32},{32,0},{1,33},{33,1},{2,34},{34,2},{3,35},{35,3},{4,36},{36... | collective-permute-start | bytes 9224 | tf_op jit(solution)/shard_map/ppermute | solution.py:22
  109.0 6.5 %collective-permute-start.28 = (f32[2304]{0:T(1024)S(1)}, f32[2304]{0:T(1024)S(1)}, u32[]{:S(2)}, u32[]{:S(2)}) collective-permute-start(f32[2304]{0:T(1024)S(1)} %add.117), channel_id=1, source_target_pairs={{0,6},{1,7},{2,4},{3,5},{4,2},{5,3},{6,0},{7,1},{8,14},{9,15},{10,... | collective-permute-start | bytes 27656 | tf_op jit(solution)/shard_map/ppermute | solution.py:22
  111.3 8.0 %collective-permute-start.27 = (f32[2304]{0:T(1024)S(1)}, f32[2304]{0:T(1024)S(1)}, u32[]{:S(2)}, u32[]{:S(2)}) collective-permute-start(f32[2304]{0:T(1024)S(1)} %add.117), channel_id=1, source_target_pairs={{0,4},{1,5},{2,6},{3,7},{4,0},{5,1},{6,2},{7,3},{8,12},{9,13},{10,... | collective-permute-start | bytes 27656 | tf_op jit(solution)/shard_map/ppermute | solution.py:22
  112.9 6.4 %collective-permute-start.26 = (f32[2304]{0:T(1024)S(1)}, f32[2304]{0:T(1024)S(1)}, u32[]{:S(2)}, u32[]{:S(2)}) collective-permute-start(f32[2304]{0:T(1024)S(1)} %add.117), channel_id=1, source_target_pairs={{0,2},{1,3},{2,0},{3,1},{4,6},{5,7},{6,4},{7,5},{8,10},{9,11},{10,... | collective-permute-start | bytes 27656 | tf_op jit(solution)/shard_map/ppermute | solution.py:22
  120.6 6.0 %collective-permute-start.31 = (f32[128]{0:T(128)S(1)}, f32[128]{0:T(128)S(1)}, u32[]{:S(2)}, u32[]{:S(2)}) collective-permute-start(f32[128]{0:T(128)S(1)} %get-tuple-element.106), channel_id=1, source_target_pairs={{0,192},{64,128},{128,64},{192,0},{1,193},{65,129},{129,65},{193,1... | collective-permute-start | bytes 1544 | tf_op jit(solution)/shard_map/ppermute | solution.py:22
  121.4 5.2 %collective-permute-start.30 = (f32[128]{0:T(128)S(1)}, f32[128]{0:T(128)S(1)}, u32[]{:S(2)}, u32[]{:S(2)}) collective-permute-start(f32[128]{0:T(128)S(1)} %get-tuple-element.106), channel_id=1, source_target_pairs={{0,128},{64,192},{128,0},{192,64},{1,129},{65,193},{129,1},{193,65... | collective-permute-start | bytes 1544 | tf_op jit(solution)/shard_map/ppermute | solution.py:22
  124.8 8.7 %collective-permute-start.33 = (f32[8,32,192]{2,1,0:T(8,128)S(1)}, f32[8,32,192]{2,1,0:T(8,128)S(1)}, u32[]{:S(2)}, u32[]{:S(2)}) collective-permute-start(f32[8,32,192]{2,1,0:T(8,128)S(1)} %slice_select_fusion), channel_id=1, source_target_pairs={{0,16},{16,0},{1,17},{17,1},{2,18},{18,2},{3,19},{19,3},{4,20},{20... | collective-permute-start | bytes 589832 | tf_op jit(solution)/shard_map/ppermute | solution.py:22
  126.6 6.9 %collective-permute-start.32 = (f32[128]{0:T(128)S(1)}, f32[128]{0:T(128)S(1)}, u32[]{:S(2)}, u32[]{:S(2)}) collective-permute-start(f32[128]{0:T(128)S(1)} %add_add_fusion.2), channel_id=1, source_target_pairs={{0,32},{32,0},{1,33},{33,1},{2,34},{34,2},{3,35},{35,3},{4,36},{36... | collective-permute-start | bytes 1544 | tf_op jit(solution)/shard_map/ppermute | solution.py:22
  (32 other events, 295.5 us)
Sparse Core Ops, SparseCore 0:
  13.4 45.8 all-gather.1
  79.0 44.6 reduce-scatter.1

commit v11 on v8

--- a/solution.py
+++ b/solution.py
@@ -12,6 +12,7 @@
 HALF = 384
 FIRST, SECOND = 3, 5
 VMEM = 28 * 1024 * 1024
+ORDER = 16
 STEP = 4
 
 epsilon = 1e-30
@@ -61,7 +62,7 @@
             out_specs=[spec, spec],
         ),
         out_shape=[jax.ShapeDtypeStruct((768, HALF), jnp.bfloat16)] * 2,
-        compiler_params=pltpu.CompilerParams(vmem_limit_bytes=60 * 1024 * 1024),
+        compiler_params=pltpu.CompilerParams(vmem_limit_bytes=VMEM),
     )(halves, weight)
 
 
@@ -106,7 +107,7 @@
         + [jax.ShapeDtypeStruct((8, 32, HALF), jnp.float32)] * FIRST,
         compiler_params=PARAMS,
         cost_estimate=pl.CostEstimate(
-            flops=FIRST * 4 * 256 * 768 * HALF, bytes_accessed=4 * 1024 * 1024, transcendentals=0
+            flops=ORDER * FIRST * 4 * 256 * 768 * HALF, bytes_accessed=ORDER * 4 * 1024 * 1024, transcendentals=0
         ),
     )(*cots, keep, send)
 
@@ -188,12 +189,12 @@
         jnp.concatenate([opposite, same], axis=1),
     )
     act_half = with_layout_constraint(act_half, Layout((0, 1)))
-    act_half, cotangent = lax.optimization_barrier((act_half, cotangent))
+    blocks = cotangent.reshape(32, 8, 768).transpose(1, 0, 2)
     act_own = lax.all_gather(act_half, "z", axis=0, tiled=True)
     act_own = with_layout_constraint(act_own, Layout((0, 1))).reshape(8, 8, 32, HALF)
 
-    own_cot = lax.all_to_all(cotangent, "z", 1, 0, tiled=True).reshape(8, 32, 768)
-    own_cot, weight = lax.optimization_barrier((own_cot, weight))
+    own_cot = lax.all_to_all(blocks, "z", 0, 0, tiled=True)
+    own_cot, weight, act_half = lax.optimization_barrier((own_cot, weight, act_half))
     right, left, far = (x + 3) % 4, (x + 1) % 4, (x + 2) % 4
     columns = [x, x, far, right, left, far, right, left]
     sides = [yh, 1 - yh, yh, yh, yh, 1 - yh, 1 - yh, 1 - yh]
@@ -213,7 +214,9 @@
     second = [right_cot, left_cot, other_far, other_right, other_left]
 
     kept, *sent = first_call(first, keep, send)
-    second[0], second[1], *sent = lax.optimization_barrier((second[0], second[1], *sent))
+    second[0], second[1], second[2], send, *sent = lax.optimization_barrier(
+        (second[0], second[1], second[2], send, *sent)
+    )
     received = [exchange(part, "core", 2, 1) for part in sent]
     others = [exchange(cot, "core", 2, 1) for cot in second]
     other_keep = exchange(send, "core", 2, 1)

time: 148 us -> 143 us (0.966)
  blocking collectives: 22.9 us -> 0 us
  waiting for transfers between devices: 35.8 us -> 49.9 us
  starting transfers between devices: 37.7 us -> 42.1 us
  local copies, waits for them, and re-layouts: 4.25 us -> 7.61 us
  Pallas kernels: 21.5 us -> 18.4 us
    all_to_all x1 -> x0, blocking collectives: 22.9 us -> none  [body(): lax.all_to_all(cotangent, 'z', 1, 0, tiled=True).reshape(8, 32, 768)]
    all_to_all x0 -> x1, waiting for transfers between devices: none -> 8.51 us  [body(): own_cot = lax.all_to_all(blocks, 'z', 0, 0, tiled=True)]
    all_to_all x0 -> x1, starting transfers between devices: none -> 8.47 us  [body(): own_cot = lax.all_to_all(blocks, 'z', 0, 0, tiled=True)]
    ppermute x27, starting transfers between devices: 30.6 us -> 26.4 us  [exchange(): return lax.ppermute(value, axis, [(i, i ^ bit) for i in range(size)])]
    ppermute x27, waiting for transfers between devices: 24.8 us -> 28.4 us  [exchange(): return lax.ppermute(value, axis, [(i, i ^ bit) for i in range(size)])]
    pallas_call x1, Pallas kernels: 4 us -> 1 us  [weight_call(): pl.pallas_call(weight_kernel, grid_spec=pltpu.PrefetchScalarGridSpec(num_...]
    unnamed x42 -> x52, local copies, waits for them, and re-layouts: 2.54 us -> 5.06 us
    reshape x0 -> x1, local copies, waits for them, and re-layouts: none -> 1.87 us  [body(): blocks = cotangent.reshape(32, 8, 768).transpose(1, 0, 2)]
  transfers between devices with their start and end apart: 36 -> 37, of which waited for: 17 -> 24; matrix products, arithmetic and copies ran while one was open for 5% -> 5% of each run, Pallas kernels for 15% -> 13%
where the time goes in v11:
time: 143 us
  waiting for transfers between devices  49.9 us (35%)
  starting transfers between devices  42.1 us (29%)
  Pallas kernels  18.4 us (13%)
  between operations  15.6 us (11%)
  other arithmetic  9.13 us (6%)
  local copies, waits for them, and re-layouts  7.61 us (5%)
    ppermute x27, waiting for transfers between devices, exchange(): return lax.ppermute(value, axis, [(i, i ^ bit) for i in range(size)])  28.4 us
    ppermute x27, starting transfers between devices, exchange(): return lax.ppermute(value, axis, [(i, i ^ bit) for i in range(size)])  26.4 us
    ppermute x5, waiting for transfers between devices, shift(): lax.ppermute(value, axis, [(i, (i + step) % size) for i in range(size)])  10.9 us
    all_to_all x1, waiting for transfers between devices, body(): own_cot = lax.all_to_all(blocks, 'z', 0, 0, tiled=True)  8.51 us
    all_to_all x1, starting transfers between devices, body(): own_cot = lax.all_to_all(blocks, 'z', 0, 0, tiled=True)  8.47 us
    pallas_call x1, Pallas kernels, gradient_call(): pl.pallas_call(gradient_kernel, in_specs=[SCALARS] * 2 + [VECTORS] * 10,...  7.04 us
    pallas_call x1, Pallas kernels, second_call(): pl.pallas_call(second_kernel, grid_spec=pltpu.PrefetchScalarGridSpec(num_...  6.55 us
    unnamed x52, local copies, waits for them, and re-layouts  5.06 us
  transfers between devices with their start and end apart: 37, of which 24 were waited for; matrix products, arithmetic and copies ran while one was open for 5% of the time, Pallas kernels for 13%

profile of v11, /device:TPU:4, one launch (start us, length us, event | category | flops | bytes accessed | tf_op | source)
XLA Modules:
  0.0 142.7 jit_solution(8058006715415932711)
XLA Ops:
  9.0 8.5 %all-to-all-start = ((bf16[8,32,768]{2,1,0:T(8,128)(2,1)}), bf16[8,32,768]{2,1,0:T(8,128)(2,1)S(1)}, u32[]{:S(2)}, u32[]{:S(2)}) async-start(bf16[8,32,768]{2,1,0:T(8,128)(2,1)} %bitcast.23), calls=%async_computation | async-start | bytes 786432 | tf_op jit(solution)/shard_map/all_to_all | solution.py:196
  23.7 8.5 %all-to-all-done.refs_0_ = bf16[8,32,768]{2,1,0:T(8,128)(2,1)S(1)} async-done(((bf16[8,32,768]{2,1,0:T(8,128)(2,1)}), bf16[8,32,768]{2,1,0:T(8,128)(2,1)S(1)}, u32[]{:S(2)}, u32[]{:S(2)}) %all-to-all-start) | async-done | bytes 393248 | tf_op jit(solution)/shard_map/all_to_all | solution.py:196
  32.2 3.2 %collective-permute-start.2 = (bf16[8,32,768]{2,1,0:T(8,128)(2,1)S(1)}, bf16[8,32,768]{2,1,0:T(8,128)(2,1)S(1)}, u32[]{:S(2)}, u32[]{:S(2)}) collective-permute-start(bf16[8,32,768]{2,1,0:T(8,128)(2,1)S(1)} %all-to-all-done.refs_0_), channel_id=1, source_target_pairs={{0,32},{32,0},{1,33},{33,1},{2,34},{34,2},{3,35},{35,3},{4,36},{36... | collective-permute-start | bytes 1179656 | tf_op jit(solution)/shard_map/ppermute | solution.py:23
  36.7 2.1 %collective-permute-start.4 = (bf16[8,32,768]{2,1,0:T(8,128)(2,1)S(1)}, bf16[8,32,768]{2,1,0:T(8,128)(2,1)S(1)}, u32[]{:S(2)}, u32[]{:S(2)}) collective-permute-start(bf16[8,32,768]{2,1,0:T(8,128)(2,1)S(1)} %all-to-all-done.refs_0_), channel_id=1, source_target_pairs={{0,64},{64,128},{128,192},{192,0},{1,65},{65,129},{129,193},{193,1... | collective-permute-start | bytes 1179656 | tf_op jit(solution)/shard_map/ppermute | solution.py:27
  41.6 2.2 %collective-permute-done.2.refs_1_ = bf16[8,32,768]{2,1,0:T(8,128)(2,1)S(1)} collective-permute-done((bf16[8,32,768]{2,1,0:T(8,128)(2,1)S(1)}, bf16[8,32,768]{2,1,0:T(8,128)(2,1)S(1)}, u32[]{:S(2)}, u32[]{:S(2)}) %collective-permute-start.2) | collective-permute-done | bytes 393248 | tf_op jit(solution)/shard_map/ppermute | solution.py:23
  45.8 3.2 %collective-permute-done.3.refs_2_ = bf16[8,32,768]{2,1,0:T(8,128)(2,1)} collective-permute-done((bf16[8,32,768]{2,1,0:T(8,128)(2,1)S(1)}, bf16[8,32,768]{2,1,0:T(8,128)(2,1)}, u32[]{:S(2)}, u32[]{:S(2)}) %collective-permute-start.3) | collective-permute-done | bytes 393248 | tf_op jit(solution)/shard_map/ppermute | solution.py:27
  49.4 3.9 %shard_map.69 = (f32[8,3,32,384]{3,2,1,0:T(8,128)}, f32[8,32,384]{2,1,0:T(8,128)}, f32[8,32,384]{2,1,0:T(8,128)}, f32[8,32,384]{2,1,0:T(8,128)}) custom-call(bf16[8,32,768]{2,1,0:T(8,128)(2,1)} %copy-done.7, bf16[8,32,768]{2,1,0:T(8,128)(2,1)} %copy-done.24, bf16[8,32,768]{2,1,0:T(8,128)(2,1)} %collective-permute-done.3.refs_2_, bf16[768,384]{1,0:T(8,128)(2,1)} %copy-done.1, ...), custom_call_target="tpu_custom_call" | custom-call | flops 14495514624 | bytes 67108864 | tf_op jit(solution)/shard_map/pallas_call | solution.py:102
  53.3 2.0 %collective-permute-done.4.refs_0_.refs_3_ = bf16[8,32,768]{2,1,0:T(8,128)(2,1)S(1)} collective-permute-done((bf16[8,32,768]{2,1,0:T(8,128)(2,1)S(1)}, bf16[8,32,768]{2,1,0:T(8,128)(2,1)S(1)}, u32[]{:S(2)}, u32[]{:S(2)}) %collective-permute-start.4) | collective-permute-done | bytes 393248 | tf_op jit(solution)/shard_map/ppermute | solution.py:27
  56.5 2.1 %collective-permute-done.6.refs_2_.refs_5_ = bf16[8,32,768]{2,1,0:T(8,128)(2,1)S(1)} collective-permute-done((bf16[8,32,768]{2,1,0:T(8,128)(2,1)}, bf16[8,32,768]{2,1,0:T(8,128)(2,1)S(1)}, u32[]{:S(2)}, u32[]{:S(2)}) %collective-permute-start.6) | collective-permute-done | bytes 393248 | tf_op jit(solution)/shard_map/ppermute | solution.py:23
  59.1 4.4 %collective-permute-done.7.refs_3_.refs_6_ = bf16[8,32,768]{2,1,0:T(8,128)(2,1)S(1)} collective-permute-done((bf16[8,32,768]{2,1,0:T(8,128)(2,1)S(1)}, bf16[8,32,768]{2,1,0:T(8,128)(2,1)S(1)}, u32[]{:S(2)}, u32[]{:S(2)}) %collective-permute-start.7) | collective-permute-done | bytes 393248 | tf_op jit(solution)/shard_map/ppermute | solution.py:27
  70.3 6.5 %shard_map.70 = f32[8,8,32,384]{3,2,1,0:T(8,128)} custom-call(s32[8]{0:T(128)} %stack.47.rows_ref, bf16[8,32,768]{2,1,0:T(8,128)(2,1)} %copy-done.8, bf16[8,32,768]{2,1,0:T(8,128)(2,1)} %copy-done.9, bf16[8,32,768]{2,1,0:T(8,128)(2,1)} %copy-done.12, bf16[8,32,768]{2,1,0:T(8,128)(2,1)} %copy-done.10, bf16[8,32,768]{2,1,0:T(8,128)(2,1)} %copy-done.11, ...), custom_call_target="tpu_custom_call" | custom-call | flops 1509949440 | bytes 8388608 | tf_op jit(solution)/shard_map/pallas_call | solution.py:120
  76.9 7.0 %shard_map.71 = (f32[768,768]{1,0:T(8,128)}, f32[768]{0:T(1024)}, f32[768]{0:T(1024)}) custom-call(s32[8]{0:T(128)} %stack.47.rows_ref, s32[2]{0:T(128)} %copy-done.2, bf16[8,32,768]{2,1,0:T(8,128)(2,1)} %copy-done.7, bf16[8,32,768]{2,1,0:T(8,128)(2,1)} %copy-done.24, bf16[8,32,768]{2,1,0:T(8,128)(2,1)} %collective-permute-done.3.refs_2_, ...), custom_call_target="tpu_custom_call" | custom-call | flops 2415919104 | bytes 9437184 | tf_op jit(solution)/shard_map/pallas_call | solution.py:162
  84.7 2.1 %collective-permute-start.20 = (f32[768]{0:T(1024)}, f32[768]{0:T(1024)S(1)}, u32[]{:S(2)}, u32[]{:S(2)}) collective-permute-start(f32[768]{0:T(1024)} %get-tuple-element.92), channel_id=1, source_target_pairs={{0,128},{64,192},{128,0},{192,64},{1,129},{65,193},{129,1},{193,65... | collective-permute-start | bytes 9224 | tf_op jit(solution)/shard_map/ppermute | solution.py:23
  88.1 1.9 %collective-permute-done.20 = f32[768]{0:T(1024)S(1)} collective-permute-done((f32[768]{0:T(1024)}, f32[768]{0:T(1024)S(1)}, u32[]{:S(2)}, u32[]{:S(2)}) %collective-permute-start.20) | collective-permute-done | bytes 3104 | tf_op jit(solution)/shard_map/ppermute | solution.py:23
  92.6 3.9 %collective-permute-done.22 = f32[768]{0:T(1024)S(1)} collective-permute-done((f32[768]{0:T(1024)S(1)}, f32[768]{0:T(1024)S(1)}, u32[]{:S(2)}, u32[]{:S(2)}) %collective-permute-start.22) | collective-permute-done | bytes 3104 | tf_op jit(solution)/shard_map/ppermute | solution.py:23
  96.5 2.0 %multiply_reduce_fusion = f32[768]{0:T(1024)S(1)} fusion(f32[768,768]{1,0:T(8,128)} %get-tuple-element.91, f32[768]{0:T(1024)S(1)} %get-tuple-element.106), kind=kLoop, calls=%fused_computation.1 | loop fusion | flops 1768704 | bytes 2365440 | tf_op jit(solution)/shard_map/reduce_sum | solution.py:236
  100.5 3.0 %collective-permute-done.24 = f32[2304]{0:T(1024)S(1)} collective-permute-done((f32[2304]{0:T(1024)S(1)}, f32[2304]{0:T(1024)S(1)}, u32[]{:S(2)}, u32[]{:S(2)}) %collective-permute-start.24) | collective-permute-done | bytes 9248 | tf_op jit(solution)/shard_map/ppermute | solution.py:23
  103.5 4.1 %collective-permute-done.25 = f32[2304]{0:T(1024)S(1)} collective-permute-done((f32[2304]{0:T(1024)S(1)}, f32[2304]{0:T(1024)S(1)}, u32[]{:S(2)}, u32[]{:S(2)}) %collective-permute-start.25) | collective-permute-done | bytes 9248 | tf_op jit(solution)/shard_map/ppermute | solution.py:23
  108.0 2.8 %collective-permute-start.27 = (f32[2304]{0:T(1024)S(1)}, f32[2304]{0:T(1024)S(1)}, u32[]{:S(2)}, u32[]{:S(2)}) collective-permute-start(f32[2304]{0:T(1024)S(1)} %add.117), channel_id=1, source_target_pairs={{0,4},{1,5},{2,6},{3,7},{4,0},{5,1},{6,2},{7,3},{8,12},{9,13},{10,... | collective-permute-start | bytes 27656 | tf_op jit(solution)/shard_map/ppermute | solution.py:23
  110.8 3.3 %collective-permute-start.26 = (f32[2304]{0:T(1024)S(1)}, f32[2304]{0:T(1024)S(1)}, u32[]{:S(2)}, u32[]{:S(2)}) collective-permute-start(f32[2304]{0:T(1024)S(1)} %add.117), channel_id=1, source_target_pairs={{0,2},{1,3},{2,0},{3,1},{4,6},{5,7},{6,4},{7,5},{8,10},{9,11},{10,... | collective-permute-start | bytes 27656 | tf_op jit(solution)/shard_map/ppermute | solution.py:23
  114.1 2.0 %collective-permute-done.27 = f32[2304]{0:T(1024)S(1)} collective-permute-done((f32[2304]{0:T(1024)S(1)}, f32[2304]{0:T(1024)S(1)}, u32[]{:S(2)}, u32[]{:S(2)}) %collective-permute-start.27) | collective-permute-done | bytes 9248 | tf_op jit(solution)/shard_map/ppermute | solution.py:23
  118.4 2.1 %collective-permute-start.30 = (f32[128]{0:T(128)S(1)}, f32[128]{0:T(128)S(1)}, u32[]{:S(2)}, u32[]{:S(2)}) collective-permute-start(f32[128]{0:T(128)S(1)} %get-tuple-element.104), channel_id=1, source_target_pairs={{0,128},{64,192},{128,0},{192,64},{1,129},{65,193},{129,1},{193,65... | collective-permute-start | bytes 1544 | tf_op jit(solution)/shard_map/ppermute | solution.py:23
  123.4 2.7 %collective-permute-start.32 = (f32[128]{0:T(128)S(1)}, f32[128]{0:T(128)S(1)}, u32[]{:S(2)}, u32[]{:S(2)}) collective-permute-start(f32[128]{0:T(128)S(1)} %add_add_fusion.2), channel_id=1, source_target_pairs={{0,32},{32,0},{1,33},{33,1},{2,34},{34,2},{3,35},{35,3},{4,36},{36... | collective-permute-start | bytes 1544 | tf_op jit(solution)/shard_map/ppermute | solution.py:23
  127.4 3.4 %collective-permute-done.32 = f32[128]{0:T(128)S(1)} collective-permute-done((f32[128]{0:T(128)S(1)}, f32[128]{0:T(128)S(1)}, u32[]{:S(2)}, u32[]{:S(2)}) %collective-permute-start.32) | collective-permute-done | bytes 544 | tf_op jit(solution)/shard_map/ppermute | solution.py:23
  (130 shorter events, 40.1 us)
Async XLA Ops:
  9.0 23.2 %all-to-all-start = ((bf16[8,32,768]{2,1,0:T(8,128)(2,1)}), bf16[8,32,768]{2,1,0:T(8,128)(2,1)S(1)}, u32[]{:S(2)}, u32[]{:S(2)}) async-start(bf16[8,32,768]{2,1,0:T(8,128)(2,1)} %bitcast.23), calls=%async_computation | async-start | bytes 786432 | tf_op jit(solution)/shard_map/all_to_all | solution.py:196
  17.5 51.9 %all-gather.2.cloned.1.call-start = ((), (), s32[]{:S(2)}) async-start(), calls=%async_computation.2 | async-start | bytes 1769472 | tf_op jit(solution)/shard_map/all_gather | solution.py:193
  23.6 97.0 %reduce-scatter.2.cloned.1.call-start = ((), (), s32[]{:S(2)}) async-start(), calls=%async_computation.3 | async-start | bytes 3538944 | tf_op jit(solution)/shard_map/reduce_scatter | solution.py:230
  32.2 11.6 %collective-permute-start.2 = (bf16[8,32,768]{2,1,0:T(8,128)(2,1)S(1)}, bf16[8,32,768]{2,1,0:T(8,128)(2,1)S(1)}, u32[]{:S(2)}, u32[]{:S(2)}) collective-permute-start(bf16[8,32,768]{2,1,0:T(8,128)(2,1)S(1)} %all-to-all-done.refs_0_), channel_id=1, source_target_pairs={{0,32},{32,0},{1,33},{33,1},{2,34},{34,2},{3,35},{35,3},{4,36},{36... | collective-permute-start | bytes 1179656 | tf_op jit(solution)/shard_map/ppermute | solution.py:23
  35.4 13.7 %collective-permute-start.3 = (bf16[8,32,768]{2,1,0:T(8,128)(2,1)S(1)}, bf16[8,32,768]{2,1,0:T(8,128)(2,1)}, u32[]{:S(2)}, u32[]{:S(2)}) collective-permute-start(bf16[8,32,768]{2,1,0:T(8,128)(2,1)S(1)} %all-to-all-done.refs_0_), channel_id=1, source_target_pairs={{0,128},{64,192},{128,0},{192,64},{1,129},{65,193},{129,1},{193,65... | collective-permute-start | bytes 1179656 | tf_op jit(solution)/shard_map/ppermute | solution.py:27
  36.7 18.6 %collective-permute-start.4 = (bf16[8,32,768]{2,1,0:T(8,128)(2,1)S(1)}, bf16[8,32,768]{2,1,0:T(8,128)(2,1)S(1)}, u32[]{:S(2)}, u32[]{:S(2)}) collective-permute-start(bf16[8,32,768]{2,1,0:T(8,128)(2,1)S(1)} %all-to-all-done.refs_0_), channel_id=1, source_target_pairs={{0,64},{64,128},{128,192},{192,0},{1,65},{65,129},{129,193},{193,1... | collective-permute-start | bytes 1179656 | tf_op jit(solution)/shard_map/ppermute | solution.py:27
  38.8 17.7 %collective-permute-start.5 = (bf16[8,32,768]{2,1,0:T(8,128)(2,1)S(1)}, bf16[8,32,768]{2,1,0:T(8,128)(2,1)S(1)}, u32[]{:S(2)}, u32[]{:S(2)}) collective-permute-start(bf16[8,32,768]{2,1,0:T(8,128)(2,1)S(1)} %all-to-all-done.refs_0_), channel_id=1, source_target_pairs={{0,192},{64,0},{128,64},{192,128},{1,193},{65,1},{129,65},{193,129... | collective-permute-start | bytes 1179656 | tf_op jit(solution)/shard_map/ppermute | solution.py:27
  43.8 19.7 %collective-permute-start.7 = (bf16[8,32,768]{2,1,0:T(8,128)(2,1)S(1)}, bf16[8,32,768]{2,1,0:T(8,128)(2,1)S(1)}, u32[]{:S(2)}, u32[]{:S(2)}) collective-permute-start(bf16[8,32,768]{2,1,0:T(8,128)(2,1)S(1)} %collective-permute-done.2.refs_1_), channel_id=1, source_target_pairs={{0,64},{64,128},{128,192},{192,0},{1,65},{65,129},{129,193},{193,1... | collective-permute-start | bytes 1179656 | tf_op jit(solution)/shard_map/ppermute | solution.py:27
  45.0 18.5 %collective-permute-start.8 = (bf16[8,32,768]{2,1,0:T(8,128)(2,1)S(1)}, bf16[8,32,768]{2,1,0:T(8,128)(2,1)S(1)}, u32[]{:S(2)}, u32[]{:S(2)}) collective-permute-start(bf16[8,32,768]{2,1,0:T(8,128)(2,1)S(1)} %collective-permute-done.2.refs_1_), channel_id=1, source_target_pairs={{0,192},{64,0},{128,64},{192,128},{1,193},{65,1},{129,65},{193,129... | collective-permute-start | bytes 1179656 | tf_op jit(solution)/shard_map/ppermute | solution.py:27
  49.1 9.5 %collective-permute-start.6 = (bf16[8,32,768]{2,1,0:T(8,128)(2,1)}, bf16[8,32,768]{2,1,0:T(8,128)(2,1)S(1)}, u32[]{:S(2)}, u32[]{:S(2)}) collective-permute-start(bf16[8,32,768]{2,1,0:T(8,128)(2,1)} %collective-permute-done.3.refs_2_), channel_id=1, source_target_pairs={{0,32},{32,0},{1,33},{33,1},{2,34},{34,2},{3,35},{35,3},{4,36},{36... | collective-permute-start | bytes 1179656 | tf_op jit(solution)/shard_map/ppermute | solution.py:23
  58.5 5.5 %collective-permute-start.9 = (bf16[8,32,768]{2,1,0:T(8,128)(2,1)S(1)}, bf16[8,32,768]{2,1,0:T(8,128)(2,1)S(1)}, u32[]{:S(2)}, u32[]{:S(2)}) collective-permute-start(bf16[8,32,768]{2,1,0:T(8,128)(2,1)S(1)} %collective-permute-done.4.refs_0_.refs_3_), channel_id=1, source_target_pairs={{0,8},{8,0},{1,9},{9,1},{2,10},{10,2},{3,11},{11,3},{4,12},{12,4},... | collective-permute-start | bytes 1179656 | tf_op jit(solution)/shard_map/ppermute | solution.py:23
  58.6 5.6 %collective-permute-start.10 = (bf16[8,32,768]{2,1,0:T(8,128)(2,1)S(1)}, bf16[8,32,768]{2,1,0:T(8,128)(2,1)S(1)}, u32[]{:S(2)}, u32[]{:S(2)}) collective-permute-start(bf16[8,32,768]{2,1,0:T(8,128)(2,1)S(1)} %collective-permute-done.5.refs_1_.refs_4_), channel_id=1, source_target_pairs={{0,8},{8,0},{1,9},{9,1},{2,10},{10,2},{3,11},{11,3},{4,12},{12,4},... | collective-permute-start | bytes 1179656 | tf_op jit(solution)/shard_map/ppermute | solution.py:23
  59.1 5.5 %collective-permute-start.11 = (bf16[8,32,768]{2,1,0:T(8,128)(2,1)S(1)}, bf16[8,32,768]{2,1,0:T(8,128)(2,1)S(1)}, u32[]{:S(2)}, u32[]{:S(2)}) collective-permute-start(bf16[8,32,768]{2,1,0:T(8,128)(2,1)S(1)} %collective-permute-done.6.refs_2_.refs_5_), channel_id=1, source_target_pairs={{0,8},{8,0},{1,9},{9,1},{2,10},{10,2},{3,11},{11,3},{4,12},{12,4},... | collective-permute-start | bytes 1179656 | tf_op jit(solution)/shard_map/ppermute | solution.py:23
  63.5 5.9 %collective-permute-start.17 = (bf16[768,384]{1,0:T(8,128)(2,1)S(1)}, bf16[768,384]{1,0:T(8,128)(2,1)S(1)}, u32[]{:S(2)}, u32[]{:S(2)}) collective-permute-start(bf16[768,384]{1,0:T(8,128)(2,1)S(1)} %copy-done.4), channel_id=1, source_target_pairs={{0,8},{8,0},{1,9},{9,1},{2,10},{10,2},{3,11},{11,3},{4,12},{12,4},... | collective-permute-start | bytes 1769480 | tf_op jit(solution)/shard_map/ppermute | solution.py:23
  69.5 7.4 %collective-permute-start.18 = (bf16[8,8,32,384]{3,2,1,0:T(8,128)(2,1)}, bf16[8,8,32,384]{3,2,1,0:T(8,128)(2,1)}, u32[]{:S(2)}, u32[]{:S(2)}) collective-permute-start(bf16[8,8,32,384]{3,2,1,0:T(8,128)(2,1)} %bitcast.28), channel_id=1, source_target_pairs={{0,8},{8,0},{1,9},{9,1},{2,10},{10,2},{3,11},{11,3},{4,12},{12,4},... | collective-permute-start | bytes 4718600 | tf_op jit(solution)/shard_map/ppermute | solution.py:23
  84.7 5.3 %collective-permute-start.20 = (f32[768]{0:T(1024)}, f32[768]{0:T(1024)S(1)}, u32[]{:S(2)}, u32[]{:S(2)}) collective-permute-start(f32[768]{0:T(1024)} %get-tuple-element.92), channel_id=1, source_target_pairs={{0,128},{64,192},{128,0},{192,64},{1,129},{65,193},{129,1},{193,65... | collective-permute-start | bytes 9224 | tf_op jit(solution)/shard_map/ppermute | solution.py:23
  91.4 5.1 %collective-permute-start.22 = (f32[768]{0:T(1024)S(1)}, f32[768]{0:T(1024)S(1)}, u32[]{:S(2)}, u32[]{:S(2)}) collective-permute-start(f32[768]{0:T(1024)S(1)} %add_add_fusion.1), channel_id=1, source_target_pairs={{0,32},{32,0},{1,33},{33,1},{2,34},{34,2},{3,35},{35,3},{4,36},{36... | collective-permute-start | bytes 9224 | tf_op jit(solution)/shard_map/ppermute | solution.py:23
  107.6 6.5 %collective-permute-start.28 = (f32[2304]{0:T(1024)S(1)}, f32[2304]{0:T(1024)S(1)}, u32[]{:S(2)}, u32[]{:S(2)}) collective-permute-start(f32[2304]{0:T(1024)S(1)} %add.117), channel_id=1, source_target_pairs={{0,6},{1,7},{2,4},{3,5},{4,2},{5,3},{6,0},{7,1},{8,14},{9,15},{10,... | collective-permute-start | bytes 27656 | tf_op jit(solution)/shard_map/ppermute | solution.py:23
  108.0 8.1 %collective-permute-start.27 = (f32[2304]{0:T(1024)S(1)}, f32[2304]{0:T(1024)S(1)}, u32[]{:S(2)}, u32[]{:S(2)}) collective-permute-start(f32[2304]{0:T(1024)S(1)} %add.117), channel_id=1, source_target_pairs={{0,4},{1,5},{2,6},{3,7},{4,0},{5,1},{6,2},{7,3},{8,12},{9,13},{10,... | collective-permute-start | bytes 27656 | tf_op jit(solution)/shard_map/ppermute | solution.py:23
  110.8 5.5 %collective-permute-start.26 = (f32[2304]{0:T(1024)S(1)}, f32[2304]{0:T(1024)S(1)}, u32[]{:S(2)}, u32[]{:S(2)}) collective-permute-start(f32[2304]{0:T(1024)S(1)} %add.117), channel_id=1, source_target_pairs={{0,2},{1,3},{2,0},{3,1},{4,6},{5,7},{6,4},{7,5},{8,10},{9,11},{10,... | collective-permute-start | bytes 27656 | tf_op jit(solution)/shard_map/ppermute | solution.py:23
  117.5 5.7 %collective-permute-start.31 = (f32[128]{0:T(128)S(1)}, f32[128]{0:T(128)S(1)}, u32[]{:S(2)}, u32[]{:S(2)}) collective-permute-start(f32[128]{0:T(128)S(1)} %get-tuple-element.104), channel_id=1, source_target_pairs={{0,192},{64,128},{128,64},{192,0},{1,193},{65,129},{129,65},{193,1... | collective-permute-start | bytes 1544 | tf_op jit(solution)/shard_map/ppermute | solution.py:23
  118.4 5.0 %collective-permute-start.30 = (f32[128]{0:T(128)S(1)}, f32[128]{0:T(128)S(1)}, u32[]{:S(2)}, u32[]{:S(2)}) collective-permute-start(f32[128]{0:T(128)S(1)} %get-tuple-element.104), channel_id=1, source_target_pairs={{0,128},{64,192},{128,0},{192,64},{1,129},{65,193},{129,1},{193,65... | collective-permute-start | bytes 1544 | tf_op jit(solution)/shard_map/ppermute | solution.py:23
  121.9 8.9 %collective-permute-start.33 = (f32[8,32,192]{2,1,0:T(8,128)S(1)}, f32[8,32,192]{2,1,0:T(8,128)S(1)}, u32[]{:S(2)}, u32[]{:S(2)}) collective-permute-start(f32[8,32,192]{2,1,0:T(8,128)S(1)} %slice_select_fusion), channel_id=1, source_target_pairs={{0,16},{16,0},{1,17},{17,1},{2,18},{18,2},{3,19},{19,3},{4,20},{20... | collective-permute-start | bytes 589832 | tf_op jit(solution)/shard_map/ppermute | solution.py:23
  123.4 7.4 %collective-permute-start.32 = (f32[128]{0:T(128)S(1)}, f32[128]{0:T(128)S(1)}, u32[]{:S(2)}, u32[]{:S(2)}) collective-permute-start(f32[128]{0:T(128)S(1)} %add_add_fusion.2), channel_id=1, source_target_pairs={{0,32},{32,0},{1,33},{33,1},{2,34},{34,2},{3,35},{35,3},{4,36},{36... | collective-permute-start | bytes 1544 | tf_op jit(solution)/shard_map/ppermute | solution.py:23
  (38 other events, 323.8 us)
Sparse Core Ops, SparseCore 0:
  23.8 43.6 all-gather.1
  77.0 43.6 reduce-scatter.1

commit v12 on v11

--- a/solution.py
+++ b/solution.py
@@ -129,7 +129,7 @@
             out_specs=step_spec(8, 32, HALF),
         ),
         out_shape=jax.ShapeDtypeStruct((8, 8, 32, HALF), jnp.float32),
-        compiler_params=pltpu.CompilerParams(vmem_limit_bytes=60 * 1024 * 1024),
+        compiler_params=pltpu.CompilerParams(vmem_limit_bytes=50 * 1024 * 1024),
         cost_estimate=pl.CostEstimate(
             flops=SECOND * 4 * 256 * 768 * HALF, bytes_accessed=8 * 1024 * 1024, transcendentals=0
         ),

time: 143 us -> 143 us (level)
  starting transfers between devices: 42.1 us -> 45.1 us
  waiting for transfers between devices: 49.9 us -> 47.8 us
    ppermute x27, starting transfers between devices: 26.4 us -> 29.4 us  [exchange(): return lax.ppermute(value, axis, [(i, i ^ bit) for i in range(size)])]
    ppermute x27, waiting for transfers between devices: 28.4 us -> 26.8 us  [exchange(): return lax.ppermute(value, axis, [(i, i ^ bit) for i in range(size)])]
    unnamed x52 -> x38, local copies, waits for them, and re-layouts: 5.06 us -> 5.63 us
  transfers between devices with their start and end apart: 37 -> 37, of which waited for: 24 -> 22; matrix products, arithmetic and copies ran while one was open for 5% -> 5% of each run, Pallas kernels for 13% -> 12%
where the time goes in v12:
time: 143 us
  waiting for transfers between devices  47.8 us (33%)
  starting transfers between devices  45.1 us (32%)
  Pallas kernels  17.7 us (12%)
  between operations  15.6 us (11%)
  other arithmetic  9.1 us (6%)
  local copies, waits for them, and re-layouts  7.58 us (5%)
    ppermute x27, starting transfers between devices, exchange(): return lax.ppermute(value, axis, [(i, i ^ bit) for i in range(size)])  29.4 us
    ppermute x27, waiting for transfers between devices, exchange(): return lax.ppermute(value, axis, [(i, i ^ bit) for i in range(size)])  26.8 us
    ppermute x5, waiting for transfers between devices, shift(): lax.ppermute(value, axis, [(i, (i + step) % size) for i in range(size)])  10.1 us
    all_to_all x1, waiting for transfers between devices, body(): own_cot = lax.all_to_all(blocks, 'z', 0, 0, tiled=True)  8.52 us
    all_to_all x1, starting transfers between devices, body(): own_cot = lax.all_to_all(blocks, 'z', 0, 0, tiled=True)  8.47 us
    pallas_call x1, Pallas kernels, gradient_call(): pl.pallas_call(gradient_kernel, in_specs=[SCALARS] * 2 + [VECTORS] * 10,...  7.06 us
    pallas_call x1, Pallas kernels, second_call(): pl.pallas_call(second_kernel, grid_spec=pltpu.PrefetchScalarGridSpec(num_...  5.81 us
    unnamed x38, local copies, waits for them, and re-layouts  5.63 us
  transfers between devices with their start and end apart: 37, of which 22 were waited for; matrix products, arithmetic and copies ran while one was open for 5% of the time, Pallas kernels for 12%

profile of v12, /device:TPU:4, one launch (start us, length us, event | category | flops | bytes accessed | tf_op | source)
XLA Modules:
  0.0 142.9 jit_solution(14583673218122854361)
XLA Ops:
  7.2 1.9 %copy.23 = bf16[4,8,8,768]{3,2,0,1:T(8,128)(2,1)} copy(bf16[4,8,8,768]{3,2,1,0:T(8,128)(2,1)} %bitcast.27) | data formatting | bytes 786432 | tf_op jit(solution)/shard_map/reshape | solution.py:192
  9.0 8.5 %all-to-all-start = ((bf16[8,32,768]{2,1,0:T(8,128)(2,1)}), bf16[8,32,768]{2,1,0:T(8,128)(2,1)S(1)}, u32[]{:S(2)}, u32[]{:S(2)}) async-start(bf16[8,32,768]{2,1,0:T(8,128)(2,1)} %bitcast.23), calls=%async_computation | async-start | bytes 786432 | tf_op jit(solution)/shard_map/all_to_all | solution.py:196
  23.7 8.5 %all-to-all-done.refs_0_ = bf16[8,32,768]{2,1,0:T(8,128)(2,1)S(1)} async-done(((bf16[8,32,768]{2,1,0:T(8,128)(2,1)}), bf16[8,32,768]{2,1,0:T(8,128)(2,1)S(1)}, u32[]{:S(2)}, u32[]{:S(2)}) %all-to-all-start) | async-done | bytes 393248 | tf_op jit(solution)/shard_map/all_to_all | solution.py:196
  32.2 3.2 %collective-permute-start.2 = (bf16[8,32,768]{2,1,0:T(8,128)(2,1)S(1)}, bf16[8,32,768]{2,1,0:T(8,128)(2,1)}, u32[]{:S(2)}, u32[]{:S(2)}) collective-permute-start(bf16[8,32,768]{2,1,0:T(8,128)(2,1)S(1)} %all-to-all-done.refs_0_), channel_id=1, source_target_pairs={{0,32},{32,0},{1,33},{33,1},{2,34},{34,2},{3,35},{35,3},{4,36},{36... | collective-permute-start | bytes 1179656 | tf_op jit(solution)/shard_map/ppermute | solution.py:23
  36.1 2.1 %collective-permute-start.4 = (bf16[8,32,768]{2,1,0:T(8,128)(2,1)S(1)}, bf16[8,32,768]{2,1,0:T(8,128)(2,1)S(1)}, u32[]{:S(2)}, u32[]{:S(2)}) collective-permute-start(bf16[8,32,768]{2,1,0:T(8,128)(2,1)S(1)} %all-to-all-done.refs_0_), channel_id=1, source_target_pairs={{0,64},{64,128},{128,192},{192,0},{1,65},{65,129},{129,193},{193,1... | collective-permute-start | bytes 1179656 | tf_op jit(solution)/shard_map/ppermute | solution.py:27
  41.0 2.9 %collective-permute-done.2.refs_1_ = bf16[8,32,768]{2,1,0:T(8,128)(2,1)} collective-permute-done((bf16[8,32,768]{2,1,0:T(8,128)(2,1)S(1)}, bf16[8,32,768]{2,1,0:T(8,128)(2,1)}, u32[]{:S(2)}, u32[]{:S(2)}) %collective-permute-start.2) | collective-permute-done | bytes 393248 | tf_op jit(solution)/shard_map/ppermute | solution.py:23
  45.9 3.0 %collective-permute-done.3.refs_2_ = bf16[8,32,768]{2,1,0:T(8,128)(2,1)S(1)} collective-permute-done((bf16[8,32,768]{2,1,0:T(8,128)(2,1)S(1)}, bf16[8,32,768]{2,1,0:T(8,128)(2,1)S(1)}, u32[]{:S(2)}, u32[]{:S(2)}) %collective-permute-start.3) | collective-permute-done | bytes 393248 | tf_op jit(solution)/shard_map/ppermute | solution.py:27
  49.7 3.8 %shard_map.69 = (f32[8,3,32,384]{3,2,1,0:T(8,128)}, f32[8,32,384]{2,1,0:T(8,128)}, f32[8,32,384]{2,1,0:T(8,128)}, f32[8,32,384]{2,1,0:T(8,128)}) custom-call(bf16[8,32,768]{2,1,0:T(8,128)(2,1)} %copy-done.13, bf16[8,32,768]{2,1,0:T(8,128)(2,1)} %collective-permute-done.2.refs_1_, bf16[8,32,768]{2,1,0:T(8,128)(2,1)} %copy-done.17, ...), custom_call_target="tpu_custom_call" | custom-call | flops 14495514624 | bytes 67108864 | tf_op jit(solution)/shard_map/pallas_call | solution.py:102
  58.8 4.1 %collective-permute-done.7.refs_3_.refs_6_ = bf16[8,32,768]{2,1,0:T(8,128)(2,1)S(1)} collective-permute-done((bf16[8,32,768]{2,1,0:T(8,128)(2,1)}, bf16[8,32,768]{2,1,0:T(8,128)(2,1)S(1)}, u32[]{:S(2)}, u32[]{:S(2)}) %collective-permute-start.7) | collective-permute-done | bytes 393248 | tf_op jit(solution)/shard_map/ppermute | solution.py:27
  69.2 5.8 %shard_map.70 = f32[8,8,32,384]{3,2,1,0:T(8,128)} custom-call(s32[8]{0:T(128)S(1)} %stack.47.rows_ref, bf16[8,32,768]{2,1,0:T(8,128)(2,1)S(1)} %collective-permute-done.4.refs_0_.refs_3_, bf16[8,32,768]{2,1,0:T(8,128)(2,1)S(1)} %collective-permute-done.5.refs_1_.refs_4_, bf16[8,32,768]{2,1,0:T(8,128)(2,1)S(1)} %collective-permute-done.6.refs_2_.refs_5_, ...), custom_call_target="tpu_custom_call" | custom-call | flops 1509949440 | bytes 8388608 | tf_op jit(solution)/shard_map/pallas_call | solution.py:120
  75.1 7.1 %shard_map.71 = (f32[768,768]{1,0:T(8,128)}, f32[768]{0:T(1024)}, f32[768]{0:T(1024)}) custom-call(s32[8]{0:T(128)} %copy-done.9, s32[2]{0:T(128)} %copy-done.10, bf16[8,32,768]{2,1,0:T(8,128)(2,1)} %copy-done.13, bf16[8,32,768]{2,1,0:T(8,128)(2,1)} %collective-permute-done.2.refs_1_, bf16[8,32,768]{2,1,0:T(8,128)(2,1)} %copy-done.17, ...), custom_call_target="tpu_custom_call" | custom-call | flops 2415919104 | bytes 9437184 | tf_op jit(solution)/shard_map/pallas_call | solution.py:162
  83.6 2.1 %collective-permute-start.20 = (f32[768]{0:T(1024)}, f32[768]{0:T(1024)S(1)}, u32[]{:S(2)}, u32[]{:S(2)}) collective-permute-start(f32[768]{0:T(1024)} %get-tuple-element.92), channel_id=1, source_target_pairs={{0,128},{64,192},{128,0},{192,64},{1,129},{65,193},{129,1},{193,65... | collective-permute-start | bytes 9224 | tf_op jit(solution)/shard_map/ppermute | solution.py:23
  86.4 2.5 %collective-permute-done.20 = f32[768]{0:T(1024)S(1)} collective-permute-done((f32[768]{0:T(1024)}, f32[768]{0:T(1024)S(1)}, u32[]{:S(2)}, u32[]{:S(2)}) %collective-permute-start.20) | collective-permute-done | bytes 3104 | tf_op jit(solution)/shard_map/ppermute | solution.py:23
  90.2 2.7 %collective-permute-start.22 = (f32[768]{0:T(1024)S(1)}, f32[768]{0:T(1024)S(1)}, u32[]{:S(2)}, u32[]{:S(2)}) collective-permute-start(f32[768]{0:T(1024)S(1)} %add_add_fusion.1), channel_id=1, source_target_pairs={{0,32},{32,0},{1,33},{33,1},{2,34},{34,2},{3,35},{35,3},{4,36},{36... | collective-permute-start | bytes 9224 | tf_op jit(solution)/shard_map/ppermute | solution.py:23
  92.8 2.4 %collective-permute-done.22 = f32[768]{0:T(1024)S(1)} collective-permute-done((f32[768]{0:T(1024)S(1)}, f32[768]{0:T(1024)S(1)}, u32[]{:S(2)}, u32[]{:S(2)}) %collective-permute-start.22) | collective-permute-done | bytes 3104 | tf_op jit(solution)/shard_map/ppermute | solution.py:23
  95.3 2.0 %multiply_reduce_fusion = f32[768]{0:T(1024)S(1)} fusion(f32[768,768]{1,0:T(8,128)} %get-tuple-element.91, f32[768]{0:T(1024)S(1)} %get-tuple-element.106), kind=kLoop, calls=%fused_computation.1 | loop fusion | flops 1768704 | bytes 2365440 | tf_op jit(solution)/shard_map/reduce_sum | solution.py:236
  99.7 2.6 %collective-permute-done.24 = f32[2304]{0:T(1024)S(1)} collective-permute-done((f32[2304]{0:T(1024)S(1)}, f32[2304]{0:T(1024)S(1)}, u32[]{:S(2)}, u32[]{:S(2)}) %collective-permute-start.24) | collective-permute-done | bytes 9248 | tf_op jit(solution)/shard_map/ppermute | solution.py:23
  103.2 2.9 %collective-permute-done.25 = f32[2304]{0:T(1024)S(1)} collective-permute-done((f32[2304]{0:T(1024)S(1)}, f32[2304]{0:T(1024)S(1)}, u32[]{:S(2)}, u32[]{:S(2)}) %collective-permute-start.25) | collective-permute-done | bytes 9248 | tf_op jit(solution)/shard_map/ppermute | solution.py:23
  107.8 3.3 %collective-permute-start.27 = (f32[2304]{0:T(1024)S(1)}, f32[2304]{0:T(1024)S(1)}, u32[]{:S(2)}, u32[]{:S(2)}) collective-permute-start(f32[2304]{0:T(1024)S(1)} %add.117), channel_id=1, source_target_pairs={{0,4},{1,5},{2,6},{3,7},{4,0},{5,1},{6,2},{7,3},{8,12},{9,13},{10,... | collective-permute-start | bytes 27656 | tf_op jit(solution)/shard_map/ppermute | solution.py:23
  112.5 3.3 %collective-permute-done.27 = f32[2304]{0:T(1024)S(1)} collective-permute-done((f32[2304]{0:T(1024)S(1)}, f32[2304]{0:T(1024)S(1)}, u32[]{:S(2)}, u32[]{:S(2)}) %collective-permute-start.27) | collective-permute-done | bytes 9248 | tf_op jit(solution)/shard_map/ppermute | solution.py:23
  118.3 2.0 %collective-permute-start.30 = (f32[128]{0:T(128)S(1)}, f32[128]{0:T(128)S(1)}, u32[]{:S(2)}, u32[]{:S(2)}) collective-permute-start(f32[128]{0:T(128)S(1)} %get-tuple-element.104), channel_id=1, source_target_pairs={{0,128},{64,192},{128,0},{192,64},{1,129},{65,193},{129,1},{193,65... | collective-permute-start | bytes 1544 | tf_op jit(solution)/shard_map/ppermute | solution.py:23
  123.6 2.8 %collective-permute-start.32 = (f32[128]{0:T(128)S(1)}, f32[128]{0:T(128)S(1)}, u32[]{:S(2)}, u32[]{:S(2)}) collective-permute-start(f32[128]{0:T(128)S(1)} %add_add_fusion.2), channel_id=1, source_target_pairs={{0,32},{32,0},{1,33},{33,1},{2,34},{34,2},{3,35},{35,3},{4,36},{36... | collective-permute-start | bytes 1544 | tf_op jit(solution)/shard_map/ppermute | solution.py:23
  127.6 3.4 %collective-permute-done.32 = f32[128]{0:T(128)S(1)} collective-permute-done((f32[128]{0:T(128)S(1)}, f32[128]{0:T(128)S(1)}, u32[]{:S(2)}, u32[]{:S(2)}) %collective-permute-start.32) | collective-permute-done | bytes 544 | tf_op jit(solution)/shard_map/ppermute | solution.py:23
  134.2 1.9 %multiply_divide_fusion = f32[768,768]{1,0:T(8,128)} fusion(f32[768,768]{1,0:T(8,128)S(1)} %copy-done.12, f32[]{:T(128)S(6)} %max_shard_map.3, f32[]{:T(128)S(6)} %div.26, f32[768]{0:T(1024)S(1)} %get-tuple-element.105, f32[768]{0:T(1024)S(1)} %get-tuple-element.107), kind=kLoop, calls=%fused_computation | loop fusion | flops 2359296 | bytes 4724744 | tf_op jit(solution)/shard_map/div | solution.py:259
  (116 shorter events, 42.7 us)
Async XLA Ops:
  9.0 23.2 %all-to-all-start = ((bf16[8,32,768]{2,1,0:T(8,128)(2,1)}), bf16[8,32,768]{2,1,0:T(8,128)(2,1)S(1)}, u32[]{:S(2)}, u32[]{:S(2)}) async-start(bf16[8,32,768]{2,1,0:T(8,128)(2,1)} %bitcast.23), calls=%async_computation | async-start | bytes 786432 | tf_op jit(solution)/shard_map/all_to_all | solution.py:196
  17.5 50.5 %all-gather.2.cloned.1.call-start = ((), (), s32[]{:S(2)}) async-start(), calls=%async_computation.2 | async-start | bytes 1769472 | tf_op jit(solution)/shard_map/all_gather | solution.py:193
  23.6 97.2 %reduce-scatter.2.cloned.1.call-start = ((), (), s32[]{:S(2)}) async-start(), calls=%async_computation.3 | async-start | bytes 3538944 | tf_op jit(solution)/shard_map/reduce_scatter | solution.py:230
  32.2 11.7 %collective-permute-start.2 = (bf16[8,32,768]{2,1,0:T(8,128)(2,1)S(1)}, bf16[8,32,768]{2,1,0:T(8,128)(2,1)}, u32[]{:S(2)}, u32[]{:S(2)}) collective-permute-start(bf16[8,32,768]{2,1,0:T(8,128)(2,1)S(1)} %all-to-all-done.refs_0_), channel_id=1, source_target_pairs={{0,32},{32,0},{1,33},{33,1},{2,34},{34,2},{3,35},{35,3},{4,36},{36... | collective-permute-start | bytes 1179656 | tf_op jit(solution)/shard_map/ppermute | solution.py:23
  35.4 13.6 %collective-permute-start.3 = (bf16[8,32,768]{2,1,0:T(8,128)(2,1)S(1)}, bf16[8,32,768]{2,1,0:T(8,128)(2,1)S(1)}, u32[]{:S(2)}, u32[]{:S(2)}) collective-permute-start(bf16[8,32,768]{2,1,0:T(8,128)(2,1)S(1)} %all-to-all-done.refs_0_), channel_id=1, source_target_pairs={{0,128},{64,192},{128,0},{192,64},{1,129},{65,193},{129,1},{193,65... | collective-permute-start | bytes 1179656 | tf_op jit(solution)/shard_map/ppermute | solution.py:27
  36.1 19.2 %collective-permute-start.4 = (bf16[8,32,768]{2,1,0:T(8,128)(2,1)S(1)}, bf16[8,32,768]{2,1,0:T(8,128)(2,1)S(1)}, u32[]{:S(2)}, u32[]{:S(2)}) collective-permute-start(bf16[8,32,768]{2,1,0:T(8,128)(2,1)S(1)} %all-to-all-done.refs_0_), channel_id=1, source_target_pairs={{0,64},{64,128},{128,192},{192,0},{1,65},{65,129},{129,193},{193,1... | collective-permute-start | bytes 1179656 | tf_op jit(solution)/shard_map/ppermute | solution.py:27
  38.2 18.3 %collective-permute-start.5 = (bf16[8,32,768]{2,1,0:T(8,128)(2,1)S(1)}, bf16[8,32,768]{2,1,0:T(8,128)(2,1)S(1)}, u32[]{:S(2)}, u32[]{:S(2)}) collective-permute-start(bf16[8,32,768]{2,1,0:T(8,128)(2,1)S(1)} %all-to-all-done.refs_0_), channel_id=1, source_target_pairs={{0,192},{64,0},{128,64},{192,128},{1,193},{65,1},{129,65},{193,129... | collective-permute-start | bytes 1179656 | tf_op jit(solution)/shard_map/ppermute | solution.py:27
  43.9 19.0 %collective-permute-start.7 = (bf16[8,32,768]{2,1,0:T(8,128)(2,1)}, bf16[8,32,768]{2,1,0:T(8,128)(2,1)S(1)}, u32[]{:S(2)}, u32[]{:S(2)}) collective-permute-start(bf16[8,32,768]{2,1,0:T(8,128)(2,1)} %collective-permute-done.2.refs_1_), channel_id=1, source_target_pairs={{0,64},{64,128},{128,192},{192,0},{1,65},{65,129},{129,193},{193,1... | collective-permute-start | bytes 1179656 | tf_op jit(solution)/shard_map/ppermute | solution.py:27
  45.1 17.8 %collective-permute-start.8 = (bf16[8,32,768]{2,1,0:T(8,128)(2,1)}, bf16[8,32,768]{2,1,0:T(8,128)(2,1)S(1)}, u32[]{:S(2)}, u32[]{:S(2)}) collective-permute-start(bf16[8,32,768]{2,1,0:T(8,128)(2,1)} %collective-permute-done.2.refs_1_), channel_id=1, source_target_pairs={{0,192},{64,0},{128,64},{192,128},{1,193},{65,1},{129,65},{193,129... | collective-permute-start | bytes 1179656 | tf_op jit(solution)/shard_map/ppermute | solution.py:27
  49.0 9.3 %collective-permute-start.6 = (bf16[8,32,768]{2,1,0:T(8,128)(2,1)S(1)}, bf16[8,32,768]{2,1,0:T(8,128)(2,1)S(1)}, u32[]{:S(2)}, u32[]{:S(2)}) collective-permute-start(bf16[8,32,768]{2,1,0:T(8,128)(2,1)S(1)} %collective-permute-done.3.refs_2_), channel_id=1, source_target_pairs={{0,32},{32,0},{1,33},{33,1},{2,34},{34,2},{3,35},{35,3},{4,36},{36... | collective-permute-start | bytes 1179656 | tf_op jit(solution)/shard_map/ppermute | solution.py:23
  58.2 5.2 %collective-permute-start.9 = (bf16[8,32,768]{2,1,0:T(8,128)(2,1)S(1)}, bf16[8,32,768]{2,1,0:T(8,128)(2,1)S(1)}, u32[]{:S(2)}, u32[]{:S(2)}) collective-permute-start(bf16[8,32,768]{2,1,0:T(8,128)(2,1)S(1)} %collective-permute-done.4.refs_0_.refs_3_), channel_id=1, source_target_pairs={{0,8},{8,0},{1,9},{9,1},{2,10},{10,2},{3,11},{11,3},{4,12},{12,4},... | collective-permute-start | bytes 1179656 | tf_op jit(solution)/shard_map/ppermute | solution.py:23
  58.2 5.3 %collective-permute-start.10 = (bf16[8,32,768]{2,1,0:T(8,128)(2,1)S(1)}, bf16[8,32,768]{2,1,0:T(8,128)(2,1)S(1)}, u32[]{:S(2)}, u32[]{:S(2)}) collective-permute-start(bf16[8,32,768]{2,1,0:T(8,128)(2,1)S(1)} %collective-permute-done.5.refs_1_.refs_4_), channel_id=1, source_target_pairs={{0,8},{8,0},{1,9},{9,1},{2,10},{10,2},{3,11},{11,3},{4,12},{12,4},... | collective-permute-start | bytes 1179656 | tf_op jit(solution)/shard_map/ppermute | solution.py:23
  58.7 5.2 %collective-permute-start.11 = (bf16[8,32,768]{2,1,0:T(8,128)(2,1)S(1)}, bf16[8,32,768]{2,1,0:T(8,128)(2,1)S(1)}, u32[]{:S(2)}, u32[]{:S(2)}) collective-permute-start(bf16[8,32,768]{2,1,0:T(8,128)(2,1)S(1)} %collective-permute-done.6.refs_2_.refs_5_), channel_id=1, source_target_pairs={{0,8},{8,0},{1,9},{9,1},{2,10},{10,2},{3,11},{11,3},{4,12},{12,4},... | collective-permute-start | bytes 1179656 | tf_op jit(solution)/shard_map/ppermute | solution.py:23
  62.9 5.1 %collective-permute-start.17 = (bf16[768,384]{1,0:T(8,128)(2,1)}, bf16[768,384]{1,0:T(8,128)(2,1)}, u32[]{:S(2)}, u32[]{:S(2)}) collective-permute-start(bf16[768,384]{1,0:T(8,128)(2,1)} %copy-done.11), channel_id=1, source_target_pairs={{0,8},{8,0},{1,9},{9,1},{2,10},{10,2},{3,11},{11,3},{4,12},{12,4},... | collective-permute-start | bytes 1769480 | tf_op jit(solution)/shard_map/ppermute | solution.py:23
  68.0 7.0 %collective-permute-start.18 = (bf16[8,8,32,384]{3,2,1,0:T(8,128)(2,1)}, bf16[8,8,32,384]{3,2,1,0:T(8,128)(2,1)}, u32[]{:S(2)}, u32[]{:S(2)}) collective-permute-start(bf16[8,8,32,384]{3,2,1,0:T(8,128)(2,1)} %bitcast.28), channel_id=1, source_target_pairs={{0,8},{8,0},{1,9},{9,1},{2,10},{10,2},{3,11},{11,3},{4,12},{12,4},... | collective-permute-start | bytes 4718600 | tf_op jit(solution)/shard_map/ppermute | solution.py:23
  83.6 5.3 %collective-permute-start.20 = (f32[768]{0:T(1024)}, f32[768]{0:T(1024)S(1)}, u32[]{:S(2)}, u32[]{:S(2)}) collective-permute-start(f32[768]{0:T(1024)} %get-tuple-element.92), channel_id=1, source_target_pairs={{0,128},{64,192},{128,0},{192,64},{1,129},{65,193},{129,1},{193,65... | collective-permute-start | bytes 9224 | tf_op jit(solution)/shard_map/ppermute | solution.py:23
  90.2 5.1 %collective-permute-start.22 = (f32[768]{0:T(1024)S(1)}, f32[768]{0:T(1024)S(1)}, u32[]{:S(2)}, u32[]{:S(2)}) collective-permute-start(f32[768]{0:T(1024)S(1)} %add_add_fusion.1), channel_id=1, source_target_pairs={{0,32},{32,0},{1,33},{33,1},{2,34},{34,2},{3,35},{35,3},{4,36},{36... | collective-permute-start | bytes 9224 | tf_op jit(solution)/shard_map/ppermute | solution.py:23
  106.0 6.5 %collective-permute-start.28 = (f32[2304]{0:T(1024)S(1)}, f32[2304]{0:T(1024)S(1)}, u32[]{:S(2)}, u32[]{:S(2)}) collective-permute-start(f32[2304]{0:T(1024)S(1)} %add.117), channel_id=1, source_target_pairs={{0,6},{1,7},{2,4},{3,5},{4,2},{5,3},{6,0},{7,1},{8,14},{9,15},{10,... | collective-permute-start | bytes 27656 | tf_op jit(solution)/shard_map/ppermute | solution.py:23
  107.8 8.0 %collective-permute-start.27 = (f32[2304]{0:T(1024)S(1)}, f32[2304]{0:T(1024)S(1)}, u32[]{:S(2)}, u32[]{:S(2)}) collective-permute-start(f32[2304]{0:T(1024)S(1)} %add.117), channel_id=1, source_target_pairs={{0,4},{1,5},{2,6},{3,7},{4,0},{5,1},{6,2},{7,3},{8,12},{9,13},{10,... | collective-permute-start | bytes 27656 | tf_op jit(solution)/shard_map/ppermute | solution.py:23
  111.1 5.0 %collective-permute-start.26 = (f32[2304]{0:T(1024)S(1)}, f32[2304]{0:T(1024)S(1)}, u32[]{:S(2)}, u32[]{:S(2)}) collective-permute-start(f32[2304]{0:T(1024)S(1)} %add.117), channel_id=1, source_target_pairs={{0,2},{1,3},{2,0},{3,1},{4,6},{5,7},{6,4},{7,5},{8,10},{9,11},{10,... | collective-permute-start | bytes 27656 | tf_op jit(solution)/shard_map/ppermute | solution.py:23
  117.0 6.6 %collective-permute-start.31 = (f32[128]{0:T(128)S(1)}, f32[128]{0:T(128)S(1)}, u32[]{:S(2)}, u32[]{:S(2)}) collective-permute-start(f32[128]{0:T(128)S(1)} %get-tuple-element.104), channel_id=1, source_target_pairs={{0,192},{64,128},{128,64},{192,0},{1,193},{65,129},{129,65},{193,1... | collective-permute-start | bytes 1544 | tf_op jit(solution)/shard_map/ppermute | solution.py:23
  118.3 5.3 %collective-permute-start.30 = (f32[128]{0:T(128)S(1)}, f32[128]{0:T(128)S(1)}, u32[]{:S(2)}, u32[]{:S(2)}) collective-permute-start(f32[128]{0:T(128)S(1)} %get-tuple-element.104), channel_id=1, source_target_pairs={{0,128},{64,192},{128,0},{192,64},{1,129},{65,193},{129,1},{193,65... | collective-permute-start | bytes 1544 | tf_op jit(solution)/shard_map/ppermute | solution.py:23
  122.0 9.0 %collective-permute-start.33 = (f32[8,32,192]{2,1,0:T(8,128)S(1)}, f32[8,32,192]{2,1,0:T(8,128)S(1)}, u32[]{:S(2)}, u32[]{:S(2)}) collective-permute-start(f32[8,32,192]{2,1,0:T(8,128)S(1)} %slice_select_fusion), channel_id=1, source_target_pairs={{0,16},{16,0},{1,17},{17,1},{2,18},{18,2},{3,19},{19,3},{4,20},{20... | collective-permute-start | bytes 589832 | tf_op jit(solution)/shard_map/ppermute | solution.py:23
  123.6 7.4 %collective-permute-start.32 = (f32[128]{0:T(128)S(1)}, f32[128]{0:T(128)S(1)}, u32[]{:S(2)}, u32[]{:S(2)}) collective-permute-start(f32[128]{0:T(128)S(1)} %add_add_fusion.2), channel_id=1, source_target_pairs={{0,32},{32,0},{1,33},{33,1},{2,34},{34,2},{3,35},{35,3},{4,36},{36... | collective-permute-start | bytes 1544 | tf_op jit(solution)/shard_map/ppermute | solution.py:23
  (31 other events, 346.2 us)
Sparse Core Ops, SparseCore 0:
  23.7 44.1 all-gather.1
  75.2 45.6 reduce-scatter.1

commit v13 on v11

--- a/solution.py
+++ b/solution.py
@@ -194,7 +194,8 @@
     act_own = with_layout_constraint(act_own, Layout((0, 1))).reshape(8, 8, 32, HALF)
 
     own_cot = lax.all_to_all(blocks, "z", 0, 0, tiled=True)
-    own_cot, weight, act_half = lax.optimization_barrier((own_cot, weight, act_half))
+    act_half, weight = lax.optimization_barrier((act_half, weight))
+    own_cot, act_half = lax.optimization_barrier((own_cot, act_half))
     right, left, far = (x + 3) % 4, (x + 1) % 4, (x + 2) % 4
     columns = [x, x, far, right, left, far, right, left]
     sides = [yh, 1 - yh, yh, yh, yh, 1 - yh, 1 - yh, 1 - yh]
@@ -203,7 +204,10 @@
     keep, send = weight_call(halves, weight)
 
     other_cot = exchange(own_cot, "yh", 2, 1)
-    other_cot, keep, send, rows, halves = lax.optimization_barrier((other_cot, keep, send, rows, halves))
+    other_keep = exchange(send, "core", 2, 1)
+    other_cot, keep, send, other_keep, rows, halves = lax.optimization_barrier(
+        (other_cot, keep, send, other_keep, rows, halves)
+    )
     right_cot = shift(own_cot, "x", 4, 1)
     left_cot = shift(own_cot, "x", 4, -1)
     far_cot = shift(own_cot, "x", 4, 2)
@@ -214,14 +218,13 @@
     second = [right_cot, left_cot, other_far, other_right, other_left]
 
     kept, *sent = first_call(first, keep, send)
-    second[0], second[1], second[2], send, *sent = lax.optimization_barrier(
-        (second[0], second[1], second[2], send, *sent)
+    second[0], second[1], second[2], *sent = lax.optimization_barrier(
+        (second[0], second[1], second[2], *sent)
     )
     received = [exchange(part, "core", 2, 1) for part in sent]
     others = [exchange(cot, "core", 2, 1) for cot in second]
-    other_keep = exchange(send, "core", 2, 1)
-    *arrived, other_keep, kept, act_own = lax.optimization_barrier(
-        (*first, *second, *others, *received, other_keep, kept, act_own)
+    *arrived, kept, act_own = lax.optimization_barrier(
+        (*first, *second, *others, *received, kept, act_own)
     )
     first, second, others, received = arrived[:FIRST], arrived[FIRST:8], arrived[8:13], arrived[13:]
     act_recv = exchange(act_own, "core", 2, 1)

time: 143 us -> 145 us (1.014)
  waiting for transfers between devices: 49.9 us -> 54.6 us
  starting transfers between devices: 42.1 us -> 40 us
  local copies, waits for them, and re-layouts: 7.61 us -> 5.94 us
    ppermute x27, waiting for transfers between devices: 28.4 us -> 33.9 us  [exchange(): return lax.ppermute(value, axis, [(i, i ^ bit) for i in range(size)])]
    all_to_all x1, waiting for transfers between devices: 8.51 us -> 12.1 us  [body(): own_cot = lax.all_to_all(blocks, 'z', 0, 0, tiled=True)]
    ppermute x5, waiting for transfers between devices: 10.9 us -> 8.59 us  [shift(): lax.ppermute(value, axis, [(i, (i + step) % size) for i in range(size)])]
    ppermute x27, starting transfers between devices: 26.4 us -> 24.4 us  [exchange(): return lax.ppermute(value, axis, [(i, i ^ bit) for i in range(size)])]
    ppermute x1, waiting for transfers between devices: 1.85 us -> 0.01 us  [body(): lax.ppermute(activations, ('yl', 'core'), [(0, 2), (3, 1), (1, 0), (2, 3)])]
    unnamed x52 -> x46, local copies, waits for them, and re-layouts: 5.06 us -> 3.48 us
  transfers between devices with their start and end apart: 37 -> 37, of which waited for: 24 -> 19; matrix products, arithmetic and copies ran while one was open for 5% -> 6% of each run, Pallas kernels for 13% -> 13%
where the time goes in v13:
time: 145 us; the launch traced here: 144 us
  waiting for transfers between devices  54.6 us (38%)
  starting transfers between devices  40 us (28%)
  Pallas kernels  18.5 us (13%)
  between operations  15.6 us (11%)
  other arithmetic  9.12 us (6%)
  local copies, waits for them, and re-layouts  5.94 us (4%)
    ppermute x27, waiting for transfers between devices, exchange(): return lax.ppermute(value, axis, [(i, i ^ bit) for i in range(size)])  33.9 us
    ppermute x27, starting transfers between devices, exchange(): return lax.ppermute(value, axis, [(i, i ^ bit) for i in range(size)])  24.4 us
    all_to_all x1, waiting for transfers between devices, body(): own_cot = lax.all_to_all(blocks, 'z', 0, 0, tiled=True)  12.1 us
    ppermute x5, waiting for transfers between devices, shift(): lax.ppermute(value, axis, [(i, (i + step) % size) for i in range(size)])  8.59 us
    all_to_all x1, starting transfers between devices, body(): own_cot = lax.all_to_all(blocks, 'z', 0, 0, tiled=True)  8.47 us
    pallas_call x1, Pallas kernels, gradient_call(): pl.pallas_call(gradient_kernel, in_specs=[SCALARS] * 2 + [VECTORS] * 10,...  7.04 us
    pallas_call x1, Pallas kernels, second_call(): pl.pallas_call(second_kernel, grid_spec=pltpu.PrefetchScalarGridSpec(num_...  6.57 us
    ppermute x5, starting transfers between devices, shift(): lax.ppermute(value, axis, [(i, (i + step) % size) for i in range(size)])  4.69 us
  transfers between devices with their start and end apart: 37, of which 19 were waited for; matrix products, arithmetic and copies ran while one was open for 6% of the time, Pallas kernels for 13%

profile of v13, /device:TPU:4, one launch (start us, length us, event | category | flops | bytes accessed | tf_op | source)
XLA Modules:
  0.0 143.7 jit_solution(7780147168918770011)
XLA Ops:
  10.6 1.8 %copy.23 = bf16[4,8,8,768]{3,2,0,1:T(8,128)(2,1)} copy(bf16[4,8,8,768]{3,2,1,0:T(8,128)(2,1)} %bitcast.27) | data formatting | bytes 786432 | tf_op jit(solution)/shard_map/reshape | solution.py:192
  12.4 8.5 %all-to-all-start = ((bf16[8,32,768]{2,1,0:T(8,128)(2,1)}), bf16[8,32,768]{2,1,0:T(8,128)(2,1)S(1)}, u32[]{:S(2)}, u32[]{:S(2)}) async-start(bf16[8,32,768]{2,1,0:T(8,128)(2,1)} %bitcast.23), calls=%async_computation | async-start | bytes 786432 | tf_op jit(solution)/shard_map/all_to_all | solution.py:196
  24.9 12.1 %all-to-all-done.refs_0_ = bf16[8,32,768]{2,1,0:T(8,128)(2,1)S(1)} async-done(((bf16[8,32,768]{2,1,0:T(8,128)(2,1)}), bf16[8,32,768]{2,1,0:T(8,128)(2,1)S(1)}, u32[]{:S(2)}, u32[]{:S(2)}) %all-to-all-start) | async-done | bytes 393248 | tf_op jit(solution)/shard_map/all_to_all | solution.py:196
  36.9 2.9 %collective-permute-start = (bf16[8,32,768]{2,1,0:T(8,128)(2,1)S(1)}, bf16[8,32,768]{2,1,0:T(8,128)(2,1)S(1)}, u32[]{:S(2)}, u32[]{:S(2)}) collective-permute-start(bf16[8,32,768]{2,1,0:T(8,128)(2,1)S(1)} %all-to-all-done.refs_0_), channel_id=1, source_target_pairs={{0,32},{32,0},{1,33},{33,1},{2,34},{34,2},{3,35},{35,3},{4,36},{36... | collective-permute-start | bytes 1179656 | tf_op jit(solution)/shard_map/ppermute | solution.py:23
  41.0 2.1 %collective-permute-start.5 = (bf16[8,32,768]{2,1,0:T(8,128)(2,1)S(1)}, bf16[8,32,768]{2,1,0:T(8,128)(2,1)S(1)}, u32[]{:S(2)}, u32[]{:S(2)}) collective-permute-start(bf16[8,32,768]{2,1,0:T(8,128)(2,1)S(1)} %all-to-all-done.refs_0_), channel_id=1, source_target_pairs={{0,64},{64,128},{128,192},{192,0},{1,65},{65,129},{129,193},{193,1... | collective-permute-start | bytes 1179656 | tf_op jit(solution)/shard_map/ppermute | solution.py:27
  43.2 6.4 %collective-permute-done.refs_1_ = bf16[8,32,768]{2,1,0:T(8,128)(2,1)S(1)} collective-permute-done((bf16[8,32,768]{2,1,0:T(8,128)(2,1)S(1)}, bf16[8,32,768]{2,1,0:T(8,128)(2,1)S(1)}, u32[]{:S(2)}, u32[]{:S(2)}) %collective-permute-start) | collective-permute-done | bytes 393248 | tf_op jit(solution)/shard_map/ppermute | solution.py:23
  51.6 1.8 %collective-permute-done.4.refs_2_ = bf16[8,32,768]{2,1,0:T(8,128)(2,1)} collective-permute-done((bf16[8,32,768]{2,1,0:T(8,128)(2,1)S(1)}, bf16[8,32,768]{2,1,0:T(8,128)(2,1)}, u32[]{:S(2)}, u32[]{:S(2)}) %collective-permute-start.4) | collective-permute-done | bytes 393248 | tf_op jit(solution)/shard_map/ppermute | solution.py:27
  54.5 3.9 %shard_map.69 = (f32[8,3,32,384]{3,2,1,0:T(8,128)}, f32[8,32,384]{2,1,0:T(8,128)}, f32[8,32,384]{2,1,0:T(8,128)}, f32[8,32,384]{2,1,0:T(8,128)}) custom-call(bf16[8,32,768]{2,1,0:T(8,128)(2,1)} %copy-done.6, bf16[8,32,768]{2,1,0:T(8,128)(2,1)} %copy-done.21, bf16[8,32,768]{2,1,0:T(8,128)(2,1)} %collective-permute-done.4.refs_2_, bf16[768,384]{1,0:T(8,128)(2,1)} %copy-done.1, ...), custom_call_target="tpu_custom_call" | custom-call | flops 14495514624 | bytes 67108864 | tf_op jit(solution)/shard_map/pallas_call | solution.py:102
  58.4 2.3 %collective-permute-done.5.refs_0_.refs_3_ = bf16[8,32,768]{2,1,0:T(8,128)(2,1)S(1)} collective-permute-done((bf16[8,32,768]{2,1,0:T(8,128)(2,1)S(1)}, bf16[8,32,768]{2,1,0:T(8,128)(2,1)S(1)}, u32[]{:S(2)}, u32[]{:S(2)}) %collective-permute-start.5) | collective-permute-done | bytes 393248 | tf_op jit(solution)/shard_map/ppermute | solution.py:27
  60.9 3.2 %collective-permute-done.7.refs_2_.refs_5_ = bf16[8,32,768]{2,1,0:T(8,128)(2,1)S(1)} collective-permute-done((bf16[8,32,768]{2,1,0:T(8,128)(2,1)}, bf16[8,32,768]{2,1,0:T(8,128)(2,1)S(1)}, u32[]{:S(2)}, u32[]{:S(2)}) %collective-permute-start.7) | collective-permute-done | bytes 393248 | tf_op jit(solution)/shard_map/ppermute | solution.py:23
  64.6 4.3 %collective-permute-done.8.refs_3_.refs_6_ = bf16[8,32,768]{2,1,0:T(8,128)(2,1)S(1)} collective-permute-done((bf16[8,32,768]{2,1,0:T(8,128)(2,1)S(1)}, bf16[8,32,768]{2,1,0:T(8,128)(2,1)S(1)}, u32[]{:S(2)}, u32[]{:S(2)}) %collective-permute-start.8) | collective-permute-done | bytes 393248 | tf_op jit(solution)/shard_map/ppermute | solution.py:27
  73.8 6.6 %shard_map.70 = f32[8,8,32,384]{3,2,1,0:T(8,128)} custom-call(s32[8]{0:T(128)} %stack.47.rows_ref, bf16[8,32,768]{2,1,0:T(8,128)(2,1)} %copy-done.7, bf16[8,32,768]{2,1,0:T(8,128)(2,1)} %copy-done.8, bf16[8,32,768]{2,1,0:T(8,128)(2,1)} %copy-done.11, bf16[8,32,768]{2,1,0:T(8,128)(2,1)} %copy-done.9, bf16[8,32,768]{2,1,0:T(8,128)(2,1)} %copy-done.10, ...), custom_call_target="tpu_custom_call" | custom-call | flops 1509949440 | bytes 8388608 | tf_op jit(solution)/shard_map/pallas_call | solution.py:120
  80.4 7.0 %shard_map.71 = (f32[768,768]{1,0:T(8,128)}, f32[768]{0:T(1024)}, f32[768]{0:T(1024)}) custom-call(s32[8]{0:T(128)} %stack.47.rows_ref, s32[2]{0:T(128)} %copy-done.2, bf16[8,32,768]{2,1,0:T(8,128)(2,1)} %copy-done.6, bf16[8,32,768]{2,1,0:T(8,128)(2,1)} %copy-done.21, bf16[8,32,768]{2,1,0:T(8,128)(2,1)} %collective-permute-done.4.refs_2_, ...), custom_call_target="tpu_custom_call" | custom-call | flops 2415919104 | bytes 9437184 | tf_op jit(solution)/shard_map/pallas_call | solution.py:162
  88.4 2.1 %collective-permute-start.20 = (f32[768]{0:T(1024)}, f32[768]{0:T(1024)S(1)}, u32[]{:S(2)}, u32[]{:S(2)}) collective-permute-start(f32[768]{0:T(1024)} %get-tuple-element.88), channel_id=1, source_target_pairs={{0,128},{64,192},{128,0},{192,64},{1,129},{65,193},{129,1},{193,65... | collective-permute-start | bytes 9224 | tf_op jit(solution)/shard_map/ppermute | solution.py:23
  91.7 2.0 %collective-permute-done.20 = f32[768]{0:T(1024)S(1)} collective-permute-done((f32[768]{0:T(1024)}, f32[768]{0:T(1024)S(1)}, u32[]{:S(2)}, u32[]{:S(2)}) %collective-permute-start.20) | collective-permute-done | bytes 3104 | tf_op jit(solution)/shard_map/ppermute | solution.py:23
  95.6 4.5 %collective-permute-done.22 = f32[768]{0:T(1024)S(1)} collective-permute-done((f32[768]{0:T(1024)S(1)}, f32[768]{0:T(1024)S(1)}, u32[]{:S(2)}, u32[]{:S(2)}) %collective-permute-start.22) | collective-permute-done | bytes 3104 | tf_op jit(solution)/shard_map/ppermute | solution.py:23
  100.1 2.0 %multiply_reduce_fusion = f32[768]{0:T(1024)S(1)} fusion(f32[768,768]{1,0:T(8,128)} %get-tuple-element.87, f32[768]{0:T(1024)S(1)} %get-tuple-element.102), kind=kLoop, calls=%fused_computation.1 | loop fusion | flops 1768704 | bytes 2365440 | tf_op jit(solution)/shard_map/reduce_sum | solution.py:239
  103.4 3.7 %collective-permute-done.24 = f32[2304]{0:T(1024)S(1)} collective-permute-done((f32[2304]{0:T(1024)S(1)}, f32[2304]{0:T(1024)S(1)}, u32[]{:S(2)}, u32[]{:S(2)}) %collective-permute-start.24) | collective-permute-done | bytes 9248 | tf_op jit(solution)/shard_map/ppermute | solution.py:23
  107.6 3.7 %collective-permute-done.25 = f32[2304]{0:T(1024)S(1)} collective-permute-done((f32[2304]{0:T(1024)S(1)}, f32[2304]{0:T(1024)S(1)}, u32[]{:S(2)}, u32[]{:S(2)}) %collective-permute-start.25) | collective-permute-done | bytes 9248 | tf_op jit(solution)/shard_map/ppermute | solution.py:23
  111.3 3.0 %collective-permute-start.27 = (f32[2304]{0:T(1024)S(1)}, f32[2304]{0:T(1024)S(1)}, u32[]{:S(2)}, u32[]{:S(2)}) collective-permute-start(f32[2304]{0:T(1024)S(1)} %add.117), channel_id=1, source_target_pairs={{0,4},{1,5},{2,6},{3,7},{4,0},{5,1},{6,2},{7,3},{8,12},{9,13},{10,... | collective-permute-start | bytes 27656 | tf_op jit(solution)/shard_map/ppermute | solution.py:23
  114.3 3.5 %collective-permute-start.26 = (f32[2304]{0:T(1024)S(1)}, f32[2304]{0:T(1024)S(1)}, u32[]{:S(2)}, u32[]{:S(2)}) collective-permute-start(f32[2304]{0:T(1024)S(1)} %add.117), channel_id=1, source_target_pairs={{0,2},{1,3},{2,0},{3,1},{4,6},{5,7},{6,4},{7,5},{8,10},{9,11},{10,... | collective-permute-start | bytes 27656 | tf_op jit(solution)/shard_map/ppermute | solution.py:23
  121.7 2.2 %collective-permute-start.30 = (f32[128]{0:T(128)S(1)}, f32[128]{0:T(128)S(1)}, u32[]{:S(2)}, u32[]{:S(2)}) collective-permute-start(f32[128]{0:T(128)S(1)} %get-tuple-element.100), channel_id=1, source_target_pairs={{0,128},{64,192},{128,0},{192,64},{1,129},{65,193},{129,1},{193,65... | collective-permute-start | bytes 1544 | tf_op jit(solution)/shard_map/ppermute | solution.py:23
  128.9 2.9 %collective-permute-done.32 = f32[128]{0:T(128)S(1)} collective-permute-done((f32[128]{0:T(128)S(1)}, f32[128]{0:T(128)S(1)}, u32[]{:S(2)}, u32[]{:S(2)}) %collective-permute-start.32) | collective-permute-done | bytes 544 | tf_op jit(solution)/shard_map/ppermute | solution.py:23
  135.0 1.9 %multiply_divide_fusion = f32[768,768]{1,0:T(8,128)} fusion(f32[768,768]{1,0:T(8,128)S(1)} %copy-done.4, f32[]{:T(128)S(6)} %max_shard_map.3, f32[]{:T(128)S(6)} %div.26, f32[768]{0:T(1024)S(1)} %get-tuple-element.101, f32[768]{0:T(1024)S(1)} %get-tuple-element.103), kind=kLoop, calls=%fused_computation | loop fusion | flops 2359296 | bytes 4724744 | tf_op jit(solution)/shard_map/div | solution.py:262
  (124 shorter events, 33.8 us)
Async XLA Ops:
  8.3 12.6 %collective-permute-start.1 = (bf16[256,192]{1,0:T(8,128)(2,1)S(1)}, bf16[256,192]{1,0:T(8,128)(2,1)S(1)}, u32[]{:S(2)}, u32[]{:S(2)}) collective-permute-start(bf16[256,192]{1,0:T(8,128)(2,1)S(1)} %copy.18), channel_id=1, source_target_pairs={{0,16},{24,8},{8,0},{16,24},{1,17},{25,9},{9,1},{17,25},{2,18},{26... | collective-permute-start | bytes 294920 | tf_op jit(solution)/shard_map/ppermute | solution.py:182
  9.9 11.0 %collective-permute-start.2 = (bf16[256,192]{1,0:T(8,128)(2,1)S(1)}, bf16[256,192]{1,0:T(8,128)(2,1)S(1)}, u32[]{:S(2)}, u32[]{:S(2)}) collective-permute-start(bf16[256,192]{1,0:T(8,128)(2,1)S(1)} %copy.18), channel_id=1, source_target_pairs={{8,16},{16,8},{9,17},{17,9},{10,18},{18,10},{11,19},{19,11},{12,20... | collective-permute-start | bytes 294920 | tf_op jit(solution)/shard_map/ppermute | solution.py:183
  12.4 24.6 %all-to-all-start = ((bf16[8,32,768]{2,1,0:T(8,128)(2,1)}), bf16[8,32,768]{2,1,0:T(8,128)(2,1)S(1)}, u32[]{:S(2)}, u32[]{:S(2)}) async-start(bf16[8,32,768]{2,1,0:T(8,128)(2,1)} %bitcast.23), calls=%async_computation | async-start | bytes 786432 | tf_op jit(solution)/shard_map/all_to_all | solution.py:196
  20.8 52.8 %all-gather.2.cloned.1.call-start = ((), (), s32[]{:S(2)}) async-start(), calls=%async_computation.2 | async-start | bytes 1769472 | tf_op jit(solution)/shard_map/all_gather | solution.py:193
  21.8 102.1 %reduce-scatter.2.cloned.1.call-start = ((), (), s32[]{:S(2)}) async-start(), calls=%async_computation.3 | async-start | bytes 3538944 | tf_op jit(solution)/shard_map/reduce_scatter | solution.py:233
  23.8 19.4 %collective-permute-start.3 = (bf16[768,384]{1,0:T(8,128)(2,1)S(1)}, bf16[768,384]{1,0:T(8,128)(2,1)S(1)}, u32[]{:S(2)}, u32[]{:S(2)}) collective-permute-start(bf16[768,384]{1,0:T(8,128)(2,1)S(1)} %get-tuple-element.55.refs_4_), channel_id=1, source_target_pairs={{0,8},{8,0},{1,9},{9,1},{2,10},{10,2},{3,11},{11,3},{4,12},{12,4},... | collective-permute-start | bytes 1769480 | tf_op jit(solution)/shard_map/ppermute | solution.py:23
  36.9 12.6 %collective-permute-start = (bf16[8,32,768]{2,1,0:T(8,128)(2,1)S(1)}, bf16[8,32,768]{2,1,0:T(8,128)(2,1)S(1)}, u32[]{:S(2)}, u32[]{:S(2)}) collective-permute-start(bf16[8,32,768]{2,1,0:T(8,128)(2,1)S(1)} %all-to-all-done.refs_0_), channel_id=1, source_target_pairs={{0,32},{32,0},{1,33},{33,1},{2,34},{34,2},{3,35},{35,3},{4,36},{36... | collective-permute-start | bytes 1179656 | tf_op jit(solution)/shard_map/ppermute | solution.py:23
  39.8 13.6 %collective-permute-start.4 = (bf16[8,32,768]{2,1,0:T(8,128)(2,1)S(1)}, bf16[8,32,768]{2,1,0:T(8,128)(2,1)}, u32[]{:S(2)}, u32[]{:S(2)}) collective-permute-start(bf16[8,32,768]{2,1,0:T(8,128)(2,1)S(1)} %all-to-all-done.refs_0_), channel_id=1, source_target_pairs={{0,128},{64,192},{128,0},{192,64},{1,129},{65,193},{129,1},{193,65... | collective-permute-start | bytes 1179656 | tf_op jit(solution)/shard_map/ppermute | solution.py:27
  41.0 19.7 %collective-permute-start.5 = (bf16[8,32,768]{2,1,0:T(8,128)(2,1)S(1)}, bf16[8,32,768]{2,1,0:T(8,128)(2,1)S(1)}, u32[]{:S(2)}, u32[]{:S(2)}) collective-permute-start(bf16[8,32,768]{2,1,0:T(8,128)(2,1)S(1)} %all-to-all-done.refs_0_), channel_id=1, source_target_pairs={{0,64},{64,128},{128,192},{192,0},{1,65},{65,129},{129,193},{193,1... | collective-permute-start | bytes 1179656 | tf_op jit(solution)/shard_map/ppermute | solution.py:27
  43.1 17.8 %collective-permute-start.6 = (bf16[8,32,768]{2,1,0:T(8,128)(2,1)S(1)}, bf16[8,32,768]{2,1,0:T(8,128)(2,1)S(1)}, u32[]{:S(2)}, u32[]{:S(2)}) collective-permute-start(bf16[8,32,768]{2,1,0:T(8,128)(2,1)S(1)} %all-to-all-done.refs_0_), channel_id=1, source_target_pairs={{0,192},{64,0},{128,64},{192,128},{1,193},{65,1},{129,65},{193,129... | collective-permute-start | bytes 1179656 | tf_op jit(solution)/shard_map/ppermute | solution.py:27
  49.6 19.3 %collective-permute-start.8 = (bf16[8,32,768]{2,1,0:T(8,128)(2,1)S(1)}, bf16[8,32,768]{2,1,0:T(8,128)(2,1)S(1)}, u32[]{:S(2)}, u32[]{:S(2)}) collective-permute-start(bf16[8,32,768]{2,1,0:T(8,128)(2,1)S(1)} %collective-permute-done.refs_1_), channel_id=1, source_target_pairs={{0,64},{64,128},{128,192},{192,0},{1,65},{65,129},{129,193},{193,1... | collective-permute-start | bytes 1179656 | tf_op jit(solution)/shard_map/ppermute | solution.py:27
  50.8 18.1 %collective-permute-start.9 = (bf16[8,32,768]{2,1,0:T(8,128)(2,1)S(1)}, bf16[8,32,768]{2,1,0:T(8,128)(2,1)S(1)}, u32[]{:S(2)}, u32[]{:S(2)}) collective-permute-start(bf16[8,32,768]{2,1,0:T(8,128)(2,1)S(1)} %collective-permute-done.refs_1_), channel_id=1, source_target_pairs={{0,192},{64,0},{128,64},{192,128},{1,193},{65,1},{129,65},{193,129... | collective-permute-start | bytes 1179656 | tf_op jit(solution)/shard_map/ppermute | solution.py:27
  53.4 10.6 %collective-permute-start.7 = (bf16[8,32,768]{2,1,0:T(8,128)(2,1)}, bf16[8,32,768]{2,1,0:T(8,128)(2,1)S(1)}, u32[]{:S(2)}, u32[]{:S(2)}) collective-permute-start(bf16[8,32,768]{2,1,0:T(8,128)(2,1)} %collective-permute-done.4.refs_2_), channel_id=1, source_target_pairs={{0,32},{32,0},{1,33},{33,1},{2,34},{34,2},{3,35},{35,3},{4,36},{36... | collective-permute-start | bytes 1179656 | tf_op jit(solution)/shard_map/ppermute | solution.py:23
  64.1 5.3 %collective-permute-start.10 = (bf16[8,32,768]{2,1,0:T(8,128)(2,1)S(1)}, bf16[8,32,768]{2,1,0:T(8,128)(2,1)S(1)}, u32[]{:S(2)}, u32[]{:S(2)}) collective-permute-start(bf16[8,32,768]{2,1,0:T(8,128)(2,1)S(1)} %collective-permute-done.5.refs_0_.refs_3_), channel_id=1, source_target_pairs={{0,8},{8,0},{1,9},{9,1},{2,10},{10,2},{3,11},{11,3},{4,12},{12,4},... | collective-permute-start | bytes 1179656 | tf_op jit(solution)/shard_map/ppermute | solution.py:23
  64.1 5.4 %collective-permute-start.11 = (bf16[8,32,768]{2,1,0:T(8,128)(2,1)S(1)}, bf16[8,32,768]{2,1,0:T(8,128)(2,1)S(1)}, u32[]{:S(2)}, u32[]{:S(2)}) collective-permute-start(bf16[8,32,768]{2,1,0:T(8,128)(2,1)S(1)} %collective-permute-done.6.refs_1_.refs_4_), channel_id=1, source_target_pairs={{0,8},{8,0},{1,9},{9,1},{2,10},{10,2},{3,11},{11,3},{4,12},{12,4},... | collective-permute-start | bytes 1179656 | tf_op jit(solution)/shard_map/ppermute | solution.py:23
  64.6 5.3 %collective-permute-start.12 = (bf16[8,32,768]{2,1,0:T(8,128)(2,1)S(1)}, bf16[8,32,768]{2,1,0:T(8,128)(2,1)S(1)}, u32[]{:S(2)}, u32[]{:S(2)}) collective-permute-start(bf16[8,32,768]{2,1,0:T(8,128)(2,1)S(1)} %collective-permute-done.7.refs_2_.refs_5_), channel_id=1, source_target_pairs={{0,8},{8,0},{1,9},{9,1},{2,10},{10,2},{3,11},{11,3},{4,12},{12,4},... | collective-permute-start | bytes 1179656 | tf_op jit(solution)/shard_map/ppermute | solution.py:23
  73.6 6.8 %collective-permute-start.18 = (bf16[8,8,32,384]{3,2,1,0:T(8,128)(2,1)}, bf16[8,8,32,384]{3,2,1,0:T(8,128)(2,1)}, u32[]{:S(2)}, u32[]{:S(2)}) collective-permute-start(bf16[8,8,32,384]{3,2,1,0:T(8,128)(2,1)} %bitcast.28), channel_id=1, source_target_pairs={{0,8},{8,0},{1,9},{9,1},{2,10},{10,2},{3,11},{11,3},{4,12},{12,4},... | collective-permute-start | bytes 4718600 | tf_op jit(solution)/shard_map/ppermute | solution.py:23
  88.4 5.3 %collective-permute-start.20 = (f32[768]{0:T(1024)}, f32[768]{0:T(1024)S(1)}, u32[]{:S(2)}, u32[]{:S(2)}) collective-permute-start(f32[768]{0:T(1024)} %get-tuple-element.88), channel_id=1, source_target_pairs={{0,128},{64,192},{128,0},{192,64},{1,129},{65,193},{129,1},{193,65... | collective-permute-start | bytes 9224 | tf_op jit(solution)/shard_map/ppermute | solution.py:23
  95.0 5.1 %collective-permute-start.22 = (f32[768]{0:T(1024)S(1)}, f32[768]{0:T(1024)S(1)}, u32[]{:S(2)}, u32[]{:S(2)}) collective-permute-start(f32[768]{0:T(1024)S(1)} %add_add_fusion.1), channel_id=1, source_target_pairs={{0,32},{32,0},{1,33},{33,1},{2,34},{34,2},{3,35},{35,3},{4,36},{36... | collective-permute-start | bytes 9224 | tf_op jit(solution)/shard_map/ppermute | solution.py:23
  111.3 6.5 %collective-permute-start.28 = (f32[2304]{0:T(1024)S(1)}, f32[2304]{0:T(1024)S(1)}, u32[]{:S(2)}, u32[]{:S(2)}) collective-permute-start(f32[2304]{0:T(1024)S(1)} %add.117), channel_id=1, source_target_pairs={{0,6},{1,7},{2,4},{3,5},{4,2},{5,3},{6,0},{7,1},{8,14},{9,15},{10,... | collective-permute-start | bytes 27656 | tf_op jit(solution)/shard_map/ppermute | solution.py:23
  111.3 8.0 %collective-permute-start.27 = (f32[2304]{0:T(1024)S(1)}, f32[2304]{0:T(1024)S(1)}, u32[]{:S(2)}, u32[]{:S(2)}) collective-permute-start(f32[2304]{0:T(1024)S(1)} %add.117), channel_id=1, source_target_pairs={{0,4},{1,5},{2,6},{3,7},{4,0},{5,1},{6,2},{7,3},{8,12},{9,13},{10,... | collective-permute-start | bytes 27656 | tf_op jit(solution)/shard_map/ppermute | solution.py:23
  114.3 5.4 %collective-permute-start.26 = (f32[2304]{0:T(1024)S(1)}, f32[2304]{0:T(1024)S(1)}, u32[]{:S(2)}, u32[]{:S(2)}) collective-permute-start(f32[2304]{0:T(1024)S(1)} %add.117), channel_id=1, source_target_pairs={{0,2},{1,3},{2,0},{3,1},{4,6},{5,7},{6,4},{7,5},{8,10},{9,11},{10,... | collective-permute-start | bytes 27656 | tf_op jit(solution)/shard_map/ppermute | solution.py:23
  121.7 5.0 %collective-permute-start.30 = (f32[128]{0:T(128)S(1)}, f32[128]{0:T(128)S(1)}, u32[]{:S(2)}, u32[]{:S(2)}) collective-permute-start(f32[128]{0:T(128)S(1)} %get-tuple-element.100), channel_id=1, source_target_pairs={{0,128},{64,192},{128,0},{192,64},{1,129},{65,193},{129,1},{193,65... | collective-permute-start | bytes 1544 | tf_op jit(solution)/shard_map/ppermute | solution.py:23
  125.1 6.7 %collective-permute-start.33 = (f32[8,32,192]{2,1,0:T(8,128)S(1)}, f32[8,32,192]{2,1,0:T(8,128)S(1)}, u32[]{:S(2)}, u32[]{:S(2)}) collective-permute-start(f32[8,32,192]{2,1,0:T(8,128)S(1)} %slice_select_fusion), channel_id=1, source_target_pairs={{0,16},{16,0},{1,17},{17,1},{2,18},{18,2},{3,19},{19,3},{4,20},{20... | collective-permute-start | bytes 589832 | tf_op jit(solution)/shard_map/ppermute | solution.py:23
  (35 other events, 343.0 us)
Sparse Core Ops, SparseCore 0:
  23.5 41.5 all-gather.1
  80.6 41.0 reduce-scatter.1
